TPU v7x, 32 devices: a whole 2x2x4 slice. The times are simulated.
32 devices in a mesh: expert: 8 (over z, x), dp: 4 (over y, core).
Axes of the slice: x: 2, y: 2, z: 4, core: 2. Of those that a mesh axis runs over, the one named last changes fastest.
Arguments:
- tokens: bfloat16 [2048, 2048], P(('expert', 'dp')), may hold values from -6 to 6
- routes: int32 [2048, 8], P(('expert', 'dp')), may hold values from 0 to 31, all different within a row; in each aligned block of 64 rows (0 to 63, 64 to 127, ...) at most 20 rows name the same one
- probs: float32 [2048, 8], P(('expert', 'dp')), may hold values from 0.02 to 1
- cotangent: bfloat16 [2048, 2048], P(('expert', 'dp')), may hold values from -6 to 6
- w_gate: bfloat16 [32, 2048, 384], P('expert'), may hold values from -0.125 to 0.125
- w_up: bfloat16 [32, 2048, 384], P('expert'), may hold values from -0.125 to 0.125
- w_down: bfloat16 [32, 2048, 384], P('expert'), may hold values from -0.3125 to 0.3125
Outputs:
- mixed: bfloat16 [2048, 2048], P(('expert', 'dp'))
- token_grad: bfloat16 [2048, 2048], P(('expert', 'dp'))
- prob_grad: float32 [2048, 8], P(('expert', 'dp'))
- gate_grad: bfloat16 [32, 2048, 384], P('expert', 'dp')
- up_grad: bfloat16 [32, 2048, 384], P('expert', 'dp')
- down_grad: bfloat16 [32, 2048, 384], P('expert', 'dp')
Inputs may be any that keep to these rules, and one draw needn't show every extreme that they name: `routes`: each row names 8 different experts. Among the 64 rows of one device no expert is named by more than 20 rows, a bound that some block reaches.
All inputs are finite; a program needn't handle non-finite values.
Results may differ from a plain program's by a relative error of at most 0.0095.
Values may be sent and summed in bfloat16 or wider, within the bound.
No kernel may reach another device: no remote copies, remote signals or barrier semaphores. Data moves between devices by JAX's collectives and lax.ppermute only.
A program may use at most 128 MiB of HBM per device.

v0:
```python
import functools

import jax
import jax.numpy as jnp
from jax import lax
from jax.experimental import pallas as pl
from jax.experimental.pallas import tpu as pltpu
from jax.sharding import PartitionSpec as P


F32 = jnp.float32
BF16 = jnp.bfloat16
LANES = 128
VMEM_LIMIT = 60 * 1024 * 1024


def round_up(value, unit):
    return -(-value // unit) * unit


def dot(a, b):
    return jnp.dot(a, b, preferred_element_type=F32)


def dot_nt(a, b):
    return lax.dot_general(a, b, (((1,), (1,)), ((), ())), preferred_element_type=F32)


def dot_tn(a, b):
    return lax.dot_general(a, b, (((0,), (0,)), ((), ())), preferred_element_type=F32)


def iota(shape, dim):
    return lax.broadcasted_iota(jnp.int32, shape, dim)


def load_blocks(blocks, held, sems):
    copies, start = [], 0
    for i, block in enumerate(blocks):
        size = block.shape[0]
        copies.append(pltpu.make_async_copy(block, held.at[pl.ds(start, size), :], sems.at[i]))
        start += size
    for copy in copies:
        copy.start()
    for copy in copies:
        copy.wait()


def tiles(width, tile=512):
    return [(start, min(start + tile, width)) for start in range(0, width, tile)]


def half_of(which, width):
    return pl.ds(pl.multiple_of(which * (width // 2), LANES), width // 2)


def hidden_kernel(cfg, first_ref, far_ref, *refs):
    parts, local, cap, cap_pad, top = cfg
    blocks, refs = refs[:parts], refs[parts:]
    gate_ref, up_ref, pre_ref, act_ref, info_ref, pick_ref, combine_ref, keep_ref = refs[:8]
    held, rows_ref, sems = refs[8:]
    expert = pl.program_id(0)
    tokens = held.shape[0]
    width, hidden = gate_ref.shape[1:]

    @pl.when(expert == 0)
    def _():
        load_blocks(blocks, held, sems)
        meta = held[:, width:].astype(F32).astype(jnp.int32)
        lane = iota(meta.shape, 1)
        hits = jnp.zeros(meta.shape, F32)
        for i in range(local):
            named = (meta == first_ref[0] + i) & (lane < top)
            hit = jnp.sum(jnp.where(named, 1.0, 0.0), axis=1, keepdims=True)
            hits = hits + jnp.where(lane == i, hit, 0.0)
        step = min(tokens, 256)
        below = (iota((step, step), 0) >= iota((step, step), 1)).astype(F32).astype(BF16)
        carry = jnp.zeros((1, LANES), F32)
        slots = []
        for start in range(0, tokens, step):
            part = hits[start:start + step]
            rank = dot(below, part.astype(BF16)) + carry
            carry = rank[step - 1:step]
            slots.append(jnp.where(part > 0.0, rank - 1.0, -1.0))
        slots = jnp.concatenate(slots, axis=0)
        slots_t = jnp.transpose(slots)
        places = iota((tokens, cap_pad), 1).astype(F32)
        places_t = iota((cap, tokens), 0).astype(F32)
        for i in range(local):
            hit = slots[:, i:i + 1] == places
            combine_ref[:, i * cap_pad:(i + 1) * cap_pad] = jnp.where(hit, 1.0, 0.0).astype(BF16)
            hit = slots_t[i:i + 1, :] == places_t
            pick_ref[i * cap:(i + 1) * cap, :] = jnp.where(hit, 1.0, 0.0).astype(BF16)
        for start, stop in tiles(held.shape[1]):
            rows_ref[:, start:stop] = dot(pick_ref[...], held[:, start:stop]).astype(BF16)
        keep_ref[...] = held[:, half_of(far_ref[0], width)]

    here = pl.ds(pl.multiple_of(expert * cap, 16), cap)
    pick = pick_ref[here, :].astype(F32)
    token = jnp.sum(pick * iota(pick.shape, 1).astype(F32), axis=1, keepdims=True)
    token = jnp.where(jnp.sum(pick, axis=1, keepdims=True) > 0.0, token, -128.0).astype(jnp.int32)
    meta = rows_ref[here, width:].astype(F32)
    lane = iota(meta.shape, 1)
    named = (meta.astype(jnp.int32) == first_ref[0] + expert) & (lane < top)
    shares = sum(pltpu.roll(meta, LANES - top * (i + 1), 1) for i in range(3))
    share = jnp.sum(jnp.where(named, shares, 0.0), axis=1, keepdims=True)
    info_ref[0] = jnp.where(lane < top, jnp.where(named, 1.0, 0.0), share)

    rows = rows_ref[here, :width]
    gate_pre = dot(rows, gate_ref[0])
    up_pre = dot(rows, up_ref[0])
    pre_ref[0, :, :hidden] = gate_pre
    pre_ref[0, :, hidden:] = up_pre
    active = gate_pre * jax.nn.sigmoid(gate_pre) * up_pre
    act_ref[0, :, :hidden] = (share * active).astype(BF16)
    token_pair = jnp.where(lane == 0, token >> 7, jnp.where(lane == 1, token & 127, 0))
    act_ref[0, :, hidden:] = token_pair.astype(F32).astype(BF16)


def store_parts(plan, value, here, refs):
    refs[0][:, here] = value[:refs[0].shape[0]]
    line, size = refs[0].shape[0], refs[0].shape[0] // sum(len(items) for items in plan)
    for ref, items in zip(refs[1:], plan):
        for i, block in enumerate(items):
            start = line + block * size
            ref[i * size:(i + 1) * size, here] = value[start:start + size]


def mixed_kernel(cfg, far_ref, act_ref, combine_ref, down_ref, *refs):
    plan, levels, local, cap, cap_pad = cfg
    blocks, refs = refs[:levels], refs[levels:]
    outs, give_ref, spread, sems = refs[:-3], refs[-3], refs[-2], refs[-1]
    size = blocks[0].shape[0]
    here = half_of(1 - far_ref[0], blocks[0].shape[1])
    copies = [pltpu.make_async_copy(block.at[:, here], give_ref.at[pl.ds(i * size, size), :], sems.at[i])
              for i, block in enumerate(blocks)]
    hidden = down_ref.shape[2]
    tile = down_ref.shape[1]
    step = pl.program_id(0)

    @pl.when(step == 0)
    def _():
        for copy in copies:
            copy.start()
        for e in range(local):
            here = combine_ref[:, e * cap_pad:e * cap_pad + cap]
            spread[:, e * hidden:(e + 1) * hidden] = dot(here, act_ref[e, :, :hidden]).astype(BF16)

    total = dot_nt(spread[:, :hidden], down_ref[0])
    for e in range(1, local):
        total = total + dot_nt(spread[:, e * hidden:(e + 1) * hidden], down_ref[e])
    store_parts(plan, total.astype(BF16), pl.ds(pl.multiple_of(step * tile, tile), tile), outs)

    @pl.when(step == pl.num_programs(0) - 1)
    def _():
        for copy in copies:
            copy.wait()


def grad_kernel(cfg, far_ref, *refs):
    parts, local, cap, cap_pad, top = cfg
    blocks, refs = refs[:parts], refs[parts:]
    pick_ref, combine_ref, down_ref, pre_ref, info_ref, d_gate_ref, d_up_ref, tail_ref, keep_ref, give_ref = refs[:10]
    held, rows_ref, tails, sems = refs[10:]
    expert = pl.program_id(0)
    hidden = down_ref.shape[2]

    @pl.when(expert == 0)
    def _():
        load_blocks(blocks, held, sems)
        tails[...] = jnp.zeros(tails.shape, BF16)
        for start, stop in tiles(held.shape[1]):
            rows_ref[:, start:stop] = dot(pick_ref[...], held[:, start:stop]).astype(BF16)
        width = held.shape[1]
        keep_ref[...] = held[:, half_of(far_ref[0], width)]
        give_ref[...] = held[give_ref.shape[0]:, half_of(1 - far_ref[0], width)]

    info = info_ref[0]
    lane = iota(info.shape, 1)
    share = info[:, top:top + 1]
    gate_pre, up_pre = pre_ref[0, :, :hidden], pre_ref[0, :, hidden:]
    sig = jax.nn.sigmoid(gate_pre)
    silu = gate_pre * sig
    d_raw = dot(rows_ref[pl.ds(pl.multiple_of(expert * cap, 16), cap), :], down_ref[0])
    share_grad = jnp.sum(silu * up_pre * d_raw, axis=1, keepdims=True)
    d_active = share * d_raw
    d_gate_ref[0] = (d_active * up_pre * sig * (1.0 + gate_pre * (1.0 - sig))).astype(BF16)
    d_up_ref[0] = (d_active * silu).astype(BF16)
    placed = jnp.where((lane < top) & (info > 0.0), share_grad, 0.0)
    high = placed.astype(BF16)
    rest = placed - high.astype(F32)
    middle = rest.astype(BF16)
    low = (rest - middle.astype(F32)).astype(BF16)
    tail = high.astype(F32) + pltpu.roll(middle.astype(F32), top, 1) + pltpu.roll(low.astype(F32), 2 * top, 1)
    tails[pl.ds(pl.multiple_of(expert * cap_pad, cap_pad), cap), :] = tail.astype(BF16)

    @pl.when(expert == local - 1)
    def _():
        tail_ref[...] = dot(combine_ref[...], tails[...]).astype(BF16)


def input_kernel(cfg, d_gate_ref, d_up_ref, combine_ref, tail_ref, gate_ref, up_ref, *refs):
    plan, local, cap, cap_pad = cfg
    outs, rows = refs[:-1], refs[-1]
    tile, hidden = gate_ref.shape[1:]
    step = pl.program_id(0)

    @pl.when(step == 0)
    def _():
        rows[...] = jnp.zeros(rows.shape, BF16)
        width = outs[0].shape[1] - LANES
        store_parts(plan, tail_ref[...], slice(width, width + LANES), outs)

    for e in range(local):
        part = dot_nt(d_gate_ref[e], gate_ref[e]) + dot_nt(d_up_ref[e], up_ref[e])
        rows[e * cap_pad:e * cap_pad + cap, :] = part.astype(BF16)
    total = dot(combine_ref[...], rows[...]).astype(BF16)
    store_parts(plan, total, pl.ds(pl.multiple_of(step * tile, tile), tile), outs)


def store_halves(part, near_ref, both, keep_ref, give_ref):
    both[...] = part.astype(BF16)
    size = keep_ref.shape[1]
    keep_ref[0] = both[pl.ds(pl.multiple_of(near_ref[0] * size, 16), size), :]
    give_ref[0] = both[pl.ds(pl.multiple_of((1 - near_ref[0]) * size, 16), size), :]


def down_kernel(cap, near_ref, pick_ref, *refs):
    x_refs, c_refs, (act_ref, act_far_ref, rows_ref, keep_ref, give_ref, c_rows, acts, both) = refs[:3], refs[3:6], refs[6:]
    hidden = acts.shape[1]
    line = x_refs[1].shape[0]
    acts[:cap, :] = act_ref[0, :, :hidden]
    acts[cap:, :] = act_far_ref[0, :, :hidden]
    pair = act_far_ref[0, :, hidden:].astype(F32)
    token = pair[:, 0:1] * 128.0 + pair[:, 1:2]
    pick = pick_ref[...]
    pick_far = jnp.where(token == iota(pick.shape, 1).astype(F32), 1.0, 0.0).astype(BF16)
    for (own, far, far_pair), rows in ((x_refs, rows_ref.at[0]), (c_refs, c_rows)):
        rows[:cap, :] = dot(pick, own[...]).astype(BF16)
        rows[cap:, :] = (dot(pick_far[:, :line], far[...]) + dot(pick_far[:, line:], far_pair[...])).astype(BF16)
    store_halves(dot_tn(c_rows[...], acts[...]), near_ref, both, keep_ref, give_ref)


def partial_kernel(cap, near_ref, rows_ref, own_ref, far_ref, keep_ref, give_ref, grads, both):
    grads[:cap, :] = own_ref[0]
    grads[cap:, :] = far_ref[0]
    store_halves(dot_tn(rows_ref[0], grads[...]), near_ref, both, keep_ref, give_ref)


def cut_kernel(half, plan, word_ref, *refs):
    count = 1 + max(i for i, _, _, _ in plan)
    blocks, outs, sems = refs[:count], refs[count:-1], refs[-1]
    copies = []
    for i, flip, out, row in plan:
        which = 1 - word_ref[0] if flip else word_ref[0]
        here = pl.ds(pl.multiple_of(which * half, LANES), half)
        there = outs[out].at[pl.ds(row, blocks[i].shape[0]), :]
        copies.append(pltpu.make_async_copy(blocks[i].at[:, here], there, sems.at[len(copies)]))
    for copy in copies:
        copy.start()
    for copy in copies:
        copy.wait()


def swap(value, bit, count):
    return lax.ppermute(value, "dp", [(i, i ^ bit) for i in range(count)])


def exchange(value, bit, count):
    return lax.ppermute(value, "expert", [(i, i ^ bit) for i in range(count)])


def fence(*values):
    leaves, tree = jax.tree.flatten(values)
    return jax.tree.unflatten(tree, lax.optimization_barrier(tuple(leaves)))


def split3(value):
    high = lax.reduce_precision(value, 8, 7)
    rest = value - high
    middle = lax.reduce_precision(rest, 8, 7)
    return [high.astype(BF16), middle.astype(BF16), (rest - middle).astype(BF16)]


def shards(tokens, routes, probs, cotangent, w_gate, w_up, w_down):
    tok_rows, top = routes.shape
    local, width, hidden = w_gate.shape
    n_exp = lax.axis_size("expert")
    n_dp = lax.axis_size("dp")
    experts = local * n_exp
    cap = 5 * tok_rows * top // (4 * experts) * n_exp
    cap_pad = round_up(cap, LANES)
    total = n_exp * tok_rows
    levels = n_exp // 2
    line = levels * tok_rows
    wide = width + LANES
    tile = min(width, 512)
    columns = width // n_dp
    half = width // 2
    far_bit = n_dp // 2
    my_dp = lax.axis_index("dp")
    far = jnp.where((my_dp & far_bit) > 0, 1, 0)
    near = jnp.where((my_dp & 1) > 0, 1, 0)
    near_word = near.astype(jnp.int32).reshape(1)
    far_word = far.astype(jnp.int32).reshape(1)
    first = (lax.axis_index("expert") * local).astype(jnp.int32).reshape(1)
    line_blocks = list(range(0, n_exp, 2))
    sides = [k for k in line_blocks if k & 2 and k > 2]
    folds = [k ^ 2 for k in sides]
    groups = [sides, folds, [2, 0]]
    plan = [[k // 2 for k in group] for group in groups]
    upper_bits = [1 << i for i in range(2, n_exp.bit_length() - 1)]

    def send(value, bit):
        return exchange(value, bit, n_exp)

    def gather_upper(value):
        blocks = {0: value}
        for bit in reversed(upper_bits):
            blocks.update({k | bit: send(block, bit) for k, block in list(blocks.items())})
        return blocks

    any_space = pl.BlockSpec(memory_space=pl.ANY)
    smem = pl.BlockSpec(memory_space=pltpu.SMEM)
    params = pltpu.CompilerParams(dimension_semantics=("arbitrary",), vmem_limit_bytes=VMEM_LIMIT)

    def by_expert(*shape):
        return pl.BlockSpec((1,) + shape, lambda e: (e,) + (0,) * len(shape))

    def whole(*shape):
        return pl.BlockSpec(shape, lambda e: (0,) * len(shape))

    def sds(shape, dtype):
        return jax.ShapeDtypeStruct(shape, dtype)

    def cost(gflop, mbyte):
        return pl.CostEstimate(flops=gflop * 10**6, bytes_accessed=mbyte * 10**3, transcendentals=0)

    def cut_blocks(word, blocks, size, wanted, name):
        plan, rows = [], []
        for out, items in enumerate(wanted):
            rows.append(0)
            for i, flip in items:
                plan.append((i, flip, out, rows[out]))
                rows[out] += blocks[i].shape[0]
        return pl.pallas_call(
            functools.partial(cut_kernel, size, plan),
            in_specs=[smem] + [any_space] * len(blocks),
            out_specs=[pl.BlockSpec(memory_space=pltpu.VMEM)] * len(wanted),
            out_shape=[sds((n, size), BF16) for n in rows],
            scratch_shapes=[pltpu.SemaphoreType.DMA((len(plan),))],
            compiler_params=pltpu.CompilerParams(vmem_limit_bytes=VMEM_LIMIT),
            cost_estimate=cost(0, 2),
            name=name,
        )(word, *blocks)

    def cut_far(blocks, name):
        return cut_blocks(far_word, blocks, width // 2, [[(i, 1) for i in range(len(blocks))]], name)[0]

    by_columns = pl.BlockSpec((local, tile, hidden), lambda j: (0, j, 0))
    weight_spec = by_expert(width, hidden)
    parts = n_exp
    cfg = (parts, local, cap, cap_pad, top)

    totals = jnp.sum(probs, axis=1, keepdims=True)
    share = probs / totals
    meta = jnp.concatenate([routes.astype(BF16)] + split3(share), axis=1)
    meta = jnp.pad(meta, ((0, 0), (0, LANES - 4 * top)))

    x_own = jnp.concatenate([tokens, meta], axis=1)
    x_line = gather_upper(x_own)
    x_line[2] = send(x_own, 2)
    x_pair = {k: send(x_line[k], 1) for k in (0, 2)}
    x_line, x_pair, cot = fence(x_line, x_pair, cotangent)

    x_line.update({k | 2: send(x_line[k], 2) for k in folds})
    x_pair.update({k: send(x_line[k], 1) for k in folds})
    c_line = gather_upper(cot)
    c_line[2] = send(cot, 2)
    c_pair = {0: send(cot, 1)}
    x_line, c_line, x_pair, c_pair = fence(x_line, c_line, x_pair, c_pair)
    x_pair.update({k: send(x_line[k], 1) for k in sides})
    x_far = swap(cut_far([x_line[k] for k in line_blocks], "cut_x"), far_bit, n_dp)
    x_pair, c_line = fence(x_pair, c_line)

    c_line.update({k | 2: send(c_line[k], 2) for k in folds})
    c_pair.update({k: send(c_line[k], 1) for k in [2] + folds})
    x_far_pair = swap(cut_far([x_pair[k] for k in line_blocks], "cut_x_pair"), far_bit, n_dp)
    pre, act, info, pick, combine, x_keep = pl.pallas_call(
        functools.partial(hidden_kernel, cfg),
        grid=(local,),
        in_specs=[smem] * 2 + [any_space] * parts + [weight_spec] * 2,
        out_specs=[by_expert(cap, 2 * hidden), by_expert(cap, hidden + LANES), by_expert(cap, LANES),
                   whole(local * cap, total), whole(total, local * cap_pad), whole(total, half)],
        out_shape=[sds((local, cap, 2 * hidden), F32), sds((local, cap, hidden + LANES), BF16),
                   sds((local, cap, LANES), F32), sds((local * cap, total), BF16), sds((total, local * cap_pad), BF16),
                   sds((total, half), BF16)],
        scratch_shapes=[
            pltpu.VMEM((total, wide), BF16),
            pltpu.VMEM((local * cap, wide), BF16),
            pltpu.SemaphoreType.DMA((parts,)),
        ],
        compiler_params=params,
        cost_estimate=cost(6, 20),
        name="hidden",
    )(first, far_word, *[x_line[k] for k in line_blocks], *[x_pair[k] for k in line_blocks], w_gate, w_up)
    act, c_line, c_pair, x_far = fence(act, c_line, c_pair, x_far)

    c_pair.update({k: send(c_line[k], 1) for k in sides})
    act_far = swap(act, far_bit, n_dp)
    level_rows = [line] + [len(group) * tok_rows for group in groups]
    level_specs = [whole(rows, width) for rows in level_rows]
    mixed_keep, *mixed_out, c_give = pl.pallas_call(
        functools.partial(mixed_kernel, (plan, levels, local, cap, cap_pad)),
        grid=(width // tile,),
        in_specs=[smem, whole(local, cap, hidden + LANES), whole(total, local * cap_pad), by_columns] + [any_space] * levels,
        out_specs=level_specs + [whole(line, half)],
        out_shape=[sds((rows, width), BF16) for rows in level_rows] + [sds((line, half), BF16)],
        scratch_shapes=[pltpu.VMEM((total, local * hidden), BF16), pltpu.SemaphoreType.DMA((levels,))],
        compiler_params=params,
        cost_estimate=cost(6, 10),
        name="mixed",
    )(far_word, act, combine, w_down, *[c_line[k] for k in line_blocks])
    c_pair, mixed_keep, mixed_out, c_give, x_far_pair = fence(c_pair, mixed_keep, mixed_out, c_give, x_far_pair)

    def back_rows(keep, got):
        return keep.astype(F32) + got.astype(F32)

    def pair_sums(keep, got, group):
        mine = jnp.concatenate([keep[k // 2 * tok_rows:(k // 2 + 1) * tok_rows] for k in group], axis=0)
        return back_rows(mine, got)

    def fold_upper(sums):
        blocks = {k: sums[i * tok_rows:(i + 1) * tok_rows] for i, k in enumerate(folds)}
        landed = []
        for bit in upper_bits:
            for k in [k for k in blocks if k & bit]:
                got = send(blocks.pop(k).astype(BF16), bit)
                if k == bit:
                    landed.append(got)
                else:
                    blocks[k ^ bit] = back_rows(blocks[k ^ bit], got)
        return landed

    def finish(sums, landed):
        return sum([part.astype(F32) for part in landed], sums[tok_rows:].astype(F32))

    mixed_got = [send(part, 1) for part in mixed_out[:2]]
    c_far = swap(c_give, far_bit, n_dp)
    d_gate, d_up, tail, c_keep, c_give = pl.pallas_call(
        functools.partial(grad_kernel, cfg),
        grid=(local,),
        in_specs=[smem] + [any_space] * parts + [whole(local * cap, total), whole(total, local * cap_pad), weight_spec,
                                                 by_expert(cap, 2 * hidden), by_expert(cap, LANES)],
        out_specs=[by_expert(cap, hidden)] * 2 + [whole(total, LANES), whole(total, half), whole(line, half)],
        out_shape=[sds((local, cap, hidden), BF16)] * 2 + [sds((total, LANES), BF16),
                   sds((total, half), BF16), sds((line, half), BF16)],
        scratch_shapes=[
            pltpu.VMEM((total, width), BF16),
            pltpu.VMEM((local * cap, width), BF16),
            pltpu.VMEM((local * cap_pad, LANES), BF16),
            pltpu.SemaphoreType.DMA((parts,)),
        ],
        compiler_params=params,
        cost_estimate=cost(6, 12),
        name="hidden_grads",
    )(far_word, *[c_line[k] for k in line_blocks], *[c_pair[k] for k in line_blocks], pick, combine, w_down, pre, info)
    mixed_sides, mixed_got, mixed_out, d_gate, d_up, tail, c_give, act_far = fence(
        pair_sums(mixed_keep, mixed_got[0], sides).astype(BF16), mixed_got, mixed_out, d_gate, d_up, tail, c_give, act_far)

    mixed_sides = send(mixed_sides, 2)
    mixed_got.append(send(mixed_out[2], 1))
    c_far_pair = swap(c_give, far_bit, n_dp)
    gate_far = swap(d_gate, far_bit, n_dp)
    wide_specs = [whole(rows, wide) for rows in level_rows]
    input_keep, *input_out = pl.pallas_call(
        functools.partial(input_kernel, (plan, local, cap, cap_pad)),
        grid=(width // tile,),
        in_specs=[whole(local, cap, hidden)] * 2 + [whole(total, local * cap_pad), whole(total, LANES),
                                                    by_columns, by_columns],
        out_specs=wide_specs,
        out_shape=[sds((rows, wide), BF16) for rows in level_rows],
        scratch_shapes=[pltpu.VMEM((local * cap_pad, tile), BF16)],
        compiler_params=params,
        cost_estimate=cost(6, 16),
        name="input_grads",
    )(d_gate, d_up, combine, tail, w_gate, w_up)
    input_keep, input_out, mixed_sides, mixed_got, c_far, d_up = fence(
        input_keep, input_out, mixed_sides, mixed_got, c_far, d_up)

    input_got = [send(part, 1) for part in input_out[:2]]
    mixed_landed = fold_upper(back_rows(pair_sums(mixed_keep, mixed_got[1], folds), mixed_sides))
    mixed_ends = pair_sums(mixed_keep, mixed_got[2], [2, 0])
    mixed_landed.append(send(mixed_ends[:tok_rows].astype(BF16), 2))
    input_sides, input_out = fence(pair_sums(input_keep, input_got[0], sides).astype(BF16), input_out)
    input_sides = send(input_sides, 2)
    input_folds, c_far_pair, mixed_landed, d_up, x_keep = fence(
        back_rows(pair_sums(input_keep, input_got[1], folds), input_sides).astype(BF16), c_far_pair, mixed_landed, d_up, x_keep)
    input_landed = fold_upper(input_folds)
    input_got.append(send(input_out[2], 1))
    up_far = swap(d_up, far_bit, n_dp)
    partial_specs = [by_expert(columns, hidden)] * 2
    partial_shapes = [sds((local, columns, hidden), BF16)] * 2
    x_rows, down_keep, down_give = pl.pallas_call(
        functools.partial(down_kernel, cap),
        grid=(local,),
        in_specs=[smem, pl.BlockSpec((cap, total), lambda e: (e, 0))] + [whole(total, half), whole(line, half), whole(line, half)] * 2
        + [by_expert(cap, hidden + LANES)] * 2,
        out_specs=[by_expert(2 * cap, half)] + partial_specs,
        out_shape=[sds((local, 2 * cap, half), BF16)] + partial_shapes,
        scratch_shapes=[pltpu.VMEM((2 * cap, half), BF16), pltpu.VMEM((2 * cap, hidden), BF16), pltpu.VMEM((half, hidden), BF16)],
        compiler_params=params,
        cost_estimate=cost(6, 12),
        name="down_grads",
    )(near_word, pick, x_keep, x_far, x_far_pair, c_keep, c_far, c_far_pair, act, act_far)
    input_ends, input_landed, x_rows, down_keep, down_give, gate_far = fence(
        pair_sums(input_keep, input_got[2], [2, 0]), input_landed, x_rows, down_keep, down_give, gate_far)

    input_landed.append(send(input_ends[:tok_rows].astype(BF16), 2))
    down_got = swap(down_give, 1, n_dp)

    def partial_grads(grads, grads_far, name):
        return pl.pallas_call(
            functools.partial(partial_kernel, cap),
            grid=(local,),
            in_specs=[smem, by_expert(2 * cap, half)] + [by_expert(cap, hidden)] * 2,
            out_specs=partial_specs,
            out_shape=partial_shapes,
            scratch_shapes=[pltpu.VMEM((2 * cap, hidden), BF16), pltpu.VMEM((half, hidden), BF16)],
            compiler_params=params,
            cost_estimate=cost(3, 10),
            name=name,
        )(near_word, x_rows, grads, grads_far)

    gate_keep, gate_give = partial_grads(d_gate, gate_far, "gate_grads")
    gate_got = swap(gate_give, 1, n_dp)
    down_grad = back_rows(down_keep, down_got).astype(BF16)
    gate_grad = back_rows(gate_keep, gate_got).astype(BF16)
    up_far, input_landed, gate_grad, down_grad = fence(up_far, input_landed, gate_grad, down_grad)
    up_keep, up_give = partial_grads(d_up, up_far, "up_grads")
    up_got = swap(up_give, 1, n_dp)
    up_grad = back_rows(up_keep, up_got).astype(BF16)

    mixed = finish(mixed_ends, mixed_landed).astype(BF16)
    back = finish(input_ends, input_landed)
    token_grad = back[:, :width].astype(BF16)
    tail = back[:, width:]
    slot_sg = tail[:, :top] + tail[:, top:2 * top] + tail[:, 2 * top:3 * top]
    prob_grad = (slot_sg - jnp.sum(share * slot_sg, axis=1, keepdims=True)) / totals
    return mixed, token_grad, prob_grad, gate_grad, up_grad, down_grad


def solution(mesh):
    rows = P(("expert", "dp"), None)
    weight = P("expert", None, None)
    grad = P("expert", "dp", None)
    return jax.shard_map(
        shards,
        mesh=mesh,
        in_specs=(rows, rows, rows, rows, weight, weight, weight),
        out_specs=(rows, rows, rows, grad, grad, grad),
        check_vma=False,
    )
```

profile of v0, /device:TPU:0, one launch (start us, length us, event | category | flops | bytes accessed | tf_op | source)
XLA Modules:
  0.0 184.5 jit_solution(6902264327990072208)
XLA Ops:
  0.6 0.8 copy.16
  1.4 0.7 reduce_sum.18
  2.1 0.7 convert_element_type.113
  3.1 1.0 pad_maximum_fusion.refs_0_
  4.1 3.1 %collective-permute-start = (bf16[64,2176]{1,0:T(8,128)(2,1)S(1)}, bf16[64,2176]{1,0:T(8,128)(2,1)S(1)}, u32[]{:S(2)}, u32[]{:S(2)}) collective-permute-start(bf16[64,2176]{1,0:T(8,128)(2,1)S(1)} %pad_maximum_fusion.refs_0_), channel_id=1, source_target_pairs={{0,8},{4,12},{8,0},{12,4},{16,24},{20,28},{24,16},{28,20},{1,9},{5... | collective-permute-start | bytes 835592 | tf_op jit(solution)/shard_map/ppermute | solution.py:270
  7.2 2.6 %collective-permute-start.1 = (bf16[64,2176]{1,0:T(8,128)(2,1)S(1)}, bf16[64,2176]{1,0:T(8,128)(2,1)S(1)}, u32[]{:S(2)}, u32[]{:S(2)}) collective-permute-start(bf16[64,2176]{1,0:T(8,128)(2,1)S(1)} %pad_maximum_fusion.refs_0_), channel_id=1, source_target_pairs={{0,16},{4,20},{8,24},{12,28},{16,0},{20,4},{24,8},{28,12},{1,17},{... | collective-permute-start | bytes 835592 | tf_op jit(solution)/shard_map/ppermute | solution.py:270
  9.8 1.5 collective-permute-start.2
  11.2 8.4 %collective-permute-done.refs_1_ = bf16[64,2176]{1,0:T(8,128)(2,1)S(1)} collective-permute-done((bf16[64,2176]{1,0:T(8,128)(2,1)S(1)}, bf16[64,2176]{1,0:T(8,128)(2,1)S(1)}, u32[]{:S(2)}, u32[]{:S(2)}) %collective-permute-start) | collective-permute-done | bytes 278560 | tf_op jit(solution)/shard_map/ppermute | solution.py:270
  19.7 1.7 collective-permute-start.3
  21.3 0.9 collective-permute-done.1.refs_2_
  22.2 5.3 %collective-permute-done.3.refs_5_.refs_1_ = bf16[64,2176]{1,0:T(8,128)(2,1)S(1)} collective-permute-done((bf16[64,2176]{1,0:T(8,128)(2,1)S(1)}, bf16[64,2176]{1,0:T(8,128)(2,1)S(1)}, u32[]{:S(2)}, u32[]{:S(2)}) %collective-permute-start.3) | collective-permute-done | bytes 278560 | tf_op jit(solution)/shard_map/ppermute | solution.py:270
  27.5 1.3 collective-permute-start.7
  28.9 2.0 %collective-permute-start.5 = (bf16[64,2048]{1,0:T(8,128)(2,1)}, bf16[64,2048]{1,0:T(8,128)(2,1)S(1)}, u32[]{:S(2)}, u32[]{:S(2)}) collective-permute-start(bf16[64,2048]{1,0:T(8,128)(2,1)} %refs_0_.1), channel_id=1, source_target_pairs={{0,8},{4,12},{8,0},{12,4},{16,24},{20,28},{24,16},{28,20},{1,9},{5... | collective-permute-start | bytes 786440 | tf_op jit(solution)/shard_map/ppermute | solution.py:270
  30.9 1.0 collective-permute-start.6
  31.9 0.5 collective-permute-start.8
  32.5 13.2 %collective-permute-done.5.refs_1_ = bf16[64,2048]{1,0:T(8,128)(2,1)S(1)} collective-permute-done((bf16[64,2048]{1,0:T(8,128)(2,1)}, bf16[64,2048]{1,0:T(8,128)(2,1)S(1)}, u32[]{:S(2)}, u32[]{:S(2)}) %collective-permute-start.5) | collective-permute-done | bytes 262176 | tf_op jit(solution)/shard_map/ppermute | solution.py:270
  45.7 0.7 copy-done.23
  46.4 1.0 collective-permute-start.9
  47.5 1.9 %cut_x.1 = bf16[256,1024]{1,0:T(8,128)(2,1)} custom-call(s32[1]{0:T(128)} %bitcast.1.far_ref.word_ref, bf16[64,2176]{1,0:T(8,128)(2,1)} %copy-done.1, bf16[64,2176]{1,0:T(8,128)(2,1)} %copy-done.7, bf16[64,2176]{1,0:T(8,128)(2,1)} %copy-done.8, bf16[64,2176]{1,0:T(8,128)(2,1)} %copy-done.11), custom_call_target="tpu_custom_call" | custom-call | bytes 2000 | tf_op jit(solution)/shard_map/cut_x/pallas_call | solution.py:346
  49.4 1.6 collective-permute-start.13
  51.0 2.5 %collective-permute-done.9.refs_7_.refs_3_ = bf16[64,2176]{1,0:T(8,128)(2,1)S(1)} collective-permute-done((bf16[64,2176]{1,0:T(8,128)(2,1)S(1)}, bf16[64,2176]{1,0:T(8,128)(2,1)S(1)}, u32[]{:S(2)}, u32[]{:S(2)}) %collective-permute-start.9) | collective-permute-done | bytes 278560 | tf_op jit(solution)/shard_map/ppermute | solution.py:270
  54.0 2.3 %collective-permute-start.11 = (bf16[64,2048]{1,0:T(8,128)(2,1)S(1)}, bf16[64,2048]{1,0:T(8,128)(2,1)S(1)}, u32[]{:S(2)}, u32[]{:S(2)}) collective-permute-start(bf16[64,2048]{1,0:T(8,128)(2,1)S(1)} %collective-permute-done.5.refs_1_), channel_id=1, source_target_pairs={{0,4},{4,0},{8,12},{12,8},{16,20},{20,16},{24,28},{28,24},{1,5},{5... | collective-permute-start | bytes 786440 | tf_op jit(solution)/shard_map/ppermute | solution.py:270
  56.3 1.9 %cut_x_pair.1 = bf16[256,1024]{1,0:T(8,128)(2,1)} custom-call(s32[1]{0:T(128)} %bitcast.1.far_ref.word_ref, bf16[64,2176]{1,0:T(8,128)(2,1)} %copy-done.9, bf16[64,2176]{1,0:T(8,128)(2,1)} %copy-done.10, bf16[64,2176]{1,0:T(8,128)(2,1)} %copy-done.12, bf16[64,2176]{1,0:T(8,128)(2,1)} %copy-done.13), custom_call_target="tpu_custom_call" | custom-call | bytes 2000 | tf_op jit(solution)/shard_map/cut_x_pair/pallas_call | solution.py:346
  58.2 2.1 %collective-permute-start.15 = (bf16[256,1024]{1,0:T(8,128)(2,1)}, bf16[256,1024]{1,0:T(8,128)(2,1)S(1)}, u32[]{:S(2)}, u32[]{:S(2)}) collective-permute-start(bf16[256,1024]{1,0:T(8,128)(2,1)} %cut_x_pair.1), channel_id=1, source_target_pairs={{0,2},{1,3},{2,0},{3,1},{4,6},{5,7},{6,4},{7,5},{8,10},{9,11},{10,... | collective-permute-start | bytes 1572872 | tf_op jit(solution)/shard_map/ppermute | solution.py:266
  60.3 12.7 %hidden.1 = (f32[4,160,768]{2,1,0:T(8,128)}, bf16[4,160,512]{2,1,0:T(8,128)(2,1)}, f32[4,160,128]{2,1,0:T(8,128)}, bf16[640,512]{1,0:T(8,128)(2,1)}, bf16[512,10...) custom-call(s32[1]{0:T(128)} %bitcast.first_ref, s32[1]{0:T(128)} %bitcast.1.far_ref.word_ref, bf16[64,2176]{1,0:T(8,128)(2,1)} %copy-done.1, ...), custom_call_target="tpu_custom_call" | custom-call | flops 6000000 | bytes 20000 | tf_op jit(solution)/shard_map/hidden/pallas_call | solution.py:389
  73.2 1.5 collective-permute-start.14
  74.7 9.6 %mixed.1 = (bf16[256,2048]{1,0:T(8,128)(2,1)}, bf16[64,2048]{1,0:T(8,128)(2,1)}, bf16[64,2048]{1,0:T(8,128)(2,1)}, bf16[128,2048]{1,0:T(8,128)(2,1)}, bf16[256,1024]{1,0:T(8,128)(2,1)}) custom-call(s32[1]{0:T(128)} %bitcast.1.far_ref.word_ref, bf16[4,160,512]{2,1,0:T(8,128)(2,1)} %get-tuple-element.141.act_ref.refs_6_, ...), custom_call_target="tpu_custom_call" | custom-call | flops 6000000 | bytes 10000 | tf_op jit(solution)/shard_map/mixed/pallas_call | solution.py:413
  84.4 0.8 collective-permute-start.16
  85.1 0.5 collective-permute-start.18
  85.6 1.3 collective-permute-start.17
  87.0 1.5 collective-permute-start.21
  88.5 11.3 %hidden_grads.1 = (bf16[4,160,384]{2,1,0:T(8,128)(2,1)}, bf16[4,160,384]{2,1,0:T(8,128)(2,1)}, bf16[512,128]{1,0:T(8,128)(2,1)}, bf16[512,1024]{1,0:T(8,128)(2,1)}, bf16[256,1024]{1,0:T(8,128)(2,1)}) custom-call(s32[1]{0:T(128)} %bitcast.1.far_ref.word_ref, bf16[64,2048]{1,0:T(8,128)(2,1)} %refs_0_.1, bf16[64,2048]{1,0:T(8,128)(2,1)} %copy-done.14, ...), custom_call_target="tpu_custom_call" | custom-call | flops 6000000 | bytes 12000 | tf_op jit(solution)/shard_map/hidden_grads/pallas_call | solution.py:450
  99.8 0.8 add_convert_fusion.6
  100.6 2.2 %collective-permute-done.18.refs_7_ = bf16[4,160,512]{2,1,0:T(8,128)(2,1)S(1)} collective-permute-done((bf16[4,160,512]{2,1,0:T(8,128)(2,1)S(1)}, bf16[4,160,512]{2,1,0:T(8,128)(2,1)S(1)}, u32[]{:S(2)}, u32[]{:S(2)}) %collective-permute-start.18) | collective-permute-done | bytes 655392 | tf_op jit(solution)/shard_map/ppermute | solution.py:266
  102.8 1.3 collective-permute-start.20
  104.2 0.6 collective-permute-start.25
  104.8 1.5 collective-permute-start.30
  106.3 10.9 %input_grads.1 = (bf16[256,2176]{1,0:T(8,128)(2,1)}, bf16[64,2176]{1,0:T(8,128)(2,1)}, bf16[64,2176]{1,0:T(8,128)(2,1)}, bf16[128,2176]{1,0:T(8,128)(2,1)}) custom-call(bf16[4,160,384]{2,1,0:T(8,128)(2,1)} %get-tuple-element.166.d_gate_ref.own_ref, bf16[4,160,384]{2,1,0:T(8,128)(2,1)} %get-tuple-element.203.d_up_ref.own_ref, ...), custom_call_target="tpu_custom_call" | custom-call | flops 6000000 | bytes 16000 | tf_op jit(solution)/shard_map/input_grads/pallas_call | solution.py:476
  117.3 0.8 collective-permute-start.23
  118.0 1.3 collective-permute-start.22
  119.5 2.1 %collective-permute-start.26 = (bf16[64,2048]{1,0:T(8,128)(2,1)S(1)}, bf16[64,2048]{1,0:T(8,128)(2,1)}, u32[]{:S(2)}, u32[]{:S(2)}) collective-permute-start(bf16[64,2048]{1,0:T(8,128)(2,1)S(1)} %add_convert_fusion.5), channel_id=1, source_target_pairs={{0,16},{4,20},{8,24},{12,28},{16,0},{20,4},{24,8},{28,12},{1,17},{... | collective-permute-start | bytes 786440 | tf_op jit(solution)/shard_map/ppermute | solution.py:270
  121.6 1.1 fusion.10
  122.7 1.4 collective-permute-done.23
  124.2 3.7 %collective-permute-start.24 = (bf16[64,2176]{1,0:T(8,128)(2,1)S(1)}, bf16[64,2176]{1,0:T(8,128)(2,1)S(1)}, u32[]{:S(2)}, u32[]{:S(2)}) collective-permute-start(bf16[64,2176]{1,0:T(8,128)(2,1)S(1)} %add_convert_fusion.4), channel_id=1, source_target_pairs={{0,8},{4,12},{8,0},{12,4},{16,24},{20,28},{24,16},{28,20},{1,9},{5... | collective-permute-start | bytes 835592 | tf_op jit(solution)/shard_map/ppermute | solution.py:270
  127.9 1.2 convert_add_fusion.1
  129.1 0.6 collective-permute-done.22
  129.7 4.0 %collective-permute-start.27 = (bf16[64,2048]{1,0:T(8,128)(2,1)S(1)}, bf16[64,2048]{1,0:T(8,128)(2,1)}, u32[]{:S(2)}, u32[]{:S(2)}) collective-permute-start(bf16[64,2048]{1,0:T(8,128)(2,1)S(1)} %slice.110), channel_id=1, source_target_pairs={{0,8},{4,12},{8,0},{12,4},{16,24},{20,28},{24,16},{28,20},{1,9},{5... | collective-permute-start | bytes 786440 | tf_op jit(solution)/shard_map/ppermute | solution.py:270
  133.8 3.0 %collective-permute-done.24 = bf16[64,2176]{1,0:T(8,128)(2,1)S(1)} collective-permute-done((bf16[64,2176]{1,0:T(8,128)(2,1)S(1)}, bf16[64,2176]{1,0:T(8,128)(2,1)S(1)}, u32[]{:S(2)}, u32[]{:S(2)}) %collective-permute-start.24) | collective-permute-done | bytes 278560 | tf_op jit(solution)/shard_map/ppermute | solution.py:270
  136.7 0.8 add_convert_fusion.3
  137.6 2.1 %collective-permute-done.27 = bf16[64,2048]{1,0:T(8,128)(2,1)} collective-permute-done((bf16[64,2048]{1,0:T(8,128)(2,1)S(1)}, bf16[64,2048]{1,0:T(8,128)(2,1)}, u32[]{:S(2)}, u32[]{:S(2)}) %collective-permute-start.27) | collective-permute-done | bytes 262176 | tf_op jit(solution)/shard_map/ppermute | solution.py:270
  139.7 1.0 collective-permute-start.29
  140.7 9.8 %down_grads.1 = (bf16[4,320,1024]{2,1,0:T(8,128)(2,1)}, bf16[4,512,384]{2,1,0:T(8,128)(2,1)}, bf16[4,512,384]{2,1,0:T(8,128)(2,1)}) custom-call(s32[1]{0:T(128)} %bitcast.2.near_ref, bf16[640,512]{1,0:T(8,128)(2,1)} %get-tuple-element.159.refs_8_.pick_ref, bf16[512,1024]{1,0:T(8,128)(2,1)} %get-tuple-element.192.refs_0_, bf16[256,1024]{1,0:T(8,128)(2,1)} %copy-done.19, ...), custom_call_target="tpu_custom_call" | custom-call | flops 6000000 | bytes 12000 | tf_op jit(solution)/shard_map/down_grads/pallas_call | solution.py:504
  150.6 6.0 %gate_grads.1 = (bf16[4,512,384]{2,1,0:T(8,128)(2,1)}, bf16[4,512,384]{2,1,0:T(8,128)(2,1)}) custom-call(s32[1]{0:T(128)} %bitcast.2.near_ref, bf16[4,320,1024]{2,1,0:T(8,128)(2,1)} %get-tuple-element.205.rows_ref, bf16[4,160,384]{2,1,0:T(8,128)(2,1)} %get-tuple-element.166.d_gate_ref.own_ref, bf16[4,160,384]{2,1,0:T(8,128)(2,1)} %collective-permute-done.30.far_ref), custom_call_target="tpu_custom_call" | custom-call | flops 3000000 | bytes 10000 | tf_op jit(solution)/shard_map/gate_grads/pallas_call | solution.py:523
  157.2 2.6 %collective-permute-start.32 = (bf16[64,2176]{1,0:T(8,128)(2,1)S(1)}, bf16[64,2176]{1,0:T(8,128)(2,1)S(1)}, u32[]{:S(2)}, u32[]{:S(2)}) collective-permute-start(bf16[64,2176]{1,0:T(8,128)(2,1)S(1)} %slice.108), channel_id=1, source_target_pairs={{0,8},{4,12},{8,0},{12,4},{16,24},{20,28},{24,16},{28,20},{1,9},{5... | collective-permute-start | bytes 835592 | tf_op jit(solution)/shard_map/ppermute | solution.py:270
  160.2 3.1 %add_convert_fusion.2 = bf16[4,512,384]{2,1,0:T(8,128)(2,1)} fusion(bf16[4,512,384]{2,1,0:T(8,128)(2,1)S(1)} %collective-permute-done.33, bf16[4,512,384]{2,1,0:T(8,128)(2,1)} %get-tuple-element.207), kind=kLoop, calls=%fused_computation.2 | loop fusion | flops 3145728 | bytes 4718592 | tf_op jit(solution)/shard_map/convert_element_type | solution.py:538
  163.3 1.5 add_convert_fusion.1
  164.8 5.4 %collective-permute-done.31.far_ref = bf16[4,160,384]{2,1,0:T(8,128)(2,1)S(1)} collective-permute-done((bf16[4,160,384]{2,1,0:T(8,128)(2,1)S(1)}, bf16[4,160,384]{2,1,0:T(8,128)(2,1)S(1)}, u32[]{:S(2)}, u32[]{:S(2)}) %collective-permute-start.31) | collective-permute-done | bytes 491552 | tf_op jit(solution)/shard_map/ppermute | solution.py:266
  170.3 0.8 copy-done.22
  171.1 5.8 %up_grads.1 = (bf16[4,512,384]{2,1,0:T(8,128)(2,1)}, bf16[4,512,384]{2,1,0:T(8,128)(2,1)}) custom-call(s32[1]{0:T(128)} %bitcast.2.near_ref, bf16[4,320,1024]{2,1,0:T(8,128)(2,1)} %get-tuple-element.205.rows_ref, bf16[4,160,384]{2,1,0:T(8,128)(2,1)} %get-tuple-element.203.d_up_ref.own_ref, bf16[4,160,384]{2,1,0:T(8,128)(2,1)} %copy-done.22), custom_call_target="tpu_custom_call" | custom-call | flops 3000000 | bytes 10000 | tf_op jit(solution)/shard_map/up_grads/pallas_call | solution.py:523
  176.9 1.8 fusion.1
  178.7 1.1 convert_add_fusion.2
  179.9 0.7 slice.109
  180.9 0.7 copy.20
  181.6 2.9 %add_convert_fusion = bf16[4,512,384]{2,1,0:T(8,128)(2,1)} fusion(bf16[4,512,384]{2,1,0:T(8,128)(2,1)} %collective-permute-done.35, bf16[4,512,384]{2,1,0:T(8,128)(2,1)S(1)} %copy-done.5), kind=kLoop, calls=%fused_computation | loop fusion | flops 3145728 | bytes 4718592 | tf_op jit(solution)/shard_map/convert_element_type | solution.py:542
  (101 shorter events, 2.6 us)
Async XLA Ops:
  4.1 43.4 %copy-start.1 = (bf16[64,2176]{1,0:T(8,128)(2,1)}, bf16[64,2176]{1,0:T(8,128)(2,1)S(1)}, u32[]{:S(2)}) copy-start(bf16[64,2176]{1,0:T(8,128)(2,1)S(1)} %pad_maximum_fusion.refs_0_) | copy-start | bytes 835588
  4.1 15.6 %collective-permute-start = (bf16[64,2176]{1,0:T(8,128)(2,1)S(1)}, bf16[64,2176]{1,0:T(8,128)(2,1)S(1)}, u32[]{:S(2)}, u32[]{:S(2)}) collective-permute-start(bf16[64,2176]{1,0:T(8,128)(2,1)S(1)} %pad_maximum_fusion.refs_0_), channel_id=1, source_target_pairs={{0,8},{4,12},{8,0},{12,4},{16,24},{20,28},{24,16},{28,20},{1,9},{5... | collective-permute-start | bytes 835592 | tf_op jit(solution)/shard_map/ppermute | solution.py:270
  7.2 15.0 %collective-permute-start.1 = (bf16[64,2176]{1,0:T(8,128)(2,1)S(1)}, bf16[64,2176]{1,0:T(8,128)(2,1)S(1)}, u32[]{:S(2)}, u32[]{:S(2)}) collective-permute-start(bf16[64,2176]{1,0:T(8,128)(2,1)S(1)} %pad_maximum_fusion.refs_0_), channel_id=1, source_target_pairs={{0,16},{4,20},{8,24},{12,28},{16,0},{20,4},{24,8},{28,12},{1,17},{... | collective-permute-start | bytes 835592 | tf_op jit(solution)/shard_map/ppermute | solution.py:270
  9.8 12.4 %collective-permute-start.2 = (bf16[64,2176]{1,0:T(8,128)(2,1)S(1)}, bf16[64,2176]{1,0:T(8,128)(2,1)S(1)}, u32[]{:S(2)}, u32[]{:S(2)}) collective-permute-start(bf16[64,2176]{1,0:T(8,128)(2,1)S(1)} %pad_maximum_fusion.refs_0_), channel_id=1, source_target_pairs={{0,4},{4,0},{8,12},{12,8},{16,20},{20,16},{24,28},{28,24},{1,5},{5... | collective-permute-start | bytes 835592 | tf_op jit(solution)/shard_map/ppermute | solution.py:270
  19.7 27.8 %copy-start.7 = (bf16[64,2176]{1,0:T(8,128)(2,1)}, bf16[64,2176]{1,0:T(8,128)(2,1)S(1)}, u32[]{:S(2)}) copy-start(bf16[64,2176]{1,0:T(8,128)(2,1)S(1)} %collective-permute-done.refs_1_) | copy-start | bytes 835588
  19.7 7.8 %collective-permute-start.3 = (bf16[64,2176]{1,0:T(8,128)(2,1)S(1)}, bf16[64,2176]{1,0:T(8,128)(2,1)S(1)}, u32[]{:S(2)}, u32[]{:S(2)}) collective-permute-start(bf16[64,2176]{1,0:T(8,128)(2,1)S(1)} %collective-permute-done.refs_1_), channel_id=1, source_target_pairs={{0,4},{4,0},{8,12},{12,8},{16,20},{20,16},{24,28},{28,24},{1,5},{5... | collective-permute-start | bytes 835592 | tf_op jit(solution)/shard_map/ppermute | solution.py:270
  22.2 25.3 %copy-start.8 = (bf16[64,2176]{1,0:T(8,128)(2,1)}, bf16[64,2176]{1,0:T(8,128)(2,1)S(1)}, u32[]{:S(2)}) copy-start(bf16[64,2176]{1,0:T(8,128)(2,1)S(1)} %collective-permute-done.1.refs_2_) | copy-start | bytes 835588
  22.2 34.1 %copy-start.9 = (bf16[64,2176]{1,0:T(8,128)(2,1)}, bf16[64,2176]{1,0:T(8,128)(2,1)S(1)}, u32[]{:S(2)}) copy-start(bf16[64,2176]{1,0:T(8,128)(2,1)S(1)} %collective-permute-done.2.refs_4_.refs_0_) | copy-start | bytes 835588
  27.5 28.8 %copy-start.10 = (bf16[64,2176]{1,0:T(8,128)(2,1)}, bf16[64,2176]{1,0:T(8,128)(2,1)S(1)}, u32[]{:S(2)}) copy-start(bf16[64,2176]{1,0:T(8,128)(2,1)S(1)} %collective-permute-done.3.refs_5_.refs_1_) | copy-start | bytes 835588
  27.5 18.2 %collective-permute-start.4 = (bf16[64,2176]{1,0:T(8,128)(2,1)S(1)}, bf16[64,2176]{1,0:T(8,128)(2,1)S(1)}, u32[]{:S(2)}, u32[]{:S(2)}) collective-permute-start(bf16[64,2176]{1,0:T(8,128)(2,1)S(1)} %collective-permute-done.1.refs_2_), channel_id=1, source_target_pairs={{0,8},{4,12},{8,0},{12,4},{16,24},{20,28},{24,16},{28,20},{1,9},{5... | collective-permute-start | bytes 835592 | tf_op jit(solution)/shard_map/ppermute | solution.py:270
  27.5 18.9 %collective-permute-start.7 = (bf16[64,2176]{1,0:T(8,128)(2,1)S(1)}, bf16[64,2176]{1,0:T(8,128)(2,1)S(1)}, u32[]{:S(2)}, u32[]{:S(2)}) collective-permute-start(bf16[64,2176]{1,0:T(8,128)(2,1)S(1)} %collective-permute-done.1.refs_2_), channel_id=1, source_target_pairs={{0,4},{4,0},{8,12},{12,8},{16,20},{20,16},{24,28},{28,24},{1,5},{5... | collective-permute-start | bytes 835592 | tf_op jit(solution)/shard_map/ppermute | solution.py:270
  28.9 16.8 %collective-permute-start.5 = (bf16[64,2048]{1,0:T(8,128)(2,1)}, bf16[64,2048]{1,0:T(8,128)(2,1)S(1)}, u32[]{:S(2)}, u32[]{:S(2)}) collective-permute-start(bf16[64,2048]{1,0:T(8,128)(2,1)} %refs_0_.1), channel_id=1, source_target_pairs={{0,8},{4,12},{8,0},{12,4},{16,24},{20,28},{24,16},{28,20},{1,9},{5... | collective-permute-start | bytes 786440 | tf_op jit(solution)/shard_map/ppermute | solution.py:270
  30.9 14.8 %collective-permute-start.6 = (bf16[64,2048]{1,0:T(8,128)(2,1)}, bf16[64,2048]{1,0:T(8,128)(2,1)S(1)}, u32[]{:S(2)}, u32[]{:S(2)}) collective-permute-start(bf16[64,2048]{1,0:T(8,128)(2,1)} %refs_0_.1), channel_id=1, source_target_pairs={{0,16},{4,20},{8,24},{12,28},{16,0},{20,4},{24,8},{28,12},{1,17},{... | collective-permute-start | bytes 786440 | tf_op jit(solution)/shard_map/ppermute | solution.py:270
  31.9 13.8 %collective-permute-start.8 = (bf16[64,2048]{1,0:T(8,128)(2,1)}, bf16[64,2048]{1,0:T(8,128)(2,1)S(1)}, u32[]{:S(2)}, u32[]{:S(2)}) collective-permute-start(bf16[64,2048]{1,0:T(8,128)(2,1)} %refs_0_.1), channel_id=1, source_target_pairs={{0,4},{4,0},{8,12},{12,8},{16,20},{20,16},{24,28},{28,24},{1,5},{5... | collective-permute-start | bytes 786440 | tf_op jit(solution)/shard_map/ppermute | solution.py:270
  45.7 27.4 %copy-start.14 = (bf16[64,2048]{1,0:T(8,128)(2,1)}, bf16[64,2048]{1,0:T(8,128)(2,1)S(1)}, u32[]{:S(2)}) copy-start(bf16[64,2048]{1,0:T(8,128)(2,1)S(1)} %collective-permute-done.5.refs_1_) | copy-start | bytes 786436
  45.7 27.4 %copy-start.15 = (bf16[64,2048]{1,0:T(8,128)(2,1)}, bf16[64,2048]{1,0:T(8,128)(2,1)S(1)}, u32[]{:S(2)}) copy-start(bf16[64,2048]{1,0:T(8,128)(2,1)S(1)} %collective-permute-done.6.refs_2_) | copy-start | bytes 786436
  46.4 1.0 copy-start.11
  46.4 9.8 %copy-start.12 = (bf16[64,2176]{1,0:T(8,128)(2,1)}, bf16[64,2176]{1,0:T(8,128)(2,1)S(1)}, u32[]{:S(2)}) copy-start(bf16[64,2176]{1,0:T(8,128)(2,1)S(1)} %collective-permute-done.7.refs_6_.refs_2_) | copy-start | bytes 835588
  46.4 7.1 %collective-permute-start.9 = (bf16[64,2176]{1,0:T(8,128)(2,1)S(1)}, bf16[64,2176]{1,0:T(8,128)(2,1)S(1)}, u32[]{:S(2)}, u32[]{:S(2)}) collective-permute-start(bf16[64,2176]{1,0:T(8,128)(2,1)S(1)} %collective-permute-done.4.refs_3_), channel_id=1, source_target_pairs={{0,4},{4,0},{8,12},{12,8},{16,20},{20,16},{24,28},{28,24},{1,5},{5... | collective-permute-start | bytes 835592 | tf_op jit(solution)/shard_map/ppermute | solution.py:270
  49.4 23.7 %collective-permute-start.13 = (bf16[256,1024]{1,0:T(8,128)(2,1)}, bf16[256,1024]{1,0:T(8,128)(2,1)S(1)}, u32[]{:S(2)}, u32[]{:S(2)}) collective-permute-start(bf16[256,1024]{1,0:T(8,128)(2,1)} %cut_x.1), channel_id=1, source_target_pairs={{0,2},{1,3},{2,0},{3,1},{4,6},{5,7},{6,4},{7,5},{8,10},{9,11},{10,... | collective-permute-start | bytes 1572872 | tf_op jit(solution)/shard_map/ppermute | solution.py:266
  53.5 2.8 %copy-start.13 = (bf16[64,2176]{1,0:T(8,128)(2,1)}, bf16[64,2176]{1,0:T(8,128)(2,1)S(1)}, u32[]{:S(2)}) copy-start(bf16[64,2176]{1,0:T(8,128)(2,1)S(1)} %collective-permute-done.9.refs_7_.refs_3_) | copy-start | bytes 835588
  53.5 19.6 %collective-permute-start.10 = (bf16[64,2048]{1,0:T(8,128)(2,1)S(1)}, bf16[64,2048]{1,0:T(8,128)(2,1)S(1)}, u32[]{:S(2)}, u32[]{:S(2)}) collective-permute-start(bf16[64,2048]{1,0:T(8,128)(2,1)S(1)} %collective-permute-done.6.refs_2_), channel_id=1, source_target_pairs={{0,8},{4,12},{8,0},{12,4},{16,24},{20,28},{24,16},{28,20},{1,9},{5... | collective-permute-start | bytes 786440 | tf_op jit(solution)/shard_map/ppermute | solution.py:270
  54.0 19.2 %collective-permute-start.11 = (bf16[64,2048]{1,0:T(8,128)(2,1)S(1)}, bf16[64,2048]{1,0:T(8,128)(2,1)S(1)}, u32[]{:S(2)}, u32[]{:S(2)}) collective-permute-start(bf16[64,2048]{1,0:T(8,128)(2,1)S(1)} %collective-permute-done.5.refs_1_), channel_id=1, source_target_pairs={{0,4},{4,0},{8,12},{12,8},{16,20},{20,16},{24,28},{28,24},{1,5},{5... | collective-permute-start | bytes 786440 | tf_op jit(solution)/shard_map/ppermute | solution.py:270
  56.2 16.9 %collective-permute-start.12 = (bf16[64,2048]{1,0:T(8,128)(2,1)S(1)}, bf16[64,2048]{1,0:T(8,128)(2,1)S(1)}, u32[]{:S(2)}, u32[]{:S(2)}) collective-permute-start(bf16[64,2048]{1,0:T(8,128)(2,1)S(1)} %collective-permute-done.6.refs_2_), channel_id=1, source_target_pairs={{0,4},{4,0},{8,12},{12,8},{16,20},{20,16},{24,28},{28,24},{1,5},{5... | collective-permute-start | bytes 786440 | tf_op jit(solution)/shard_map/ppermute | solution.py:270
  58.2 26.1 %collective-permute-start.15 = (bf16[256,1024]{1,0:T(8,128)(2,1)}, bf16[256,1024]{1,0:T(8,128)(2,1)S(1)}, u32[]{:S(2)}, u32[]{:S(2)}) collective-permute-start(bf16[256,1024]{1,0:T(8,128)(2,1)} %cut_x_pair.1), channel_id=1, source_target_pairs={{0,2},{1,3},{2,0},{3,1},{4,6},{5,7},{6,4},{7,5},{8,10},{9,11},{10,... | collective-permute-start | bytes 1572872 | tf_op jit(solution)/shard_map/ppermute | solution.py:266
  73.1 15.4 %copy-start.19 = (bf16[256,1024]{1,0:T(8,128)(2,1)}, bf16[256,1024]{1,0:T(8,128)(2,1)S(1)}, u32[]{:S(2)}) copy-start(bf16[256,1024]{1,0:T(8,128)(2,1)S(1)} %collective-permute-done.13.refs_1_) | copy-start | bytes 1572868
  73.1 1.6 copy-start.16
  73.1 1.6 copy-start.24
  73.1 11.2 %copy-start.25 = (bf16[64,2048]{1,0:T(8,128)(2,1)}, bf16[64,2048]{1,0:T(8,128)(2,1)S(1)}, u32[]{:S(2)}) copy-start(bf16[64,2048]{1,0:T(8,128)(2,1)S(1)} %collective-permute-done.12.refs_6_) | copy-start | bytes 786436
  73.2 11.2 %collective-permute-start.14 = (bf16[64,2048]{1,0:T(8,128)(2,1)S(1)}, bf16[64,2048]{1,0:T(8,128)(2,1)S(1)}, u32[]{:S(2)}, u32[]{:S(2)}) collective-permute-start(bf16[64,2048]{1,0:T(8,128)(2,1)S(1)} %collective-permute-done.10.refs_3_), channel_id=1, source_target_pairs={{0,4},{4,0},{8,12},{12,8},{16,20},{20,16},{24,28},{28,24},{1,5},{5... | collective-permute-start | bytes 786440 | tf_op jit(solution)/shard_map/ppermute | solution.py:270
  74.7 10.4 %copy-start = (bf16[4,160,512]{2,1,0:T(8,128)(2,1)S(1)}, bf16[4,160,512]{2,1,0:T(8,128)(2,1)}, u32[]{:S(2)}) copy-start(bf16[4,160,512]{2,1,0:T(8,128)(2,1)} %get-tuple-element.141.act_ref.refs_6_) | copy-start | bytes 1966084
  84.3 4.2 %copy-start.26 = (bf16[64,2048]{1,0:T(8,128)(2,1)}, bf16[64,2048]{1,0:T(8,128)(2,1)S(1)}, u32[]{:S(2)}) copy-start(bf16[64,2048]{1,0:T(8,128)(2,1)S(1)} %collective-permute-done.14.refs_7_) | copy-start | bytes 786436
  84.3 4.1 %copy-start.20 = (bf16[256,1024]{1,0:T(8,128)(2,1)}, bf16[256,1024]{1,0:T(8,128)(2,1)S(1)}, u32[]{:S(2)}) copy-start(bf16[256,1024]{1,0:T(8,128)(2,1)S(1)} %collective-permute-done.15.refs_2_) | copy-start | bytes 1572868
  84.4 15.5 %collective-permute-start.16 = (bf16[64,2048]{1,0:T(8,128)(2,1)}, bf16[64,2048]{1,0:T(8,128)(2,1)S(1)}, u32[]{:S(2)}, u32[]{:S(2)}) collective-permute-start(bf16[64,2048]{1,0:T(8,128)(2,1)} %get-tuple-element.152), channel_id=1, source_target_pairs={{0,4},{4,0},{8,12},{12,8},{16,20},{20,16},{24,28},{28,24},{1,5},{5... | collective-permute-start | bytes 786440 | tf_op jit(solution)/shard_map/ppermute | solution.py:270
  85.1 17.7 %collective-permute-start.18 = (bf16[4,160,512]{2,1,0:T(8,128)(2,1)S(1)}, bf16[4,160,512]{2,1,0:T(8,128)(2,1)S(1)}, u32[]{:S(2)}, u32[]{:S(2)}) collective-permute-start(bf16[4,160,512]{2,1,0:T(8,128)(2,1)S(1)} %copy-done), channel_id=1, source_target_pairs={{0,2},{1,3},{2,0},{3,1},{4,6},{5,7},{6,4},{7,5},{8,10},{9,11},{10,... | collective-permute-start | bytes 1966088 | tf_op jit(solution)/shard_map/ppermute | solution.py:266
  85.6 15.0 %collective-permute-start.17 = (bf16[64,2048]{1,0:T(8,128)(2,1)}, bf16[64,2048]{1,0:T(8,128)(2,1)S(1)}, u32[]{:S(2)}, u32[]{:S(2)}) collective-permute-start(bf16[64,2048]{1,0:T(8,128)(2,1)} %get-tuple-element.153), channel_id=1, source_target_pairs={{0,4},{4,0},{8,12},{12,8},{16,20},{20,16},{24,28},{28,24},{1,5},{5... | collective-permute-start | bytes 786440 | tf_op jit(solution)/shard_map/ppermute | solution.py:270
  87.0 30.3 %collective-permute-start.21 = (bf16[256,1024]{1,0:T(8,128)(2,1)}, bf16[256,1024]{1,0:T(8,128)(2,1)}, u32[]{:S(2)}, u32[]{:S(2)}) collective-permute-start(bf16[256,1024]{1,0:T(8,128)(2,1)} %get-tuple-element.176), channel_id=1, source_target_pairs={{0,2},{1,3},{2,0},{3,1},{4,6},{5,7},{6,4},{7,5},{8,10},{9,11},{10,... | collective-permute-start | bytes 1572872 | tf_op jit(solution)/shard_map/ppermute | solution.py:266
  88.5 11.3 %copy-start.17 = (bf16[256,2048]{1,0:T(8,128)(2,1)S(1)}, bf16[256,2048]{1,0:T(8,128)(2,1)}, u32[]{:S(2)}) copy-start(bf16[256,2048]{1,0:T(8,128)(2,1)} %get-tuple-element.151) | copy-start | bytes 3145732
  99.8 5.0 %copy-start.3 = (bf16[4,160,384]{2,1,0:T(8,128)(2,1)S(1)}, bf16[4,160,384]{2,1,0:T(8,128)(2,1)}, u32[]{:S(2)}) copy-start(bf16[4,160,384]{2,1,0:T(8,128)(2,1)} %get-tuple-element.166.d_gate_ref.own_ref) | copy-start | bytes 1474564
  100.6 2.2 %copy-start.27 = (bf16[64,2048]{1,0:T(8,128)(2,1)}, bf16[64,2048]{1,0:T(8,128)(2,1)S(1)}, u32[]{:S(2)}) copy-start(bf16[64,2048]{1,0:T(8,128)(2,1)S(1)} %collective-permute-done.17) | copy-start | bytes 786436
  102.8 14.4 %copy-start.18 = (bf16[4,160,512]{2,1,0:T(8,128)(2,1)}, bf16[4,160,512]{2,1,0:T(8,128)(2,1)S(1)}, u32[]{:S(2)}) copy-start(bf16[4,160,512]{2,1,0:T(8,128)(2,1)S(1)} %collective-permute-done.18.refs_7_) | copy-start | bytes 1966084
  102.8 14.5 %collective-permute-start.20 = (bf16[128,2048]{1,0:T(8,128)(2,1)}, bf16[128,2048]{1,0:T(8,128)(2,1)S(1)}, u32[]{:S(2)}, u32[]{:S(2)}) collective-permute-start(bf16[128,2048]{1,0:T(8,128)(2,1)} %get-tuple-element.175), channel_id=1, source_target_pairs={{0,4},{4,0},{8,12},{12,8},{16,20},{20,16},{24,28},{28,24},{1,5},{5... | collective-permute-start | bytes 1572872 | tf_op jit(solution)/shard_map/ppermute | solution.py:270
  104.1 13.1 %collective-permute-start.19 = (bf16[64,2048]{1,0:T(8,128)(2,1)}, bf16[64,2048]{1,0:T(8,128)(2,1)S(1)}, u32[]{:S(2)}, u32[]{:S(2)}) collective-permute-start(bf16[64,2048]{1,0:T(8,128)(2,1)} %add_convert_fusion.6), channel_id=1, source_target_pairs={{0,8},{4,12},{8,0},{12,4},{16,24},{20,28},{24,16},{28,20},{1,9},{5... | collective-permute-start | bytes 786440 | tf_op jit(solution)/shard_map/ppermute | solution.py:270
  104.2 15.2 %copy-start.28 = (bf16[64,2048]{1,0:T(8,128)(2,1)S(1)}, bf16[64,2048]{1,0:T(8,128)(2,1)}, u32[]{:S(2)}) copy-start(bf16[64,2048]{1,0:T(8,128)(2,1)} %copy-done.27) | copy-start | bytes 786436
  104.2 33.4 %collective-permute-start.25 = (bf16[256,1024]{1,0:T(8,128)(2,1)}, bf16[256,1024]{1,0:T(8,128)(2,1)}, u32[]{:S(2)}, u32[]{:S(2)}) collective-permute-start(bf16[256,1024]{1,0:T(8,128)(2,1)} %get-tuple-element.183), channel_id=1, source_target_pairs={{0,2},{1,3},{2,0},{3,1},{4,6},{5,7},{6,4},{7,5},{8,10},{9,11},{10,... | collective-permute-start | bytes 1572872 | tf_op jit(solution)/shard_map/ppermute | solution.py:266
  104.8 45.8 %collective-permute-start.30 = (bf16[4,160,384]{2,1,0:T(8,128)(2,1)S(1)}, bf16[4,160,384]{2,1,0:T(8,128)(2,1)}, u32[]{:S(2)}, u32[]{:S(2)}) collective-permute-start(bf16[4,160,384]{2,1,0:T(8,128)(2,1)S(1)} %copy-done.3), channel_id=1, source_target_pairs={{0,2},{1,3},{2,0},{3,1},{4,6},{5,7},{6,4},{7,5},{8,10},{9,11},{10,... | collective-permute-start | bytes 1474568 | tf_op jit(solution)/shard_map/ppermute | solution.py:266
  117.2 6.9 %copy-start.6 = (bf16[256,2176]{1,0:T(8,128)(2,1)S(1)}, bf16[256,2176]{1,0:T(8,128)(2,1)}, u32[]{:S(2)}) copy-start(bf16[256,2176]{1,0:T(8,128)(2,1)} %get-tuple-element.178) | copy-start | bytes 3342340
  117.3 10.7 %copy-start.21 = (bf16[128,2048]{1,0:T(8,128)(2,1)}, bf16[128,2048]{1,0:T(8,128)(2,1)S(1)}, u32[]{:S(2)}) copy-start(bf16[128,2048]{1,0:T(8,128)(2,1)S(1)} %collective-permute-done.20) | copy-start | bytes 1572868
  117.3 6.8 %collective-permute-start.23 = (bf16[64,2176]{1,0:T(8,128)(2,1)}, bf16[64,2176]{1,0:T(8,128)(2,1)S(1)}, u32[]{:S(2)}, u32[]{:S(2)}) collective-permute-start(bf16[64,2176]{1,0:T(8,128)(2,1)} %get-tuple-element.180), channel_id=1, source_target_pairs={{0,4},{4,0},{8,12},{12,8},{16,20},{20,16},{24,28},{28,24},{1,5},{5... | collective-permute-start | bytes 835592 | tf_op jit(solution)/shard_map/ppermute | solution.py:270
  118.0 11.7 %collective-permute-start.22 = (bf16[64,2176]{1,0:T(8,128)(2,1)}, bf16[64,2176]{1,0:T(8,128)(2,1)S(1)}, u32[]{:S(2)}, u32[]{:S(2)}) collective-permute-start(bf16[64,2176]{1,0:T(8,128)(2,1)} %get-tuple-element.179), channel_id=1, source_target_pairs={{0,4},{4,0},{8,12},{12,8},{16,20},{20,16},{24,28},{28,24},{1,5},{5... | collective-permute-start | bytes 835592 | tf_op jit(solution)/shard_map/ppermute | solution.py:270
  119.5 18.1 %collective-permute-start.26 = (bf16[64,2048]{1,0:T(8,128)(2,1)S(1)}, bf16[64,2048]{1,0:T(8,128)(2,1)}, u32[]{:S(2)}, u32[]{:S(2)}) collective-permute-start(bf16[64,2048]{1,0:T(8,128)(2,1)S(1)} %add_convert_fusion.5), channel_id=1, source_target_pairs={{0,16},{4,20},{8,24},{12,28},{16,0},{20,4},{24,8},{28,12},{1,17},{... | collective-permute-start | bytes 786440 | tf_op jit(solution)/shard_map/ppermute | solution.py:270
  124.2 12.6 %collective-permute-start.24 = (bf16[64,2176]{1,0:T(8,128)(2,1)S(1)}, bf16[64,2176]{1,0:T(8,128)(2,1)S(1)}, u32[]{:S(2)}, u32[]{:S(2)}) collective-permute-start(bf16[64,2176]{1,0:T(8,128)(2,1)S(1)} %add_convert_fusion.4), channel_id=1, source_target_pairs={{0,8},{4,12},{8,0},{12,4},{16,24},{20,28},{24,16},{28,20},{1,9},{5... | collective-permute-start | bytes 835592 | tf_op jit(solution)/shard_map/ppermute | solution.py:270
  129.7 9.9 %collective-permute-start.27 = (bf16[64,2048]{1,0:T(8,128)(2,1)S(1)}, bf16[64,2048]{1,0:T(8,128)(2,1)}, u32[]{:S(2)}, u32[]{:S(2)}) collective-permute-start(bf16[64,2048]{1,0:T(8,128)(2,1)S(1)} %slice.110), channel_id=1, source_target_pairs={{0,8},{4,12},{8,0},{12,4},{16,24},{20,28},{24,16},{28,20},{1,9},{5... | collective-permute-start | bytes 786440 | tf_op jit(solution)/shard_map/ppermute | solution.py:270
  136.7 13.7 %collective-permute-start.28 = (bf16[128,2176]{1,0:T(8,128)(2,1)}, bf16[128,2176]{1,0:T(8,128)(2,1)S(1)}, u32[]{:S(2)}, u32[]{:S(2)}) collective-permute-start(bf16[128,2176]{1,0:T(8,128)(2,1)} %get-tuple-element.190), channel_id=1, source_target_pairs={{0,4},{4,0},{8,12},{12,8},{16,20},{20,16},{24,28},{28,24},{1,5},{5... | collective-permute-start | bytes 1671176 | tf_op jit(solution)/shard_map/ppermute | solution.py:270
  139.7 10.9 %collective-permute-start.29 = (bf16[64,2176]{1,0:T(8,128)(2,1)}, bf16[64,2176]{1,0:T(8,128)(2,1)}, u32[]{:S(2)}, u32[]{:S(2)}) collective-permute-start(bf16[64,2176]{1,0:T(8,128)(2,1)} %add_convert_fusion.3), channel_id=1, source_target_pairs={{0,16},{4,20},{8,24},{12,28},{16,0},{20,4},{24,8},{28,12},{1,17},{... | collective-permute-start | bytes 835592 | tf_op jit(solution)/shard_map/ppermute | solution.py:270
  150.6 6.5 %copy-start.2 = (bf16[4,160,384]{2,1,0:T(8,128)(2,1)S(1)}, bf16[4,160,384]{2,1,0:T(8,128)(2,1)}, u32[]{:S(2)}) copy-start(bf16[4,160,384]{2,1,0:T(8,128)(2,1)} %get-tuple-element.203.d_up_ref.own_ref) | copy-start | bytes 1474564
  156.6 3.6 %collective-permute-start.33 = (bf16[4,512,384]{2,1,0:T(8,128)(2,1)}, bf16[4,512,384]{2,1,0:T(8,128)(2,1)S(1)}, u32[]{:S(2)}, u32[]{:S(2)}) collective-permute-start(bf16[4,512,384]{2,1,0:T(8,128)(2,1)} %get-tuple-element.208), channel_id=1, source_target_pairs={{0,1},{1,0},{2,3},{3,2},{4,5},{5,4},{6,7},{7,6},{8,9},{9,8},{10,11... | collective-permute-start | bytes 4718600 | tf_op jit(solution)/shard_map/ppermute | solution.py:266
  156.6 6.7 %collective-permute-start.34 = (bf16[4,512,384]{2,1,0:T(8,128)(2,1)}, bf16[4,512,384]{2,1,0:T(8,128)(2,1)S(1)}, u32[]{:S(2)}, u32[]{:S(2)}) collective-permute-start(bf16[4,512,384]{2,1,0:T(8,128)(2,1)} %get-tuple-element.210), channel_id=1, source_target_pairs={{0,1},{1,0},{2,3},{3,2},{4,5},{5,4},{6,7},{7,6},{8,9},{9,8},{10,11... | collective-permute-start | bytes 4718600 | tf_op jit(solution)/shard_map/ppermute | solution.py:266
  157.1 13.1 %collective-permute-start.31 = (bf16[4,160,384]{2,1,0:T(8,128)(2,1)S(1)}, bf16[4,160,384]{2,1,0:T(8,128)(2,1)S(1)}, u32[]{:S(2)}, u32[]{:S(2)}) collective-permute-start(bf16[4,160,384]{2,1,0:T(8,128)(2,1)S(1)} %copy-done.2), channel_id=1, source_target_pairs={{0,2},{1,3},{2,0},{3,1},{4,6},{5,7},{6,4},{7,5},{8,10},{9,11},{10,... | collective-permute-start | bytes 1474568 | tf_op jit(solution)/shard_map/ppermute | solution.py:266
  157.2 13.1 %collective-permute-start.32 = (bf16[64,2176]{1,0:T(8,128)(2,1)S(1)}, bf16[64,2176]{1,0:T(8,128)(2,1)S(1)}, u32[]{:S(2)}, u32[]{:S(2)}) collective-permute-start(bf16[64,2176]{1,0:T(8,128)(2,1)S(1)} %slice.108), channel_id=1, source_target_pairs={{0,8},{4,12},{8,0},{12,4},{16,24},{20,28},{24,16},{28,20},{1,9},{5... | collective-permute-start | bytes 835592 | tf_op jit(solution)/shard_map/ppermute | solution.py:270
  160.2 3.1 %copy-start.4 = (bf16[4,512,384]{2,1,0:T(8,128)(2,1)S(1)}, bf16[4,512,384]{2,1,0:T(8,128)(2,1)}, u32[]{:S(2)}) copy-start(bf16[4,512,384]{2,1,0:T(8,128)(2,1)} %get-tuple-element.209) | copy-start | bytes 4718596
  170.3 0.8 copy-start.22
  176.9 4.7 %collective-permute-start.35 = (bf16[4,512,384]{2,1,0:T(8,128)(2,1)}, bf16[4,512,384]{2,1,0:T(8,128)(2,1)}, u32[]{:S(2)}, u32[]{:S(2)}) collective-permute-start(bf16[4,512,384]{2,1,0:T(8,128)(2,1)} %get-tuple-element.216), channel_id=1, source_target_pairs={{0,1},{1,0},{2,3},{3,2},{4,5},{5,4},{6,7},{7,6},{8,9},{9,8},{10,11... | collective-permute-start | bytes 4718600 | tf_op jit(solution)/shard_map/ppermute | solution.py:266
  178.7 2.9 %copy-start.5 = (bf16[4,512,384]{2,1,0:T(8,128)(2,1)S(1)}, bf16[4,512,384]{2,1,0:T(8,128)(2,1)}, u32[]{:S(2)}) copy-start(bf16[4,512,384]{2,1,0:T(8,128)(2,1)} %get-tuple-element.215) | copy-start | bytes 4718596
  (1 other events, 0.7 us)
where the time goes:
time: 185 us; the launch traced here: 184 us
  Pallas kernels  70 us (38%)
  starting transfers between devices  46.5 us (25%)
  waiting for transfers between devices  45.5 us (25%)
  other arithmetic  16.3 us (9%)
  local copies, waits for them, and re-layouts  5.08 us (3%)
    ppermute x26, starting transfers between devices, exchange(): return lax.ppermute(value, 'expert', [(i, i ^ bit) for i in range(count)])  38.2 us
    ppermute x26, waiting for transfers between devices, exchange(): return lax.ppermute(value, 'expert', [(i, i ^ bit) for i in range(count)])  37.5 us
    pallas_call x1, Pallas kernels, shards(): pl.pallas_call(functools.partial(hidden_kernel, cfg), grid=(local,), in_s...  12.7 us
    pallas_call x2, Pallas kernels, partial_grads(): pl.pallas_call(functools.partial(partial_kernel, cap), grid=(local,), in_...  11.8 us
    pallas_call x1, Pallas kernels, shards(): pl.pallas_call(functools.partial(grad_kernel, cfg), grid=(local,), in_spe...  11.3 us
    pallas_call x1, Pallas kernels, shards(): pl.pallas_call(functools.partial(input_kernel, (plan, local, cap, cap_pad...  10.9 us
    pallas_call x1, Pallas kernels, shards(): pl.pallas_call(functools.partial(down_kernel, cap), grid=(local,), in_spe...  9.76 us
    pallas_call x1, Pallas kernels, shards(): pl.pallas_call(functools.partial(mixed_kernel, (plan, levels, local, cap,...  9.59 us
  transfers between devices with their start and end apart: 36, of which 12 were waited for; matrix products, arithmetic and copies ran while one was open for 7% of the time, Pallas kernels for 32%

commit v1 on v0

--- a/solution.py
+++ b/solution.py
@@ -57,8 +57,8 @@
 def hidden_kernel(cfg, first_ref, far_ref, *refs):
     parts, local, cap, cap_pad, top = cfg
     blocks, refs = refs[:parts], refs[parts:]
-    gate_ref, up_ref, pre_ref, act_ref, info_ref, pick_ref, combine_ref, keep_ref = refs[:8]
-    held, rows_ref, sems = refs[8:]
+    gate_ref, up_ref, pre_ref, act_ref, info_ref, pick_ref, combine_ref, keep_ref, give_ref = refs[:9]
+    held, rows_ref, sems = refs[9:]
     expert = pl.program_id(0)
     tokens = held.shape[0]
     width, hidden = gate_ref.shape[1:]
@@ -94,6 +94,7 @@
         for start, stop in tiles(held.shape[1]):
             rows_ref[:, start:stop] = dot(pick_ref[...], held[:, start:stop]).astype(BF16)
         keep_ref[...] = held[:, half_of(far_ref[0], width)]
+        give_ref[...] = held[give_ref.shape[0]:, half_of(1 - far_ref[0], width)]
 
     here = pl.ds(pl.multiple_of(expert * cap, 16), cap)
     pick = pick_ref[here, :].astype(F32)
@@ -241,9 +242,12 @@
     store_halves(dot_tn(c_rows[...], acts[...]), near_ref, both, keep_ref, give_ref)
 
 
-def partial_kernel(cap, near_ref, rows_ref, own_ref, far_ref, keep_ref, give_ref, grads, both):
-    grads[:cap, :] = own_ref[0]
-    grads[cap:, :] = far_ref[0]
+def both_kernel(cap, near_ref, rows_ref, d_gate_ref, gate_far_ref, d_up_ref, up_far_ref, keep_ref, give_ref, grads, both):
+    hidden = d_gate_ref.shape[2]
+    grads[:cap, :hidden] = d_gate_ref[0]
+    grads[cap:, :hidden] = gate_far_ref[0]
+    grads[:cap, hidden:] = d_up_ref[0]
+    grads[cap:, hidden:] = up_far_ref[0]
     store_halves(dot_tn(rows_ref[0], grads[...]), near_ref, both, keep_ref, give_ref)
 
 
@@ -371,30 +375,26 @@
     x_line = gather_upper(x_own)
     x_line[2] = send(x_own, 2)
     x_pair = {k: send(x_line[k], 1) for k in (0, 2)}
-    x_line, x_pair, cot = fence(x_line, x_pair, cotangent)
+    x_line, x_pair[0], cot = fence(x_line, x_pair[0], cotangent)
 
     x_line.update({k | 2: send(x_line[k], 2) for k in folds})
+    c_line = gather_upper(cot)
     x_pair.update({k: send(x_line[k], 1) for k in folds})
-    c_line = gather_upper(cot)
-    c_line[2] = send(cot, 2)
-    c_pair = {0: send(cot, 1)}
-    x_line, c_line, x_pair, c_pair = fence(x_line, c_line, x_pair, c_pair)
+    x_line, c_line, x_pair = fence(x_line, c_line, x_pair)
     x_pair.update({k: send(x_line[k], 1) for k in sides})
     x_far = swap(cut_far([x_line[k] for k in line_blocks], "cut_x"), far_bit, n_dp)
-    x_pair, c_line = fence(x_pair, c_line)
-
+    c_line[2] = send(c_line[0], 2)
     c_line.update({k | 2: send(c_line[k], 2) for k in folds})
-    c_pair.update({k: send(c_line[k], 1) for k in [2] + folds})
-    x_far_pair = swap(cut_far([x_pair[k] for k in line_blocks], "cut_x_pair"), far_bit, n_dp)
-    pre, act, info, pick, combine, x_keep = pl.pallas_call(
+    c_pair = {k: send(c_line[k], 1) for k in [0] + folds}
+    pre, act, info, pick, combine, x_keep, x_give = pl.pallas_call(
         functools.partial(hidden_kernel, cfg),
         grid=(local,),
         in_specs=[smem] * 2 + [any_space] * parts + [weight_spec] * 2,
         out_specs=[by_expert(cap, 2 * hidden), by_expert(cap, hidden + LANES), by_expert(cap, LANES),
-                   whole(local * cap, total), whole(total, local * cap_pad), whole(total, half)],
+                   whole(local * cap, total), whole(total, local * cap_pad), whole(total, half), whole(line, half)],
         out_shape=[sds((local, cap, 2 * hidden), F32), sds((local, cap, hidden + LANES), BF16),
                    sds((local, cap, LANES), F32), sds((local * cap, total), BF16), sds((total, local * cap_pad), BF16),
-                   sds((total, half), BF16)],
+                   sds((total, half), BF16), sds((line, half), BF16)],
         scratch_shapes=[
             pltpu.VMEM((total, wide), BF16),
             pltpu.VMEM((local * cap, wide), BF16),
@@ -406,7 +406,8 @@
     )(first, far_word, *[x_line[k] for k in line_blocks], *[x_pair[k] for k in line_blocks], w_gate, w_up)
     act, c_line, c_pair, x_far = fence(act, c_line, c_pair, x_far)
 
-    c_pair.update({k: send(c_line[k], 1) for k in sides})
+    c_pair.update({k: send(c_line[k], 1) for k in [2] + sides})
+    x_far_pair = swap(x_give, far_bit, n_dp)
     act_far = swap(act, far_bit, n_dp)
     level_rows = [line] + [len(group) * tok_rows for group in groups]
     level_specs = [whole(rows, width) for rows in level_rows]
@@ -471,7 +472,6 @@
     mixed_sides = send(mixed_sides, 2)
     mixed_got.append(send(mixed_out[2], 1))
     c_far_pair = swap(c_give, far_bit, n_dp)
-    gate_far = swap(d_gate, far_bit, n_dp)
     wide_specs = [whole(rows, wide) for rows in level_rows]
     input_keep, *input_out = pl.pallas_call(
         functools.partial(input_kernel, (plan, local, cap, cap_pad)),
@@ -485,20 +485,18 @@
         cost_estimate=cost(6, 16),
         name="input_grads",
     )(d_gate, d_up, combine, tail, w_gate, w_up)
-    input_keep, input_out, mixed_sides, mixed_got, c_far, d_up = fence(
-        input_keep, input_out, mixed_sides, mixed_got, c_far, d_up)
+    input_keep, input_out, mixed_sides, mixed_got, c_far, d_gate = fence(
+        input_keep, input_out, mixed_sides, mixed_got, c_far, d_gate)
 
     input_got = [send(part, 1) for part in input_out[:2]]
     mixed_landed = fold_upper(back_rows(pair_sums(mixed_keep, mixed_got[1], folds), mixed_sides))
-    mixed_ends = pair_sums(mixed_keep, mixed_got[2], [2, 0])
-    mixed_landed.append(send(mixed_ends[:tok_rows].astype(BF16), 2))
-    input_sides, input_out = fence(pair_sums(input_keep, input_got[0], sides).astype(BF16), input_out)
+    gate_far = swap(d_gate, far_bit, n_dp)
+    input_sides, input_out, c_far_pair, x_keep, d_up, mixed_got[2] = fence(
+        pair_sums(input_keep, input_got[0], sides).astype(BF16), input_out, c_far_pair, x_keep, d_up, mixed_got[2])
     input_sides = send(input_sides, 2)
-    input_folds, c_far_pair, mixed_landed, d_up, x_keep = fence(
-        back_rows(pair_sums(input_keep, input_got[1], folds), input_sides).astype(BF16), c_far_pair, mixed_landed, d_up, x_keep)
-    input_landed = fold_upper(input_folds)
     input_got.append(send(input_out[2], 1))
     up_far = swap(d_up, far_bit, n_dp)
+    mixed_ends = pair_sums(mixed_keep, mixed_got[2], [2, 0])
     partial_specs = [by_expert(columns, hidden)] * 2
     partial_shapes = [sds((local, columns, hidden), BF16)] * 2
     x_rows, down_keep, down_give = pl.pallas_call(
@@ -513,35 +511,34 @@
         cost_estimate=cost(6, 12),
         name="down_grads",
     )(near_word, pick, x_keep, x_far, x_far_pair, c_keep, c_far, c_far_pair, act, act_far)
-    input_ends, input_landed, x_rows, down_keep, down_give, gate_far = fence(
-        pair_sums(input_keep, input_got[2], [2, 0]), input_landed, x_rows, down_keep, down_give, gate_far)
-
+    input_folds, mixed_landed, x_rows, down_keep, down_give = fence(
+        back_rows(pair_sums(input_keep, input_got[1], folds), input_sides).astype(BF16),
+        mixed_landed, x_rows, down_keep, down_give)
+
+    input_landed = fold_upper(input_folds)
+    mixed_landed.append(send(mixed_ends[:tok_rows].astype(BF16), 2))
+    input_ends = pair_sums(input_keep, input_got[2], [2, 0])
     input_landed.append(send(input_ends[:tok_rows].astype(BF16), 2))
     down_got = swap(down_give, 1, n_dp)
-
-    def partial_grads(grads, grads_far, name):
-        return pl.pallas_call(
-            functools.partial(partial_kernel, cap),
-            grid=(local,),
-            in_specs=[smem, by_expert(2 * cap, half)] + [by_expert(cap, hidden)] * 2,
-            out_specs=partial_specs,
-            out_shape=partial_shapes,
-            scratch_shapes=[pltpu.VMEM((2 * cap, hidden), BF16), pltpu.VMEM((half, hidden), BF16)],
-            compiler_params=params,
-            cost_estimate=cost(3, 10),
-            name=name,
-        )(near_word, x_rows, grads, grads_far)
-
-    gate_keep, gate_give = partial_grads(d_gate, gate_far, "gate_grads")
-    gate_got = swap(gate_give, 1, n_dp)
+    mixed = finish(mixed_ends, mixed_landed).astype(BF16)
+    mixed, input_ends, input_landed, gate_far, up_far = fence(mixed, input_ends, input_landed, gate_far, up_far)
+    both_specs = [by_expert(columns, 2 * hidden)] * 2
+    both_keep, both_give = pl.pallas_call(
+        functools.partial(both_kernel, cap),
+        grid=(local,),
+        in_specs=[smem, by_expert(2 * cap, half)] + [by_expert(cap, hidden)] * 4,
+        out_specs=both_specs,
+        out_shape=[sds((local, columns, 2 * hidden), BF16)] * 2,
+        scratch_shapes=[pltpu.VMEM((2 * cap, 2 * hidden), BF16), pltpu.VMEM((half, 2 * hidden), BF16)],
+        compiler_params=params,
+        cost_estimate=cost(3, 10),
+        name="gate_up_grads",
+    )(near_word, x_rows, d_gate, gate_far, d_up, up_far)
+    both_got = swap(both_give, 1, n_dp)
     down_grad = back_rows(down_keep, down_got).astype(BF16)
-    gate_grad = back_rows(gate_keep, gate_got).astype(BF16)
-    up_far, input_landed, gate_grad, down_grad = fence(up_far, input_landed, gate_grad, down_grad)
-    up_keep, up_give = partial_grads(d_up, up_far, "up_grads")
-    up_got = swap(up_give, 1, n_dp)
-    up_grad = back_rows(up_keep, up_got).astype(BF16)
-
-    mixed = finish(mixed_ends, mixed_landed).astype(BF16)
+    gate_grad = back_rows(both_keep[:, :, :hidden], both_got[:, :, :hidden]).astype(BF16)
+    up_grad = back_rows(both_keep[:, :, hidden:], both_got[:, :, hidden:]).astype(BF16)
+
     back = finish(input_ends, input_landed)
     token_grad = back[:, :width].astype(BF16)
     tail = back[:, width:]

time: 185 us -> 171 us (0.924)
  waiting for transfers between devices: 45.5 us -> 38.8 us
  Pallas kernels: 70 us -> 64.1 us
  starting transfers between devices: 46.5 us -> 41.6 us
    ppermute x26, waiting for transfers between devices: 37.5 us -> 31 us  [exchange(): return lax.ppermute(value, 'expert', [(i, i ^ bit) for i in range(count)])]
    pallas_call x2 -> x1, Pallas kernels: 11.8 us -> 7.72 us  [shards(): pl.pallas_call(functools.partial(both_kernel, cap), grid=(local,), in_spe...]
    ppermute x26, starting transfers between devices: 38.2 us -> 34.9 us  [exchange(): return lax.ppermute(value, 'expert', [(i, i ^ bit) for i in range(count)])]
    pallas_call x2 -> x1, Pallas kernels: 3.87 us -> 1.93 us  [cut_blocks(): pl.pallas_call(functools.partial(cut_kernel, size, plan), in_specs=[smem]...]
    ppermute x10 -> x9, starting transfers between devices: 8.3 us -> 6.68 us  [swap(): return lax.ppermute(value, 'dp', [(i, i ^ bit) for i in range(count)])]
    convert_element_type x2 -> x1, other arithmetic: 5.99 us -> 4.4 us  [shards(): back_rows(both_keep[:, :, hidden:], both_got[:, :, hidden:]).astype(BF16)]
    unnamed x60 -> x58, local copies, waits for them, and re-layouts: 3.07 us -> 3.92 us
    ppermute x10 -> x9, waiting for transfers between devices: 8.04 us -> 7.85 us  [swap(): return lax.ppermute(value, 'dp', [(i, i ^ bit) for i in range(count)])]
  transfers between devices with their start and end apart: 36 -> 35, of which waited for: 12 -> 10; matrix products, arithmetic and copies ran while one was open for 7% -> 8% of each run, Pallas kernels for 32% -> 33%
where the time goes in v1:
time: 171 us; the launch traced here: 170 us
  Pallas kernels  64.1 us (37%)
  starting transfers between devices  41.6 us (24%)
  waiting for transfers between devices  38.8 us (23%)
  other arithmetic  18 us (11%)
  local copies, waits for them, and re-layouts  6.64 us (4%)
    ppermute x26, starting transfers between devices, exchange(): return lax.ppermute(value, 'expert', [(i, i ^ bit) for i in range(count)])  34.9 us
    ppermute x26, waiting for transfers between devices, exchange(): return lax.ppermute(value, 'expert', [(i, i ^ bit) for i in range(count)])  31 us
    pallas_call x1, Pallas kernels, shards(): pl.pallas_call(functools.partial(hidden_kernel, cfg), grid=(local,), in_s...  12.8 us
    pallas_call x1, Pallas kernels, shards(): pl.pallas_call(functools.partial(grad_kernel, cfg), grid=(local,), in_spe...  11.4 us
    pallas_call x1, Pallas kernels, shards(): pl.pallas_call(functools.partial(input_kernel, (plan, local, cap, cap_pad...  10.9 us
    pallas_call x1, Pallas kernels, shards(): pl.pallas_call(functools.partial(down_kernel, cap), grid=(local,), in_spe...  9.82 us
    pallas_call x1, Pallas kernels, shards(): pl.pallas_call(functools.partial(mixed_kernel, (plan, levels, local, cap,...  9.52 us
    ppermute x9, waiting for transfers between devices, swap(): return lax.ppermute(value, 'dp', [(i, i ^ bit) for i in range(count)])  7.85 us
  transfers between devices with their start and end apart: 35, of which 10 were waited for; matrix products, arithmetic and copies ran while one was open for 8% of the time, Pallas kernels for 33%

profile of v1, /device:TPU:0, one launch (start us, length us, event | category | flops | bytes accessed | tf_op | source)
XLA Modules:
  0.0 170.3 jit_solution(831160508694648239)
XLA Ops:
  0.6 0.8 copy.16
  1.5 0.7 reduce_sum.18
  2.2 0.7 convert_element_type.113
  3.1 1.0 pad_maximum_fusion.refs_0_
  4.1 3.1 %collective-permute-start = (bf16[64,2176]{1,0:T(8,128)(2,1)S(1)}, bf16[64,2176]{1,0:T(8,128)(2,1)S(1)}, u32[]{:S(2)}, u32[]{:S(2)}) collective-permute-start(bf16[64,2176]{1,0:T(8,128)(2,1)S(1)} %pad_maximum_fusion.refs_0_), channel_id=1, source_target_pairs={{0,8},{4,12},{8,0},{12,4},{16,24},{20,28},{24,16},{28,20},{1,9},{5... | collective-permute-start | bytes 835592 | tf_op jit(solution)/shard_map/ppermute | solution.py:274
  7.2 2.6 %collective-permute-start.1 = (bf16[64,2176]{1,0:T(8,128)(2,1)S(1)}, bf16[64,2176]{1,0:T(8,128)(2,1)S(1)}, u32[]{:S(2)}, u32[]{:S(2)}) collective-permute-start(bf16[64,2176]{1,0:T(8,128)(2,1)S(1)} %pad_maximum_fusion.refs_0_), channel_id=1, source_target_pairs={{0,16},{4,20},{8,24},{12,28},{16,0},{20,4},{24,8},{28,12},{1,17},{... | collective-permute-start | bytes 835592 | tf_op jit(solution)/shard_map/ppermute | solution.py:274
  9.8 1.5 collective-permute-start.2
  11.3 8.4 %collective-permute-done.refs_1_ = bf16[64,2176]{1,0:T(8,128)(2,1)S(1)} collective-permute-done((bf16[64,2176]{1,0:T(8,128)(2,1)S(1)}, bf16[64,2176]{1,0:T(8,128)(2,1)S(1)}, u32[]{:S(2)}, u32[]{:S(2)}) %collective-permute-start) | collective-permute-done | bytes 278560 | tf_op jit(solution)/shard_map/ppermute | solution.py:274
  19.7 2.5 %collective-permute-done.1.refs_2_ = bf16[64,2176]{1,0:T(8,128)(2,1)S(1)} collective-permute-done((bf16[64,2176]{1,0:T(8,128)(2,1)S(1)}, bf16[64,2176]{1,0:T(8,128)(2,1)S(1)}, u32[]{:S(2)}, u32[]{:S(2)}) %collective-permute-start.1) | collective-permute-done | bytes 278560 | tf_op jit(solution)/shard_map/ppermute | solution.py:274
  22.3 0.5 collective-permute-start.3
  22.8 1.5 collective-permute-start.5
  24.3 0.5 collective-permute-start.6
  24.8 2.7 %collective-permute-start.4 = (bf16[64,2048]{1,0:T(8,128)(2,1)}, bf16[64,2048]{1,0:T(8,128)(2,1)S(1)}, u32[]{:S(2)}, u32[]{:S(2)}) collective-permute-start(bf16[64,2048]{1,0:T(8,128)(2,1)} %refs_0_.1), channel_id=1, source_target_pairs={{0,16},{4,20},{8,24},{12,28},{16,0},{20,4},{24,8},{28,12},{1,17},{... | collective-permute-start | bytes 786440 | tf_op jit(solution)/shard_map/ppermute | solution.py:274
  27.5 10.3 %collective-permute-done.4.refs_2_ = bf16[64,2048]{1,0:T(8,128)(2,1)S(1)} collective-permute-done((bf16[64,2048]{1,0:T(8,128)(2,1)}, bf16[64,2048]{1,0:T(8,128)(2,1)S(1)}, u32[]{:S(2)}, u32[]{:S(2)}) %collective-permute-start.4) | collective-permute-done | bytes 262176 | tf_op jit(solution)/shard_map/ppermute | solution.py:274
  37.8 1.6 collective-permute-start.7
  39.4 1.9 %cut_x.1 = bf16[256,1024]{1,0:T(8,128)(2,1)} custom-call(s32[1]{0:T(128)} %bitcast.1.far_ref.word_ref, bf16[64,2176]{1,0:T(8,128)(2,1)} %copy-done.2, bf16[64,2176]{1,0:T(8,128)(2,1)} %copy-done.7, bf16[64,2176]{1,0:T(8,128)(2,1)} %copy-done.8, bf16[64,2176]{1,0:T(8,128)(2,1)} %copy-done.9), custom_call_target="tpu_custom_call" | custom-call | bytes 2000 | tf_op jit(solution)/shard_map/cut_x/pallas_call | solution.py:350
  41.3 1.6 collective-permute-start.12
  42.9 0.6 collective-permute-start.10
  43.6 2.0 %collective-permute-start.9 = (bf16[64,2048]{1,0:T(8,128)(2,1)S(1)}, bf16[64,2048]{1,0:T(8,128)(2,1)S(1)}, u32[]{:S(2)}, u32[]{:S(2)}) collective-permute-start(bf16[64,2048]{1,0:T(8,128)(2,1)S(1)} %collective-permute-done.4.refs_2_), channel_id=1, source_target_pairs={{0,8},{4,12},{8,0},{12,4},{16,24},{20,28},{24,16},{28,20},{1,9},{5... | collective-permute-start | bytes 786440 | tf_op jit(solution)/shard_map/ppermute | solution.py:274
  45.6 0.9 collective-permute-done.7.refs_7_
  46.4 2.1 %collective-permute-start.11 = (bf16[64,2048]{1,0:T(8,128)(2,1)S(1)}, bf16[64,2048]{1,0:T(8,128)(2,1)S(1)}, u32[]{:S(2)}, u32[]{:S(2)}) collective-permute-start(bf16[64,2048]{1,0:T(8,128)(2,1)S(1)} %collective-permute-done.4.refs_2_), channel_id=1, source_target_pairs={{0,4},{4,0},{8,12},{12,8},{16,20},{20,16},{24,28},{28,24},{1,5},{5... | collective-permute-start | bytes 786440 | tf_op jit(solution)/shard_map/ppermute | solution.py:274
  48.5 12.8 %hidden.1 = (f32[4,160,768]{2,1,0:T(8,128)}, bf16[4,160,512]{2,1,0:T(8,128)(2,1)}, f32[4,160,128]{2,1,0:T(8,128)}, bf16[640,512]{1,0:T(8,128)(2,1)}, bf16[512,10...) custom-call(s32[1]{0:T(128)} %bitcast.first_ref, s32[1]{0:T(128)} %bitcast.1.far_ref.word_ref, ...), custom_call_target="tpu_custom_call" | custom-call | flops 6000000 | bytes 20000 | tf_op jit(solution)/shard_map/hidden/pallas_call | solution.py:389
  61.4 2.0 %collective-permute-start.15 = (bf16[256,1024]{1,0:T(8,128)(2,1)}, bf16[256,1024]{1,0:T(8,128)(2,1)S(1)}, u32[]{:S(2)}, u32[]{:S(2)}) collective-permute-start(bf16[256,1024]{1,0:T(8,128)(2,1)} %get-tuple-element.126), channel_id=1, source_target_pairs={{0,2},{1,3},{2,0},{3,1},{4,6},{5,7},{6,4},{7,5},{8,10},{9,11},{10,... | collective-permute-start | bytes 1572872 | tf_op jit(solution)/shard_map/ppermute | solution.py:270
  63.5 0.7 collective-permute-start.13
  64.3 1.3 collective-permute-start.14
  65.7 9.5 %mixed.1 = (bf16[256,2048]{1,0:T(8,128)(2,1)}, bf16[64,2048]{1,0:T(8,128)(2,1)}, bf16[64,2048]{1,0:T(8,128)(2,1)}, bf16[128,2048]{1,0:T(8,128)(2,1)}, bf16[256,1024]{1,0:T(8,128)(2,1)}) custom-call(s32[1]{0:T(128)} %bitcast.1.far_ref.word_ref, bf16[4,160,512]{2,1,0:T(8,128)(2,1)} %get-tuple-element.117.act_ref.refs_6_, ...), custom_call_target="tpu_custom_call" | custom-call | flops 6000000 | bytes 10000 | tf_op jit(solution)/shard_map/mixed/pallas_call | solution.py:414
  75.3 0.7 copy-done.27
  76.0 0.7 collective-permute-start.16
  76.7 1.3 collective-permute-start.17
  78.0 2.0 %collective-permute-start.21 = (bf16[256,1024]{1,0:T(8,128)(2,1)}, bf16[256,1024]{1,0:T(8,128)(2,1)}, u32[]{:S(2)}, u32[]{:S(2)}) collective-permute-start(bf16[256,1024]{1,0:T(8,128)(2,1)} %get-tuple-element.152), channel_id=1, source_target_pairs={{0,2},{1,3},{2,0},{3,1},{4,6},{5,7},{6,4},{7,5},{8,10},{9,11},{10,... | collective-permute-start | bytes 1572872 | tf_op jit(solution)/shard_map/ppermute | solution.py:270
  80.0 11.4 %hidden_grads.1 = (bf16[4,160,384]{2,1,0:T(8,128)(2,1)}, bf16[4,160,384]{2,1,0:T(8,128)(2,1)}, bf16[512,128]{1,0:T(8,128)(2,1)}, bf16[512,1024]{1,0:T(8,128)(2,1)}, bf16[256,1024]{1,0:T(8,128)(2,1)}) custom-call(s32[1]{0:T(128)} %bitcast.1.far_ref.word_ref, bf16[64,2048]{1,0:T(8,128)(2,1)} %refs_0_.1, bf16[64,2048]{1,0:T(8,128)(2,1)} %copy-done.12, ...), custom_call_target="tpu_custom_call" | custom-call | flops 6000000 | bytes 12000 | tf_op jit(solution)/shard_map/hidden_grads/pallas_call | solution.py:451
  91.5 2.8 %collective-permute-done.18.refs_7_ = bf16[4,160,512]{2,1,0:T(8,128)(2,1)S(1)} collective-permute-done((bf16[4,160,512]{2,1,0:T(8,128)(2,1)S(1)}, bf16[4,160,512]{2,1,0:T(8,128)(2,1)S(1)}, u32[]{:S(2)}, u32[]{:S(2)}) %collective-permute-start.18) | collective-permute-done | bytes 655392 | tf_op jit(solution)/shard_map/ppermute | solution.py:270
  94.3 0.9 copy-done.15
  95.2 1.3 collective-permute-start.20
  96.7 10.9 %input_grads.1 = (bf16[256,2176]{1,0:T(8,128)(2,1)}, bf16[64,2176]{1,0:T(8,128)(2,1)}, bf16[64,2176]{1,0:T(8,128)(2,1)}, bf16[128,2176]{1,0:T(8,128)(2,1)}) custom-call(bf16[4,160,384]{2,1,0:T(8,128)(2,1)} %get-tuple-element.177.d_gate_ref, bf16[4,160,384]{2,1,0:T(8,128)(2,1)} %get-tuple-element.178.d_up_ref, ...), custom_call_target="tpu_custom_call" | custom-call | flops 6000000 | bytes 16000 | tf_op jit(solution)/shard_map/input_grads/pallas_call | solution.py:476
  107.7 1.3 collective-permute-done.20
  109.0 1.6 collective-permute-start.22
  110.6 0.4 collective-permute-start.24
  111.0 1.8 %add_convert_fusion.5 = bf16[64,2048]{1,0:T(8,128)(2,1)} fusion(bf16[64,2048]{1,0:T(8,128)(2,1)} %collective-permute-done.19, bf16[64,2048]{1,0:T(8,128)(2,1)} %collective-permute-done.17, bf16[256,2048]{1,0:T(8,128)(2,1)S(1)} %copy-done.14), kind=kLoop, calls=%fused_computation.14 | loop fusion | flops 786432 | bytes 1048576 | tf_op jit(solution)/shard_map/convert_element_type | solution.py:439
  112.8 1.0 collective-permute-start.26
  113.8 1.1 fusion.10
  115.0 0.7 collective-permute-done.22
  115.7 0.8 add_convert_fusion.4
  116.5 1.1 collective-permute-start.25
  117.6 1.2 convert_add_fusion.1
  118.7 0.7 slice.132
  119.5 1.0 collective-permute-start.27
  120.5 9.8 %down_grads.1 = (bf16[4,320,1024]{2,1,0:T(8,128)(2,1)}, bf16[4,512,384]{2,1,0:T(8,128)(2,1)}, bf16[4,512,384]{2,1,0:T(8,128)(2,1)}) custom-call(s32[1]{0:T(128)} %bitcast.2.near_ref, bf16[640,512]{1,0:T(8,128)(2,1)} %get-tuple-element.135.refs_8_.pick_ref, bf16[512,1024]{1,0:T(8,128)(2,1)} %get-tuple-element.164.refs_0_, bf16[256,1024]{1,0:T(8,128)(2,1)} %copy-done.16, ...), custom_call_target="tpu_custom_call" | custom-call | flops 6000000 | bytes 12000 | tf_op jit(solution)/shard_map/down_grads/pallas_call | solution.py:502
  130.3 1.7 collective-permute-start.28
  132.2 1.1 add_convert_fusion.3
  133.3 3.0 %collective-permute-start.29 = (bf16[64,2176]{1,0:T(8,128)(2,1)S(1)}, bf16[64,2176]{1,0:T(8,128)(2,1)S(1)}, u32[]{:S(2)}, u32[]{:S(2)}) collective-permute-start(bf16[64,2176]{1,0:T(8,128)(2,1)S(1)} %add_convert_fusion.3), channel_id=1, source_target_pairs={{0,16},{4,20},{8,24},{12,28},{16,0},{20,4},{24,8},{28,12},{1,17},{... | collective-permute-start | bytes 835592 | tf_op jit(solution)/shard_map/ppermute | solution.py:274
  136.3 3.8 %collective-permute-done.28 = bf16[128,2176]{1,0:T(8,128)(2,1)S(1)} collective-permute-done((bf16[128,2176]{1,0:T(8,128)(2,1)}, bf16[128,2176]{1,0:T(8,128)(2,1)S(1)}, u32[]{:S(2)}, u32[]{:S(2)}) %collective-permute-start.28) | collective-permute-done | bytes 557088 | tf_op jit(solution)/shard_map/ppermute | solution.py:274
  140.2 1.1 collective-permute-start.30
  141.4 1.8 %fusion.1 = bf16[64,2048]{1,0:T(8,128)(2,1)} fusion(f32[128,2048]{1,0:T(8,128)S(1)} %convert_add_fusion.1, bf16[64,2048]{1,0:T(8,128)(2,1)} %collective-permute-done.27, bf16[64,2048]{1,0:T(8,128)(2,1)} %collective-permute-done.26), kind=kLoop, calls=%fused_computation.13 | loop fusion | flops 655360 | bytes 1310720 | tf_op jit(solution)/shard_map/convert_element_type | solution.py:523
  143.2 0.8 copy-done.19
  144.0 3.0 %collective-permute-done.30 = bf16[64,2176]{1,0:T(8,128)(2,1)} collective-permute-done((bf16[64,2176]{1,0:T(8,128)(2,1)S(1)}, bf16[64,2176]{1,0:T(8,128)(2,1)}, u32[]{:S(2)}, u32[]{:S(2)}) %collective-permute-start.30) | collective-permute-done | bytes 278560 | tf_op jit(solution)/shard_map/ppermute | solution.py:274
  147.0 7.7 %gate_up_grads.1 = (bf16[4,512,768]{2,1,0:T(8,128)(2,1)}, bf16[4,512,768]{2,1,0:T(8,128)(2,1)}) custom-call(s32[1]{0:T(128)} %bitcast.2.near_ref, bf16[4,320,1024]{2,1,0:T(8,128)(2,1)} %get-tuple-element.183.rows_ref, bf16[4,160,384]{2,1,0:T(8,128)(2,1)} %get-tuple-element.177.d_gate_ref, bf16[4,160,384]{2,1,0:T(8,128)(2,1)} %collective-permute-done.31.gate_far_ref, ...), custom_call_target="tpu_custom_call" | custom-call | flops 3000000 | bytes 10000 | tf_op jit(solution)/shard_map/gate_up_grads/pallas_call | solution.py:526
  154.7 0.5 collective-permute-start.34
  155.2 1.0 convert_add_fusion.2
  156.2 0.7 slice.131
  157.3 0.7 copy.20
  157.9 5.0 %collective-permute-done.34 = bf16[4,512,384]{2,1,0:T(8,128)(2,1)} collective-permute-done((bf16[4,512,384]{2,1,0:T(8,128)(2,1)}, bf16[4,512,384]{2,1,0:T(8,128)(2,1)}, u32[]{:S(2)}, u32[]{:S(2)}) %collective-permute-start.34) | collective-permute-done | bytes 1572896 | tf_op jit(solution)/shard_map/ppermute | solution.py:270
  162.9 2.9 %add_convert_fusion = bf16[4,512,384]{2,1,0:T(8,128)(2,1)} fusion(bf16[4,512,384]{2,1,0:T(8,128)(2,1)} %collective-permute-done.34, bf16[4,512,384]{2,1,0:T(8,128)(2,1)S(1)} %copy-done.5), kind=kLoop, calls=%fused_computation | loop fusion | flops 3145728 | bytes 4718592 | tf_op jit(solution)/shard_map/convert_element_type | solution.py:538
  165.9 4.4 %add_convert_fusion.1 = (bf16[4,512,384]{2,1,0:T(8,128)(2,1)}, bf16[4,512,384]{2,1,0:T(8,128)(2,1)}) fusion(bf16[4,512,768]{2,1,0:T(8,128)(2,1)} %collective-permute-done.33, bf16[4,512,768]{2,1,0:T(8,128)(2,1)S(1)} %copy-done), kind=kLoop, calls=%fused_computation.1 | loop fusion | flops 6291456 | bytes 9437184 | tf_op jit(solution)/shard_map/convert_element_type | solution.py:540
  (94 shorter events, 1.6 us)
Async XLA Ops:
  0.6 42.3 %copy-start.10 = (bf16[64,2048]{1,0:T(8,128)(2,1)S(1)}, bf16[64,2048]{1,0:T(8,128)(2,1)}, u32[]{:S(2)}) copy-start(bf16[64,2048]{1,0:T(8,128)(2,1)} %refs_0_.1) | copy-start | bytes 786436
  4.1 35.3 %copy-start.2 = (bf16[64,2176]{1,0:T(8,128)(2,1)}, bf16[64,2176]{1,0:T(8,128)(2,1)S(1)}, u32[]{:S(2)}) copy-start(bf16[64,2176]{1,0:T(8,128)(2,1)S(1)} %pad_maximum_fusion.refs_0_) | copy-start | bytes 835588
  4.1 15.6 %collective-permute-start = (bf16[64,2176]{1,0:T(8,128)(2,1)S(1)}, bf16[64,2176]{1,0:T(8,128)(2,1)S(1)}, u32[]{:S(2)}, u32[]{:S(2)}) collective-permute-start(bf16[64,2176]{1,0:T(8,128)(2,1)S(1)} %pad_maximum_fusion.refs_0_), channel_id=1, source_target_pairs={{0,8},{4,12},{8,0},{12,4},{16,24},{20,28},{24,16},{28,20},{1,9},{5... | collective-permute-start | bytes 835592 | tf_op jit(solution)/shard_map/ppermute | solution.py:274
  7.2 15.0 %collective-permute-start.1 = (bf16[64,2176]{1,0:T(8,128)(2,1)S(1)}, bf16[64,2176]{1,0:T(8,128)(2,1)S(1)}, u32[]{:S(2)}, u32[]{:S(2)}) collective-permute-start(bf16[64,2176]{1,0:T(8,128)(2,1)S(1)} %pad_maximum_fusion.refs_0_), channel_id=1, source_target_pairs={{0,16},{4,20},{8,24},{12,28},{16,0},{20,4},{24,8},{28,12},{1,17},{... | collective-permute-start | bytes 835592 | tf_op jit(solution)/shard_map/ppermute | solution.py:274
  9.8 12.4 %collective-permute-start.2 = (bf16[64,2176]{1,0:T(8,128)(2,1)S(1)}, bf16[64,2176]{1,0:T(8,128)(2,1)S(1)}, u32[]{:S(2)}, u32[]{:S(2)}) collective-permute-start(bf16[64,2176]{1,0:T(8,128)(2,1)S(1)} %pad_maximum_fusion.refs_0_), channel_id=1, source_target_pairs={{0,4},{4,0},{8,12},{12,8},{16,20},{20,16},{24,28},{28,24},{1,5},{5... | collective-permute-start | bytes 835592 | tf_op jit(solution)/shard_map/ppermute | solution.py:274
  19.7 19.7 %copy-start.7 = (bf16[64,2176]{1,0:T(8,128)(2,1)}, bf16[64,2176]{1,0:T(8,128)(2,1)S(1)}, u32[]{:S(2)}) copy-start(bf16[64,2176]{1,0:T(8,128)(2,1)S(1)} %collective-permute-done.refs_1_) | copy-start | bytes 835588
  22.3 17.2 %copy-start.8 = (bf16[64,2176]{1,0:T(8,128)(2,1)}, bf16[64,2176]{1,0:T(8,128)(2,1)S(1)}, u32[]{:S(2)}) copy-start(bf16[64,2176]{1,0:T(8,128)(2,1)S(1)} %collective-permute-done.1.refs_2_) | copy-start | bytes 835588
  22.3 26.3 %copy-start.20 = (bf16[64,2176]{1,0:T(8,128)(2,1)}, bf16[64,2176]{1,0:T(8,128)(2,1)S(1)}, u32[]{:S(2)}) copy-start(bf16[64,2176]{1,0:T(8,128)(2,1)S(1)} %collective-permute-done.2.refs_4_) | copy-start | bytes 835588
  22.3 15.5 %collective-permute-start.3 = (bf16[64,2176]{1,0:T(8,128)(2,1)S(1)}, bf16[64,2176]{1,0:T(8,128)(2,1)S(1)}, u32[]{:S(2)}, u32[]{:S(2)}) collective-permute-start(bf16[64,2176]{1,0:T(8,128)(2,1)S(1)} %collective-permute-done.1.refs_2_), channel_id=1, source_target_pairs={{0,8},{4,12},{8,0},{12,4},{16,24},{20,28},{24,16},{28,20},{1,9},{5... | collective-permute-start | bytes 835592 | tf_op jit(solution)/shard_map/ppermute | solution.py:274
  22.8 15.0 %collective-permute-start.5 = (bf16[64,2176]{1,0:T(8,128)(2,1)S(1)}, bf16[64,2176]{1,0:T(8,128)(2,1)S(1)}, u32[]{:S(2)}, u32[]{:S(2)}) collective-permute-start(bf16[64,2176]{1,0:T(8,128)(2,1)S(1)} %collective-permute-done.refs_1_), channel_id=1, source_target_pairs={{0,4},{4,0},{8,12},{12,8},{16,20},{20,16},{24,28},{28,24},{1,5},{5... | collective-permute-start | bytes 835592 | tf_op jit(solution)/shard_map/ppermute | solution.py:274
  24.3 13.6 %collective-permute-start.6 = (bf16[64,2176]{1,0:T(8,128)(2,1)S(1)}, bf16[64,2176]{1,0:T(8,128)(2,1)S(1)}, u32[]{:S(2)}, u32[]{:S(2)}) collective-permute-start(bf16[64,2176]{1,0:T(8,128)(2,1)S(1)} %collective-permute-done.1.refs_2_), channel_id=1, source_target_pairs={{0,4},{4,0},{8,12},{12,8},{16,20},{20,16},{24,28},{28,24},{1,5},{5... | collective-permute-start | bytes 835592 | tf_op jit(solution)/shard_map/ppermute | solution.py:274
  24.8 13.0 %collective-permute-start.4 = (bf16[64,2048]{1,0:T(8,128)(2,1)}, bf16[64,2048]{1,0:T(8,128)(2,1)S(1)}, u32[]{:S(2)}, u32[]{:S(2)}) collective-permute-start(bf16[64,2048]{1,0:T(8,128)(2,1)} %refs_0_.1), channel_id=1, source_target_pairs={{0,16},{4,20},{8,24},{12,28},{16,0},{20,4},{24,8},{28,12},{1,17},{... | collective-permute-start | bytes 786440 | tf_op jit(solution)/shard_map/ppermute | solution.py:274
  37.8 23.6 %copy-start.11 = (bf16[64,2048]{1,0:T(8,128)(2,1)}, bf16[64,2048]{1,0:T(8,128)(2,1)S(1)}, u32[]{:S(2)}) copy-start(bf16[64,2048]{1,0:T(8,128)(2,1)S(1)} %collective-permute-done.4.refs_2_) | copy-start | bytes 786436
  37.8 1.6 copy-start.9
  37.8 10.7 %copy-start.21 = (bf16[64,2176]{1,0:T(8,128)(2,1)}, bf16[64,2176]{1,0:T(8,128)(2,1)S(1)}, u32[]{:S(2)}) copy-start(bf16[64,2176]{1,0:T(8,128)(2,1)S(1)} %collective-permute-done.5.refs_5_) | copy-start | bytes 835588
  37.8 10.7 %copy-start.22 = (bf16[64,2176]{1,0:T(8,128)(2,1)}, bf16[64,2176]{1,0:T(8,128)(2,1)S(1)}, u32[]{:S(2)}) copy-start(bf16[64,2176]{1,0:T(8,128)(2,1)S(1)} %collective-permute-done.6.refs_6_) | copy-start | bytes 835588
  37.8 8.6 %collective-permute-start.7 = (bf16[64,2176]{1,0:T(8,128)(2,1)S(1)}, bf16[64,2176]{1,0:T(8,128)(2,1)S(1)}, u32[]{:S(2)}, u32[]{:S(2)}) collective-permute-start(bf16[64,2176]{1,0:T(8,128)(2,1)S(1)} %collective-permute-done.3.refs_3_), channel_id=1, source_target_pairs={{0,4},{4,0},{8,12},{12,8},{16,20},{20,16},{24,28},{28,24},{1,5},{5... | collective-permute-start | bytes 835592 | tf_op jit(solution)/shard_map/ppermute | solution.py:274
  41.3 22.2 %collective-permute-start.12 = (bf16[256,1024]{1,0:T(8,128)(2,1)}, bf16[256,1024]{1,0:T(8,128)(2,1)S(1)}, u32[]{:S(2)}, u32[]{:S(2)}) collective-permute-start(bf16[256,1024]{1,0:T(8,128)(2,1)} %cut_x.1), channel_id=1, source_target_pairs={{0,2},{1,3},{2,0},{3,1},{4,6},{5,7},{6,4},{7,5},{8,10},{9,11},{10,... | collective-permute-start | bytes 1572872 | tf_op jit(solution)/shard_map/ppermute | solution.py:270
  42.9 18.5 %collective-permute-start.8 = (bf16[64,2048]{1,0:T(8,128)(2,1)S(1)}, bf16[64,2048]{1,0:T(8,128)(2,1)S(1)}, u32[]{:S(2)}, u32[]{:S(2)}) collective-permute-start(bf16[64,2048]{1,0:T(8,128)(2,1)S(1)} %copy-done.10), channel_id=1, source_target_pairs={{0,8},{4,12},{8,0},{12,4},{16,24},{20,28},{24,16},{28,20},{1,9},{5... | collective-permute-start | bytes 786440 | tf_op jit(solution)/shard_map/ppermute | solution.py:274
  42.9 20.6 %collective-permute-start.10 = (bf16[64,2048]{1,0:T(8,128)(2,1)S(1)}, bf16[64,2048]{1,0:T(8,128)(2,1)S(1)}, u32[]{:S(2)}, u32[]{:S(2)}) collective-permute-start(bf16[64,2048]{1,0:T(8,128)(2,1)S(1)} %copy-done.10), channel_id=1, source_target_pairs={{0,4},{4,0},{8,12},{12,8},{16,20},{20,16},{24,28},{28,24},{1,5},{5... | collective-permute-start | bytes 786440 | tf_op jit(solution)/shard_map/ppermute | solution.py:274
  43.6 19.9 %collective-permute-start.9 = (bf16[64,2048]{1,0:T(8,128)(2,1)S(1)}, bf16[64,2048]{1,0:T(8,128)(2,1)S(1)}, u32[]{:S(2)}, u32[]{:S(2)}) collective-permute-start(bf16[64,2048]{1,0:T(8,128)(2,1)S(1)} %collective-permute-done.4.refs_2_), channel_id=1, source_target_pairs={{0,8},{4,12},{8,0},{12,4},{16,24},{20,28},{24,16},{28,20},{1,9},{5... | collective-permute-start | bytes 786440 | tf_op jit(solution)/shard_map/ppermute | solution.py:274
  46.4 2.1 %copy-start.23 = (bf16[64,2176]{1,0:T(8,128)(2,1)}, bf16[64,2176]{1,0:T(8,128)(2,1)S(1)}, u32[]{:S(2)}) copy-start(bf16[64,2176]{1,0:T(8,128)(2,1)S(1)} %collective-permute-done.7.refs_7_) | copy-start | bytes 835588
  46.4 17.1 %collective-permute-start.11 = (bf16[64,2048]{1,0:T(8,128)(2,1)S(1)}, bf16[64,2048]{1,0:T(8,128)(2,1)S(1)}, u32[]{:S(2)}, u32[]{:S(2)}) collective-permute-start(bf16[64,2048]{1,0:T(8,128)(2,1)S(1)} %collective-permute-done.4.refs_2_), channel_id=1, source_target_pairs={{0,4},{4,0},{8,12},{12,8},{16,20},{20,16},{24,28},{28,24},{1,5},{5... | collective-permute-start | bytes 786440 | tf_op jit(solution)/shard_map/ppermute | solution.py:274
  61.4 4.2 %copy-start.12 = (bf16[64,2048]{1,0:T(8,128)(2,1)}, bf16[64,2048]{1,0:T(8,128)(2,1)S(1)}, u32[]{:S(2)}) copy-start(bf16[64,2048]{1,0:T(8,128)(2,1)S(1)} %collective-permute-done.8.refs_1_) | copy-start | bytes 786436
  61.4 13.8 %collective-permute-start.15 = (bf16[256,1024]{1,0:T(8,128)(2,1)}, bf16[256,1024]{1,0:T(8,128)(2,1)S(1)}, u32[]{:S(2)}, u32[]{:S(2)}) collective-permute-start(bf16[256,1024]{1,0:T(8,128)(2,1)} %get-tuple-element.126), channel_id=1, source_target_pairs={{0,2},{1,3},{2,0},{3,1},{4,6},{5,7},{6,4},{7,5},{8,10},{9,11},{10,... | collective-permute-start | bytes 1572872 | tf_op jit(solution)/shard_map/ppermute | solution.py:270
  63.5 2.2 %copy-start.13 = (bf16[64,2048]{1,0:T(8,128)(2,1)}, bf16[64,2048]{1,0:T(8,128)(2,1)S(1)}, u32[]{:S(2)}) copy-start(bf16[64,2048]{1,0:T(8,128)(2,1)S(1)} %collective-permute-done.9.refs_3_) | copy-start | bytes 786436
  63.5 11.7 %copy-start.24 = (bf16[64,2048]{1,0:T(8,128)(2,1)}, bf16[64,2048]{1,0:T(8,128)(2,1)S(1)}, u32[]{:S(2)}) copy-start(bf16[64,2048]{1,0:T(8,128)(2,1)S(1)} %collective-permute-done.10.refs_4_) | copy-start | bytes 786436
  63.5 2.1 %copy-start.25 = (bf16[64,2048]{1,0:T(8,128)(2,1)}, bf16[64,2048]{1,0:T(8,128)(2,1)S(1)}, u32[]{:S(2)}) copy-start(bf16[64,2048]{1,0:T(8,128)(2,1)S(1)} %collective-permute-done.11.refs_6_) | copy-start | bytes 786436
  63.5 11.7 %copy-start.16 = (bf16[256,1024]{1,0:T(8,128)(2,1)}, bf16[256,1024]{1,0:T(8,128)(2,1)S(1)}, u32[]{:S(2)}) copy-start(bf16[256,1024]{1,0:T(8,128)(2,1)S(1)} %collective-permute-done.12.refs_1_) | copy-start | bytes 1572868
  63.5 11.7 %collective-permute-start.13 = (bf16[64,2048]{1,0:T(8,128)(2,1)S(1)}, bf16[64,2048]{1,0:T(8,128)(2,1)S(1)}, u32[]{:S(2)}, u32[]{:S(2)}) collective-permute-start(bf16[64,2048]{1,0:T(8,128)(2,1)S(1)} %collective-permute-done.8.refs_1_), channel_id=1, source_target_pairs={{0,4},{4,0},{8,12},{12,8},{16,20},{20,16},{24,28},{28,24},{1,5},{5... | collective-permute-start | bytes 786440 | tf_op jit(solution)/shard_map/ppermute | solution.py:274
  64.3 10.9 %collective-permute-start.14 = (bf16[64,2048]{1,0:T(8,128)(2,1)S(1)}, bf16[64,2048]{1,0:T(8,128)(2,1)S(1)}, u32[]{:S(2)}, u32[]{:S(2)}) collective-permute-start(bf16[64,2048]{1,0:T(8,128)(2,1)S(1)} %collective-permute-done.9.refs_3_), channel_id=1, source_target_pairs={{0,4},{4,0},{8,12},{12,8},{16,20},{20,16},{24,28},{28,24},{1,5},{5... | collective-permute-start | bytes 786440 | tf_op jit(solution)/shard_map/ppermute | solution.py:274
  65.6 11.0 %copy-start.1 = (bf16[4,160,512]{2,1,0:T(8,128)(2,1)S(1)}, bf16[4,160,512]{2,1,0:T(8,128)(2,1)}, u32[]{:S(2)}) copy-start(bf16[4,160,512]{2,1,0:T(8,128)(2,1)} %get-tuple-element.117.act_ref.refs_6_) | copy-start | bytes 1966084
  75.2 4.8 %copy-start.26 = (bf16[64,2048]{1,0:T(8,128)(2,1)}, bf16[64,2048]{1,0:T(8,128)(2,1)S(1)}, u32[]{:S(2)}) copy-start(bf16[64,2048]{1,0:T(8,128)(2,1)S(1)} %collective-permute-done.13.refs_5_) | copy-start | bytes 786436
  75.2 0.7 copy-start.27
  75.3 16.1 %copy-start.17 = (bf16[256,1024]{1,0:T(8,128)(2,1)}, bf16[256,1024]{1,0:T(8,128)(2,1)S(1)}, u32[]{:S(2)}) copy-start(bf16[256,1024]{1,0:T(8,128)(2,1)S(1)} %collective-permute-done.15.refs_2_) | copy-start | bytes 1572868
  76.0 15.4 %collective-permute-start.16 = (bf16[64,2048]{1,0:T(8,128)(2,1)}, bf16[64,2048]{1,0:T(8,128)(2,1)S(1)}, u32[]{:S(2)}, u32[]{:S(2)}) collective-permute-start(bf16[64,2048]{1,0:T(8,128)(2,1)} %get-tuple-element.128), channel_id=1, source_target_pairs={{0,4},{4,0},{8,12},{12,8},{16,20},{20,16},{24,28},{28,24},{1,5},{5... | collective-permute-start | bytes 786440 | tf_op jit(solution)/shard_map/ppermute | solution.py:274
  76.6 17.7 %collective-permute-start.18 = (bf16[4,160,512]{2,1,0:T(8,128)(2,1)S(1)}, bf16[4,160,512]{2,1,0:T(8,128)(2,1)S(1)}, u32[]{:S(2)}, u32[]{:S(2)}) collective-permute-start(bf16[4,160,512]{2,1,0:T(8,128)(2,1)S(1)} %copy-done.1), channel_id=1, source_target_pairs={{0,2},{1,3},{2,0},{3,1},{4,6},{5,7},{6,4},{7,5},{8,10},{9,11},{10,... | collective-permute-start | bytes 1966088 | tf_op jit(solution)/shard_map/ppermute | solution.py:270
  76.7 14.8 %collective-permute-start.17 = (bf16[64,2048]{1,0:T(8,128)(2,1)}, bf16[64,2048]{1,0:T(8,128)(2,1)}, u32[]{:S(2)}, u32[]{:S(2)}) collective-permute-start(bf16[64,2048]{1,0:T(8,128)(2,1)} %get-tuple-element.129), channel_id=1, source_target_pairs={{0,4},{4,0},{8,12},{12,8},{16,20},{20,16},{24,28},{28,24},{1,5},{5... | collective-permute-start | bytes 786440 | tf_op jit(solution)/shard_map/ppermute | solution.py:274
  78.0 29.6 %collective-permute-start.21 = (bf16[256,1024]{1,0:T(8,128)(2,1)}, bf16[256,1024]{1,0:T(8,128)(2,1)}, u32[]{:S(2)}, u32[]{:S(2)}) collective-permute-start(bf16[256,1024]{1,0:T(8,128)(2,1)} %get-tuple-element.152), channel_id=1, source_target_pairs={{0,2},{1,3},{2,0},{3,1},{4,6},{5,7},{6,4},{7,5},{8,10},{9,11},{10,... | collective-permute-start | bytes 1572872 | tf_op jit(solution)/shard_map/ppermute | solution.py:270
  80.0 11.4 %copy-start.14 = (bf16[256,2048]{1,0:T(8,128)(2,1)S(1)}, bf16[256,2048]{1,0:T(8,128)(2,1)}, u32[]{:S(2)}) copy-start(bf16[256,2048]{1,0:T(8,128)(2,1)} %get-tuple-element.127) | copy-start | bytes 3145732
  94.3 0.9 copy-start.15
  95.2 13.8 %collective-permute-start.20 = (bf16[128,2048]{1,0:T(8,128)(2,1)}, bf16[128,2048]{1,0:T(8,128)(2,1)S(1)}, u32[]{:S(2)}, u32[]{:S(2)}) collective-permute-start(bf16[128,2048]{1,0:T(8,128)(2,1)} %get-tuple-element.151), channel_id=1, source_target_pairs={{0,4},{4,0},{8,12},{12,8},{16,20},{20,16},{24,28},{28,24},{1,5},{5... | collective-permute-start | bytes 1572872 | tf_op jit(solution)/shard_map/ppermute | solution.py:274
  96.5 11.1 %collective-permute-start.19 = (bf16[64,2048]{1,0:T(8,128)(2,1)S(1)}, bf16[64,2048]{1,0:T(8,128)(2,1)}, u32[]{:S(2)}, u32[]{:S(2)}) collective-permute-start(bf16[64,2048]{1,0:T(8,128)(2,1)S(1)} %add_convert_fusion.6), channel_id=1, source_target_pairs={{0,8},{4,12},{8,0},{12,4},{16,24},{20,28},{24,16},{28,20},{1,9},{5... | collective-permute-start | bytes 786440 | tf_op jit(solution)/shard_map/ppermute | solution.py:274
  96.6 19.9 %collective-permute-start.23 = (bf16[256,1024]{1,0:T(8,128)(2,1)}, bf16[256,1024]{1,0:T(8,128)(2,1)}, u32[]{:S(2)}, u32[]{:S(2)}) collective-permute-start(bf16[256,1024]{1,0:T(8,128)(2,1)} %get-tuple-element.157), channel_id=1, source_target_pairs={{0,2},{1,3},{2,0},{3,1},{4,6},{5,7},{6,4},{7,5},{8,10},{9,11},{10,... | collective-permute-start | bytes 1572872 | tf_op jit(solution)/shard_map/ppermute | solution.py:270
  107.6 7.3 %copy-start.3 = (bf16[4,160,384]{2,1,0:T(8,128)(2,1)S(1)}, bf16[4,160,384]{2,1,0:T(8,128)(2,1)}, u32[]{:S(2)}) copy-start(bf16[4,160,384]{2,1,0:T(8,128)(2,1)} %get-tuple-element.177.d_gate_ref) | copy-start | bytes 1474564
  107.6 8.1 %copy-start.6 = (bf16[256,2176]{1,0:T(8,128)(2,1)S(1)}, bf16[256,2176]{1,0:T(8,128)(2,1)}, u32[]{:S(2)}) copy-start(bf16[256,2176]{1,0:T(8,128)(2,1)} %get-tuple-element.153) | copy-start | bytes 3342340
  109.0 8.6 %copy-start.18 = (bf16[128,2048]{1,0:T(8,128)(2,1)}, bf16[128,2048]{1,0:T(8,128)(2,1)S(1)}, u32[]{:S(2)}) copy-start(bf16[128,2048]{1,0:T(8,128)(2,1)S(1)} %collective-permute-done.20) | copy-start | bytes 1572868
  109.0 6.8 %collective-permute-start.22 = (bf16[64,2176]{1,0:T(8,128)(2,1)}, bf16[64,2176]{1,0:T(8,128)(2,1)S(1)}, u32[]{:S(2)}, u32[]{:S(2)}) collective-permute-start(bf16[64,2176]{1,0:T(8,128)(2,1)} %get-tuple-element.154), channel_id=1, source_target_pairs={{0,4},{4,0},{8,12},{12,8},{16,20},{20,16},{24,28},{28,24},{1,5},{5... | collective-permute-start | bytes 835592 | tf_op jit(solution)/shard_map/ppermute | solution.py:274
  110.6 19.7 %collective-permute-start.24 = (bf16[64,2176]{1,0:T(8,128)(2,1)}, bf16[64,2176]{1,0:T(8,128)(2,1)S(1)}, u32[]{:S(2)}, u32[]{:S(2)}) collective-permute-start(bf16[64,2176]{1,0:T(8,128)(2,1)} %get-tuple-element.155), channel_id=1, source_target_pairs={{0,4},{4,0},{8,12},{12,8},{16,20},{20,16},{24,28},{28,24},{1,5},{5... | collective-permute-start | bytes 835592 | tf_op jit(solution)/shard_map/ppermute | solution.py:274
  112.8 20.5 %collective-permute-start.26 = (bf16[64,2048]{1,0:T(8,128)(2,1)}, bf16[64,2048]{1,0:T(8,128)(2,1)}, u32[]{:S(2)}, u32[]{:S(2)}) collective-permute-start(bf16[64,2048]{1,0:T(8,128)(2,1)} %add_convert_fusion.5), channel_id=1, source_target_pairs={{0,16},{4,20},{8,24},{12,28},{16,0},{20,4},{24,8},{28,12},{1,17},{... | collective-permute-start | bytes 786440 | tf_op jit(solution)/shard_map/ppermute | solution.py:274
  114.9 28.3 %collective-permute-start.31 = (bf16[4,160,384]{2,1,0:T(8,128)(2,1)S(1)}, bf16[4,160,384]{2,1,0:T(8,128)(2,1)}, u32[]{:S(2)}, u32[]{:S(2)}) collective-permute-start(bf16[4,160,384]{2,1,0:T(8,128)(2,1)S(1)} %copy-done.3), channel_id=1, source_target_pairs={{0,2},{1,3},{2,0},{3,1},{4,6},{5,7},{6,4},{7,5},{8,10},{9,11},{10,... | collective-permute-start | bytes 1474568 | tf_op jit(solution)/shard_map/ppermute | solution.py:270
  116.5 15.4 %collective-permute-start.25 = (bf16[64,2176]{1,0:T(8,128)(2,1)}, bf16[64,2176]{1,0:T(8,128)(2,1)}, u32[]{:S(2)}, u32[]{:S(2)}) collective-permute-start(bf16[64,2176]{1,0:T(8,128)(2,1)} %add_convert_fusion.4), channel_id=1, source_target_pairs={{0,8},{4,12},{8,0},{12,4},{16,24},{20,28},{24,16},{28,20},{1,9},{5... | collective-permute-start | bytes 835592 | tf_op jit(solution)/shard_map/ppermute | solution.py:274
  119.5 21.9 %collective-permute-start.27 = (bf16[64,2048]{1,0:T(8,128)(2,1)}, bf16[64,2048]{1,0:T(8,128)(2,1)}, u32[]{:S(2)}, u32[]{:S(2)}) collective-permute-start(bf16[64,2048]{1,0:T(8,128)(2,1)} %slice.132), channel_id=1, source_target_pairs={{0,8},{4,12},{8,0},{12,4},{16,24},{20,28},{24,16},{28,20},{1,9},{5... | collective-permute-start | bytes 786440 | tf_op jit(solution)/shard_map/ppermute | solution.py:274
  120.5 11.5 %copy-start.4 = (bf16[4,160,384]{2,1,0:T(8,128)(2,1)S(1)}, bf16[4,160,384]{2,1,0:T(8,128)(2,1)}, u32[]{:S(2)}) copy-start(bf16[4,160,384]{2,1,0:T(8,128)(2,1)} %get-tuple-element.178.d_up_ref) | copy-start | bytes 1474564
  130.3 9.8 %collective-permute-start.28 = (bf16[128,2176]{1,0:T(8,128)(2,1)}, bf16[128,2176]{1,0:T(8,128)(2,1)S(1)}, u32[]{:S(2)}, u32[]{:S(2)}) collective-permute-start(bf16[128,2176]{1,0:T(8,128)(2,1)} %get-tuple-element.175), channel_id=1, source_target_pairs={{0,4},{4,0},{8,12},{12,8},{16,20},{20,16},{24,28},{28,24},{1,5},{5... | collective-permute-start | bytes 1671176 | tf_op jit(solution)/shard_map/ppermute | solution.py:274
  131.9 11.2 %collective-permute-start.32 = (bf16[4,160,384]{2,1,0:T(8,128)(2,1)S(1)}, bf16[4,160,384]{2,1,0:T(8,128)(2,1)S(1)}, u32[]{:S(2)}, u32[]{:S(2)}) collective-permute-start(bf16[4,160,384]{2,1,0:T(8,128)(2,1)S(1)} %copy-done.4), channel_id=1, source_target_pairs={{0,2},{1,3},{2,0},{3,1},{4,6},{5,7},{6,4},{7,5},{8,10},{9,11},{10,... | collective-permute-start | bytes 1474568 | tf_op jit(solution)/shard_map/ppermute | solution.py:270
  133.3 10.7 %collective-permute-start.29 = (bf16[64,2176]{1,0:T(8,128)(2,1)S(1)}, bf16[64,2176]{1,0:T(8,128)(2,1)S(1)}, u32[]{:S(2)}, u32[]{:S(2)}) collective-permute-start(bf16[64,2176]{1,0:T(8,128)(2,1)S(1)} %add_convert_fusion.3), channel_id=1, source_target_pairs={{0,16},{4,20},{8,24},{12,28},{16,0},{20,4},{24,8},{28,12},{1,17},{... | collective-permute-start | bytes 835592 | tf_op jit(solution)/shard_map/ppermute | solution.py:274
  140.2 6.7 %collective-permute-start.30 = (bf16[64,2176]{1,0:T(8,128)(2,1)S(1)}, bf16[64,2176]{1,0:T(8,128)(2,1)}, u32[]{:S(2)}, u32[]{:S(2)}) collective-permute-start(bf16[64,2176]{1,0:T(8,128)(2,1)S(1)} %slice.130), channel_id=1, source_target_pairs={{0,8},{4,12},{8,0},{12,4},{16,24},{20,28},{24,16},{28,20},{1,9},{5... | collective-permute-start | bytes 835592 | tf_op jit(solution)/shard_map/ppermute | solution.py:274
  143.2 0.8 copy-start.19
  154.7 8.3 %copy-start.5 = (bf16[4,512,384]{2,1,0:T(8,128)(2,1)S(1)}, bf16[4,512,384]{2,1,0:T(8,128)(2,1)}, u32[]{:S(2)}) copy-start(bf16[4,512,384]{2,1,0:T(8,128)(2,1)} %get-tuple-element.188) | copy-start | bytes 4718596
  154.7 11.2 %collective-permute-start.33 = (bf16[4,512,768]{2,1,0:T(8,128)(2,1)}, bf16[4,512,768]{2,1,0:T(8,128)(2,1)}, u32[]{:S(2)}, u32[]{:S(2)}) collective-permute-start(bf16[4,512,768]{2,1,0:T(8,128)(2,1)} %get-tuple-element.187), channel_id=1, source_target_pairs={{0,1},{1,0},{2,3},{3,2},{4,5},{5,4},{6,7},{7,6},{8,9},{9,8},{10,11... | collective-permute-start | bytes 9437192 | tf_op jit(solution)/shard_map/ppermute | solution.py:270
  154.7 8.2 %collective-permute-start.34 = (bf16[4,512,384]{2,1,0:T(8,128)(2,1)}, bf16[4,512,384]{2,1,0:T(8,128)(2,1)}, u32[]{:S(2)}, u32[]{:S(2)}) collective-permute-start(bf16[4,512,384]{2,1,0:T(8,128)(2,1)} %get-tuple-element.189), channel_id=1, source_target_pairs={{0,1},{1,0},{2,3},{3,2},{4,5},{5,4},{6,7},{7,6},{8,9},{9,8},{10,11... | collective-permute-start | bytes 4718600 | tf_op jit(solution)/shard_map/ppermute | solution.py:270
  157.9 8.0 %copy-start = (bf16[4,512,768]{2,1,0:T(8,128)(2,1)S(1)}, bf16[4,512,768]{2,1,0:T(8,128)(2,1)}, u32[]{:S(2)}) copy-start(bf16[4,512,768]{2,1,0:T(8,128)(2,1)} %get-tuple-element.186) | copy-start | bytes 9437188

commit v2 on v1

--- a/solution.py
+++ b/solution.py
@@ -407,7 +407,6 @@
     act, c_line, c_pair, x_far = fence(act, c_line, c_pair, x_far)
 
     c_pair.update({k: send(c_line[k], 1) for k in [2] + sides})
-    x_far_pair = swap(x_give, far_bit, n_dp)
     act_far = swap(act, far_bit, n_dp)
     level_rows = [line] + [len(group) * tok_rows for group in groups]
     level_specs = [whole(rows, width) for rows in level_rows]
@@ -422,7 +421,7 @@
         cost_estimate=cost(6, 10),
         name="mixed",
     )(far_word, act, combine, w_down, *[c_line[k] for k in line_blocks])
-    c_pair, mixed_keep, mixed_out, c_give, x_far_pair = fence(c_pair, mixed_keep, mixed_out, c_give, x_far_pair)
+    c_pair, mixed_keep, mixed_out, c_give, act_far = fence(c_pair, mixed_keep, mixed_out, c_give, act_far)
 
     def back_rows(keep, got):
         return keep.astype(F32) + got.astype(F32)
@@ -466,8 +465,8 @@
         cost_estimate=cost(6, 12),
         name="hidden_grads",
     )(far_word, *[c_line[k] for k in line_blocks], *[c_pair[k] for k in line_blocks], pick, combine, w_down, pre, info)
-    mixed_sides, mixed_got, mixed_out, d_gate, d_up, tail, c_give, act_far = fence(
-        pair_sums(mixed_keep, mixed_got[0], sides).astype(BF16), mixed_got, mixed_out, d_gate, d_up, tail, c_give, act_far)
+    mixed_sides, mixed_got, mixed_out, d_gate, d_up, tail, c_give, c_far = fence(
+        pair_sums(mixed_keep, mixed_got[0], sides).astype(BF16), mixed_got, mixed_out, d_gate, d_up, tail, c_give, c_far)
 
     mixed_sides = send(mixed_sides, 2)
     mixed_got.append(send(mixed_out[2], 1))
@@ -485,18 +484,18 @@
         cost_estimate=cost(6, 16),
         name="input_grads",
     )(d_gate, d_up, combine, tail, w_gate, w_up)
-    input_keep, input_out, mixed_sides, mixed_got, c_far, d_gate = fence(
-        input_keep, input_out, mixed_sides, mixed_got, c_far, d_gate)
+    input_keep, input_out, mixed_sides, mixed_got, c_far_pair, d_gate, x_give = fence(
+        input_keep, input_out, mixed_sides, mixed_got, c_far_pair, d_gate, x_give)
+    x_far_pair = swap(x_give, far_bit, n_dp)
 
     input_got = [send(part, 1) for part in input_out[:2]]
     mixed_landed = fold_upper(back_rows(pair_sums(mixed_keep, mixed_got[1], folds), mixed_sides))
     gate_far = swap(d_gate, far_bit, n_dp)
-    input_sides, input_out, c_far_pair, x_keep, d_up, mixed_got[2] = fence(
-        pair_sums(input_keep, input_got[0], sides).astype(BF16), input_out, c_far_pair, x_keep, d_up, mixed_got[2])
+    input_sides, input_out, x_far_pair, x_keep, d_up = fence(
+        pair_sums(input_keep, input_got[0], sides).astype(BF16), input_out, x_far_pair, x_keep, d_up)
     input_sides = send(input_sides, 2)
     input_got.append(send(input_out[2], 1))
     up_far = swap(d_up, far_bit, n_dp)
-    mixed_ends = pair_sums(mixed_keep, mixed_got[2], [2, 0])
     partial_specs = [by_expert(columns, hidden)] * 2
     partial_shapes = [sds((local, columns, hidden), BF16)] * 2
     x_rows, down_keep, down_give = pl.pallas_call(
@@ -516,12 +515,13 @@
         mixed_landed, x_rows, down_keep, down_give)
 
     input_landed = fold_upper(input_folds)
-    mixed_landed.append(send(mixed_ends[:tok_rows].astype(BF16), 2))
     input_ends = pair_sums(input_keep, input_got[2], [2, 0])
     input_landed.append(send(input_ends[:tok_rows].astype(BF16), 2))
     down_got = swap(down_give, 1, n_dp)
+    input_ends, mixed_got[2], gate_far, up_far, down_got = fence(input_ends, mixed_got[2], gate_far, up_far, down_got)
+    mixed_ends = pair_sums(mixed_keep, mixed_got[2], [2, 0])
+    mixed_landed.append(send(mixed_ends[:tok_rows].astype(BF16), 2))
     mixed = finish(mixed_ends, mixed_landed).astype(BF16)
-    mixed, input_ends, input_landed, gate_far, up_far = fence(mixed, input_ends, input_landed, gate_far, up_far)
     both_specs = [by_expert(columns, 2 * hidden)] * 2
     both_keep, both_give = pl.pallas_call(
         functools.partial(both_kernel, cap),
@@ -534,6 +534,7 @@
         cost_estimate=cost(3, 10),
         name="gate_up_grads",
     )(near_word, x_rows, d_gate, gate_far, d_up, up_far)
+    both_give, input_landed = fence(both_give, input_landed)
     both_got = swap(both_give, 1, n_dp)
     down_grad = back_rows(down_keep, down_got).astype(BF16)
     gate_grad = back_rows(both_keep[:, :, :hidden], both_got[:, :, :hidden]).astype(BF16)

time: 171 us -> 183 us (1.070)
  waiting for transfers between devices: 38.8 us -> 46.9 us
  starting transfers between devices: 41.6 us -> 45 us
  local copies, waits for them, and re-layouts: 6.64 us -> 4.72 us
    ppermute x9, waiting for transfers between devices: 7.85 us -> 18.4 us  [swap(): return lax.ppermute(value, 'dp', [(i, i ^ bit) for i in range(count)])]
    ppermute x9, starting transfers between devices: 6.68 us -> 10.3 us  [swap(): return lax.ppermute(value, 'dp', [(i, i ^ bit) for i in range(count)])]
    ppermute x26, waiting for transfers between devices: 31 us -> 28.5 us  [exchange(): return lax.ppermute(value, 'expert', [(i, i ^ bit) for i in range(count)])]
  transfers between devices with their start and end apart: 35 -> 35, of which waited for: 10 -> 9; matrix products, arithmetic and copies ran while one was open for 8% -> 8% of each run, Pallas kernels for 33% -> 35%
where the time goes in v2:
time: 183 us; the launch traced here: 182 us
  Pallas kernels  64.2 us (35%)
  waiting for transfers between devices  46.9 us (26%)
  starting transfers between devices  45 us (25%)
  other arithmetic  19.8 us (11%)
  local copies, waits for them, and re-layouts  4.72 us (3%)
    ppermute x26, starting transfers between devices, exchange(): return lax.ppermute(value, 'expert', [(i, i ^ bit) for i in range(count)])  34.8 us
    ppermute x26, waiting for transfers between devices, exchange(): return lax.ppermute(value, 'expert', [(i, i ^ bit) for i in range(count)])  28.5 us
    ppermute x9, waiting for transfers between devices, swap(): return lax.ppermute(value, 'dp', [(i, i ^ bit) for i in range(count)])  18.4 us
    pallas_call x1, Pallas kernels, shards(): pl.pallas_call(functools.partial(hidden_kernel, cfg), grid=(local,), in_s...  12.9 us
    pallas_call x1, Pallas kernels, shards(): pl.pallas_call(functools.partial(grad_kernel, cfg), grid=(local,), in_spe...  11.3 us
    pallas_call x1, Pallas kernels, shards(): pl.pallas_call(functools.partial(input_kernel, (plan, local, cap, cap_pad...  10.9 us
    ppermute x9, starting transfers between devices, swap(): return lax.ppermute(value, 'dp', [(i, i ^ bit) for i in range(count)])  10.3 us
    pallas_call x1, Pallas kernels, shards(): pl.pallas_call(functools.partial(down_kernel, cap), grid=(local,), in_spe...  9.85 us
  transfers between devices with their start and end apart: 35, of which 9 were waited for; matrix products, arithmetic and copies ran while one was open for 8% of the time, Pallas kernels for 35%

profile of v2, /device:TPU:0, one launch (start us, length us, event | category | flops | bytes accessed | tf_op | source)
XLA Modules:
  0.0 181.8 jit_solution(6507439122794226940)
XLA Ops:
  0.6 0.8 copy.16
  1.5 0.7 reduce_sum.18
  2.2 0.7 convert_element_type.113
  3.1 1.0 pad_maximum_fusion.refs_0_
  4.1 3.0 %collective-permute-start.2 = (bf16[64,2176]{1,0:T(8,128)(2,1)S(1)}, bf16[64,2176]{1,0:T(8,128)(2,1)S(1)}, u32[]{:S(2)}, u32[]{:S(2)}) collective-permute-start(bf16[64,2176]{1,0:T(8,128)(2,1)S(1)} %pad_maximum_fusion.refs_0_), channel_id=1, source_target_pairs={{0,4},{4,0},{8,12},{12,8},{16,20},{20,16},{24,28},{28,24},{1,5},{5... | collective-permute-start | bytes 835592 | tf_op jit(solution)/shard_map/ppermute | solution.py:274
  7.1 2.6 %collective-permute-start.1 = (bf16[64,2176]{1,0:T(8,128)(2,1)S(1)}, bf16[64,2176]{1,0:T(8,128)(2,1)S(1)}, u32[]{:S(2)}, u32[]{:S(2)}) collective-permute-start(bf16[64,2176]{1,0:T(8,128)(2,1)S(1)} %pad_maximum_fusion.refs_0_), channel_id=1, source_target_pairs={{0,16},{4,20},{8,24},{12,28},{16,0},{20,4},{24,8},{28,12},{1,17},{... | collective-permute-start | bytes 835592 | tf_op jit(solution)/shard_map/ppermute | solution.py:274
  9.7 1.6 collective-permute-start
  11.3 2.5 %collective-permute-done.2.refs_4_ = bf16[64,2176]{1,0:T(8,128)(2,1)S(1)} collective-permute-done((bf16[64,2176]{1,0:T(8,128)(2,1)S(1)}, bf16[64,2176]{1,0:T(8,128)(2,1)S(1)}, u32[]{:S(2)}, u32[]{:S(2)}) %collective-permute-start.2) | collective-permute-done | bytes 278560 | tf_op jit(solution)/shard_map/ppermute | solution.py:274
  13.8 8.4 %collective-permute-done.1.refs_2_ = bf16[64,2176]{1,0:T(8,128)(2,1)S(1)} collective-permute-done((bf16[64,2176]{1,0:T(8,128)(2,1)S(1)}, bf16[64,2176]{1,0:T(8,128)(2,1)S(1)}, u32[]{:S(2)}, u32[]{:S(2)}) %collective-permute-start.1) | collective-permute-done | bytes 278560 | tf_op jit(solution)/shard_map/ppermute | solution.py:274
  22.2 0.2 collective-permute-done.refs_1_
  22.4 0.5 collective-permute-start.6
  22.9 1.5 collective-permute-start.3
  24.4 1.5 collective-permute-start.5
  25.9 2.4 %collective-permute-start.4 = (bf16[64,2048]{1,0:T(8,128)(2,1)}, bf16[64,2048]{1,0:T(8,128)(2,1)S(1)}, u32[]{:S(2)}, u32[]{:S(2)}) collective-permute-start(bf16[64,2048]{1,0:T(8,128)(2,1)} %refs_0_.1), channel_id=1, source_target_pairs={{0,16},{4,20},{8,24},{12,28},{16,0},{20,4},{24,8},{28,12},{1,17},{... | collective-permute-start | bytes 786440 | tf_op jit(solution)/shard_map/ppermute | solution.py:274
  28.3 11.5 %collective-permute-done.4.refs_2_ = bf16[64,2048]{1,0:T(8,128)(2,1)S(1)} collective-permute-done((bf16[64,2048]{1,0:T(8,128)(2,1)}, bf16[64,2048]{1,0:T(8,128)(2,1)S(1)}, u32[]{:S(2)}, u32[]{:S(2)}) %collective-permute-start.4) | collective-permute-done | bytes 262176 | tf_op jit(solution)/shard_map/ppermute | solution.py:274
  39.8 0.6 collective-permute-start.7
  40.5 1.9 %cut_x.1 = bf16[256,1024]{1,0:T(8,128)(2,1)} custom-call(s32[1]{0:T(128)} %bitcast.1.far_ref.word_ref, bf16[64,2176]{1,0:T(8,128)(2,1)} %copy-done.1, bf16[64,2176]{1,0:T(8,128)(2,1)} %copy-done.7, bf16[64,2176]{1,0:T(8,128)(2,1)} %copy-done.6, bf16[64,2176]{1,0:T(8,128)(2,1)} %copy-done.8), custom_call_target="tpu_custom_call" | custom-call | bytes 2000 | tf_op jit(solution)/shard_map/cut_x/pallas_call | solution.py:350
  42.5 1.6 collective-permute-start.12
  44.0 1.4 collective-permute-start.10
  45.5 0.8 collective-permute-start.11
  46.2 0.9 collective-permute-done.7.refs_7_
  47.2 1.1 collective-permute-start.9
  48.3 12.9 %hidden.1 = (f32[4,160,768]{2,1,0:T(8,128)}, bf16[4,160,512]{2,1,0:T(8,128)(2,1)}, f32[4,160,128]{2,1,0:T(8,128)}, bf16[640,512]{1,0:T(8,128)(2,1)}, bf16[512,10...) custom-call(s32[1]{0:T(128)} %bitcast.first_ref, s32[1]{0:T(128)} %bitcast.1.far_ref.word_ref, ...), custom_call_target="tpu_custom_call" | custom-call | flops 6000000 | bytes 20000 | tf_op jit(solution)/shard_map/hidden/pallas_call | solution.py:389
  61.3 2.5 %collective-permute-start.15 = (bf16[4,160,512]{2,1,0:T(8,128)(2,1)}, bf16[4,160,512]{2,1,0:T(8,128)(2,1)S(1)}, u32[]{:S(2)}, u32[]{:S(2)}) collective-permute-start(bf16[4,160,512]{2,1,0:T(8,128)(2,1)} %get-tuple-element.119.act_ref.refs_6_), channel_id=1, source_target_pairs={{0,2},{1,3},{2,0},{3,1},{4,6},{5,7},{6,4},{7,5},{8,10},{9,11},{10,... | collective-permute-start | bytes 1966088 | tf_op jit(solution)/shard_map/ppermute | solution.py:270
  63.7 1.1 collective-permute-start.13
  64.8 0.9 collective-permute-start.14
  65.7 9.5 %mixed.1 = (bf16[256,2048]{1,0:T(8,128)(2,1)}, bf16[64,2048]{1,0:T(8,128)(2,1)}, bf16[64,2048]{1,0:T(8,128)(2,1)}, bf16[128,2048]{1,0:T(8,128)(2,1)}, bf16[256,1024]{1,0:T(8,128)(2,1)}) custom-call(s32[1]{0:T(128)} %bitcast.1.far_ref.word_ref, bf16[4,160,512]{2,1,0:T(8,128)(2,1)} %get-tuple-element.119.act_ref.refs_6_, ...), custom_call_target="tpu_custom_call" | custom-call | flops 6000000 | bytes 10000 | tf_op jit(solution)/shard_map/mixed/pallas_call | solution.py:413
  75.3 2.5 %collective-permute-start.16 = (bf16[64,2048]{1,0:T(8,128)(2,1)}, bf16[64,2048]{1,0:T(8,128)(2,1)S(1)}, u32[]{:S(2)}, u32[]{:S(2)}) collective-permute-start(bf16[64,2048]{1,0:T(8,128)(2,1)} %get-tuple-element.129), channel_id=1, source_target_pairs={{0,4},{4,0},{8,12},{12,8},{16,20},{20,16},{24,28},{28,24},{1,5},{5... | collective-permute-start | bytes 786440 | tf_op jit(solution)/shard_map/ppermute | solution.py:274
  77.7 2.0 %collective-permute-start.18 = (bf16[256,1024]{1,0:T(8,128)(2,1)}, bf16[256,1024]{1,0:T(8,128)(2,1)S(1)}, u32[]{:S(2)}, u32[]{:S(2)}) collective-permute-start(bf16[256,1024]{1,0:T(8,128)(2,1)} %get-tuple-element.143), channel_id=1, source_target_pairs={{0,2},{1,3},{2,0},{3,1},{4,6},{5,7},{6,4},{7,5},{8,10},{9,11},{10,... | collective-permute-start | bytes 1572872 | tf_op jit(solution)/shard_map/ppermute | solution.py:270
  79.7 11.3 %hidden_grads.1 = (bf16[4,160,384]{2,1,0:T(8,128)(2,1)}, bf16[4,160,384]{2,1,0:T(8,128)(2,1)}, bf16[512,128]{1,0:T(8,128)(2,1)}, bf16[512,1024]{1,0:T(8,128)(2,1)}, bf16[256,1024]{1,0:T(8,128)(2,1)}) custom-call(s32[1]{0:T(128)} %bitcast.1.far_ref.word_ref, bf16[64,2048]{1,0:T(8,128)(2,1)} %refs_0_.1, bf16[64,2048]{1,0:T(8,128)(2,1)} %copy-done.11, ...), custom_call_target="tpu_custom_call" | custom-call | flops 6000000 | bytes 12000 | tf_op jit(solution)/shard_map/hidden_grads/pallas_call | solution.py:450
  91.2 2.1 %collective-permute-start.20 = (bf16[128,2048]{1,0:T(8,128)(2,1)}, bf16[128,2048]{1,0:T(8,128)(2,1)}, u32[]{:S(2)}, u32[]{:S(2)}) collective-permute-start(bf16[128,2048]{1,0:T(8,128)(2,1)} %get-tuple-element.153), channel_id=1, source_target_pairs={{0,4},{4,0},{8,12},{12,8},{16,20},{20,16},{24,28},{28,24},{1,5},{5... | collective-permute-start | bytes 1572872 | tf_op jit(solution)/shard_map/ppermute | solution.py:274
  93.3 1.0 collective-permute-start.19
  94.3 10.9 %input_grads.1 = (bf16[256,2176]{1,0:T(8,128)(2,1)}, bf16[64,2176]{1,0:T(8,128)(2,1)}, bf16[64,2176]{1,0:T(8,128)(2,1)}, bf16[128,2176]{1,0:T(8,128)(2,1)}) custom-call(bf16[4,160,384]{2,1,0:T(8,128)(2,1)} %get-tuple-element.164.d_gate_ref, bf16[4,160,384]{2,1,0:T(8,128)(2,1)} %get-tuple-element.165.d_up_ref, ...), custom_call_target="tpu_custom_call" | custom-call | flops 6000000 | bytes 16000 | tf_op jit(solution)/shard_map/input_grads/pallas_call | solution.py:475
  105.3 0.1 collective-permute-start.22
  105.4 2.0 %collective-permute-start.27 = (bf16[64,2176]{1,0:T(8,128)(2,1)}, bf16[64,2176]{1,0:T(8,128)(2,1)S(1)}, u32[]{:S(2)}, u32[]{:S(2)}) collective-permute-start(bf16[64,2176]{1,0:T(8,128)(2,1)} %get-tuple-element.158), channel_id=1, source_target_pairs={{0,4},{4,0},{8,12},{12,8},{16,20},{20,16},{24,28},{28,24},{1,5},{5... | collective-permute-start | bytes 835592 | tf_op jit(solution)/shard_map/ppermute | solution.py:274
  107.4 1.7 collective-permute-start.23
  109.1 3.0 %collective-permute-done.22 = bf16[64,2176]{1,0:T(8,128)(2,1)S(1)} collective-permute-done((bf16[64,2176]{1,0:T(8,128)(2,1)}, bf16[64,2176]{1,0:T(8,128)(2,1)S(1)}, u32[]{:S(2)}, u32[]{:S(2)}) %collective-permute-start.22) | collective-permute-done | bytes 278560 | tf_op jit(solution)/shard_map/ppermute | solution.py:274
  112.1 1.7 add_convert_fusion.4
  113.8 5.9 %collective-permute-done.23.refs_2_ = bf16[256,1024]{1,0:T(8,128)(2,1)S(1)} collective-permute-done((bf16[256,1024]{1,0:T(8,128)(2,1)}, bf16[256,1024]{1,0:T(8,128)(2,1)S(1)}, u32[]{:S(2)}, u32[]{:S(2)}) %collective-permute-start.23) | collective-permute-done | bytes 524320 | tf_op jit(solution)/shard_map/ppermute | solution.py:270
  119.7 1.6 collective-permute-start.28
  121.4 1.7 add_convert_fusion.5
  123.1 1.6 collective-permute-start.29
  124.7 2.4 %collective-permute-start.25 = (bf16[4,160,384]{2,1,0:T(8,128)(2,1)S(1)}, bf16[4,160,384]{2,1,0:T(8,128)(2,1)}, u32[]{:S(2)}, u32[]{:S(2)}) collective-permute-start(bf16[4,160,384]{2,1,0:T(8,128)(2,1)S(1)} %copy-done.2), channel_id=1, source_target_pairs={{0,2},{1,3},{2,0},{3,1},{4,6},{5,7},{6,4},{7,5},{8,10},{9,11},{10,... | collective-permute-start | bytes 1474568 | tf_op jit(solution)/shard_map/ppermute | solution.py:270
  127.1 3.3 %collective-permute-start.24 = (bf16[128,2176]{1,0:T(8,128)(2,1)}, bf16[128,2176]{1,0:T(8,128)(2,1)S(1)}, u32[]{:S(2)}, u32[]{:S(2)}) collective-permute-start(bf16[128,2176]{1,0:T(8,128)(2,1)} %get-tuple-element.162), channel_id=1, source_target_pairs={{0,4},{4,0},{8,12},{12,8},{16,20},{20,16},{24,28},{28,24},{1,5},{5... | collective-permute-start | bytes 1671176 | tf_op jit(solution)/shard_map/ppermute | solution.py:274
  130.4 9.8 %down_grads.1 = (bf16[4,320,1024]{2,1,0:T(8,128)(2,1)}, bf16[4,512,384]{2,1,0:T(8,128)(2,1)}, bf16[4,512,384]{2,1,0:T(8,128)(2,1)}) custom-call(s32[1]{0:T(128)} %bitcast.2.near_ref, bf16[640,512]{1,0:T(8,128)(2,1)} %get-tuple-element.136.refs_8_.pick_ref, bf16[512,1024]{1,0:T(8,128)(2,1)} %get-tuple-element.169.refs_0_, bf16[256,1024]{1,0:T(8,128)(2,1)} %copy-done.15, ...), custom_call_target="tpu_custom_call" | custom-call | flops 6000000 | bytes 12000 | tf_op jit(solution)/shard_map/down_grads/pallas_call | solution.py:501
  140.2 1.8 add_convert_fusion.3
  142.3 0.1 convert_add_fusion
  142.4 0.9 collective-permute-start.33
  143.3 12.5 %collective-permute-done.26.up_far_ref = bf16[4,160,384]{2,1,0:T(8,128)(2,1)S(1)} collective-permute-done((bf16[4,160,384]{2,1,0:T(8,128)(2,1)S(1)}, bf16[4,160,384]{2,1,0:T(8,128)(2,1)S(1)}, u32[]{:S(2)}, u32[]{:S(2)}) %collective-permute-start.26) | collective-permute-done | bytes 491552 | tf_op jit(solution)/shard_map/ppermute | solution.py:270
  155.8 0.8 copy-done.18
  156.6 7.9 %gate_up_grads.1 = (bf16[4,512,768]{2,1,0:T(8,128)(2,1)}, bf16[4,512,768]{2,1,0:T(8,128)(2,1)}) custom-call(s32[1]{0:T(128)} %bitcast.2.near_ref, bf16[4,320,1024]{2,1,0:T(8,128)(2,1)} %get-tuple-element.183.rows_ref, bf16[4,160,384]{2,1,0:T(8,128)(2,1)} %get-tuple-element.164.d_gate_ref, bf16[4,160,384]{2,1,0:T(8,128)(2,1)} %collective-permute-done.25.gate_far_ref, ...), custom_call_target="tpu_custom_call" | custom-call | flops 3000000 | bytes 10000 | tf_op jit(solution)/shard_map/gate_up_grads/pallas_call | solution.py:526
  164.7 0.6 copy-done.19
  165.2 1.2 convert_add_fusion.1
  166.4 0.7 slice.132
  167.1 0.8 collective-permute-start.31
  167.9 1.0 convert_add_fusion.2
  169.0 0.7 slice.131
  169.7 0.2 multiply_reduce_fusion
  169.9 0.1 subtract_divide_fusion
  170.0 0.7 copy.20
  170.7 3.1 %add_convert_fusion = bf16[4,512,384]{2,1,0:T(8,128)(2,1)} fusion(bf16[4,512,384]{2,1,0:T(8,128)(2,1)} %collective-permute-done.30, bf16[4,512,384]{2,1,0:T(8,128)(2,1)S(1)} %copy-done.4), kind=kLoop, calls=%fused_computation | loop fusion | flops 3145728 | bytes 4718592 | tf_op jit(solution)/shard_map/convert_element_type | solution.py:539
  173.8 1.8 %collective-permute-done.31 = bf16[64,2048]{1,0:T(8,128)(2,1)} collective-permute-done((bf16[64,2048]{1,0:T(8,128)(2,1)}, bf16[64,2048]{1,0:T(8,128)(2,1)}, u32[]{:S(2)}, u32[]{:S(2)}) %collective-permute-start.31) | collective-permute-done | bytes 262176 | tf_op jit(solution)/shard_map/ppermute | solution.py:274
  175.6 1.8 fusion.1
  177.4 4.4 %add_convert_fusion.1 = (bf16[4,512,384]{2,1,0:T(8,128)(2,1)}, bf16[4,512,384]{2,1,0:T(8,128)(2,1)}) fusion(bf16[4,512,768]{2,1,0:T(8,128)(2,1)} %collective-permute-done.34, bf16[4,512,768]{2,1,0:T(8,128)(2,1)S(1)} %copy-done), kind=kLoop, calls=%fused_computation.1 | loop fusion | flops 6291456 | bytes 9437184 | tf_op jit(solution)/shard_map/convert_element_type | solution.py:541
  (94 shorter events, 1.0 us)
Async XLA Ops:
  0.6 43.4 %copy-start.9 = (bf16[64,2048]{1,0:T(8,128)(2,1)S(1)}, bf16[64,2048]{1,0:T(8,128)(2,1)}, u32[]{:S(2)}) copy-start(bf16[64,2048]{1,0:T(8,128)(2,1)} %refs_0_.1) | copy-start | bytes 786436
  4.1 36.3 %copy-start.1 = (bf16[64,2176]{1,0:T(8,128)(2,1)}, bf16[64,2176]{1,0:T(8,128)(2,1)S(1)}, u32[]{:S(2)}) copy-start(bf16[64,2176]{1,0:T(8,128)(2,1)S(1)} %pad_maximum_fusion.refs_0_) | copy-start | bytes 835588
  4.1 9.7 %collective-permute-start.2 = (bf16[64,2176]{1,0:T(8,128)(2,1)S(1)}, bf16[64,2176]{1,0:T(8,128)(2,1)S(1)}, u32[]{:S(2)}, u32[]{:S(2)}) collective-permute-start(bf16[64,2176]{1,0:T(8,128)(2,1)S(1)} %pad_maximum_fusion.refs_0_), channel_id=1, source_target_pairs={{0,4},{4,0},{8,12},{12,8},{16,20},{20,16},{24,28},{28,24},{1,5},{5... | collective-permute-start | bytes 835592 | tf_op jit(solution)/shard_map/ppermute | solution.py:274
  7.1 15.1 %collective-permute-start.1 = (bf16[64,2176]{1,0:T(8,128)(2,1)S(1)}, bf16[64,2176]{1,0:T(8,128)(2,1)S(1)}, u32[]{:S(2)}, u32[]{:S(2)}) collective-permute-start(bf16[64,2176]{1,0:T(8,128)(2,1)S(1)} %pad_maximum_fusion.refs_0_), channel_id=1, source_target_pairs={{0,16},{4,20},{8,24},{12,28},{16,0},{20,4},{24,8},{28,12},{1,17},{... | collective-permute-start | bytes 835592 | tf_op jit(solution)/shard_map/ppermute | solution.py:274
  9.7 12.7 %collective-permute-start = (bf16[64,2176]{1,0:T(8,128)(2,1)S(1)}, bf16[64,2176]{1,0:T(8,128)(2,1)S(1)}, u32[]{:S(2)}, u32[]{:S(2)}) collective-permute-start(bf16[64,2176]{1,0:T(8,128)(2,1)S(1)} %pad_maximum_fusion.refs_0_), channel_id=1, source_target_pairs={{0,8},{4,12},{8,0},{12,4},{16,24},{20,28},{24,16},{28,20},{1,9},{5... | collective-permute-start | bytes 835592 | tf_op jit(solution)/shard_map/ppermute | solution.py:274
  13.8 34.5 %copy-start.20 = (bf16[64,2176]{1,0:T(8,128)(2,1)}, bf16[64,2176]{1,0:T(8,128)(2,1)S(1)}, u32[]{:S(2)}) copy-start(bf16[64,2176]{1,0:T(8,128)(2,1)S(1)} %collective-permute-done.2.refs_4_) | copy-start | bytes 835588
  22.2 18.2 %copy-start.6 = (bf16[64,2176]{1,0:T(8,128)(2,1)}, bf16[64,2176]{1,0:T(8,128)(2,1)S(1)}, u32[]{:S(2)}) copy-start(bf16[64,2176]{1,0:T(8,128)(2,1)S(1)} %collective-permute-done.1.refs_2_) | copy-start | bytes 835588
  22.4 18.0 %copy-start.7 = (bf16[64,2176]{1,0:T(8,128)(2,1)}, bf16[64,2176]{1,0:T(8,128)(2,1)S(1)}, u32[]{:S(2)}) copy-start(bf16[64,2176]{1,0:T(8,128)(2,1)S(1)} %collective-permute-done.refs_1_) | copy-start | bytes 835588
  22.4 17.4 %collective-permute-start.6 = (bf16[64,2176]{1,0:T(8,128)(2,1)S(1)}, bf16[64,2176]{1,0:T(8,128)(2,1)S(1)}, u32[]{:S(2)}, u32[]{:S(2)}) collective-permute-start(bf16[64,2176]{1,0:T(8,128)(2,1)S(1)} %collective-permute-done.1.refs_2_), channel_id=1, source_target_pairs={{0,4},{4,0},{8,12},{12,8},{16,20},{20,16},{24,28},{28,24},{1,5},{5... | collective-permute-start | bytes 835592 | tf_op jit(solution)/shard_map/ppermute | solution.py:274
  22.9 16.9 %collective-permute-start.3 = (bf16[64,2176]{1,0:T(8,128)(2,1)S(1)}, bf16[64,2176]{1,0:T(8,128)(2,1)S(1)}, u32[]{:S(2)}, u32[]{:S(2)}) collective-permute-start(bf16[64,2176]{1,0:T(8,128)(2,1)S(1)} %collective-permute-done.1.refs_2_), channel_id=1, source_target_pairs={{0,8},{4,12},{8,0},{12,4},{16,24},{20,28},{24,16},{28,20},{1,9},{5... | collective-permute-start | bytes 835592 | tf_op jit(solution)/shard_map/ppermute | solution.py:274
  24.4 15.4 %collective-permute-start.5 = (bf16[64,2176]{1,0:T(8,128)(2,1)S(1)}, bf16[64,2176]{1,0:T(8,128)(2,1)S(1)}, u32[]{:S(2)}, u32[]{:S(2)}) collective-permute-start(bf16[64,2176]{1,0:T(8,128)(2,1)S(1)} %collective-permute-done.refs_1_), channel_id=1, source_target_pairs={{0,4},{4,0},{8,12},{12,8},{16,20},{20,16},{24,28},{28,24},{1,5},{5... | collective-permute-start | bytes 835592 | tf_op jit(solution)/shard_map/ppermute | solution.py:274
  25.9 13.9 %collective-permute-start.4 = (bf16[64,2048]{1,0:T(8,128)(2,1)}, bf16[64,2048]{1,0:T(8,128)(2,1)S(1)}, u32[]{:S(2)}, u32[]{:S(2)}) collective-permute-start(bf16[64,2048]{1,0:T(8,128)(2,1)} %refs_0_.1), channel_id=1, source_target_pairs={{0,16},{4,20},{8,24},{12,28},{16,0},{20,4},{24,8},{28,12},{1,17},{... | collective-permute-start | bytes 786440 | tf_op jit(solution)/shard_map/ppermute | solution.py:274
  39.8 21.4 %copy-start.10 = (bf16[64,2048]{1,0:T(8,128)(2,1)}, bf16[64,2048]{1,0:T(8,128)(2,1)S(1)}, u32[]{:S(2)}) copy-start(bf16[64,2048]{1,0:T(8,128)(2,1)S(1)} %collective-permute-done.4.refs_2_) | copy-start | bytes 786436
  39.8 8.5 %copy-start.21 = (bf16[64,2176]{1,0:T(8,128)(2,1)}, bf16[64,2176]{1,0:T(8,128)(2,1)S(1)}, u32[]{:S(2)}) copy-start(bf16[64,2176]{1,0:T(8,128)(2,1)S(1)} %collective-permute-done.6.refs_6_) | copy-start | bytes 835588
  39.8 0.7 copy-start.8
  39.8 8.5 %copy-start.22 = (bf16[64,2176]{1,0:T(8,128)(2,1)}, bf16[64,2176]{1,0:T(8,128)(2,1)S(1)}, u32[]{:S(2)}) copy-start(bf16[64,2176]{1,0:T(8,128)(2,1)S(1)} %collective-permute-done.5.refs_5_) | copy-start | bytes 835588
  39.8 7.3 %collective-permute-start.7 = (bf16[64,2176]{1,0:T(8,128)(2,1)S(1)}, bf16[64,2176]{1,0:T(8,128)(2,1)S(1)}, u32[]{:S(2)}, u32[]{:S(2)}) collective-permute-start(bf16[64,2176]{1,0:T(8,128)(2,1)S(1)} %collective-permute-done.3.refs_3_), channel_id=1, source_target_pairs={{0,4},{4,0},{8,12},{12,8},{16,20},{20,16},{24,28},{28,24},{1,5},{5... | collective-permute-start | bytes 835592 | tf_op jit(solution)/shard_map/ppermute | solution.py:274
  42.5 18.8 %collective-permute-start.12 = (bf16[256,1024]{1,0:T(8,128)(2,1)}, bf16[256,1024]{1,0:T(8,128)(2,1)S(1)}, u32[]{:S(2)}, u32[]{:S(2)}) collective-permute-start(bf16[256,1024]{1,0:T(8,128)(2,1)} %cut_x.1), channel_id=1, source_target_pairs={{0,2},{1,3},{2,0},{3,1},{4,6},{5,7},{6,4},{7,5},{8,10},{9,11},{10,... | collective-permute-start | bytes 1572872 | tf_op jit(solution)/shard_map/ppermute | solution.py:270
  44.0 17.1 %collective-permute-start.10 = (bf16[64,2048]{1,0:T(8,128)(2,1)S(1)}, bf16[64,2048]{1,0:T(8,128)(2,1)S(1)}, u32[]{:S(2)}, u32[]{:S(2)}) collective-permute-start(bf16[64,2048]{1,0:T(8,128)(2,1)S(1)} %copy-done.9), channel_id=1, source_target_pairs={{0,4},{4,0},{8,12},{12,8},{16,20},{20,16},{24,28},{28,24},{1,5},{5... | collective-permute-start | bytes 786440 | tf_op jit(solution)/shard_map/ppermute | solution.py:274
  45.5 15.7 %collective-permute-start.8 = (bf16[64,2048]{1,0:T(8,128)(2,1)S(1)}, bf16[64,2048]{1,0:T(8,128)(2,1)S(1)}, u32[]{:S(2)}, u32[]{:S(2)}) collective-permute-start(bf16[64,2048]{1,0:T(8,128)(2,1)S(1)} %copy-done.9), channel_id=1, source_target_pairs={{0,8},{4,12},{8,0},{12,4},{16,24},{20,28},{24,16},{28,20},{1,9},{5... | collective-permute-start | bytes 786440 | tf_op jit(solution)/shard_map/ppermute | solution.py:274
  45.5 15.7 %collective-permute-start.11 = (bf16[64,2048]{1,0:T(8,128)(2,1)S(1)}, bf16[64,2048]{1,0:T(8,128)(2,1)}, u32[]{:S(2)}, u32[]{:S(2)}) collective-permute-start(bf16[64,2048]{1,0:T(8,128)(2,1)S(1)} %collective-permute-done.4.refs_2_), channel_id=1, source_target_pairs={{0,4},{4,0},{8,12},{12,8},{16,20},{20,16},{24,28},{28,24},{1,5},{5... | collective-permute-start | bytes 786440 | tf_op jit(solution)/shard_map/ppermute | solution.py:274
  47.2 1.1 copy-start.23
  47.2 14.1 %collective-permute-start.9 = (bf16[64,2048]{1,0:T(8,128)(2,1)S(1)}, bf16[64,2048]{1,0:T(8,128)(2,1)S(1)}, u32[]{:S(2)}, u32[]{:S(2)}) collective-permute-start(bf16[64,2048]{1,0:T(8,128)(2,1)S(1)} %collective-permute-done.4.refs_2_), channel_id=1, source_target_pairs={{0,8},{4,12},{8,0},{12,4},{16,24},{20,28},{24,16},{28,20},{1,9},{5... | collective-permute-start | bytes 786440 | tf_op jit(solution)/shard_map/ppermute | solution.py:274
  61.2 18.5 %copy-start.24 = (bf16[64,2048]{1,0:T(8,128)(2,1)}, bf16[64,2048]{1,0:T(8,128)(2,1)S(1)}, u32[]{:S(2)}) copy-start(bf16[64,2048]{1,0:T(8,128)(2,1)S(1)} %collective-permute-done.10.refs_4_) | copy-start | bytes 786436
  61.2 4.5 %copy-start.11 = (bf16[64,2048]{1,0:T(8,128)(2,1)}, bf16[64,2048]{1,0:T(8,128)(2,1)S(1)}, u32[]{:S(2)}) copy-start(bf16[64,2048]{1,0:T(8,128)(2,1)S(1)} %collective-permute-done.8.refs_1_) | copy-start | bytes 786436
  61.2 4.5 %copy-start.12 = (bf16[64,2048]{1,0:T(8,128)(2,1)}, bf16[64,2048]{1,0:T(8,128)(2,1)S(1)}, u32[]{:S(2)}) copy-start(bf16[64,2048]{1,0:T(8,128)(2,1)S(1)} %collective-permute-done.9.refs_3_) | copy-start | bytes 786436
  61.2 14.0 %copy-start.15 = (bf16[256,1024]{1,0:T(8,128)(2,1)}, bf16[256,1024]{1,0:T(8,128)(2,1)S(1)}, u32[]{:S(2)}) copy-start(bf16[256,1024]{1,0:T(8,128)(2,1)S(1)} %collective-permute-done.12.refs_1_) | copy-start | bytes 1572868
  61.3 14.0 %collective-permute-start.15 = (bf16[4,160,512]{2,1,0:T(8,128)(2,1)}, bf16[4,160,512]{2,1,0:T(8,128)(2,1)S(1)}, u32[]{:S(2)}, u32[]{:S(2)}) collective-permute-start(bf16[4,160,512]{2,1,0:T(8,128)(2,1)} %get-tuple-element.119.act_ref.refs_6_), channel_id=1, source_target_pairs={{0,2},{1,3},{2,0},{3,1},{4,6},{5,7},{6,4},{7,5},{8,10},{9,11},{10,... | collective-permute-start | bytes 1966088 | tf_op jit(solution)/shard_map/ppermute | solution.py:270
  63.7 11.5 %collective-permute-start.13 = (bf16[64,2048]{1,0:T(8,128)(2,1)S(1)}, bf16[64,2048]{1,0:T(8,128)(2,1)S(1)}, u32[]{:S(2)}, u32[]{:S(2)}) collective-permute-start(bf16[64,2048]{1,0:T(8,128)(2,1)S(1)} %collective-permute-done.8.refs_1_), channel_id=1, source_target_pairs={{0,4},{4,0},{8,12},{12,8},{16,20},{20,16},{24,28},{28,24},{1,5},{5... | collective-permute-start | bytes 786440 | tf_op jit(solution)/shard_map/ppermute | solution.py:274
  64.8 10.4 %collective-permute-start.14 = (bf16[64,2048]{1,0:T(8,128)(2,1)S(1)}, bf16[64,2048]{1,0:T(8,128)(2,1)S(1)}, u32[]{:S(2)}, u32[]{:S(2)}) collective-permute-start(bf16[64,2048]{1,0:T(8,128)(2,1)S(1)} %collective-permute-done.9.refs_3_), channel_id=1, source_target_pairs={{0,4},{4,0},{8,12},{12,8},{16,20},{20,16},{24,28},{28,24},{1,5},{5... | collective-permute-start | bytes 786440 | tf_op jit(solution)/shard_map/ppermute | solution.py:274
  75.2 4.5 %copy-start.25 = (bf16[64,2048]{1,0:T(8,128)(2,1)}, bf16[64,2048]{1,0:T(8,128)(2,1)S(1)}, u32[]{:S(2)}) copy-start(bf16[64,2048]{1,0:T(8,128)(2,1)S(1)} %collective-permute-done.13.refs_5_) | copy-start | bytes 786436
  75.2 4.5 %copy-start.26 = (bf16[64,2048]{1,0:T(8,128)(2,1)}, bf16[64,2048]{1,0:T(8,128)(2,1)S(1)}, u32[]{:S(2)}) copy-start(bf16[64,2048]{1,0:T(8,128)(2,1)S(1)} %collective-permute-done.14.refs_7_) | copy-start | bytes 786436
  75.3 15.8 %copy-start.14 = (bf16[4,160,512]{2,1,0:T(8,128)(2,1)}, bf16[4,160,512]{2,1,0:T(8,128)(2,1)S(1)}, u32[]{:S(2)}) copy-start(bf16[4,160,512]{2,1,0:T(8,128)(2,1)S(1)} %collective-permute-done.15.refs_7_) | copy-start | bytes 1966084
  75.3 15.8 %collective-permute-start.16 = (bf16[64,2048]{1,0:T(8,128)(2,1)}, bf16[64,2048]{1,0:T(8,128)(2,1)S(1)}, u32[]{:S(2)}, u32[]{:S(2)}) collective-permute-start(bf16[64,2048]{1,0:T(8,128)(2,1)} %get-tuple-element.129), channel_id=1, source_target_pairs={{0,4},{4,0},{8,12},{12,8},{16,20},{20,16},{24,28},{28,24},{1,5},{5... | collective-permute-start | bytes 786440 | tf_op jit(solution)/shard_map/ppermute | solution.py:274
  77.7 13.4 %collective-permute-start.18 = (bf16[256,1024]{1,0:T(8,128)(2,1)}, bf16[256,1024]{1,0:T(8,128)(2,1)S(1)}, u32[]{:S(2)}, u32[]{:S(2)}) collective-permute-start(bf16[256,1024]{1,0:T(8,128)(2,1)} %get-tuple-element.143), channel_id=1, source_target_pairs={{0,2},{1,3},{2,0},{3,1},{4,6},{5,7},{6,4},{7,5},{8,10},{9,11},{10,... | collective-permute-start | bytes 1572872 | tf_op jit(solution)/shard_map/ppermute | solution.py:270
  79.7 11.4 %collective-permute-start.17 = (bf16[64,2048]{1,0:T(8,128)(2,1)}, bf16[64,2048]{1,0:T(8,128)(2,1)S(1)}, u32[]{:S(2)}, u32[]{:S(2)}) collective-permute-start(bf16[64,2048]{1,0:T(8,128)(2,1)} %get-tuple-element.130), channel_id=1, source_target_pairs={{0,4},{4,0},{8,12},{12,8},{16,20},{20,16},{24,28},{28,24},{1,5},{5... | collective-permute-start | bytes 786440 | tf_op jit(solution)/shard_map/ppermute | solution.py:274
  79.7 11.3 %copy-start.13 = (bf16[256,2048]{1,0:T(8,128)(2,1)S(1)}, bf16[256,2048]{1,0:T(8,128)(2,1)}, u32[]{:S(2)}) copy-start(bf16[256,2048]{1,0:T(8,128)(2,1)} %get-tuple-element.128) | copy-start | bytes 3145732
  91.2 14.1 %copy-start.27 = (bf16[64,2048]{1,0:T(8,128)(2,1)}, bf16[64,2048]{1,0:T(8,128)(2,1)S(1)}, u32[]{:S(2)}) copy-start(bf16[64,2048]{1,0:T(8,128)(2,1)S(1)} %collective-permute-done.17) | copy-start | bytes 786436
  91.2 14.0 %copy-start.16 = (bf16[256,1024]{1,0:T(8,128)(2,1)}, bf16[256,1024]{1,0:T(8,128)(2,1)S(1)}, u32[]{:S(2)}) copy-start(bf16[256,1024]{1,0:T(8,128)(2,1)S(1)} %collective-permute-done.18.refs_4_) | copy-start | bytes 1572868
  91.2 14.1 %collective-permute-start.20 = (bf16[128,2048]{1,0:T(8,128)(2,1)}, bf16[128,2048]{1,0:T(8,128)(2,1)}, u32[]{:S(2)}, u32[]{:S(2)}) collective-permute-start(bf16[128,2048]{1,0:T(8,128)(2,1)} %get-tuple-element.153), channel_id=1, source_target_pairs={{0,4},{4,0},{8,12},{12,8},{16,20},{20,16},{24,28},{28,24},{1,5},{5... | collective-permute-start | bytes 1572872 | tf_op jit(solution)/shard_map/ppermute | solution.py:274
  93.3 12.0 %collective-permute-start.21 = (bf16[256,1024]{1,0:T(8,128)(2,1)}, bf16[256,1024]{1,0:T(8,128)(2,1)}, u32[]{:S(2)}, u32[]{:S(2)}) collective-permute-start(bf16[256,1024]{1,0:T(8,128)(2,1)} %get-tuple-element.154), channel_id=1, source_target_pairs={{0,2},{1,3},{2,0},{3,1},{4,6},{5,7},{6,4},{7,5},{8,10},{9,11},{10,... | collective-permute-start | bytes 1572872 | tf_op jit(solution)/shard_map/ppermute | solution.py:270
  93.3 11.9 %collective-permute-start.19 = (bf16[64,2048]{1,0:T(8,128)(2,1)S(1)}, bf16[64,2048]{1,0:T(8,128)(2,1)S(1)}, u32[]{:S(2)}, u32[]{:S(2)}) collective-permute-start(bf16[64,2048]{1,0:T(8,128)(2,1)S(1)} %add_convert_fusion.6), channel_id=1, source_target_pairs={{0,8},{4,12},{8,0},{12,4},{16,24},{20,28},{24,16},{28,20},{1,9},{5... | collective-permute-start | bytes 786440 | tf_op jit(solution)/shard_map/ppermute | solution.py:274
  105.2 19.4 %copy-start.2 = (bf16[4,160,384]{2,1,0:T(8,128)(2,1)S(1)}, bf16[4,160,384]{2,1,0:T(8,128)(2,1)}, u32[]{:S(2)}) copy-start(bf16[4,160,384]{2,1,0:T(8,128)(2,1)} %get-tuple-element.164.d_gate_ref) | copy-start | bytes 1474564
  105.3 6.8 %collective-permute-start.22 = (bf16[64,2176]{1,0:T(8,128)(2,1)}, bf16[64,2176]{1,0:T(8,128)(2,1)S(1)}, u32[]{:S(2)}, u32[]{:S(2)}) collective-permute-start(bf16[64,2176]{1,0:T(8,128)(2,1)} %get-tuple-element.157), channel_id=1, source_target_pairs={{0,4},{4,0},{8,12},{12,8},{16,20},{20,16},{24,28},{28,24},{1,5},{5... | collective-permute-start | bytes 835592 | tf_op jit(solution)/shard_map/ppermute | solution.py:274
  105.4 34.8 %collective-permute-start.27 = (bf16[64,2176]{1,0:T(8,128)(2,1)}, bf16[64,2176]{1,0:T(8,128)(2,1)S(1)}, u32[]{:S(2)}, u32[]{:S(2)}) collective-permute-start(bf16[64,2176]{1,0:T(8,128)(2,1)} %get-tuple-element.158), channel_id=1, source_target_pairs={{0,4},{4,0},{8,12},{12,8},{16,20},{20,16},{24,28},{28,24},{1,5},{5... | collective-permute-start | bytes 835592 | tf_op jit(solution)/shard_map/ppermute | solution.py:274
  107.4 12.3 %collective-permute-start.23 = (bf16[256,1024]{1,0:T(8,128)(2,1)}, bf16[256,1024]{1,0:T(8,128)(2,1)S(1)}, u32[]{:S(2)}, u32[]{:S(2)}) collective-permute-start(bf16[256,1024]{1,0:T(8,128)(2,1)} %get-tuple-element.160), channel_id=1, source_target_pairs={{0,2},{1,3},{2,0},{3,1},{4,6},{5,7},{6,4},{7,5},{8,10},{9,11},{10,... | collective-permute-start | bytes 1572872 | tf_op jit(solution)/shard_map/ppermute | solution.py:270
  119.7 10.6 %copy-start.17 = (bf16[256,1024]{1,0:T(8,128)(2,1)}, bf16[256,1024]{1,0:T(8,128)(2,1)S(1)}, u32[]{:S(2)}) copy-start(bf16[256,1024]{1,0:T(8,128)(2,1)S(1)} %collective-permute-done.23.refs_2_) | copy-start | bytes 1572868
  119.7 20.5 %collective-permute-start.28 = (bf16[64,2176]{1,0:T(8,128)(2,1)}, bf16[64,2176]{1,0:T(8,128)(2,1)}, u32[]{:S(2)}, u32[]{:S(2)}) collective-permute-start(bf16[64,2176]{1,0:T(8,128)(2,1)} %add_convert_fusion.4), channel_id=1, source_target_pairs={{0,8},{4,12},{8,0},{12,4},{16,24},{20,28},{24,16},{28,20},{1,9},{5... | collective-permute-start | bytes 835592 | tf_op jit(solution)/shard_map/ppermute | solution.py:274
  123.1 18.9 %collective-permute-start.29 = (bf16[64,2048]{1,0:T(8,128)(2,1)}, bf16[64,2048]{1,0:T(8,128)(2,1)}, u32[]{:S(2)}, u32[]{:S(2)}) collective-permute-start(bf16[64,2048]{1,0:T(8,128)(2,1)} %add_convert_fusion.5), channel_id=1, source_target_pairs={{0,16},{4,20},{8,24},{12,28},{16,0},{20,4},{24,8},{28,12},{1,17},{... | collective-permute-start | bytes 786440 | tf_op jit(solution)/shard_map/ppermute | solution.py:274
  124.7 18.6 %collective-permute-start.25 = (bf16[4,160,384]{2,1,0:T(8,128)(2,1)S(1)}, bf16[4,160,384]{2,1,0:T(8,128)(2,1)}, u32[]{:S(2)}, u32[]{:S(2)}) collective-permute-start(bf16[4,160,384]{2,1,0:T(8,128)(2,1)S(1)} %copy-done.2), channel_id=1, source_target_pairs={{0,2},{1,3},{2,0},{3,1},{4,6},{5,7},{6,4},{7,5},{8,10},{9,11},{10,... | collective-permute-start | bytes 1474568 | tf_op jit(solution)/shard_map/ppermute | solution.py:270
  127.1 15.2 %collective-permute-start.24 = (bf16[128,2176]{1,0:T(8,128)(2,1)}, bf16[128,2176]{1,0:T(8,128)(2,1)S(1)}, u32[]{:S(2)}, u32[]{:S(2)}) collective-permute-start(bf16[128,2176]{1,0:T(8,128)(2,1)} %get-tuple-element.162), channel_id=1, source_target_pairs={{0,4},{4,0},{8,12},{12,8},{16,20},{20,16},{24,28},{28,24},{1,5},{5... | collective-permute-start | bytes 1671176 | tf_op jit(solution)/shard_map/ppermute | solution.py:274
  130.3 9.9 %copy-start.5 = (bf16[256,2176]{1,0:T(8,128)(2,1)S(1)}, bf16[256,2176]{1,0:T(8,128)(2,1)}, u32[]{:S(2)}) copy-start(bf16[256,2176]{1,0:T(8,128)(2,1)} %get-tuple-element.156) | copy-start | bytes 3342340
  140.2 1.9 %copy-start.3 = (bf16[4,160,384]{2,1,0:T(8,128)(2,1)S(1)}, bf16[4,160,384]{2,1,0:T(8,128)(2,1)}, u32[]{:S(2)}) copy-start(bf16[4,160,384]{2,1,0:T(8,128)(2,1)} %get-tuple-element.165.d_up_ref) | copy-start | bytes 1474564
  142.0 14.5 %collective-permute-start.30 = (bf16[4,512,384]{2,1,0:T(8,128)(2,1)}, bf16[4,512,384]{2,1,0:T(8,128)(2,1)}, u32[]{:S(2)}, u32[]{:S(2)}) collective-permute-start(bf16[4,512,384]{2,1,0:T(8,128)(2,1)} %get-tuple-element.179), channel_id=1, source_target_pairs={{0,1},{1,0},{2,3},{3,2},{4,5},{5,4},{6,7},{7,6},{8,9},{9,8},{10,11... | collective-permute-start | bytes 4718600 | tf_op jit(solution)/shard_map/ppermute | solution.py:270
  142.1 13.7 %collective-permute-start.26 = (bf16[4,160,384]{2,1,0:T(8,128)(2,1)S(1)}, bf16[4,160,384]{2,1,0:T(8,128)(2,1)S(1)}, u32[]{:S(2)}, u32[]{:S(2)}) collective-permute-start(bf16[4,160,384]{2,1,0:T(8,128)(2,1)S(1)} %copy-done.3), channel_id=1, source_target_pairs={{0,2},{1,3},{2,0},{3,1},{4,6},{5,7},{6,4},{7,5},{8,10},{9,11},{10,... | collective-permute-start | bytes 1474568 | tf_op jit(solution)/shard_map/ppermute | solution.py:270
  142.2 22.3 %collective-permute-start.32 = (bf16[64,2176]{1,0:T(8,128)(2,1)}, bf16[64,2176]{1,0:T(8,128)(2,1)S(1)}, u32[]{:S(2)}, u32[]{:S(2)}) collective-permute-start(bf16[64,2176]{1,0:T(8,128)(2,1)} %add_convert_fusion.3), channel_id=1, source_target_pairs={{0,16},{4,20},{8,24},{12,28},{16,0},{20,4},{24,8},{28,12},{1,17},{... | collective-permute-start | bytes 835592 | tf_op jit(solution)/shard_map/ppermute | solution.py:274
  142.4 22.1 %collective-permute-start.33 = (bf16[64,2176]{1,0:T(8,128)(2,1)S(1)}, bf16[64,2176]{1,0:T(8,128)(2,1)S(1)}, u32[]{:S(2)}, u32[]{:S(2)}) collective-permute-start(bf16[64,2176]{1,0:T(8,128)(2,1)S(1)} %slice.130), channel_id=1, source_target_pairs={{0,8},{4,12},{8,0},{12,4},{16,24},{20,28},{24,16},{28,20},{1,9},{5... | collective-permute-start | bytes 835592 | tf_op jit(solution)/shard_map/ppermute | solution.py:274
  155.8 0.8 copy-start.18
  164.5 0.7 copy-start.19
  164.5 12.9 %collective-permute-start.34 = (bf16[4,512,768]{2,1,0:T(8,128)(2,1)}, bf16[4,512,768]{2,1,0:T(8,128)(2,1)}, u32[]{:S(2)}, u32[]{:S(2)}) collective-permute-start(bf16[4,512,768]{2,1,0:T(8,128)(2,1)} %get-tuple-element.191), channel_id=1, source_target_pairs={{0,1},{1,0},{2,3},{3,2},{4,5},{5,4},{6,7},{7,6},{8,9},{9,8},{10,11... | collective-permute-start | bytes 9437192 | tf_op jit(solution)/shard_map/ppermute | solution.py:270
  166.4 4.3 %copy-start.4 = (bf16[4,512,384]{2,1,0:T(8,128)(2,1)S(1)}, bf16[4,512,384]{2,1,0:T(8,128)(2,1)}, u32[]{:S(2)}) copy-start(bf16[4,512,384]{2,1,0:T(8,128)(2,1)} %get-tuple-element.192) | copy-start | bytes 4718596
  167.1 8.5 %collective-permute-start.31 = (bf16[64,2048]{1,0:T(8,128)(2,1)}, bf16[64,2048]{1,0:T(8,128)(2,1)}, u32[]{:S(2)}, u32[]{:S(2)}) collective-permute-start(bf16[64,2048]{1,0:T(8,128)(2,1)} %slice.132), channel_id=1, source_target_pairs={{0,8},{4,12},{8,0},{12,4},{16,24},{20,28},{24,16},{28,20},{1,9},{5... | collective-permute-start | bytes 786440 | tf_op jit(solution)/shard_map/ppermute | solution.py:274
  170.7 6.7 %copy-start = (bf16[4,512,768]{2,1,0:T(8,128)(2,1)S(1)}, bf16[4,512,768]{2,1,0:T(8,128)(2,1)}, u32[]{:S(2)}) copy-start(bf16[4,512,768]{2,1,0:T(8,128)(2,1)} %get-tuple-element.190) | copy-start | bytes 9437188

commit v3 on v1

--- a/solution.py
+++ b/solution.py
@@ -491,12 +491,11 @@
     input_got = [send(part, 1) for part in input_out[:2]]
     mixed_landed = fold_upper(back_rows(pair_sums(mixed_keep, mixed_got[1], folds), mixed_sides))
     gate_far = swap(d_gate, far_bit, n_dp)
-    input_sides, input_out, c_far_pair, x_keep, d_up, mixed_got[2] = fence(
-        pair_sums(input_keep, input_got[0], sides).astype(BF16), input_out, c_far_pair, x_keep, d_up, mixed_got[2])
+    input_sides, input_out, c_far_pair, x_keep, d_up = fence(
+        pair_sums(input_keep, input_got[0], sides).astype(BF16), input_out, c_far_pair, x_keep, d_up)
     input_sides = send(input_sides, 2)
     input_got.append(send(input_out[2], 1))
     up_far = swap(d_up, far_bit, n_dp)
-    mixed_ends = pair_sums(mixed_keep, mixed_got[2], [2, 0])
     partial_specs = [by_expert(columns, hidden)] * 2
     partial_shapes = [sds((local, columns, hidden), BF16)] * 2
     x_rows, down_keep, down_give = pl.pallas_call(
@@ -511,17 +510,18 @@
         cost_estimate=cost(6, 12),
         name="down_grads",
     )(near_word, pick, x_keep, x_far, x_far_pair, c_keep, c_far, c_far_pair, act, act_far)
-    input_folds, mixed_landed, x_rows, down_keep, down_give = fence(
+    input_folds, mixed_landed, mixed_got[2], x_rows, down_keep, down_give = fence(
         back_rows(pair_sums(input_keep, input_got[1], folds), input_sides).astype(BF16),
-        mixed_landed, x_rows, down_keep, down_give)
+        mixed_landed, mixed_got[2], x_rows, down_keep, down_give)
 
     input_landed = fold_upper(input_folds)
+    mixed_ends = pair_sums(mixed_keep, mixed_got[2], [2, 0])
     mixed_landed.append(send(mixed_ends[:tok_rows].astype(BF16), 2))
     input_ends = pair_sums(input_keep, input_got[2], [2, 0])
     input_landed.append(send(input_ends[:tok_rows].astype(BF16), 2))
     down_got = swap(down_give, 1, n_dp)
     mixed = finish(mixed_ends, mixed_landed).astype(BF16)
-    mixed, input_ends, input_landed, gate_far, up_far = fence(mixed, input_ends, input_landed, gate_far, up_far)
+    mixed, input_ends, gate_far, up_far, down_got = fence(mixed, input_ends, gate_far, up_far, down_got)
     both_specs = [by_expert(columns, 2 * hidden)] * 2
     both_keep, both_give = pl.pallas_call(
         functools.partial(both_kernel, cap),
@@ -534,6 +534,7 @@
         cost_estimate=cost(3, 10),
         name="gate_up_grads",
     )(near_word, x_rows, d_gate, gate_far, d_up, up_far)
+    both_give, input_landed = fence(both_give, input_landed)
     both_got = swap(both_give, 1, n_dp)
     down_grad = back_rows(down_keep, down_got).astype(BF16)
     gate_grad = back_rows(both_keep[:, :, :hidden], both_got[:, :, :hidden]).astype(BF16)

time: 171 us -> 173 us (1.012)
  waiting for transfers between devices: 38.8 us -> 40.7 us
    ppermute x26, waiting for transfers between devices: 31 us -> 36.8 us  [exchange(): return lax.ppermute(value, 'expert', [(i, i ^ bit) for i in range(count)])]
    ppermute x9, waiting for transfers between devices: 7.85 us -> 3.9 us  [swap(): return lax.ppermute(value, 'dp', [(i, i ^ bit) for i in range(count)])]
    unnamed x58 -> x60, local copies, waits for them, and re-layouts: 3.92 us -> 2.51 us
  transfers between devices with their start and end apart: 35 -> 35, of which waited for: 10 -> 9; matrix products, arithmetic and copies ran while one was open for 8% -> 9% of each run, Pallas kernels for 33% -> 37%
where the time goes in v3:
time: 173 us; the launch traced here: 172 us
  Pallas kernels  64.2 us (37%)
  starting transfers between devices  41.4 us (24%)
  waiting for transfers between devices  40.7 us (24%)
  other arithmetic  18.9 us (11%)
  local copies, waits for them, and re-layouts  5.26 us (3%)
    ppermute x26, waiting for transfers between devices, exchange(): return lax.ppermute(value, 'expert', [(i, i ^ bit) for i in range(count)])  36.8 us
    ppermute x26, starting transfers between devices, exchange(): return lax.ppermute(value, 'expert', [(i, i ^ bit) for i in range(count)])  33.7 us
    pallas_call x1, Pallas kernels, shards(): pl.pallas_call(functools.partial(hidden_kernel, cfg), grid=(local,), in_s...  12.9 us
    pallas_call x1, Pallas kernels, shards(): pl.pallas_call(functools.partial(grad_kernel, cfg), grid=(local,), in_spe...  11.4 us
    pallas_call x1, Pallas kernels, shards(): pl.pallas_call(functools.partial(input_kernel, (plan, local, cap, cap_pad...  11 us
    pallas_call x1, Pallas kernels, shards(): pl.pallas_call(functools.partial(down_kernel, cap), grid=(local,), in_spe...  9.82 us
    pallas_call x1, Pallas kernels, shards(): pl.pallas_call(functools.partial(mixed_kernel, (plan, levels, local, cap,...  9.55 us
    ppermute x9, starting transfers between devices, swap(): return lax.ppermute(value, 'dp', [(i, i ^ bit) for i in range(count)])  7.76 us
  transfers between devices with their start and end apart: 35, of which 9 were waited for; matrix products, arithmetic and copies ran while one was open for 9% of the time, Pallas kernels for 37%

profile of v3, /device:TPU:0, one launch (start us, length us, event | category | flops | bytes accessed | tf_op | source)
XLA Modules:
  0.0 171.5 jit_solution(10431254837753495996)
XLA Ops:
  0.6 0.8 copy.16
  1.5 0.7 reduce_sum.18
  2.2 0.7 convert_element_type.113
  3.1 1.0 pad_maximum_fusion.refs_0_
  4.1 3.1 %collective-permute-start = (bf16[64,2176]{1,0:T(8,128)(2,1)S(1)}, bf16[64,2176]{1,0:T(8,128)(2,1)S(1)}, u32[]{:S(2)}, u32[]{:S(2)}) collective-permute-start(bf16[64,2176]{1,0:T(8,128)(2,1)S(1)} %pad_maximum_fusion.refs_0_), channel_id=1, source_target_pairs={{0,8},{4,12},{8,0},{12,4},{16,24},{20,28},{24,16},{28,20},{1,9},{5... | collective-permute-start | bytes 835592 | tf_op jit(solution)/shard_map/ppermute | solution.py:274
  7.2 2.6 %collective-permute-start.1 = (bf16[64,2176]{1,0:T(8,128)(2,1)S(1)}, bf16[64,2176]{1,0:T(8,128)(2,1)S(1)}, u32[]{:S(2)}, u32[]{:S(2)}) collective-permute-start(bf16[64,2176]{1,0:T(8,128)(2,1)S(1)} %pad_maximum_fusion.refs_0_), channel_id=1, source_target_pairs={{0,16},{4,20},{8,24},{12,28},{16,0},{20,4},{24,8},{28,12},{1,17},{... | collective-permute-start | bytes 835592 | tf_op jit(solution)/shard_map/ppermute | solution.py:274
  9.8 1.5 collective-permute-start.2
  11.3 8.4 %collective-permute-done.refs_1_ = bf16[64,2176]{1,0:T(8,128)(2,1)S(1)} collective-permute-done((bf16[64,2176]{1,0:T(8,128)(2,1)S(1)}, bf16[64,2176]{1,0:T(8,128)(2,1)S(1)}, u32[]{:S(2)}, u32[]{:S(2)}) %collective-permute-start) | collective-permute-done | bytes 278560 | tf_op jit(solution)/shard_map/ppermute | solution.py:274
  19.7 2.5 %collective-permute-done.1.refs_2_ = bf16[64,2176]{1,0:T(8,128)(2,1)S(1)} collective-permute-done((bf16[64,2176]{1,0:T(8,128)(2,1)S(1)}, bf16[64,2176]{1,0:T(8,128)(2,1)S(1)}, u32[]{:S(2)}, u32[]{:S(2)}) %collective-permute-start.1) | collective-permute-done | bytes 278560 | tf_op jit(solution)/shard_map/ppermute | solution.py:274
  22.3 0.5 collective-permute-start.3
  22.8 1.5 collective-permute-start.5
  24.3 0.5 collective-permute-start.6
  24.8 2.7 %collective-permute-start.4 = (bf16[64,2048]{1,0:T(8,128)(2,1)}, bf16[64,2048]{1,0:T(8,128)(2,1)S(1)}, u32[]{:S(2)}, u32[]{:S(2)}) collective-permute-start(bf16[64,2048]{1,0:T(8,128)(2,1)} %refs_0_.1), channel_id=1, source_target_pairs={{0,16},{4,20},{8,24},{12,28},{16,0},{20,4},{24,8},{28,12},{1,17},{... | collective-permute-start | bytes 786440 | tf_op jit(solution)/shard_map/ppermute | solution.py:274
  27.5 10.3 %collective-permute-done.4.refs_2_ = bf16[64,2048]{1,0:T(8,128)(2,1)S(1)} collective-permute-done((bf16[64,2048]{1,0:T(8,128)(2,1)}, bf16[64,2048]{1,0:T(8,128)(2,1)S(1)}, u32[]{:S(2)}, u32[]{:S(2)}) %collective-permute-start.4) | collective-permute-done | bytes 262176 | tf_op jit(solution)/shard_map/ppermute | solution.py:274
  37.8 1.6 collective-permute-start.7
  39.4 1.9 %cut_x.1 = bf16[256,1024]{1,0:T(8,128)(2,1)} custom-call(s32[1]{0:T(128)} %bitcast.1.far_ref.word_ref, bf16[64,2176]{1,0:T(8,128)(2,1)} %copy-done.2, bf16[64,2176]{1,0:T(8,128)(2,1)} %copy-done.6, bf16[64,2176]{1,0:T(8,128)(2,1)} %copy-done.7, bf16[64,2176]{1,0:T(8,128)(2,1)} %copy-done.8), custom_call_target="tpu_custom_call" | custom-call | bytes 2000 | tf_op jit(solution)/shard_map/cut_x/pallas_call | solution.py:350
  41.3 1.6 collective-permute-start.12
  42.9 0.6 collective-permute-start.10
  43.6 2.0 %collective-permute-start.9 = (bf16[64,2048]{1,0:T(8,128)(2,1)S(1)}, bf16[64,2048]{1,0:T(8,128)(2,1)S(1)}, u32[]{:S(2)}, u32[]{:S(2)}) collective-permute-start(bf16[64,2048]{1,0:T(8,128)(2,1)S(1)} %collective-permute-done.4.refs_2_), channel_id=1, source_target_pairs={{0,8},{4,12},{8,0},{12,4},{16,24},{20,28},{24,16},{28,20},{1,9},{5... | collective-permute-start | bytes 786440 | tf_op jit(solution)/shard_map/ppermute | solution.py:274
  45.6 0.8 collective-permute-done.7.refs_7_
  46.4 2.1 %collective-permute-start.11 = (bf16[64,2048]{1,0:T(8,128)(2,1)S(1)}, bf16[64,2048]{1,0:T(8,128)(2,1)S(1)}, u32[]{:S(2)}, u32[]{:S(2)}) collective-permute-start(bf16[64,2048]{1,0:T(8,128)(2,1)S(1)} %collective-permute-done.4.refs_2_), channel_id=1, source_target_pairs={{0,4},{4,0},{8,12},{12,8},{16,20},{20,16},{24,28},{28,24},{1,5},{5... | collective-permute-start | bytes 786440 | tf_op jit(solution)/shard_map/ppermute | solution.py:274
  48.5 12.9 %hidden.1 = (f32[4,160,768]{2,1,0:T(8,128)}, bf16[4,160,512]{2,1,0:T(8,128)(2,1)}, f32[4,160,128]{2,1,0:T(8,128)}, bf16[640,512]{1,0:T(8,128)(2,1)}, bf16[512,10...) custom-call(s32[1]{0:T(128)} %bitcast.first_ref, s32[1]{0:T(128)} %bitcast.1.far_ref.word_ref, ...), custom_call_target="tpu_custom_call" | custom-call | flops 6000000 | bytes 20000 | tf_op jit(solution)/shard_map/hidden/pallas_call | solution.py:389
  61.4 2.1 %collective-permute-start.15 = (bf16[256,1024]{1,0:T(8,128)(2,1)}, bf16[256,1024]{1,0:T(8,128)(2,1)S(1)}, u32[]{:S(2)}, u32[]{:S(2)}) collective-permute-start(bf16[256,1024]{1,0:T(8,128)(2,1)} %get-tuple-element.128), channel_id=1, source_target_pairs={{0,2},{1,3},{2,0},{3,1},{4,6},{5,7},{6,4},{7,5},{8,10},{9,11},{10,... | collective-permute-start | bytes 1572872 | tf_op jit(solution)/shard_map/ppermute | solution.py:270
  63.6 0.7 collective-permute-start.13
  64.3 1.4 collective-permute-start.14
  65.7 9.5 %mixed.1 = (bf16[256,2048]{1,0:T(8,128)(2,1)}, bf16[64,2048]{1,0:T(8,128)(2,1)}, bf16[64,2048]{1,0:T(8,128)(2,1)}, bf16[128,2048]{1,0:T(8,128)(2,1)}, bf16[256,1024]{1,0:T(8,128)(2,1)}) custom-call(s32[1]{0:T(128)} %bitcast.1.far_ref.word_ref, bf16[4,160,512]{2,1,0:T(8,128)(2,1)} %get-tuple-element.119.act_ref.refs_6_, ...), custom_call_target="tpu_custom_call" | custom-call | flops 6000000 | bytes 10000 | tf_op jit(solution)/shard_map/mixed/pallas_call | solution.py:414
  75.3 0.7 collective-permute-start.16
  76.0 1.4 collective-permute-start.17
  77.4 2.0 %collective-permute-start.21 = (bf16[256,1024]{1,0:T(8,128)(2,1)}, bf16[256,1024]{1,0:T(8,128)(2,1)S(1)}, u32[]{:S(2)}, u32[]{:S(2)}) collective-permute-start(bf16[256,1024]{1,0:T(8,128)(2,1)} %get-tuple-element.154), channel_id=1, source_target_pairs={{0,2},{1,3},{2,0},{3,1},{4,6},{5,7},{6,4},{7,5},{8,10},{9,11},{10,... | collective-permute-start | bytes 1572872 | tf_op jit(solution)/shard_map/ppermute | solution.py:270
  79.4 11.4 %hidden_grads.1 = (bf16[4,160,384]{2,1,0:T(8,128)(2,1)}, bf16[4,160,384]{2,1,0:T(8,128)(2,1)}, bf16[512,128]{1,0:T(8,128)(2,1)}, bf16[512,1024]{1,0:T(8,128)(2,1)}, bf16[256,1024]{1,0:T(8,128)(2,1)}) custom-call(s32[1]{0:T(128)} %bitcast.1.far_ref.word_ref, bf16[64,2048]{1,0:T(8,128)(2,1)} %refs_0_.1, bf16[64,2048]{1,0:T(8,128)(2,1)} %copy-done.11, ...), custom_call_target="tpu_custom_call" | custom-call | flops 6000000 | bytes 12000 | tf_op jit(solution)/shard_map/hidden_grads/pallas_call | solution.py:451
  90.9 2.8 %collective-permute-done.18.refs_7_ = bf16[4,160,512]{2,1,0:T(8,128)(2,1)S(1)} collective-permute-done((bf16[4,160,512]{2,1,0:T(8,128)(2,1)S(1)}, bf16[4,160,512]{2,1,0:T(8,128)(2,1)S(1)}, u32[]{:S(2)}, u32[]{:S(2)}) %collective-permute-start.18) | collective-permute-done | bytes 655392 | tf_op jit(solution)/shard_map/ppermute | solution.py:270
  93.7 1.4 collective-permute-start.20
  95.2 11.0 %input_grads.1 = (bf16[256,2176]{1,0:T(8,128)(2,1)}, bf16[64,2176]{1,0:T(8,128)(2,1)}, bf16[64,2176]{1,0:T(8,128)(2,1)}, bf16[128,2176]{1,0:T(8,128)(2,1)}) custom-call(bf16[4,160,384]{2,1,0:T(8,128)(2,1)} %get-tuple-element.178.d_gate_ref, bf16[4,160,384]{2,1,0:T(8,128)(2,1)} %get-tuple-element.179.d_up_ref, ...), custom_call_target="tpu_custom_call" | custom-call | flops 6000000 | bytes 16000 | tf_op jit(solution)/shard_map/input_grads/pallas_call | solution.py:476
  106.2 1.2 collective-permute-done.20
  107.4 1.6 collective-permute-start.23
  109.0 0.4 collective-permute-start.22
  109.4 1.1 fusion.10
  110.5 4.2 %collective-permute-done.23 = bf16[64,2176]{1,0:T(8,128)(2,1)S(1)} collective-permute-done((bf16[64,2176]{1,0:T(8,128)(2,1)}, bf16[64,2176]{1,0:T(8,128)(2,1)S(1)}, u32[]{:S(2)}, u32[]{:S(2)}) %collective-permute-start.23) | collective-permute-done | bytes 278560 | tf_op jit(solution)/shard_map/ppermute | solution.py:274
  114.7 1.7 %add_convert_fusion.4 = bf16[64,2176]{1,0:T(8,128)(2,1)} fusion(bf16[64,2176]{1,0:T(8,128)(2,1)S(1)} %collective-permute-done.23, bf16[256,2176]{1,0:T(8,128)(2,1)} %get-tuple-element.155), kind=kLoop, calls=%fused_computation.8 | loop fusion | flops 557056 | bytes 835584 | tf_op jit(solution)/shard_map/convert_element_type | solution.py:495
  116.5 1.2 collective-permute-start.25
  117.7 1.8 %add_convert_fusion.5 = bf16[64,2048]{1,0:T(8,128)(2,1)} fusion(bf16[64,2048]{1,0:T(8,128)(2,1)} %collective-permute-done.19, bf16[64,2048]{1,0:T(8,128)(2,1)} %collective-permute-done.17, bf16[256,2048]{1,0:T(8,128)(2,1)S(1)} %copy-done.13), kind=kLoop, calls=%fused_computation.14 | loop fusion | flops 786432 | bytes 1048576 | tf_op jit(solution)/shard_map/convert_element_type | solution.py:439
  119.5 2.0 %collective-permute-start.26 = (bf16[64,2048]{1,0:T(8,128)(2,1)}, bf16[64,2048]{1,0:T(8,128)(2,1)}, u32[]{:S(2)}, u32[]{:S(2)}) collective-permute-start(bf16[64,2048]{1,0:T(8,128)(2,1)} %add_convert_fusion.5), channel_id=1, source_target_pairs={{0,16},{4,20},{8,24},{12,28},{16,0},{20,4},{24,8},{28,12},{1,17},{... | collective-permute-start | bytes 786440 | tf_op jit(solution)/shard_map/ppermute | solution.py:274
  121.6 1.2 collective-permute-start.29
  122.8 0.2 collective-permute-start.28
  122.9 9.8 %down_grads.1 = (bf16[4,320,1024]{2,1,0:T(8,128)(2,1)}, bf16[4,512,384]{2,1,0:T(8,128)(2,1)}, bf16[4,512,384]{2,1,0:T(8,128)(2,1)}) custom-call(s32[1]{0:T(128)} %bitcast.2.near_ref, bf16[640,512]{1,0:T(8,128)(2,1)} %get-tuple-element.137.refs_8_.pick_ref, bf16[512,1024]{1,0:T(8,128)(2,1)} %get-tuple-element.165.refs_0_, bf16[256,1024]{1,0:T(8,128)(2,1)} %copy-done.15, ...), custom_call_target="tpu_custom_call" | custom-call | flops 6000000 | bytes 12000 | tf_op jit(solution)/shard_map/down_grads/pallas_call | solution.py:501
  132.8 0.7 collective-permute-start.30
  133.5 1.8 %add_convert_fusion.3 = bf16[64,2176]{1,0:T(8,128)(2,1)} fusion(bf16[64,2176]{1,0:T(8,128)(2,1)} %collective-permute-done.25, bf16[64,2176]{1,0:T(8,128)(2,1)S(1)} %collective-permute-done.22, bf16[256,2176]{1,0:T(8,128)(2,1)} %get-tuple-element.155), kind=kLoop, calls=%fused_computation.7 | loop fusion | flops 835584 | bytes 1114112 | tf_op jit(solution)/shard_map/convert_element_type | solution.py:514
  135.4 1.2 convert_add_fusion.1
  136.6 1.1 collective-permute-start.27
  137.7 2.9 %collective-permute-start.32 = (bf16[64,2176]{1,0:T(8,128)(2,1)}, bf16[64,2176]{1,0:T(8,128)(2,1)S(1)}, u32[]{:S(2)}, u32[]{:S(2)}) collective-permute-start(bf16[64,2176]{1,0:T(8,128)(2,1)} %add_convert_fusion.3), channel_id=1, source_target_pairs={{0,16},{4,20},{8,24},{12,28},{16,0},{20,4},{24,8},{28,12},{1,17},{... | collective-permute-start | bytes 835592 | tf_op jit(solution)/shard_map/ppermute | solution.py:274
  140.6 0.1 convert_add_fusion
  140.7 0.8 slice.130
  141.4 9.2 %collective-permute-done.27 = bf16[64,2048]{1,0:T(8,128)(2,1)S(1)} collective-permute-done((bf16[64,2048]{1,0:T(8,128)(2,1)S(1)}, bf16[64,2048]{1,0:T(8,128)(2,1)S(1)}, u32[]{:S(2)}, u32[]{:S(2)}) %collective-permute-start.27) | collective-permute-done | bytes 262176 | tf_op jit(solution)/shard_map/ppermute | solution.py:274
  150.6 1.7 %fusion.1 = bf16[64,2048]{1,0:T(8,128)(2,1)} fusion(f32[128,2048]{1,0:T(8,128)S(1)} %convert_add_fusion.1, bf16[64,2048]{1,0:T(8,128)(2,1)S(1)} %collective-permute-done.27, bf16[64,2048]{1,0:T(8,128)(2,1)} %collective-permute-done.26), kind=kLoop, calls=%fused_computation.13 | loop fusion | flops 655360 | bytes 1310720 | tf_op jit(solution)/shard_map/convert_element_type | solution.py:523
  152.4 0.8 copy-done.20
  153.2 0.1 copy-done.19
  153.3 7.7 %gate_up_grads.1 = (bf16[4,512,768]{2,1,0:T(8,128)(2,1)}, bf16[4,512,768]{2,1,0:T(8,128)(2,1)}) custom-call(s32[1]{0:T(128)} %bitcast.2.near_ref, bf16[4,320,1024]{2,1,0:T(8,128)(2,1)} %get-tuple-element.183.rows_ref, bf16[4,160,384]{2,1,0:T(8,128)(2,1)} %get-tuple-element.178.d_gate_ref, bf16[4,160,384]{2,1,0:T(8,128)(2,1)} %copy-done.19, ...), custom_call_target="tpu_custom_call" | custom-call | flops 3000000 | bytes 10000 | tf_op jit(solution)/shard_map/gate_up_grads/pallas_call | solution.py:526
  161.2 0.7 slice.131
  162.0 0.2 multiply_reduce_fusion
  162.1 0.1 subtract_divide_fusion
  162.2 0.7 copy.20
  162.9 3.1 %add_convert_fusion = bf16[4,512,384]{2,1,0:T(8,128)(2,1)} fusion(bf16[4,512,384]{2,1,0:T(8,128)(2,1)} %collective-permute-done.31, bf16[4,512,384]{2,1,0:T(8,128)(2,1)S(1)} %copy-done.5), kind=kLoop, calls=%fused_computation | loop fusion | flops 3145728 | bytes 4718592 | tf_op jit(solution)/shard_map/convert_element_type | solution.py:539
  166.0 1.1 collective-permute-done.34
  167.1 4.4 %add_convert_fusion.1 = (bf16[4,512,384]{2,1,0:T(8,128)(2,1)}, bf16[4,512,384]{2,1,0:T(8,128)(2,1)}) fusion(bf16[4,512,768]{2,1,0:T(8,128)(2,1)} %collective-permute-done.34, bf16[4,512,768]{2,1,0:T(8,128)(2,1)S(1)} %copy-done), kind=kLoop, calls=%fused_computation.1 | loop fusion | flops 6291456 | bytes 9437184 | tf_op jit(solution)/shard_map/convert_element_type | solution.py:541
  (96 shorter events, 0.9 us)
Async XLA Ops:
  0.6 42.3 %copy-start.9 = (bf16[64,2048]{1,0:T(8,128)(2,1)S(1)}, bf16[64,2048]{1,0:T(8,128)(2,1)}, u32[]{:S(2)}) copy-start(bf16[64,2048]{1,0:T(8,128)(2,1)} %refs_0_.1) | copy-start | bytes 786436
  4.1 35.3 %copy-start.2 = (bf16[64,2176]{1,0:T(8,128)(2,1)}, bf16[64,2176]{1,0:T(8,128)(2,1)S(1)}, u32[]{:S(2)}) copy-start(bf16[64,2176]{1,0:T(8,128)(2,1)S(1)} %pad_maximum_fusion.refs_0_) | copy-start | bytes 835588
  4.1 15.6 %collective-permute-start = (bf16[64,2176]{1,0:T(8,128)(2,1)S(1)}, bf16[64,2176]{1,0:T(8,128)(2,1)S(1)}, u32[]{:S(2)}, u32[]{:S(2)}) collective-permute-start(bf16[64,2176]{1,0:T(8,128)(2,1)S(1)} %pad_maximum_fusion.refs_0_), channel_id=1, source_target_pairs={{0,8},{4,12},{8,0},{12,4},{16,24},{20,28},{24,16},{28,20},{1,9},{5... | collective-permute-start | bytes 835592 | tf_op jit(solution)/shard_map/ppermute | solution.py:274
  7.2 15.0 %collective-permute-start.1 = (bf16[64,2176]{1,0:T(8,128)(2,1)S(1)}, bf16[64,2176]{1,0:T(8,128)(2,1)S(1)}, u32[]{:S(2)}, u32[]{:S(2)}) collective-permute-start(bf16[64,2176]{1,0:T(8,128)(2,1)S(1)} %pad_maximum_fusion.refs_0_), channel_id=1, source_target_pairs={{0,16},{4,20},{8,24},{12,28},{16,0},{20,4},{24,8},{28,12},{1,17},{... | collective-permute-start | bytes 835592 | tf_op jit(solution)/shard_map/ppermute | solution.py:274
  9.8 12.4 %collective-permute-start.2 = (bf16[64,2176]{1,0:T(8,128)(2,1)S(1)}, bf16[64,2176]{1,0:T(8,128)(2,1)S(1)}, u32[]{:S(2)}, u32[]{:S(2)}) collective-permute-start(bf16[64,2176]{1,0:T(8,128)(2,1)S(1)} %pad_maximum_fusion.refs_0_), channel_id=1, source_target_pairs={{0,4},{4,0},{8,12},{12,8},{16,20},{20,16},{24,28},{28,24},{1,5},{5... | collective-permute-start | bytes 835592 | tf_op jit(solution)/shard_map/ppermute | solution.py:274
  19.7 19.7 %copy-start.6 = (bf16[64,2176]{1,0:T(8,128)(2,1)}, bf16[64,2176]{1,0:T(8,128)(2,1)S(1)}, u32[]{:S(2)}) copy-start(bf16[64,2176]{1,0:T(8,128)(2,1)S(1)} %collective-permute-done.refs_1_) | copy-start | bytes 835588
  22.3 17.2 %copy-start.7 = (bf16[64,2176]{1,0:T(8,128)(2,1)}, bf16[64,2176]{1,0:T(8,128)(2,1)S(1)}, u32[]{:S(2)}) copy-start(bf16[64,2176]{1,0:T(8,128)(2,1)S(1)} %collective-permute-done.1.refs_2_) | copy-start | bytes 835588
  22.3 26.3 %copy-start.21 = (bf16[64,2176]{1,0:T(8,128)(2,1)}, bf16[64,2176]{1,0:T(8,128)(2,1)S(1)}, u32[]{:S(2)}) copy-start(bf16[64,2176]{1,0:T(8,128)(2,1)S(1)} %collective-permute-done.2.refs_4_) | copy-start | bytes 835588
  22.3 15.5 %collective-permute-start.3 = (bf16[64,2176]{1,0:T(8,128)(2,1)S(1)}, bf16[64,2176]{1,0:T(8,128)(2,1)S(1)}, u32[]{:S(2)}, u32[]{:S(2)}) collective-permute-start(bf16[64,2176]{1,0:T(8,128)(2,1)S(1)} %collective-permute-done.1.refs_2_), channel_id=1, source_target_pairs={{0,8},{4,12},{8,0},{12,4},{16,24},{20,28},{24,16},{28,20},{1,9},{5... | collective-permute-start | bytes 835592 | tf_op jit(solution)/shard_map/ppermute | solution.py:274
  22.8 15.0 %collective-permute-start.5 = (bf16[64,2176]{1,0:T(8,128)(2,1)S(1)}, bf16[64,2176]{1,0:T(8,128)(2,1)S(1)}, u32[]{:S(2)}, u32[]{:S(2)}) collective-permute-start(bf16[64,2176]{1,0:T(8,128)(2,1)S(1)} %collective-permute-done.refs_1_), channel_id=1, source_target_pairs={{0,4},{4,0},{8,12},{12,8},{16,20},{20,16},{24,28},{28,24},{1,5},{5... | collective-permute-start | bytes 835592 | tf_op jit(solution)/shard_map/ppermute | solution.py:274
  24.3 13.6 %collective-permute-start.6 = (bf16[64,2176]{1,0:T(8,128)(2,1)S(1)}, bf16[64,2176]{1,0:T(8,128)(2,1)S(1)}, u32[]{:S(2)}, u32[]{:S(2)}) collective-permute-start(bf16[64,2176]{1,0:T(8,128)(2,1)S(1)} %collective-permute-done.1.refs_2_), channel_id=1, source_target_pairs={{0,4},{4,0},{8,12},{12,8},{16,20},{20,16},{24,28},{28,24},{1,5},{5... | collective-permute-start | bytes 835592 | tf_op jit(solution)/shard_map/ppermute | solution.py:274
  24.8 13.0 %collective-permute-start.4 = (bf16[64,2048]{1,0:T(8,128)(2,1)}, bf16[64,2048]{1,0:T(8,128)(2,1)S(1)}, u32[]{:S(2)}, u32[]{:S(2)}) collective-permute-start(bf16[64,2048]{1,0:T(8,128)(2,1)} %refs_0_.1), channel_id=1, source_target_pairs={{0,16},{4,20},{8,24},{12,28},{16,0},{20,4},{24,8},{28,12},{1,17},{... | collective-permute-start | bytes 786440 | tf_op jit(solution)/shard_map/ppermute | solution.py:274
  37.8 23.6 %copy-start.10 = (bf16[64,2048]{1,0:T(8,128)(2,1)}, bf16[64,2048]{1,0:T(8,128)(2,1)S(1)}, u32[]{:S(2)}) copy-start(bf16[64,2048]{1,0:T(8,128)(2,1)S(1)} %collective-permute-done.4.refs_2_) | copy-start | bytes 786436
  37.8 1.6 copy-start.8
  37.8 10.7 %copy-start.22 = (bf16[64,2176]{1,0:T(8,128)(2,1)}, bf16[64,2176]{1,0:T(8,128)(2,1)S(1)}, u32[]{:S(2)}) copy-start(bf16[64,2176]{1,0:T(8,128)(2,1)S(1)} %collective-permute-done.5.refs_5_) | copy-start | bytes 835588
  37.8 10.7 %copy-start.23 = (bf16[64,2176]{1,0:T(8,128)(2,1)}, bf16[64,2176]{1,0:T(8,128)(2,1)S(1)}, u32[]{:S(2)}) copy-start(bf16[64,2176]{1,0:T(8,128)(2,1)S(1)} %collective-permute-done.6.refs_6_) | copy-start | bytes 835588
  37.8 8.6 %collective-permute-start.7 = (bf16[64,2176]{1,0:T(8,128)(2,1)S(1)}, bf16[64,2176]{1,0:T(8,128)(2,1)S(1)}, u32[]{:S(2)}, u32[]{:S(2)}) collective-permute-start(bf16[64,2176]{1,0:T(8,128)(2,1)S(1)} %collective-permute-done.3.refs_3_), channel_id=1, source_target_pairs={{0,4},{4,0},{8,12},{12,8},{16,20},{20,16},{24,28},{28,24},{1,5},{5... | collective-permute-start | bytes 835592 | tf_op jit(solution)/shard_map/ppermute | solution.py:274
  41.3 22.2 %collective-permute-start.12 = (bf16[256,1024]{1,0:T(8,128)(2,1)}, bf16[256,1024]{1,0:T(8,128)(2,1)S(1)}, u32[]{:S(2)}, u32[]{:S(2)}) collective-permute-start(bf16[256,1024]{1,0:T(8,128)(2,1)} %cut_x.1), channel_id=1, source_target_pairs={{0,2},{1,3},{2,0},{3,1},{4,6},{5,7},{6,4},{7,5},{8,10},{9,11},{10,... | collective-permute-start | bytes 1572872 | tf_op jit(solution)/shard_map/ppermute | solution.py:270
  42.9 18.5 %collective-permute-start.8 = (bf16[64,2048]{1,0:T(8,128)(2,1)S(1)}, bf16[64,2048]{1,0:T(8,128)(2,1)S(1)}, u32[]{:S(2)}, u32[]{:S(2)}) collective-permute-start(bf16[64,2048]{1,0:T(8,128)(2,1)S(1)} %copy-done.9), channel_id=1, source_target_pairs={{0,8},{4,12},{8,0},{12,4},{16,24},{20,28},{24,16},{28,20},{1,9},{5... | collective-permute-start | bytes 786440 | tf_op jit(solution)/shard_map/ppermute | solution.py:274
  42.9 20.6 %collective-permute-start.10 = (bf16[64,2048]{1,0:T(8,128)(2,1)S(1)}, bf16[64,2048]{1,0:T(8,128)(2,1)S(1)}, u32[]{:S(2)}, u32[]{:S(2)}) collective-permute-start(bf16[64,2048]{1,0:T(8,128)(2,1)S(1)} %copy-done.9), channel_id=1, source_target_pairs={{0,4},{4,0},{8,12},{12,8},{16,20},{20,16},{24,28},{28,24},{1,5},{5... | collective-permute-start | bytes 786440 | tf_op jit(solution)/shard_map/ppermute | solution.py:274
  43.6 19.9 %collective-permute-start.9 = (bf16[64,2048]{1,0:T(8,128)(2,1)S(1)}, bf16[64,2048]{1,0:T(8,128)(2,1)S(1)}, u32[]{:S(2)}, u32[]{:S(2)}) collective-permute-start(bf16[64,2048]{1,0:T(8,128)(2,1)S(1)} %collective-permute-done.4.refs_2_), channel_id=1, source_target_pairs={{0,8},{4,12},{8,0},{12,4},{16,24},{20,28},{24,16},{28,20},{1,9},{5... | collective-permute-start | bytes 786440 | tf_op jit(solution)/shard_map/ppermute | solution.py:274
  46.4 2.1 %copy-start.24 = (bf16[64,2176]{1,0:T(8,128)(2,1)}, bf16[64,2176]{1,0:T(8,128)(2,1)S(1)}, u32[]{:S(2)}) copy-start(bf16[64,2176]{1,0:T(8,128)(2,1)S(1)} %collective-permute-done.7.refs_7_) | copy-start | bytes 835588
  46.4 17.1 %collective-permute-start.11 = (bf16[64,2048]{1,0:T(8,128)(2,1)S(1)}, bf16[64,2048]{1,0:T(8,128)(2,1)S(1)}, u32[]{:S(2)}, u32[]{:S(2)}) collective-permute-start(bf16[64,2048]{1,0:T(8,128)(2,1)S(1)} %collective-permute-done.4.refs_2_), channel_id=1, source_target_pairs={{0,4},{4,0},{8,12},{12,8},{16,20},{20,16},{24,28},{28,24},{1,5},{5... | collective-permute-start | bytes 786440 | tf_op jit(solution)/shard_map/ppermute | solution.py:274
  61.4 4.2 %copy-start.11 = (bf16[64,2048]{1,0:T(8,128)(2,1)}, bf16[64,2048]{1,0:T(8,128)(2,1)S(1)}, u32[]{:S(2)}) copy-start(bf16[64,2048]{1,0:T(8,128)(2,1)S(1)} %collective-permute-done.8.refs_1_) | copy-start | bytes 786436
  61.4 13.8 %collective-permute-start.15 = (bf16[256,1024]{1,0:T(8,128)(2,1)}, bf16[256,1024]{1,0:T(8,128)(2,1)S(1)}, u32[]{:S(2)}, u32[]{:S(2)}) collective-permute-start(bf16[256,1024]{1,0:T(8,128)(2,1)} %get-tuple-element.128), channel_id=1, source_target_pairs={{0,2},{1,3},{2,0},{3,1},{4,6},{5,7},{6,4},{7,5},{8,10},{9,11},{10,... | collective-permute-start | bytes 1572872 | tf_op jit(solution)/shard_map/ppermute | solution.py:270
  63.5 2.2 %copy-start.12 = (bf16[64,2048]{1,0:T(8,128)(2,1)}, bf16[64,2048]{1,0:T(8,128)(2,1)S(1)}, u32[]{:S(2)}) copy-start(bf16[64,2048]{1,0:T(8,128)(2,1)S(1)} %collective-permute-done.9.refs_3_) | copy-start | bytes 786436
  63.5 15.9 %copy-start.25 = (bf16[64,2048]{1,0:T(8,128)(2,1)}, bf16[64,2048]{1,0:T(8,128)(2,1)S(1)}, u32[]{:S(2)}) copy-start(bf16[64,2048]{1,0:T(8,128)(2,1)S(1)} %collective-permute-done.10.refs_4_) | copy-start | bytes 786436
  63.5 15.9 %copy-start.26 = (bf16[64,2048]{1,0:T(8,128)(2,1)}, bf16[64,2048]{1,0:T(8,128)(2,1)S(1)}, u32[]{:S(2)}) copy-start(bf16[64,2048]{1,0:T(8,128)(2,1)S(1)} %collective-permute-done.11.refs_6_) | copy-start | bytes 786436
  63.5 2.1 %copy-start.15 = (bf16[256,1024]{1,0:T(8,128)(2,1)}, bf16[256,1024]{1,0:T(8,128)(2,1)S(1)}, u32[]{:S(2)}) copy-start(bf16[256,1024]{1,0:T(8,128)(2,1)S(1)} %collective-permute-done.12.refs_1_) | copy-start | bytes 1572868
  63.6 11.7 %collective-permute-start.13 = (bf16[64,2048]{1,0:T(8,128)(2,1)S(1)}, bf16[64,2048]{1,0:T(8,128)(2,1)S(1)}, u32[]{:S(2)}, u32[]{:S(2)}) collective-permute-start(bf16[64,2048]{1,0:T(8,128)(2,1)S(1)} %collective-permute-done.8.refs_1_), channel_id=1, source_target_pairs={{0,4},{4,0},{8,12},{12,8},{16,20},{20,16},{24,28},{28,24},{1,5},{5... | collective-permute-start | bytes 786440 | tf_op jit(solution)/shard_map/ppermute | solution.py:274
  64.3 10.9 %collective-permute-start.14 = (bf16[64,2048]{1,0:T(8,128)(2,1)S(1)}, bf16[64,2048]{1,0:T(8,128)(2,1)S(1)}, u32[]{:S(2)}, u32[]{:S(2)}) collective-permute-start(bf16[64,2048]{1,0:T(8,128)(2,1)S(1)} %collective-permute-done.9.refs_3_), channel_id=1, source_target_pairs={{0,4},{4,0},{8,12},{12,8},{16,20},{20,16},{24,28},{28,24},{1,5},{5... | collective-permute-start | bytes 786440 | tf_op jit(solution)/shard_map/ppermute | solution.py:274
  65.7 10.4 %copy-start.1 = (bf16[4,160,512]{2,1,0:T(8,128)(2,1)S(1)}, bf16[4,160,512]{2,1,0:T(8,128)(2,1)}, u32[]{:S(2)}) copy-start(bf16[4,160,512]{2,1,0:T(8,128)(2,1)} %get-tuple-element.119.act_ref.refs_6_) | copy-start | bytes 1966084
  75.2 4.2 %copy-start.27 = (bf16[64,2048]{1,0:T(8,128)(2,1)}, bf16[64,2048]{1,0:T(8,128)(2,1)S(1)}, u32[]{:S(2)}) copy-start(bf16[64,2048]{1,0:T(8,128)(2,1)S(1)} %collective-permute-done.13.refs_5_) | copy-start | bytes 786436
  75.2 4.2 %copy-start.28 = (bf16[64,2048]{1,0:T(8,128)(2,1)}, bf16[64,2048]{1,0:T(8,128)(2,1)S(1)}, u32[]{:S(2)}) copy-start(bf16[64,2048]{1,0:T(8,128)(2,1)S(1)} %collective-permute-done.14.refs_7_) | copy-start | bytes 786436
  75.3 4.1 %copy-start.16 = (bf16[256,1024]{1,0:T(8,128)(2,1)}, bf16[256,1024]{1,0:T(8,128)(2,1)S(1)}, u32[]{:S(2)}) copy-start(bf16[256,1024]{1,0:T(8,128)(2,1)S(1)} %collective-permute-done.15.refs_2_) | copy-start | bytes 1572868
  75.3 15.5 %collective-permute-start.16 = (bf16[64,2048]{1,0:T(8,128)(2,1)}, bf16[64,2048]{1,0:T(8,128)(2,1)S(1)}, u32[]{:S(2)}, u32[]{:S(2)}) collective-permute-start(bf16[64,2048]{1,0:T(8,128)(2,1)} %get-tuple-element.130), channel_id=1, source_target_pairs={{0,4},{4,0},{8,12},{12,8},{16,20},{20,16},{24,28},{28,24},{1,5},{5... | collective-permute-start | bytes 786440 | tf_op jit(solution)/shard_map/ppermute | solution.py:274
  76.0 17.7 %collective-permute-start.18 = (bf16[4,160,512]{2,1,0:T(8,128)(2,1)S(1)}, bf16[4,160,512]{2,1,0:T(8,128)(2,1)S(1)}, u32[]{:S(2)}, u32[]{:S(2)}) collective-permute-start(bf16[4,160,512]{2,1,0:T(8,128)(2,1)S(1)} %copy-done.1), channel_id=1, source_target_pairs={{0,2},{1,3},{2,0},{3,1},{4,6},{5,7},{6,4},{7,5},{8,10},{9,11},{10,... | collective-permute-start | bytes 1966088 | tf_op jit(solution)/shard_map/ppermute | solution.py:270
  76.0 14.9 %collective-permute-start.17 = (bf16[64,2048]{1,0:T(8,128)(2,1)}, bf16[64,2048]{1,0:T(8,128)(2,1)}, u32[]{:S(2)}, u32[]{:S(2)}) collective-permute-start(bf16[64,2048]{1,0:T(8,128)(2,1)} %get-tuple-element.131), channel_id=1, source_target_pairs={{0,4},{4,0},{8,12},{12,8},{16,20},{20,16},{24,28},{28,24},{1,5},{5... | collective-permute-start | bytes 786440 | tf_op jit(solution)/shard_map/ppermute | solution.py:274
  77.4 28.8 %collective-permute-start.21 = (bf16[256,1024]{1,0:T(8,128)(2,1)}, bf16[256,1024]{1,0:T(8,128)(2,1)S(1)}, u32[]{:S(2)}, u32[]{:S(2)}) collective-permute-start(bf16[256,1024]{1,0:T(8,128)(2,1)} %get-tuple-element.154), channel_id=1, source_target_pairs={{0,2},{1,3},{2,0},{3,1},{4,6},{5,7},{6,4},{7,5},{8,10},{9,11},{10,... | collective-permute-start | bytes 1572872 | tf_op jit(solution)/shard_map/ppermute | solution.py:270
  79.4 11.4 %copy-start.13 = (bf16[256,2048]{1,0:T(8,128)(2,1)S(1)}, bf16[256,2048]{1,0:T(8,128)(2,1)}, u32[]{:S(2)}) copy-start(bf16[256,2048]{1,0:T(8,128)(2,1)} %get-tuple-element.129) | copy-start | bytes 3145732
  93.7 1.5 copy-start.14
  93.7 13.7 %collective-permute-start.20 = (bf16[128,2048]{1,0:T(8,128)(2,1)}, bf16[128,2048]{1,0:T(8,128)(2,1)}, u32[]{:S(2)}, u32[]{:S(2)}) collective-permute-start(bf16[128,2048]{1,0:T(8,128)(2,1)} %get-tuple-element.153), channel_id=1, source_target_pairs={{0,4},{4,0},{8,12},{12,8},{16,20},{20,16},{24,28},{28,24},{1,5},{5... | collective-permute-start | bytes 1572872 | tf_op jit(solution)/shard_map/ppermute | solution.py:274
  95.0 11.1 %collective-permute-start.19 = (bf16[64,2048]{1,0:T(8,128)(2,1)S(1)}, bf16[64,2048]{1,0:T(8,128)(2,1)}, u32[]{:S(2)}, u32[]{:S(2)}) collective-permute-start(bf16[64,2048]{1,0:T(8,128)(2,1)S(1)} %add_convert_fusion.6), channel_id=1, source_target_pairs={{0,8},{4,12},{8,0},{12,4},{16,24},{20,28},{24,16},{28,20},{1,9},{5... | collective-permute-start | bytes 786440 | tf_op jit(solution)/shard_map/ppermute | solution.py:274
  95.1 21.4 %collective-permute-start.24 = (bf16[256,1024]{1,0:T(8,128)(2,1)}, bf16[256,1024]{1,0:T(8,128)(2,1)S(1)}, u32[]{:S(2)}, u32[]{:S(2)}) collective-permute-start(bf16[256,1024]{1,0:T(8,128)(2,1)} %get-tuple-element.159), channel_id=1, source_target_pairs={{0,2},{1,3},{2,0},{3,1},{4,6},{5,7},{6,4},{7,5},{8,10},{9,11},{10,... | collective-permute-start | bytes 1572872 | tf_op jit(solution)/shard_map/ppermute | solution.py:270
  106.2 15.4 %copy-start.3 = (bf16[4,160,384]{2,1,0:T(8,128)(2,1)S(1)}, bf16[4,160,384]{2,1,0:T(8,128)(2,1)}, u32[]{:S(2)}) copy-start(bf16[4,160,384]{2,1,0:T(8,128)(2,1)} %get-tuple-element.178.d_gate_ref) | copy-start | bytes 1474564
  106.2 2.8 %copy-start.17 = (bf16[256,1024]{1,0:T(8,128)(2,1)}, bf16[256,1024]{1,0:T(8,128)(2,1)S(1)}, u32[]{:S(2)}) copy-start(bf16[256,1024]{1,0:T(8,128)(2,1)S(1)} %collective-permute-done.21.refs_4_) | copy-start | bytes 1572868
  107.4 7.4 %collective-permute-start.23 = (bf16[64,2176]{1,0:T(8,128)(2,1)}, bf16[64,2176]{1,0:T(8,128)(2,1)S(1)}, u32[]{:S(2)}, u32[]{:S(2)}) collective-permute-start(bf16[64,2176]{1,0:T(8,128)(2,1)} %get-tuple-element.157), channel_id=1, source_target_pairs={{0,4},{4,0},{8,12},{12,8},{16,20},{20,16},{24,28},{28,24},{1,5},{5... | collective-permute-start | bytes 835592 | tf_op jit(solution)/shard_map/ppermute | solution.py:274
  109.0 23.8 %collective-permute-start.22 = (bf16[64,2176]{1,0:T(8,128)(2,1)}, bf16[64,2176]{1,0:T(8,128)(2,1)S(1)}, u32[]{:S(2)}, u32[]{:S(2)}) collective-permute-start(bf16[64,2176]{1,0:T(8,128)(2,1)} %get-tuple-element.156), channel_id=1, source_target_pairs={{0,4},{4,0},{8,12},{12,8},{16,20},{20,16},{24,28},{28,24},{1,5},{5... | collective-permute-start | bytes 835592 | tf_op jit(solution)/shard_map/ppermute | solution.py:274
  116.5 6.5 %copy-start.18 = (bf16[256,1024]{1,0:T(8,128)(2,1)}, bf16[256,1024]{1,0:T(8,128)(2,1)S(1)}, u32[]{:S(2)}) copy-start(bf16[256,1024]{1,0:T(8,128)(2,1)S(1)} %collective-permute-done.24.refs_5_) | copy-start | bytes 1572868
  116.5 17.0 %collective-permute-start.25 = (bf16[64,2176]{1,0:T(8,128)(2,1)}, bf16[64,2176]{1,0:T(8,128)(2,1)}, u32[]{:S(2)}, u32[]{:S(2)}) collective-permute-start(bf16[64,2176]{1,0:T(8,128)(2,1)} %add_convert_fusion.4), channel_id=1, source_target_pairs={{0,8},{4,12},{8,0},{12,4},{16,24},{20,28},{24,16},{28,20},{1,9},{5... | collective-permute-start | bytes 835592 | tf_op jit(solution)/shard_map/ppermute | solution.py:274
  119.5 15.8 %collective-permute-start.26 = (bf16[64,2048]{1,0:T(8,128)(2,1)}, bf16[64,2048]{1,0:T(8,128)(2,1)}, u32[]{:S(2)}, u32[]{:S(2)}) collective-permute-start(bf16[64,2048]{1,0:T(8,128)(2,1)} %add_convert_fusion.5), channel_id=1, source_target_pairs={{0,16},{4,20},{8,24},{12,28},{16,0},{20,4},{24,8},{28,12},{1,17},{... | collective-permute-start | bytes 786440 | tf_op jit(solution)/shard_map/ppermute | solution.py:274
  121.6 30.8 %collective-permute-start.29 = (bf16[4,160,384]{2,1,0:T(8,128)(2,1)S(1)}, bf16[4,160,384]{2,1,0:T(8,128)(2,1)S(1)}, u32[]{:S(2)}, u32[]{:S(2)}) collective-permute-start(bf16[4,160,384]{2,1,0:T(8,128)(2,1)S(1)} %copy-done.3), channel_id=1, source_target_pairs={{0,2},{1,3},{2,0},{3,1},{4,6},{5,7},{6,4},{7,5},{8,10},{9,11},{10,... | collective-permute-start | bytes 1474568 | tf_op jit(solution)/shard_map/ppermute | solution.py:270
  122.8 14.9 %collective-permute-start.28 = (bf16[128,2176]{1,0:T(8,128)(2,1)}, bf16[128,2176]{1,0:T(8,128)(2,1)S(1)}, u32[]{:S(2)}, u32[]{:S(2)}) collective-permute-start(bf16[128,2176]{1,0:T(8,128)(2,1)} %get-tuple-element.177), channel_id=1, source_target_pairs={{0,4},{4,0},{8,12},{12,8},{16,20},{20,16},{24,28},{28,24},{1,5},{5... | collective-permute-start | bytes 1671176 | tf_op jit(solution)/shard_map/ppermute | solution.py:274
  122.9 9.8 %copy-start.4 = (bf16[4,160,384]{2,1,0:T(8,128)(2,1)S(1)}, bf16[4,160,384]{2,1,0:T(8,128)(2,1)}, u32[]{:S(2)}) copy-start(bf16[4,160,384]{2,1,0:T(8,128)(2,1)} %get-tuple-element.179.d_up_ref) | copy-start | bytes 1474564
  132.8 19.6 %collective-permute-start.30 = (bf16[4,160,384]{2,1,0:T(8,128)(2,1)S(1)}, bf16[4,160,384]{2,1,0:T(8,128)(2,1)S(1)}, u32[]{:S(2)}, u32[]{:S(2)}) collective-permute-start(bf16[4,160,384]{2,1,0:T(8,128)(2,1)S(1)} %copy-done.4), channel_id=1, source_target_pairs={{0,2},{1,3},{2,0},{3,1},{4,6},{5,7},{6,4},{7,5},{8,10},{9,11},{10,... | collective-permute-start | bytes 1474568 | tf_op jit(solution)/shard_map/ppermute | solution.py:270
  135.4 17.8 %collective-permute-start.31 = (bf16[4,512,384]{2,1,0:T(8,128)(2,1)}, bf16[4,512,384]{2,1,0:T(8,128)(2,1)}, u32[]{:S(2)}, u32[]{:S(2)}) collective-permute-start(bf16[4,512,384]{2,1,0:T(8,128)(2,1)} %get-tuple-element.180), channel_id=1, source_target_pairs={{0,1},{1,0},{2,3},{3,2},{4,5},{5,4},{6,7},{7,6},{8,9},{9,8},{10,11... | collective-permute-start | bytes 4718600 | tf_op jit(solution)/shard_map/ppermute | solution.py:270
  136.6 14.1 %collective-permute-start.27 = (bf16[64,2048]{1,0:T(8,128)(2,1)S(1)}, bf16[64,2048]{1,0:T(8,128)(2,1)S(1)}, u32[]{:S(2)}, u32[]{:S(2)}) collective-permute-start(bf16[64,2048]{1,0:T(8,128)(2,1)S(1)} %slice.132), channel_id=1, source_target_pairs={{0,8},{4,12},{8,0},{12,4},{16,24},{20,28},{24,16},{28,20},{1,9},{5... | collective-permute-start | bytes 786440 | tf_op jit(solution)/shard_map/ppermute | solution.py:274
  137.7 23.4 %collective-permute-start.32 = (bf16[64,2176]{1,0:T(8,128)(2,1)}, bf16[64,2176]{1,0:T(8,128)(2,1)S(1)}, u32[]{:S(2)}, u32[]{:S(2)}) collective-permute-start(bf16[64,2176]{1,0:T(8,128)(2,1)} %add_convert_fusion.3), channel_id=1, source_target_pairs={{0,16},{4,20},{8,24},{12,28},{16,0},{20,4},{24,8},{28,12},{1,17},{... | collective-permute-start | bytes 835592 | tf_op jit(solution)/shard_map/ppermute | solution.py:274
  150.6 10.4 %collective-permute-start.33 = (bf16[64,2176]{1,0:T(8,128)(2,1)}, bf16[64,2176]{1,0:T(8,128)(2,1)S(1)}, u32[]{:S(2)}, u32[]{:S(2)}) collective-permute-start(bf16[64,2176]{1,0:T(8,128)(2,1)} %slice.130), channel_id=1, source_target_pairs={{0,8},{4,12},{8,0},{12,4},{16,24},{20,28},{24,16},{28,20},{1,9},{5... | collective-permute-start | bytes 835592 | tf_op jit(solution)/shard_map/ppermute | solution.py:274
  152.4 0.9 copy-start.19
  152.4 0.8 copy-start.20
  161.0 1.9 %copy-start.5 = (bf16[4,512,384]{2,1,0:T(8,128)(2,1)S(1)}, bf16[4,512,384]{2,1,0:T(8,128)(2,1)}, u32[]{:S(2)}) copy-start(bf16[4,512,384]{2,1,0:T(8,128)(2,1)} %get-tuple-element.192) | copy-start | bytes 4718596
  161.1 6.1 %collective-permute-start.34 = (bf16[4,512,768]{2,1,0:T(8,128)(2,1)}, bf16[4,512,768]{2,1,0:T(8,128)(2,1)}, u32[]{:S(2)}, u32[]{:S(2)}) collective-permute-start(bf16[4,512,768]{2,1,0:T(8,128)(2,1)} %get-tuple-element.191), channel_id=1, source_target_pairs={{0,1},{1,0},{2,3},{3,2},{4,5},{5,4},{6,7},{7,6},{8,9},{9,8},{10,11... | collective-permute-start | bytes 9437192 | tf_op jit(solution)/shard_map/ppermute | solution.py:270
  162.9 4.2 %copy-start = (bf16[4,512,768]{2,1,0:T(8,128)(2,1)S(1)}, bf16[4,512,768]{2,1,0:T(8,128)(2,1)}, u32[]{:S(2)}) copy-start(bf16[4,512,768]{2,1,0:T(8,128)(2,1)} %get-tuple-element.190) | copy-start | bytes 9437188

commit v4 on v1

--- a/solution.py
+++ b/solution.py
@@ -521,7 +521,8 @@
     input_landed.append(send(input_ends[:tok_rows].astype(BF16), 2))
     down_got = swap(down_give, 1, n_dp)
     mixed = finish(mixed_ends, mixed_landed).astype(BF16)
-    mixed, input_ends, input_landed, gate_far, up_far = fence(mixed, input_ends, input_landed, gate_far, up_far)
+    mixed, input_ends, input_landed[0], gate_far, up_far = fence(
+        mixed, input_ends, input_landed[0], gate_far, up_far)
     both_specs = [by_expert(columns, 2 * hidden)] * 2
     both_keep, both_give = pl.pallas_call(
         functools.partial(both_kernel, cap),
@@ -534,10 +535,12 @@
         cost_estimate=cost(3, 10),
         name="gate_up_grads",
     )(near_word, x_rows, d_gate, gate_far, d_up, up_far)
+    both_give, input_landed = fence(both_give, input_landed)
     both_got = swap(both_give, 1, n_dp)
-    down_grad = back_rows(down_keep, down_got).astype(BF16)
     gate_grad = back_rows(both_keep[:, :, :hidden], both_got[:, :, :hidden]).astype(BF16)
     up_grad = back_rows(both_keep[:, :, hidden:], both_got[:, :, hidden:]).astype(BF16)
+    gate_grad, up_grad, down_got = fence(gate_grad, up_grad, down_got)
+    down_grad = back_rows(down_keep, down_got).astype(BF16)
 
     back = finish(input_ends, input_landed)
     token_grad = back[:, :width].astype(BF16)

time: 171 us -> 168 us (0.982)
  waiting for transfers between devices: 38.8 us -> 36 us
    ppermute x26, waiting for transfers between devices: 31 us -> 28.1 us  [exchange(): return lax.ppermute(value, 'expert', [(i, i ^ bit) for i in range(count)])]
    unnamed x58 -> x56, local copies, waits for them, and re-layouts: 3.92 us -> 3.99 us
  transfers between devices with their start and end apart: 35 -> 35, of which waited for: 10 -> 9; matrix products, arithmetic and copies ran while one was open for 8% -> 10% of each run, Pallas kernels for 33% -> 38%
where the time goes in v4:
time: 168 us; the launch traced here: 167 us
  Pallas kernels  64.1 us (38%)
  starting transfers between devices  41.5 us (25%)
  waiting for transfers between devices  36 us (21%)
  other arithmetic  17.6 us (10%)
  local copies, waits for them, and re-layouts  6.71 us (4%)
    ppermute x26, starting transfers between devices, exchange(): return lax.ppermute(value, 'expert', [(i, i ^ bit) for i in range(count)])  34.8 us
    ppermute x26, waiting for transfers between devices, exchange(): return lax.ppermute(value, 'expert', [(i, i ^ bit) for i in range(count)])  28.1 us
    pallas_call x1, Pallas kernels, shards(): pl.pallas_call(functools.partial(hidden_kernel, cfg), grid=(local,), in_s...  12.8 us
    pallas_call x1, Pallas kernels, shards(): pl.pallas_call(functools.partial(grad_kernel, cfg), grid=(local,), in_spe...  11.3 us
    pallas_call x1, Pallas kernels, shards(): pl.pallas_call(functools.partial(input_kernel, (plan, local, cap, cap_pad...  11 us
    pallas_call x1, Pallas kernels, shards(): pl.pallas_call(functools.partial(down_kernel, cap), grid=(local,), in_spe...  9.81 us
    pallas_call x1, Pallas kernels, shards(): pl.pallas_call(functools.partial(mixed_kernel, (plan, levels, local, cap,...  9.53 us
    ppermute x9, waiting for transfers between devices, swap(): return lax.ppermute(value, 'dp', [(i, i ^ bit) for i in range(count)])  7.89 us
  transfers between devices with their start and end apart: 35, of which 9 were waited for; matrix products, arithmetic and copies ran while one was open for 10% of the time, Pallas kernels for 38%

profile of v4, /device:TPU:0, one launch (start us, length us, event | category | flops | bytes accessed | tf_op | source)
XLA Modules:
  0.0 167.0 jit_solution(16961384014698434096)
XLA Ops:
  0.6 0.8 copy.16
  1.5 0.7 reduce_sum.18
  2.2 0.7 convert_element_type.113
  3.1 1.0 pad_maximum_fusion.refs_0_
  4.1 3.1 %collective-permute-start = (bf16[64,2176]{1,0:T(8,128)(2,1)S(1)}, bf16[64,2176]{1,0:T(8,128)(2,1)S(1)}, u32[]{:S(2)}, u32[]{:S(2)}) collective-permute-start(bf16[64,2176]{1,0:T(8,128)(2,1)S(1)} %pad_maximum_fusion.refs_0_), channel_id=1, source_target_pairs={{0,8},{4,12},{8,0},{12,4},{16,24},{20,28},{24,16},{28,20},{1,9},{5... | collective-permute-start | bytes 835592 | tf_op jit(solution)/shard_map/ppermute | solution.py:274
  7.2 2.6 %collective-permute-start.1 = (bf16[64,2176]{1,0:T(8,128)(2,1)S(1)}, bf16[64,2176]{1,0:T(8,128)(2,1)S(1)}, u32[]{:S(2)}, u32[]{:S(2)}) collective-permute-start(bf16[64,2176]{1,0:T(8,128)(2,1)S(1)} %pad_maximum_fusion.refs_0_), channel_id=1, source_target_pairs={{0,16},{4,20},{8,24},{12,28},{16,0},{20,4},{24,8},{28,12},{1,17},{... | collective-permute-start | bytes 835592 | tf_op jit(solution)/shard_map/ppermute | solution.py:274
  9.8 1.5 collective-permute-start.2
  11.3 8.4 %collective-permute-done.refs_1_ = bf16[64,2176]{1,0:T(8,128)(2,1)S(1)} collective-permute-done((bf16[64,2176]{1,0:T(8,128)(2,1)S(1)}, bf16[64,2176]{1,0:T(8,128)(2,1)S(1)}, u32[]{:S(2)}, u32[]{:S(2)}) %collective-permute-start) | collective-permute-done | bytes 278560 | tf_op jit(solution)/shard_map/ppermute | solution.py:274
  19.7 2.5 %collective-permute-done.1.refs_2_ = bf16[64,2176]{1,0:T(8,128)(2,1)S(1)} collective-permute-done((bf16[64,2176]{1,0:T(8,128)(2,1)S(1)}, bf16[64,2176]{1,0:T(8,128)(2,1)S(1)}, u32[]{:S(2)}, u32[]{:S(2)}) %collective-permute-start.1) | collective-permute-done | bytes 278560 | tf_op jit(solution)/shard_map/ppermute | solution.py:274
  22.3 0.5 collective-permute-start.3
  22.8 1.5 collective-permute-start.5
  24.3 0.5 collective-permute-start.6
  24.8 2.7 %collective-permute-start.4 = (bf16[64,2048]{1,0:T(8,128)(2,1)}, bf16[64,2048]{1,0:T(8,128)(2,1)S(1)}, u32[]{:S(2)}, u32[]{:S(2)}) collective-permute-start(bf16[64,2048]{1,0:T(8,128)(2,1)} %refs_0_.1), channel_id=1, source_target_pairs={{0,16},{4,20},{8,24},{12,28},{16,0},{20,4},{24,8},{28,12},{1,17},{... | collective-permute-start | bytes 786440 | tf_op jit(solution)/shard_map/ppermute | solution.py:274
  27.5 10.3 %collective-permute-done.4.refs_2_ = bf16[64,2048]{1,0:T(8,128)(2,1)S(1)} collective-permute-done((bf16[64,2048]{1,0:T(8,128)(2,1)}, bf16[64,2048]{1,0:T(8,128)(2,1)S(1)}, u32[]{:S(2)}, u32[]{:S(2)}) %collective-permute-start.4) | collective-permute-done | bytes 262176 | tf_op jit(solution)/shard_map/ppermute | solution.py:274
  37.8 1.6 collective-permute-start.7
  39.4 1.9 %cut_x.1 = bf16[256,1024]{1,0:T(8,128)(2,1)} custom-call(s32[1]{0:T(128)} %bitcast.1.far_ref.word_ref, bf16[64,2176]{1,0:T(8,128)(2,1)} %copy-done.1, bf16[64,2176]{1,0:T(8,128)(2,1)} %copy-done.6, bf16[64,2176]{1,0:T(8,128)(2,1)} %copy-done.7, bf16[64,2176]{1,0:T(8,128)(2,1)} %copy-done.8), custom_call_target="tpu_custom_call" | custom-call | bytes 2000 | tf_op jit(solution)/shard_map/cut_x/pallas_call | solution.py:350
  41.3 1.6 collective-permute-start.12
  42.9 0.6 collective-permute-start.10
  43.6 2.0 %collective-permute-start.9 = (bf16[64,2048]{1,0:T(8,128)(2,1)S(1)}, bf16[64,2048]{1,0:T(8,128)(2,1)S(1)}, u32[]{:S(2)}, u32[]{:S(2)}) collective-permute-start(bf16[64,2048]{1,0:T(8,128)(2,1)S(1)} %collective-permute-done.4.refs_2_), channel_id=1, source_target_pairs={{0,8},{4,12},{8,0},{12,4},{16,24},{20,28},{24,16},{28,20},{1,9},{5... | collective-permute-start | bytes 786440 | tf_op jit(solution)/shard_map/ppermute | solution.py:274
  45.6 0.9 collective-permute-done.7.refs_7_
  46.4 2.1 %collective-permute-start.11 = (bf16[64,2048]{1,0:T(8,128)(2,1)S(1)}, bf16[64,2048]{1,0:T(8,128)(2,1)S(1)}, u32[]{:S(2)}, u32[]{:S(2)}) collective-permute-start(bf16[64,2048]{1,0:T(8,128)(2,1)S(1)} %collective-permute-done.4.refs_2_), channel_id=1, source_target_pairs={{0,4},{4,0},{8,12},{12,8},{16,20},{20,16},{24,28},{28,24},{1,5},{5... | collective-permute-start | bytes 786440 | tf_op jit(solution)/shard_map/ppermute | solution.py:274
  48.5 12.8 %hidden.1 = (f32[4,160,768]{2,1,0:T(8,128)}, bf16[4,160,512]{2,1,0:T(8,128)(2,1)}, f32[4,160,128]{2,1,0:T(8,128)}, bf16[640,512]{1,0:T(8,128)(2,1)}, bf16[512,10...) custom-call(s32[1]{0:T(128)} %bitcast.first_ref, s32[1]{0:T(128)} %bitcast.1.far_ref.word_ref, ...), custom_call_target="tpu_custom_call" | custom-call | flops 6000000 | bytes 20000 | tf_op jit(solution)/shard_map/hidden/pallas_call | solution.py:389
  61.4 2.1 %collective-permute-start.15 = (bf16[256,1024]{1,0:T(8,128)(2,1)}, bf16[256,1024]{1,0:T(8,128)(2,1)S(1)}, u32[]{:S(2)}, u32[]{:S(2)}) collective-permute-start(bf16[256,1024]{1,0:T(8,128)(2,1)} %get-tuple-element.131), channel_id=1, source_target_pairs={{0,2},{1,3},{2,0},{3,1},{4,6},{5,7},{6,4},{7,5},{8,10},{9,11},{10,... | collective-permute-start | bytes 1572872 | tf_op jit(solution)/shard_map/ppermute | solution.py:270
  63.5 0.8 collective-permute-start.13
  64.3 1.3 collective-permute-start.14
  65.7 9.5 %mixed.1 = (bf16[256,2048]{1,0:T(8,128)(2,1)}, bf16[64,2048]{1,0:T(8,128)(2,1)}, bf16[64,2048]{1,0:T(8,128)(2,1)}, bf16[128,2048]{1,0:T(8,128)(2,1)}, bf16[256,1024]{1,0:T(8,128)(2,1)}) custom-call(s32[1]{0:T(128)} %bitcast.1.far_ref.word_ref, bf16[4,160,512]{2,1,0:T(8,128)(2,1)} %get-tuple-element.122.act_ref.refs_6_, ...), custom_call_target="tpu_custom_call" | custom-call | flops 6000000 | bytes 10000 | tf_op jit(solution)/shard_map/mixed/pallas_call | solution.py:414
  75.3 0.8 copy-done.26
  76.0 0.7 collective-permute-start.16
  76.8 1.3 collective-permute-start.17
  78.1 2.0 %collective-permute-start.21 = (bf16[256,1024]{1,0:T(8,128)(2,1)}, bf16[256,1024]{1,0:T(8,128)(2,1)}, u32[]{:S(2)}, u32[]{:S(2)}) collective-permute-start(bf16[256,1024]{1,0:T(8,128)(2,1)} %get-tuple-element.157), channel_id=1, source_target_pairs={{0,2},{1,3},{2,0},{3,1},{4,6},{5,7},{6,4},{7,5},{8,10},{9,11},{10,... | collective-permute-start | bytes 1572872 | tf_op jit(solution)/shard_map/ppermute | solution.py:270
  80.1 11.3 %hidden_grads.1 = (bf16[4,160,384]{2,1,0:T(8,128)(2,1)}, bf16[4,160,384]{2,1,0:T(8,128)(2,1)}, bf16[512,128]{1,0:T(8,128)(2,1)}, bf16[512,1024]{1,0:T(8,128)(2,1)}, bf16[256,1024]{1,0:T(8,128)(2,1)}) custom-call(s32[1]{0:T(128)} %bitcast.1.far_ref.word_ref, bf16[64,2048]{1,0:T(8,128)(2,1)} %refs_0_.1, bf16[64,2048]{1,0:T(8,128)(2,1)} %copy-done.11, ...), custom_call_target="tpu_custom_call" | custom-call | flops 6000000 | bytes 12000 | tf_op jit(solution)/shard_map/hidden_grads/pallas_call | solution.py:451
  91.5 2.9 %collective-permute-done.18.refs_7_ = bf16[4,160,512]{2,1,0:T(8,128)(2,1)S(1)} collective-permute-done((bf16[4,160,512]{2,1,0:T(8,128)(2,1)S(1)}, bf16[4,160,512]{2,1,0:T(8,128)(2,1)S(1)}, u32[]{:S(2)}, u32[]{:S(2)}) %collective-permute-start.18) | collective-permute-done | bytes 655392 | tf_op jit(solution)/shard_map/ppermute | solution.py:270
  94.4 0.9 copy-done.14
  95.3 1.3 collective-permute-start.20
  96.8 11.0 %input_grads.1 = (bf16[256,2176]{1,0:T(8,128)(2,1)}, bf16[64,2176]{1,0:T(8,128)(2,1)}, bf16[64,2176]{1,0:T(8,128)(2,1)}, bf16[128,2176]{1,0:T(8,128)(2,1)}) custom-call(bf16[4,160,384]{2,1,0:T(8,128)(2,1)} %get-tuple-element.182.d_gate_ref, bf16[4,160,384]{2,1,0:T(8,128)(2,1)} %get-tuple-element.183.d_up_ref, ...), custom_call_target="tpu_custom_call" | custom-call | flops 6000000 | bytes 16000 | tf_op jit(solution)/shard_map/input_grads/pallas_call | solution.py:476
  107.8 1.3 collective-permute-done.20
  109.1 1.6 collective-permute-start.22
  110.6 0.5 collective-permute-start.24
  111.1 1.8 %add_convert_fusion.5 = bf16[64,2048]{1,0:T(8,128)(2,1)} fusion(bf16[64,2048]{1,0:T(8,128)(2,1)} %collective-permute-done.19, bf16[64,2048]{1,0:T(8,128)(2,1)} %collective-permute-done.17, bf16[256,2048]{1,0:T(8,128)(2,1)S(1)} %copy-done.13), kind=kLoop, calls=%fused_computation.14 | loop fusion | flops 786432 | bytes 1048576 | tf_op jit(solution)/shard_map/convert_element_type | solution.py:439
  112.9 0.9 collective-permute-start.26
  113.8 1.1 fusion.10
  115.0 0.8 collective-permute-done.22
  115.8 0.8 add_convert_fusion.4
  116.6 1.0 collective-permute-start.25
  117.7 1.2 convert_add_fusion.1
  118.8 0.7 slice.132
  119.6 1.0 collective-permute-start.27
  120.6 9.8 %down_grads.1 = (bf16[4,320,1024]{2,1,0:T(8,128)(2,1)}, bf16[4,512,384]{2,1,0:T(8,128)(2,1)}, bf16[4,512,384]{2,1,0:T(8,128)(2,1)}) custom-call(s32[1]{0:T(128)} %bitcast.2.near_ref, bf16[640,512]{1,0:T(8,128)(2,1)} %get-tuple-element.140.refs_8_.pick_ref, bf16[512,1024]{1,0:T(8,128)(2,1)} %get-tuple-element.169.refs_0_, bf16[256,1024]{1,0:T(8,128)(2,1)} %copy-done.15, ...), custom_call_target="tpu_custom_call" | custom-call | flops 6000000 | bytes 12000 | tf_op jit(solution)/shard_map/down_grads/pallas_call | solution.py:502
  130.4 1.6 collective-permute-start.28
  132.0 0.3 collective-permute-start.31
  132.3 1.1 add_convert_fusion.3
  133.4 3.0 %collective-permute-start.29 = (bf16[64,2176]{1,0:T(8,128)(2,1)S(1)}, bf16[64,2176]{1,0:T(8,128)(2,1)S(1)}, u32[]{:S(2)}, u32[]{:S(2)}) collective-permute-start(bf16[64,2176]{1,0:T(8,128)(2,1)S(1)} %add_convert_fusion.3), channel_id=1, source_target_pairs={{0,16},{4,20},{8,24},{12,28},{16,0},{20,4},{24,8},{28,12},{1,17},{... | collective-permute-start | bytes 835592 | tf_op jit(solution)/shard_map/ppermute | solution.py:274
  136.4 3.8 %collective-permute-done.28 = bf16[128,2176]{1,0:T(8,128)(2,1)S(1)} collective-permute-done((bf16[128,2176]{1,0:T(8,128)(2,1)}, bf16[128,2176]{1,0:T(8,128)(2,1)S(1)}, u32[]{:S(2)}, u32[]{:S(2)}) %collective-permute-start.28) | collective-permute-done | bytes 557088 | tf_op jit(solution)/shard_map/ppermute | solution.py:274
  140.3 1.1 collective-permute-start.32
  141.4 1.8 %fusion.1 = bf16[64,2048]{1,0:T(8,128)(2,1)} fusion(f32[128,2048]{1,0:T(8,128)S(1)} %convert_add_fusion.1, bf16[64,2048]{1,0:T(8,128)(2,1)} %collective-permute-done.27, bf16[64,2048]{1,0:T(8,128)(2,1)} %collective-permute-done.26), kind=kLoop, calls=%fused_computation.13 | loop fusion | flops 655360 | bytes 1310720 | tf_op jit(solution)/shard_map/convert_element_type | solution.py:523
  143.3 0.8 copy-done.18
  144.1 7.7 %gate_up_grads.1 = (bf16[4,512,768]{2,1,0:T(8,128)(2,1)}, bf16[4,512,768]{2,1,0:T(8,128)(2,1)}) custom-call(s32[1]{0:T(128)} %bitcast.2.near_ref, bf16[4,320,1024]{2,1,0:T(8,128)(2,1)} %get-tuple-element.186.rows_ref, bf16[4,160,384]{2,1,0:T(8,128)(2,1)} %get-tuple-element.182.d_gate_ref, bf16[4,160,384]{2,1,0:T(8,128)(2,1)} %collective-permute-done.30.gate_far_ref, ...), custom_call_target="tpu_custom_call" | custom-call | flops 3000000 | bytes 10000 | tf_op jit(solution)/shard_map/gate_up_grads/pallas_call | solution.py:527
  151.8 0.5 collective-permute-start.34
  152.3 1.0 convert_add_fusion.2
  153.4 0.7 slice.131
  154.4 0.7 copy.20
  155.1 5.0 %collective-permute-done.33 = bf16[4,512,768]{2,1,0:T(8,128)(2,1)} collective-permute-done((bf16[4,512,768]{2,1,0:T(8,128)(2,1)}, bf16[4,512,768]{2,1,0:T(8,128)(2,1)}, u32[]{:S(2)}, u32[]{:S(2)}) %collective-permute-start.33) | collective-permute-done | bytes 3145760 | tf_op jit(solution)/shard_map/ppermute | solution.py:270
  160.1 5.4 %add_convert_fusion.1 = (bf16[4,512,384]{2,1,0:T(8,128)(2,1)}, bf16[4,512,384]{2,1,0:T(8,128)(2,1)}) fusion(bf16[4,512,768]{2,1,0:T(8,128)(2,1)} %collective-permute-done.33, bf16[4,512,768]{2,1,0:T(8,128)(2,1)} %get-tuple-element.193), kind=kLoop, calls=%fused_computation.1 | loop fusion | flops 6291456 | bytes 9437184 | tf_op jit(solution)/shard_map/convert_element_type | solution.py:541
  165.5 1.6 add_convert_fusion
  (92 shorter events, 1.3 us)
Async XLA Ops:
  0.6 42.3 %copy-start.9 = (bf16[64,2048]{1,0:T(8,128)(2,1)S(1)}, bf16[64,2048]{1,0:T(8,128)(2,1)}, u32[]{:S(2)}) copy-start(bf16[64,2048]{1,0:T(8,128)(2,1)} %refs_0_.1) | copy-start | bytes 786436
  4.1 35.3 %copy-start.1 = (bf16[64,2176]{1,0:T(8,128)(2,1)}, bf16[64,2176]{1,0:T(8,128)(2,1)S(1)}, u32[]{:S(2)}) copy-start(bf16[64,2176]{1,0:T(8,128)(2,1)S(1)} %pad_maximum_fusion.refs_0_) | copy-start | bytes 835588
  4.1 15.6 %collective-permute-start = (bf16[64,2176]{1,0:T(8,128)(2,1)S(1)}, bf16[64,2176]{1,0:T(8,128)(2,1)S(1)}, u32[]{:S(2)}, u32[]{:S(2)}) collective-permute-start(bf16[64,2176]{1,0:T(8,128)(2,1)S(1)} %pad_maximum_fusion.refs_0_), channel_id=1, source_target_pairs={{0,8},{4,12},{8,0},{12,4},{16,24},{20,28},{24,16},{28,20},{1,9},{5... | collective-permute-start | bytes 835592 | tf_op jit(solution)/shard_map/ppermute | solution.py:274
  7.2 15.0 %collective-permute-start.1 = (bf16[64,2176]{1,0:T(8,128)(2,1)S(1)}, bf16[64,2176]{1,0:T(8,128)(2,1)S(1)}, u32[]{:S(2)}, u32[]{:S(2)}) collective-permute-start(bf16[64,2176]{1,0:T(8,128)(2,1)S(1)} %pad_maximum_fusion.refs_0_), channel_id=1, source_target_pairs={{0,16},{4,20},{8,24},{12,28},{16,0},{20,4},{24,8},{28,12},{1,17},{... | collective-permute-start | bytes 835592 | tf_op jit(solution)/shard_map/ppermute | solution.py:274
  9.8 12.4 %collective-permute-start.2 = (bf16[64,2176]{1,0:T(8,128)(2,1)S(1)}, bf16[64,2176]{1,0:T(8,128)(2,1)S(1)}, u32[]{:S(2)}, u32[]{:S(2)}) collective-permute-start(bf16[64,2176]{1,0:T(8,128)(2,1)S(1)} %pad_maximum_fusion.refs_0_), channel_id=1, source_target_pairs={{0,4},{4,0},{8,12},{12,8},{16,20},{20,16},{24,28},{28,24},{1,5},{5... | collective-permute-start | bytes 835592 | tf_op jit(solution)/shard_map/ppermute | solution.py:274
  19.7 19.7 %copy-start.6 = (bf16[64,2176]{1,0:T(8,128)(2,1)}, bf16[64,2176]{1,0:T(8,128)(2,1)S(1)}, u32[]{:S(2)}) copy-start(bf16[64,2176]{1,0:T(8,128)(2,1)S(1)} %collective-permute-done.refs_1_) | copy-start | bytes 835588
  22.3 17.2 %copy-start.7 = (bf16[64,2176]{1,0:T(8,128)(2,1)}, bf16[64,2176]{1,0:T(8,128)(2,1)S(1)}, u32[]{:S(2)}) copy-start(bf16[64,2176]{1,0:T(8,128)(2,1)S(1)} %collective-permute-done.1.refs_2_) | copy-start | bytes 835588
  22.3 26.3 %copy-start.19 = (bf16[64,2176]{1,0:T(8,128)(2,1)}, bf16[64,2176]{1,0:T(8,128)(2,1)S(1)}, u32[]{:S(2)}) copy-start(bf16[64,2176]{1,0:T(8,128)(2,1)S(1)} %collective-permute-done.2.refs_4_) | copy-start | bytes 835588
  22.3 15.5 %collective-permute-start.3 = (bf16[64,2176]{1,0:T(8,128)(2,1)S(1)}, bf16[64,2176]{1,0:T(8,128)(2,1)S(1)}, u32[]{:S(2)}, u32[]{:S(2)}) collective-permute-start(bf16[64,2176]{1,0:T(8,128)(2,1)S(1)} %collective-permute-done.1.refs_2_), channel_id=1, source_target_pairs={{0,8},{4,12},{8,0},{12,4},{16,24},{20,28},{24,16},{28,20},{1,9},{5... | collective-permute-start | bytes 835592 | tf_op jit(solution)/shard_map/ppermute | solution.py:274
  22.8 15.0 %collective-permute-start.5 = (bf16[64,2176]{1,0:T(8,128)(2,1)S(1)}, bf16[64,2176]{1,0:T(8,128)(2,1)S(1)}, u32[]{:S(2)}, u32[]{:S(2)}) collective-permute-start(bf16[64,2176]{1,0:T(8,128)(2,1)S(1)} %collective-permute-done.refs_1_), channel_id=1, source_target_pairs={{0,4},{4,0},{8,12},{12,8},{16,20},{20,16},{24,28},{28,24},{1,5},{5... | collective-permute-start | bytes 835592 | tf_op jit(solution)/shard_map/ppermute | solution.py:274
  24.3 13.6 %collective-permute-start.6 = (bf16[64,2176]{1,0:T(8,128)(2,1)S(1)}, bf16[64,2176]{1,0:T(8,128)(2,1)S(1)}, u32[]{:S(2)}, u32[]{:S(2)}) collective-permute-start(bf16[64,2176]{1,0:T(8,128)(2,1)S(1)} %collective-permute-done.1.refs_2_), channel_id=1, source_target_pairs={{0,4},{4,0},{8,12},{12,8},{16,20},{20,16},{24,28},{28,24},{1,5},{5... | collective-permute-start | bytes 835592 | tf_op jit(solution)/shard_map/ppermute | solution.py:274
  24.8 13.0 %collective-permute-start.4 = (bf16[64,2048]{1,0:T(8,128)(2,1)}, bf16[64,2048]{1,0:T(8,128)(2,1)S(1)}, u32[]{:S(2)}, u32[]{:S(2)}) collective-permute-start(bf16[64,2048]{1,0:T(8,128)(2,1)} %refs_0_.1), channel_id=1, source_target_pairs={{0,16},{4,20},{8,24},{12,28},{16,0},{20,4},{24,8},{28,12},{1,17},{... | collective-permute-start | bytes 786440 | tf_op jit(solution)/shard_map/ppermute | solution.py:274
  37.8 23.6 %copy-start.10 = (bf16[64,2048]{1,0:T(8,128)(2,1)}, bf16[64,2048]{1,0:T(8,128)(2,1)S(1)}, u32[]{:S(2)}) copy-start(bf16[64,2048]{1,0:T(8,128)(2,1)S(1)} %collective-permute-done.4.refs_2_) | copy-start | bytes 786436
  37.8 1.6 copy-start.8
  37.8 10.7 %copy-start.20 = (bf16[64,2176]{1,0:T(8,128)(2,1)}, bf16[64,2176]{1,0:T(8,128)(2,1)S(1)}, u32[]{:S(2)}) copy-start(bf16[64,2176]{1,0:T(8,128)(2,1)S(1)} %collective-permute-done.5.refs_5_) | copy-start | bytes 835588
  37.8 10.7 %copy-start.21 = (bf16[64,2176]{1,0:T(8,128)(2,1)}, bf16[64,2176]{1,0:T(8,128)(2,1)S(1)}, u32[]{:S(2)}) copy-start(bf16[64,2176]{1,0:T(8,128)(2,1)S(1)} %collective-permute-done.6.refs_6_) | copy-start | bytes 835588
  37.8 8.6 %collective-permute-start.7 = (bf16[64,2176]{1,0:T(8,128)(2,1)S(1)}, bf16[64,2176]{1,0:T(8,128)(2,1)S(1)}, u32[]{:S(2)}, u32[]{:S(2)}) collective-permute-start(bf16[64,2176]{1,0:T(8,128)(2,1)S(1)} %collective-permute-done.3.refs_3_), channel_id=1, source_target_pairs={{0,4},{4,0},{8,12},{12,8},{16,20},{20,16},{24,28},{28,24},{1,5},{5... | collective-permute-start | bytes 835592 | tf_op jit(solution)/shard_map/ppermute | solution.py:274
  41.3 22.2 %collective-permute-start.12 = (bf16[256,1024]{1,0:T(8,128)(2,1)}, bf16[256,1024]{1,0:T(8,128)(2,1)S(1)}, u32[]{:S(2)}, u32[]{:S(2)}) collective-permute-start(bf16[256,1024]{1,0:T(8,128)(2,1)} %cut_x.1), channel_id=1, source_target_pairs={{0,2},{1,3},{2,0},{3,1},{4,6},{5,7},{6,4},{7,5},{8,10},{9,11},{10,... | collective-permute-start | bytes 1572872 | tf_op jit(solution)/shard_map/ppermute | solution.py:270
  42.9 18.5 %collective-permute-start.8 = (bf16[64,2048]{1,0:T(8,128)(2,1)S(1)}, bf16[64,2048]{1,0:T(8,128)(2,1)S(1)}, u32[]{:S(2)}, u32[]{:S(2)}) collective-permute-start(bf16[64,2048]{1,0:T(8,128)(2,1)S(1)} %copy-done.9), channel_id=1, source_target_pairs={{0,8},{4,12},{8,0},{12,4},{16,24},{20,28},{24,16},{28,20},{1,9},{5... | collective-permute-start | bytes 786440 | tf_op jit(solution)/shard_map/ppermute | solution.py:274
  42.9 20.6 %collective-permute-start.10 = (bf16[64,2048]{1,0:T(8,128)(2,1)S(1)}, bf16[64,2048]{1,0:T(8,128)(2,1)S(1)}, u32[]{:S(2)}, u32[]{:S(2)}) collective-permute-start(bf16[64,2048]{1,0:T(8,128)(2,1)S(1)} %copy-done.9), channel_id=1, source_target_pairs={{0,4},{4,0},{8,12},{12,8},{16,20},{20,16},{24,28},{28,24},{1,5},{5... | collective-permute-start | bytes 786440 | tf_op jit(solution)/shard_map/ppermute | solution.py:274
  43.6 19.9 %collective-permute-start.9 = (bf16[64,2048]{1,0:T(8,128)(2,1)S(1)}, bf16[64,2048]{1,0:T(8,128)(2,1)S(1)}, u32[]{:S(2)}, u32[]{:S(2)}) collective-permute-start(bf16[64,2048]{1,0:T(8,128)(2,1)S(1)} %collective-permute-done.4.refs_2_), channel_id=1, source_target_pairs={{0,8},{4,12},{8,0},{12,4},{16,24},{20,28},{24,16},{28,20},{1,9},{5... | collective-permute-start | bytes 786440 | tf_op jit(solution)/shard_map/ppermute | solution.py:274
  46.4 2.1 %copy-start.22 = (bf16[64,2176]{1,0:T(8,128)(2,1)}, bf16[64,2176]{1,0:T(8,128)(2,1)S(1)}, u32[]{:S(2)}) copy-start(bf16[64,2176]{1,0:T(8,128)(2,1)S(1)} %collective-permute-done.7.refs_7_) | copy-start | bytes 835588
  46.4 17.1 %collective-permute-start.11 = (bf16[64,2048]{1,0:T(8,128)(2,1)S(1)}, bf16[64,2048]{1,0:T(8,128)(2,1)S(1)}, u32[]{:S(2)}, u32[]{:S(2)}) collective-permute-start(bf16[64,2048]{1,0:T(8,128)(2,1)S(1)} %collective-permute-done.4.refs_2_), channel_id=1, source_target_pairs={{0,4},{4,0},{8,12},{12,8},{16,20},{20,16},{24,28},{28,24},{1,5},{5... | collective-permute-start | bytes 786440 | tf_op jit(solution)/shard_map/ppermute | solution.py:274
  61.4 4.2 %copy-start.11 = (bf16[64,2048]{1,0:T(8,128)(2,1)}, bf16[64,2048]{1,0:T(8,128)(2,1)S(1)}, u32[]{:S(2)}) copy-start(bf16[64,2048]{1,0:T(8,128)(2,1)S(1)} %collective-permute-done.8.refs_1_) | copy-start | bytes 786436
  61.4 13.8 %collective-permute-start.15 = (bf16[256,1024]{1,0:T(8,128)(2,1)}, bf16[256,1024]{1,0:T(8,128)(2,1)S(1)}, u32[]{:S(2)}, u32[]{:S(2)}) collective-permute-start(bf16[256,1024]{1,0:T(8,128)(2,1)} %get-tuple-element.131), channel_id=1, source_target_pairs={{0,2},{1,3},{2,0},{3,1},{4,6},{5,7},{6,4},{7,5},{8,10},{9,11},{10,... | collective-permute-start | bytes 1572872 | tf_op jit(solution)/shard_map/ppermute | solution.py:270
  63.5 2.2 %copy-start.12 = (bf16[64,2048]{1,0:T(8,128)(2,1)}, bf16[64,2048]{1,0:T(8,128)(2,1)S(1)}, u32[]{:S(2)}) copy-start(bf16[64,2048]{1,0:T(8,128)(2,1)S(1)} %collective-permute-done.9.refs_3_) | copy-start | bytes 786436
  63.5 11.7 %copy-start.23 = (bf16[64,2048]{1,0:T(8,128)(2,1)}, bf16[64,2048]{1,0:T(8,128)(2,1)S(1)}, u32[]{:S(2)}) copy-start(bf16[64,2048]{1,0:T(8,128)(2,1)S(1)} %collective-permute-done.10.refs_4_) | copy-start | bytes 786436
  63.5 2.1 %copy-start.24 = (bf16[64,2048]{1,0:T(8,128)(2,1)}, bf16[64,2048]{1,0:T(8,128)(2,1)S(1)}, u32[]{:S(2)}) copy-start(bf16[64,2048]{1,0:T(8,128)(2,1)S(1)} %collective-permute-done.11.refs_6_) | copy-start | bytes 786436
  63.5 11.7 %copy-start.15 = (bf16[256,1024]{1,0:T(8,128)(2,1)}, bf16[256,1024]{1,0:T(8,128)(2,1)S(1)}, u32[]{:S(2)}) copy-start(bf16[256,1024]{1,0:T(8,128)(2,1)S(1)} %collective-permute-done.12.refs_1_) | copy-start | bytes 1572868
  63.5 11.7 %collective-permute-start.13 = (bf16[64,2048]{1,0:T(8,128)(2,1)S(1)}, bf16[64,2048]{1,0:T(8,128)(2,1)S(1)}, u32[]{:S(2)}, u32[]{:S(2)}) collective-permute-start(bf16[64,2048]{1,0:T(8,128)(2,1)S(1)} %collective-permute-done.8.refs_1_), channel_id=1, source_target_pairs={{0,4},{4,0},{8,12},{12,8},{16,20},{20,16},{24,28},{28,24},{1,5},{5... | collective-permute-start | bytes 786440 | tf_op jit(solution)/shard_map/ppermute | solution.py:274
  64.3 10.9 %collective-permute-start.14 = (bf16[64,2048]{1,0:T(8,128)(2,1)S(1)}, bf16[64,2048]{1,0:T(8,128)(2,1)S(1)}, u32[]{:S(2)}, u32[]{:S(2)}) collective-permute-start(bf16[64,2048]{1,0:T(8,128)(2,1)S(1)} %collective-permute-done.9.refs_3_), channel_id=1, source_target_pairs={{0,4},{4,0},{8,12},{12,8},{16,20},{20,16},{24,28},{28,24},{1,5},{5... | collective-permute-start | bytes 786440 | tf_op jit(solution)/shard_map/ppermute | solution.py:274
  65.6 11.1 %copy-start = (bf16[4,160,512]{2,1,0:T(8,128)(2,1)S(1)}, bf16[4,160,512]{2,1,0:T(8,128)(2,1)}, u32[]{:S(2)}) copy-start(bf16[4,160,512]{2,1,0:T(8,128)(2,1)} %get-tuple-element.122.act_ref.refs_6_) | copy-start | bytes 1966084
  75.2 4.9 %copy-start.25 = (bf16[64,2048]{1,0:T(8,128)(2,1)}, bf16[64,2048]{1,0:T(8,128)(2,1)S(1)}, u32[]{:S(2)}) copy-start(bf16[64,2048]{1,0:T(8,128)(2,1)S(1)} %collective-permute-done.13.refs_5_) | copy-start | bytes 786436
  75.2 0.8 copy-start.26
  75.3 16.2 %copy-start.16 = (bf16[256,1024]{1,0:T(8,128)(2,1)}, bf16[256,1024]{1,0:T(8,128)(2,1)S(1)}, u32[]{:S(2)}) copy-start(bf16[256,1024]{1,0:T(8,128)(2,1)S(1)} %collective-permute-done.15.refs_2_) | copy-start | bytes 1572868
  76.0 15.4 %collective-permute-start.16 = (bf16[64,2048]{1,0:T(8,128)(2,1)}, bf16[64,2048]{1,0:T(8,128)(2,1)S(1)}, u32[]{:S(2)}, u32[]{:S(2)}) collective-permute-start(bf16[64,2048]{1,0:T(8,128)(2,1)} %get-tuple-element.133), channel_id=1, source_target_pairs={{0,4},{4,0},{8,12},{12,8},{16,20},{20,16},{24,28},{28,24},{1,5},{5... | collective-permute-start | bytes 786440 | tf_op jit(solution)/shard_map/ppermute | solution.py:274
  76.7 17.7 %collective-permute-start.18 = (bf16[4,160,512]{2,1,0:T(8,128)(2,1)S(1)}, bf16[4,160,512]{2,1,0:T(8,128)(2,1)S(1)}, u32[]{:S(2)}, u32[]{:S(2)}) collective-permute-start(bf16[4,160,512]{2,1,0:T(8,128)(2,1)S(1)} %copy-done), channel_id=1, source_target_pairs={{0,2},{1,3},{2,0},{3,1},{4,6},{5,7},{6,4},{7,5},{8,10},{9,11},{10,... | collective-permute-start | bytes 1966088 | tf_op jit(solution)/shard_map/ppermute | solution.py:270
  76.8 14.8 %collective-permute-start.17 = (bf16[64,2048]{1,0:T(8,128)(2,1)}, bf16[64,2048]{1,0:T(8,128)(2,1)}, u32[]{:S(2)}, u32[]{:S(2)}) collective-permute-start(bf16[64,2048]{1,0:T(8,128)(2,1)} %get-tuple-element.134), channel_id=1, source_target_pairs={{0,4},{4,0},{8,12},{12,8},{16,20},{20,16},{24,28},{28,24},{1,5},{5... | collective-permute-start | bytes 786440 | tf_op jit(solution)/shard_map/ppermute | solution.py:274
  78.1 29.6 %collective-permute-start.21 = (bf16[256,1024]{1,0:T(8,128)(2,1)}, bf16[256,1024]{1,0:T(8,128)(2,1)}, u32[]{:S(2)}, u32[]{:S(2)}) collective-permute-start(bf16[256,1024]{1,0:T(8,128)(2,1)} %get-tuple-element.157), channel_id=1, source_target_pairs={{0,2},{1,3},{2,0},{3,1},{4,6},{5,7},{6,4},{7,5},{8,10},{9,11},{10,... | collective-permute-start | bytes 1572872 | tf_op jit(solution)/shard_map/ppermute | solution.py:270
  80.1 11.3 %copy-start.13 = (bf16[256,2048]{1,0:T(8,128)(2,1)S(1)}, bf16[256,2048]{1,0:T(8,128)(2,1)}, u32[]{:S(2)}) copy-start(bf16[256,2048]{1,0:T(8,128)(2,1)} %get-tuple-element.132) | copy-start | bytes 3145732
  94.4 0.9 copy-start.14
  95.3 13.8 %collective-permute-start.20 = (bf16[128,2048]{1,0:T(8,128)(2,1)}, bf16[128,2048]{1,0:T(8,128)(2,1)S(1)}, u32[]{:S(2)}, u32[]{:S(2)}) collective-permute-start(bf16[128,2048]{1,0:T(8,128)(2,1)} %get-tuple-element.156), channel_id=1, source_target_pairs={{0,4},{4,0},{8,12},{12,8},{16,20},{20,16},{24,28},{28,24},{1,5},{5... | collective-permute-start | bytes 1572872 | tf_op jit(solution)/shard_map/ppermute | solution.py:274
  96.6 11.1 %collective-permute-start.19 = (bf16[64,2048]{1,0:T(8,128)(2,1)S(1)}, bf16[64,2048]{1,0:T(8,128)(2,1)}, u32[]{:S(2)}, u32[]{:S(2)}) collective-permute-start(bf16[64,2048]{1,0:T(8,128)(2,1)S(1)} %add_convert_fusion.6), channel_id=1, source_target_pairs={{0,8},{4,12},{8,0},{12,4},{16,24},{20,28},{24,16},{28,20},{1,9},{5... | collective-permute-start | bytes 786440 | tf_op jit(solution)/shard_map/ppermute | solution.py:274
  96.7 20.0 %collective-permute-start.23 = (bf16[256,1024]{1,0:T(8,128)(2,1)}, bf16[256,1024]{1,0:T(8,128)(2,1)}, u32[]{:S(2)}, u32[]{:S(2)}) collective-permute-start(bf16[256,1024]{1,0:T(8,128)(2,1)} %get-tuple-element.162), channel_id=1, source_target_pairs={{0,2},{1,3},{2,0},{3,1},{4,6},{5,7},{6,4},{7,5},{8,10},{9,11},{10,... | collective-permute-start | bytes 1572872 | tf_op jit(solution)/shard_map/ppermute | solution.py:270
  107.7 7.2 %copy-start.2 = (bf16[4,160,384]{2,1,0:T(8,128)(2,1)S(1)}, bf16[4,160,384]{2,1,0:T(8,128)(2,1)}, u32[]{:S(2)}) copy-start(bf16[4,160,384]{2,1,0:T(8,128)(2,1)} %get-tuple-element.182.d_gate_ref) | copy-start | bytes 1474564
  107.7 8.1 %copy-start.5 = (bf16[256,2176]{1,0:T(8,128)(2,1)S(1)}, bf16[256,2176]{1,0:T(8,128)(2,1)}, u32[]{:S(2)}) copy-start(bf16[256,2176]{1,0:T(8,128)(2,1)} %get-tuple-element.158) | copy-start | bytes 3342340
  109.1 8.6 %copy-start.17 = (bf16[128,2048]{1,0:T(8,128)(2,1)}, bf16[128,2048]{1,0:T(8,128)(2,1)S(1)}, u32[]{:S(2)}) copy-start(bf16[128,2048]{1,0:T(8,128)(2,1)S(1)} %collective-permute-done.20) | copy-start | bytes 1572868
  109.1 6.8 %collective-permute-start.22 = (bf16[64,2176]{1,0:T(8,128)(2,1)}, bf16[64,2176]{1,0:T(8,128)(2,1)S(1)}, u32[]{:S(2)}, u32[]{:S(2)}) collective-permute-start(bf16[64,2176]{1,0:T(8,128)(2,1)} %get-tuple-element.159), channel_id=1, source_target_pairs={{0,4},{4,0},{8,12},{12,8},{16,20},{20,16},{24,28},{28,24},{1,5},{5... | collective-permute-start | bytes 835592 | tf_op jit(solution)/shard_map/ppermute | solution.py:274
  110.6 19.7 %collective-permute-start.24 = (bf16[64,2176]{1,0:T(8,128)(2,1)}, bf16[64,2176]{1,0:T(8,128)(2,1)S(1)}, u32[]{:S(2)}, u32[]{:S(2)}) collective-permute-start(bf16[64,2176]{1,0:T(8,128)(2,1)} %get-tuple-element.160), channel_id=1, source_target_pairs={{0,4},{4,0},{8,12},{12,8},{16,20},{20,16},{24,28},{28,24},{1,5},{5... | collective-permute-start | bytes 835592 | tf_op jit(solution)/shard_map/ppermute | solution.py:274
  112.9 20.4 %collective-permute-start.26 = (bf16[64,2048]{1,0:T(8,128)(2,1)}, bf16[64,2048]{1,0:T(8,128)(2,1)}, u32[]{:S(2)}, u32[]{:S(2)}) collective-permute-start(bf16[64,2048]{1,0:T(8,128)(2,1)} %add_convert_fusion.5), channel_id=1, source_target_pairs={{0,16},{4,20},{8,24},{12,28},{16,0},{20,4},{24,8},{28,12},{1,17},{... | collective-permute-start | bytes 786440 | tf_op jit(solution)/shard_map/ppermute | solution.py:274
  114.9 28.3 %collective-permute-start.30 = (bf16[4,160,384]{2,1,0:T(8,128)(2,1)S(1)}, bf16[4,160,384]{2,1,0:T(8,128)(2,1)}, u32[]{:S(2)}, u32[]{:S(2)}) collective-permute-start(bf16[4,160,384]{2,1,0:T(8,128)(2,1)S(1)} %copy-done.2), channel_id=1, source_target_pairs={{0,2},{1,3},{2,0},{3,1},{4,6},{5,7},{6,4},{7,5},{8,10},{9,11},{10,... | collective-permute-start | bytes 1474568 | tf_op jit(solution)/shard_map/ppermute | solution.py:270
  116.6 15.4 %collective-permute-start.25 = (bf16[64,2176]{1,0:T(8,128)(2,1)}, bf16[64,2176]{1,0:T(8,128)(2,1)}, u32[]{:S(2)}, u32[]{:S(2)}) collective-permute-start(bf16[64,2176]{1,0:T(8,128)(2,1)} %add_convert_fusion.4), channel_id=1, source_target_pairs={{0,8},{4,12},{8,0},{12,4},{16,24},{20,28},{24,16},{28,20},{1,9},{5... | collective-permute-start | bytes 835592 | tf_op jit(solution)/shard_map/ppermute | solution.py:274
  119.6 21.9 %collective-permute-start.27 = (bf16[64,2048]{1,0:T(8,128)(2,1)}, bf16[64,2048]{1,0:T(8,128)(2,1)}, u32[]{:S(2)}, u32[]{:S(2)}) collective-permute-start(bf16[64,2048]{1,0:T(8,128)(2,1)} %slice.132), channel_id=1, source_target_pairs={{0,8},{4,12},{8,0},{12,4},{16,24},{20,28},{24,16},{28,20},{1,9},{5... | collective-permute-start | bytes 786440 | tf_op jit(solution)/shard_map/ppermute | solution.py:274
  120.6 11.5 %copy-start.3 = (bf16[4,160,384]{2,1,0:T(8,128)(2,1)S(1)}, bf16[4,160,384]{2,1,0:T(8,128)(2,1)}, u32[]{:S(2)}) copy-start(bf16[4,160,384]{2,1,0:T(8,128)(2,1)} %get-tuple-element.183.d_up_ref) | copy-start | bytes 1474564
  130.4 9.8 %collective-permute-start.28 = (bf16[128,2176]{1,0:T(8,128)(2,1)}, bf16[128,2176]{1,0:T(8,128)(2,1)S(1)}, u32[]{:S(2)}, u32[]{:S(2)}) collective-permute-start(bf16[128,2176]{1,0:T(8,128)(2,1)} %get-tuple-element.180), channel_id=1, source_target_pairs={{0,4},{4,0},{8,12},{12,8},{16,20},{20,16},{24,28},{28,24},{1,5},{5... | collective-permute-start | bytes 1671176 | tf_op jit(solution)/shard_map/ppermute | solution.py:274
  132.0 11.2 %collective-permute-start.31 = (bf16[4,160,384]{2,1,0:T(8,128)(2,1)S(1)}, bf16[4,160,384]{2,1,0:T(8,128)(2,1)S(1)}, u32[]{:S(2)}, u32[]{:S(2)}) collective-permute-start(bf16[4,160,384]{2,1,0:T(8,128)(2,1)S(1)} %copy-done.3), channel_id=1, source_target_pairs={{0,2},{1,3},{2,0},{3,1},{4,6},{5,7},{6,4},{7,5},{8,10},{9,11},{10,... | collective-permute-start | bytes 1474568 | tf_op jit(solution)/shard_map/ppermute | solution.py:270
  133.4 10.7 %collective-permute-start.29 = (bf16[64,2176]{1,0:T(8,128)(2,1)S(1)}, bf16[64,2176]{1,0:T(8,128)(2,1)S(1)}, u32[]{:S(2)}, u32[]{:S(2)}) collective-permute-start(bf16[64,2176]{1,0:T(8,128)(2,1)S(1)} %add_convert_fusion.3), channel_id=1, source_target_pairs={{0,16},{4,20},{8,24},{12,28},{16,0},{20,4},{24,8},{28,12},{1,17},{... | collective-permute-start | bytes 835592 | tf_op jit(solution)/shard_map/ppermute | solution.py:274
  140.3 11.4 %collective-permute-start.32 = (bf16[64,2176]{1,0:T(8,128)(2,1)S(1)}, bf16[64,2176]{1,0:T(8,128)(2,1)}, u32[]{:S(2)}, u32[]{:S(2)}) collective-permute-start(bf16[64,2176]{1,0:T(8,128)(2,1)S(1)} %slice.130), channel_id=1, source_target_pairs={{0,8},{4,12},{8,0},{12,4},{16,24},{20,28},{24,16},{28,20},{1,9},{5... | collective-permute-start | bytes 835592 | tf_op jit(solution)/shard_map/ppermute | solution.py:274
  143.3 0.8 copy-start.18
  151.8 8.3 %collective-permute-start.33 = (bf16[4,512,768]{2,1,0:T(8,128)(2,1)}, bf16[4,512,768]{2,1,0:T(8,128)(2,1)}, u32[]{:S(2)}, u32[]{:S(2)}) collective-permute-start(bf16[4,512,768]{2,1,0:T(8,128)(2,1)} %get-tuple-element.194), channel_id=1, source_target_pairs={{0,1},{1,0},{2,3},{3,2},{4,5},{5,4},{6,7},{7,6},{8,9},{9,8},{10,11... | collective-permute-start | bytes 9437192 | tf_op jit(solution)/shard_map/ppermute | solution.py:270
  151.8 13.6 %collective-permute-start.34 = (bf16[4,512,384]{2,1,0:T(8,128)(2,1)}, bf16[4,512,384]{2,1,0:T(8,128)(2,1)S(1)}, u32[]{:S(2)}, u32[]{:S(2)}) collective-permute-start(bf16[4,512,384]{2,1,0:T(8,128)(2,1)} %get-tuple-element.195), channel_id=1, source_target_pairs={{0,1},{1,0},{2,3},{3,2},{4,5},{5,4},{6,7},{7,6},{8,9},{9,8},{10,11... | collective-permute-start | bytes 4718600 | tf_op jit(solution)/shard_map/ppermute | solution.py:270
  160.1 5.4 %copy-start.4 = (bf16[4,512,384]{2,1,0:T(8,128)(2,1)S(1)}, bf16[4,512,384]{2,1,0:T(8,128)(2,1)}, u32[]{:S(2)}) copy-start(bf16[4,512,384]{2,1,0:T(8,128)(2,1)} %get-tuple-element.198) | copy-start | bytes 4718596

commit v5 on v4

--- a/solution.py
+++ b/solution.py
@@ -520,9 +520,7 @@
     input_ends = pair_sums(input_keep, input_got[2], [2, 0])
     input_landed.append(send(input_ends[:tok_rows].astype(BF16), 2))
     down_got = swap(down_give, 1, n_dp)
-    mixed = finish(mixed_ends, mixed_landed).astype(BF16)
-    mixed, input_ends, input_landed[0], gate_far, up_far = fence(
-        mixed, input_ends, input_landed[0], gate_far, up_far)
+    input_ends, input_landed[0], gate_far, up_far = fence(input_ends, input_landed[0], gate_far, up_far)
     both_specs = [by_expert(columns, 2 * hidden)] * 2
     both_keep, both_give = pl.pallas_call(
         functools.partial(both_kernel, cap),
@@ -535,7 +533,8 @@
         cost_estimate=cost(3, 10),
         name="gate_up_grads",
     )(near_word, x_rows, d_gate, gate_far, d_up, up_far)
-    both_give, input_landed = fence(both_give, input_landed)
+    both_give, input_landed, mixed_landed = fence(both_give, input_landed, mixed_landed)
+    mixed = finish(mixed_ends, mixed_landed).astype(BF16)
     both_got = swap(both_give, 1, n_dp)
     gate_grad = back_rows(both_keep[:, :, :hidden], both_got[:, :, :hidden]).astype(BF16)
     up_grad = back_rows(both_keep[:, :, hidden:], both_got[:, :, hidden:]).astype(BF16)

time: 168 us -> 170 us (1.012)
    ppermute x9, starting transfers between devices: 6.72 us -> 9.27 us  [swap(): return lax.ppermute(value, 'dp', [(i, i ^ bit) for i in range(count)])]
    unnamed x56 -> x68, local copies, waits for them, and re-layouts: 3.99 us -> 3.78 us
  transfers between devices with their start and end apart: 35 -> 35, of which waited for: 9 -> 10; matrix products, arithmetic and copies ran while one was open for 10% -> 11% of each run, Pallas kernels for 38% -> 38%
where the time goes in v5:
time: 170 us
  Pallas kernels  64.2 us (38%)
  starting transfers between devices  42.5 us (25%)
  waiting for transfers between devices  36 us (21%)
  other arithmetic  18.7 us (11%)
  local copies, waits for them, and re-layouts  7.22 us (4%)
    ppermute x26, starting transfers between devices, exchange(): return lax.ppermute(value, 'expert', [(i, i ^ bit) for i in range(count)])  33.2 us
    ppermute x26, waiting for transfers between devices, exchange(): return lax.ppermute(value, 'expert', [(i, i ^ bit) for i in range(count)])  29.6 us
    pallas_call x1, Pallas kernels, shards(): pl.pallas_call(functools.partial(hidden_kernel, cfg), grid=(local,), in_s...  12.9 us
    pallas_call x1, Pallas kernels, shards(): pl.pallas_call(functools.partial(grad_kernel, cfg), grid=(local,), in_spe...  11.3 us
    pallas_call x1, Pallas kernels, shards(): pl.pallas_call(functools.partial(input_kernel, (plan, local, cap, cap_pad...  11 us
    pallas_call x1, Pallas kernels, shards(): pl.pallas_call(functools.partial(down_kernel, cap), grid=(local,), in_spe...  9.83 us
    pallas_call x1, Pallas kernels, shards(): pl.pallas_call(functools.partial(mixed_kernel, (plan, levels, local, cap,...  9.52 us
    ppermute x9, starting transfers between devices, swap(): return lax.ppermute(value, 'dp', [(i, i ^ bit) for i in range(count)])  9.27 us
  transfers between devices with their start and end apart: 35, of which 10 were waited for; matrix products, arithmetic and copies ran while one was open for 11% of the time, Pallas kernels for 38%

profile of v5, /device:TPU:0, one launch (start us, length us, event | category | flops | bytes accessed | tf_op | source)
XLA Modules:
  0.0 169.8 jit_solution(16204455897250387671)
XLA Ops:
  0.6 0.8 copy.16
  1.5 0.7 reduce_sum.18
  2.2 0.7 convert_element_type.113
  3.1 1.0 pad_maximum_fusion.refs_0_
  4.1 3.1 %collective-permute-start = (bf16[64,2176]{1,0:T(8,128)(2,1)S(1)}, bf16[64,2176]{1,0:T(8,128)(2,1)S(1)}, u32[]{:S(2)}, u32[]{:S(2)}) collective-permute-start(bf16[64,2176]{1,0:T(8,128)(2,1)S(1)} %pad_maximum_fusion.refs_0_), channel_id=1, source_target_pairs={{0,8},{4,12},{8,0},{12,4},{16,24},{20,28},{24,16},{28,20},{1,9},{5... | collective-permute-start | bytes 835592 | tf_op jit(solution)/shard_map/ppermute | solution.py:274
  7.2 2.6 %collective-permute-start.1 = (bf16[64,2176]{1,0:T(8,128)(2,1)S(1)}, bf16[64,2176]{1,0:T(8,128)(2,1)S(1)}, u32[]{:S(2)}, u32[]{:S(2)}) collective-permute-start(bf16[64,2176]{1,0:T(8,128)(2,1)S(1)} %pad_maximum_fusion.refs_0_), channel_id=1, source_target_pairs={{0,16},{4,20},{8,24},{12,28},{16,0},{20,4},{24,8},{28,12},{1,17},{... | collective-permute-start | bytes 835592 | tf_op jit(solution)/shard_map/ppermute | solution.py:274
  9.8 1.5 collective-permute-start.2
  11.3 8.4 %collective-permute-done.refs_1_ = bf16[64,2176]{1,0:T(8,128)(2,1)S(1)} collective-permute-done((bf16[64,2176]{1,0:T(8,128)(2,1)S(1)}, bf16[64,2176]{1,0:T(8,128)(2,1)S(1)}, u32[]{:S(2)}, u32[]{:S(2)}) %collective-permute-start) | collective-permute-done | bytes 278560 | tf_op jit(solution)/shard_map/ppermute | solution.py:274
  19.7 2.5 %collective-permute-done.1.refs_2_ = bf16[64,2176]{1,0:T(8,128)(2,1)S(1)} collective-permute-done((bf16[64,2176]{1,0:T(8,128)(2,1)S(1)}, bf16[64,2176]{1,0:T(8,128)(2,1)S(1)}, u32[]{:S(2)}, u32[]{:S(2)}) %collective-permute-start.1) | collective-permute-done | bytes 278560 | tf_op jit(solution)/shard_map/ppermute | solution.py:274
  22.3 0.5 collective-permute-start.3
  22.8 1.5 collective-permute-start.5
  24.3 0.5 collective-permute-start.6
  24.8 2.7 %collective-permute-start.4 = (bf16[64,2048]{1,0:T(8,128)(2,1)}, bf16[64,2048]{1,0:T(8,128)(2,1)S(1)}, u32[]{:S(2)}, u32[]{:S(2)}) collective-permute-start(bf16[64,2048]{1,0:T(8,128)(2,1)} %refs_0_.1), channel_id=1, source_target_pairs={{0,16},{4,20},{8,24},{12,28},{16,0},{20,4},{24,8},{28,12},{1,17},{... | collective-permute-start | bytes 786440 | tf_op jit(solution)/shard_map/ppermute | solution.py:274
  27.5 10.3 %collective-permute-done.4.refs_2_ = bf16[64,2048]{1,0:T(8,128)(2,1)S(1)} collective-permute-done((bf16[64,2048]{1,0:T(8,128)(2,1)}, bf16[64,2048]{1,0:T(8,128)(2,1)S(1)}, u32[]{:S(2)}, u32[]{:S(2)}) %collective-permute-start.4) | collective-permute-done | bytes 262176 | tf_op jit(solution)/shard_map/ppermute | solution.py:274
  37.8 1.6 collective-permute-start.7
  39.4 1.9 %cut_x.1 = bf16[256,1024]{1,0:T(8,128)(2,1)} custom-call(s32[1]{0:T(128)} %bitcast.1.far_ref.word_ref, bf16[64,2176]{1,0:T(8,128)(2,1)} %copy-done.1, bf16[64,2176]{1,0:T(8,128)(2,1)} %copy-done.5, bf16[64,2176]{1,0:T(8,128)(2,1)} %copy-done.6, bf16[64,2176]{1,0:T(8,128)(2,1)} %copy-done.7), custom_call_target="tpu_custom_call" | custom-call | bytes 2000 | tf_op jit(solution)/shard_map/cut_x/pallas_call | solution.py:350
  41.3 1.6 collective-permute-start.12
  42.9 0.6 collective-permute-start.10
  43.6 2.0 %collective-permute-start.9 = (bf16[64,2048]{1,0:T(8,128)(2,1)S(1)}, bf16[64,2048]{1,0:T(8,128)(2,1)S(1)}, u32[]{:S(2)}, u32[]{:S(2)}) collective-permute-start(bf16[64,2048]{1,0:T(8,128)(2,1)S(1)} %collective-permute-done.4.refs_2_), channel_id=1, source_target_pairs={{0,8},{4,12},{8,0},{12,4},{16,24},{20,28},{24,16},{28,20},{1,9},{5... | collective-permute-start | bytes 786440 | tf_op jit(solution)/shard_map/ppermute | solution.py:274
  45.6 0.9 collective-permute-done.7.refs_7_
  46.4 2.1 %collective-permute-start.11 = (bf16[64,2048]{1,0:T(8,128)(2,1)S(1)}, bf16[64,2048]{1,0:T(8,128)(2,1)S(1)}, u32[]{:S(2)}, u32[]{:S(2)}) collective-permute-start(bf16[64,2048]{1,0:T(8,128)(2,1)S(1)} %collective-permute-done.4.refs_2_), channel_id=1, source_target_pairs={{0,4},{4,0},{8,12},{12,8},{16,20},{20,16},{24,28},{28,24},{1,5},{5... | collective-permute-start | bytes 786440 | tf_op jit(solution)/shard_map/ppermute | solution.py:274
  48.6 12.9 %hidden.1 = (f32[4,160,768]{2,1,0:T(8,128)}, bf16[4,160,512]{2,1,0:T(8,128)(2,1)}, f32[4,160,128]{2,1,0:T(8,128)}, bf16[640,512]{1,0:T(8,128)(2,1)}, bf16[512,10...) custom-call(s32[1]{0:T(128)} %bitcast.first_ref, s32[1]{0:T(128)} %bitcast.1.far_ref.word_ref, ...), custom_call_target="tpu_custom_call" | custom-call | flops 6000000 | bytes 20000 | tf_op jit(solution)/shard_map/hidden/pallas_call | solution.py:389
  61.5 2.0 %collective-permute-start.15 = (bf16[256,1024]{1,0:T(8,128)(2,1)}, bf16[256,1024]{1,0:T(8,128)(2,1)S(1)}, u32[]{:S(2)}, u32[]{:S(2)}) collective-permute-start(bf16[256,1024]{1,0:T(8,128)(2,1)} %get-tuple-element.132), channel_id=1, source_target_pairs={{0,2},{1,3},{2,0},{3,1},{4,6},{5,7},{6,4},{7,5},{8,10},{9,11},{10,... | collective-permute-start | bytes 1572872 | tf_op jit(solution)/shard_map/ppermute | solution.py:270
  63.6 0.7 collective-permute-start.13
  64.3 1.4 collective-permute-start.14
  65.7 9.5 %mixed.1 = (bf16[256,2048]{1,0:T(8,128)(2,1)}, bf16[64,2048]{1,0:T(8,128)(2,1)}, bf16[64,2048]{1,0:T(8,128)(2,1)}, bf16[128,2048]{1,0:T(8,128)(2,1)}, bf16[256,1024]{1,0:T(8,128)(2,1)}) custom-call(s32[1]{0:T(128)} %bitcast.1.far_ref.word_ref, bf16[4,160,512]{2,1,0:T(8,128)(2,1)} %get-tuple-element.123.act_ref.refs_6_, ...), custom_call_target="tpu_custom_call" | custom-call | flops 6000000 | bytes 10000 | tf_op jit(solution)/shard_map/mixed/pallas_call | solution.py:414
  75.2 0.7 copy-done.30
  76.0 0.7 collective-permute-start.16
  76.7 1.4 collective-permute-start.17
  78.0 2.0 %collective-permute-start.21 = (bf16[256,1024]{1,0:T(8,128)(2,1)}, bf16[256,1024]{1,0:T(8,128)(2,1)}, u32[]{:S(2)}, u32[]{:S(2)}) collective-permute-start(bf16[256,1024]{1,0:T(8,128)(2,1)} %get-tuple-element.158), channel_id=1, source_target_pairs={{0,2},{1,3},{2,0},{3,1},{4,6},{5,7},{6,4},{7,5},{8,10},{9,11},{10,... | collective-permute-start | bytes 1572872 | tf_op jit(solution)/shard_map/ppermute | solution.py:270
  80.0 11.3 %hidden_grads.1 = (bf16[4,160,384]{2,1,0:T(8,128)(2,1)}, bf16[4,160,384]{2,1,0:T(8,128)(2,1)}, bf16[512,128]{1,0:T(8,128)(2,1)}, bf16[512,1024]{1,0:T(8,128)(2,1)}, bf16[256,1024]{1,0:T(8,128)(2,1)}) custom-call(s32[1]{0:T(128)} %bitcast.1.far_ref.word_ref, bf16[64,2048]{1,0:T(8,128)(2,1)} %refs_0_.1, bf16[64,2048]{1,0:T(8,128)(2,1)} %copy-done.10, ...), custom_call_target="tpu_custom_call" | custom-call | flops 6000000 | bytes 12000 | tf_op jit(solution)/shard_map/hidden_grads/pallas_call | solution.py:451
  91.5 2.8 %collective-permute-done.18.refs_7_ = bf16[4,160,512]{2,1,0:T(8,128)(2,1)S(1)} collective-permute-done((bf16[4,160,512]{2,1,0:T(8,128)(2,1)S(1)}, bf16[4,160,512]{2,1,0:T(8,128)(2,1)S(1)}, u32[]{:S(2)}, u32[]{:S(2)}) %collective-permute-start.18) | collective-permute-done | bytes 655392 | tf_op jit(solution)/shard_map/ppermute | solution.py:270
  94.3 1.4 collective-permute-start.20
  95.7 0.8 fusion.11
  96.5 11.0 %input_grads.1 = (bf16[256,2176]{1,0:T(8,128)(2,1)}, bf16[64,2176]{1,0:T(8,128)(2,1)}, bf16[64,2176]{1,0:T(8,128)(2,1)}, bf16[128,2176]{1,0:T(8,128)(2,1)}) custom-call(bf16[4,160,384]{2,1,0:T(8,128)(2,1)} %get-tuple-element.181.d_gate_ref, bf16[4,160,384]{2,1,0:T(8,128)(2,1)} %get-tuple-element.184.d_up_ref, ...), custom_call_target="tpu_custom_call" | custom-call | flops 6000000 | bytes 16000 | tf_op jit(solution)/shard_map/input_grads/pallas_call | solution.py:476
  107.5 1.4 collective-permute-start.22
  108.9 0.7 collective-permute-start.24
  109.6 1.1 fusion.10
  110.7 3.6 %collective-permute-done.22 = bf16[64,2176]{1,0:T(8,128)(2,1)S(1)} collective-permute-done((bf16[64,2176]{1,0:T(8,128)(2,1)}, bf16[64,2176]{1,0:T(8,128)(2,1)S(1)}, u32[]{:S(2)}, u32[]{:S(2)}) %collective-permute-start.22) | collective-permute-done | bytes 278560 | tf_op jit(solution)/shard_map/ppermute | solution.py:274
  114.3 1.8 %add_convert_fusion.4 = bf16[64,2176]{1,0:T(8,128)(2,1)} fusion(bf16[64,2176]{1,0:T(8,128)(2,1)S(1)} %collective-permute-done.22, bf16[256,2176]{1,0:T(8,128)(2,1)} %get-tuple-element.159), kind=kLoop, calls=%fused_computation.8 | loop fusion | flops 557056 | bytes 835584 | tf_op jit(solution)/shard_map/convert_element_type | solution.py:495
  116.1 3.4 %collective-permute-start.25 = (bf16[64,2176]{1,0:T(8,128)(2,1)}, bf16[64,2176]{1,0:T(8,128)(2,1)}, u32[]{:S(2)}, u32[]{:S(2)}) collective-permute-start(bf16[64,2176]{1,0:T(8,128)(2,1)} %add_convert_fusion.4), channel_id=1, source_target_pairs={{0,8},{4,12},{8,0},{12,4},{16,24},{20,28},{24,16},{28,20},{1,9},{5... | collective-permute-start | bytes 835592 | tf_op jit(solution)/shard_map/ppermute | solution.py:274
  119.5 1.8 %add_convert_fusion.5 = bf16[64,2048]{1,0:T(8,128)(2,1)} fusion(bf16[64,2048]{1,0:T(8,128)(2,1)} %collective-permute-done.19, bf16[64,2048]{1,0:T(8,128)(2,1)S(1)} %copy-done.32, bf16[256,2048]{1,0:T(8,128)(2,1)S(1)} %copy-done.12), kind=kLoop, calls=%fused_computation.14 | loop fusion | flops 786432 | bytes 1048576 | tf_op jit(solution)/shard_map/convert_element_type | solution.py:439
  121.3 2.9 %collective-permute-start.29 = (bf16[4,160,384]{2,1,0:T(8,128)(2,1)S(1)}, bf16[4,160,384]{2,1,0:T(8,128)(2,1)}, u32[]{:S(2)}, u32[]{:S(2)}) collective-permute-start(bf16[4,160,384]{2,1,0:T(8,128)(2,1)S(1)} %copy-done.2), channel_id=1, source_target_pairs={{0,2},{1,3},{2,0},{3,1},{4,6},{5,7},{6,4},{7,5},{8,10},{9,11},{10,... | collective-permute-start | bytes 1474568 | tf_op jit(solution)/shard_map/ppermute | solution.py:270
  124.4 9.8 %down_grads.1 = (bf16[4,320,1024]{2,1,0:T(8,128)(2,1)}, bf16[4,512,384]{2,1,0:T(8,128)(2,1)}, bf16[4,512,384]{2,1,0:T(8,128)(2,1)}) custom-call(s32[1]{0:T(128)} %bitcast.2.near_ref, bf16[640,512]{1,0:T(8,128)(2,1)} %get-tuple-element.141.refs_8_.pick_ref, bf16[512,1024]{1,0:T(8,128)(2,1)} %get-tuple-element.170.refs_0_, bf16[256,1024]{1,0:T(8,128)(2,1)} %copy-done.15, ...), custom_call_target="tpu_custom_call" | custom-call | flops 6000000 | bytes 12000 | tf_op jit(solution)/shard_map/down_grads/pallas_call | solution.py:502
  134.4 1.1 add_convert_fusion.3
  135.5 1.6 collective-permute-done.26
  137.1 1.4 collective-permute-start.28
  138.5 1.2 convert_add_fusion
  139.6 0.7 slice.130
  140.4 0.2 collective-permute-start.31
  140.8 1.9 %collective-permute-start.32 = (bf16[64,2048]{1,0:T(8,128)(2,1)S(1)}, bf16[64,2048]{1,0:T(8,128)(2,1)S(1)}, u32[]{:S(2)}, u32[]{:S(2)}) collective-permute-start(bf16[64,2048]{1,0:T(8,128)(2,1)S(1)} %slice.132), channel_id=1, source_target_pairs={{0,8},{4,12},{8,0},{12,4},{16,24},{20,28},{24,16},{28,20},{1,9},{5... | collective-permute-start | bytes 786440 | tf_op jit(solution)/shard_map/ppermute | solution.py:274
  142.6 0.5 collective-permute-done.30.up_far_ref
  143.1 0.8 copy-done.20
  143.9 2.2 %collective-permute-done.28 = bf16[64,2176]{1,0:T(8,128)(2,1)S(1)} collective-permute-done((bf16[64,2176]{1,0:T(8,128)(2,1)S(1)}, bf16[64,2176]{1,0:T(8,128)(2,1)S(1)}, u32[]{:S(2)}, u32[]{:S(2)}) %collective-permute-start.28) | collective-permute-done | bytes 278560 | tf_op jit(solution)/shard_map/ppermute | solution.py:274
  146.1 7.8 %gate_up_grads.1 = (bf16[4,512,768]{2,1,0:T(8,128)(2,1)}, bf16[4,512,768]{2,1,0:T(8,128)(2,1)}) custom-call(s32[1]{0:T(128)} %bitcast.2.near_ref, bf16[4,320,1024]{2,1,0:T(8,128)(2,1)} %get-tuple-element.180.rows_ref, bf16[4,160,384]{2,1,0:T(8,128)(2,1)} %get-tuple-element.181.d_gate_ref, bf16[4,160,384]{2,1,0:T(8,128)(2,1)} %collective-permute-done.29.gate_far_ref, ...), custom_call_target="tpu_custom_call" | custom-call | flops 3000000 | bytes 10000 | tf_op jit(solution)/shard_map/gate_up_grads/pallas_call | solution.py:525
  153.9 0.7 copy-done.29
  154.6 0.5 collective-permute-start.34
  155.1 1.1 convert_add_fusion.2
  156.2 0.7 slice.131
  157.3 0.7 copy.20
  157.9 1.8 %fusion.1 = bf16[64,2048]{1,0:T(8,128)(2,1)} fusion(f32[128,2048]{1,0:T(8,128)S(1)} %convert_add_fusion.1, bf16[64,2048]{1,0:T(8,128)(2,1)} %copy-done.29, bf16[64,2048]{1,0:T(8,128)(2,1)} %collective-permute-done.26), kind=kLoop, calls=%fused_computation.13 | loop fusion | flops 655360 | bytes 1310720 | tf_op jit(solution)/shard_map/convert_element_type | solution.py:537
  159.7 3.1 %collective-permute-done.33 = bf16[4,512,768]{2,1,0:T(8,128)(2,1)} collective-permute-done((bf16[4,512,768]{2,1,0:T(8,128)(2,1)}, bf16[4,512,768]{2,1,0:T(8,128)(2,1)}, u32[]{:S(2)}, u32[]{:S(2)}) %collective-permute-start.33) | collective-permute-done | bytes 3145760 | tf_op jit(solution)/shard_map/ppermute | solution.py:270
  162.8 5.4 %add_convert_fusion.1 = (bf16[4,512,384]{2,1,0:T(8,128)(2,1)}, bf16[4,512,384]{2,1,0:T(8,128)(2,1)}) fusion(bf16[4,512,768]{2,1,0:T(8,128)(2,1)} %collective-permute-done.33, bf16[4,512,768]{2,1,0:T(8,128)(2,1)} %get-tuple-element.195), kind=kLoop, calls=%fused_computation.1 | loop fusion | flops 6291456 | bytes 9437184 | tf_op jit(solution)/shard_map/convert_element_type | solution.py:540
  168.2 1.6 add_convert_fusion
  (104 shorter events, 1.4 us)
Async XLA Ops:
  0.6 42.3 %copy-start.8 = (bf16[64,2048]{1,0:T(8,128)(2,1)S(1)}, bf16[64,2048]{1,0:T(8,128)(2,1)}, u32[]{:S(2)}) copy-start(bf16[64,2048]{1,0:T(8,128)(2,1)} %refs_0_.1) | copy-start | bytes 786436
  4.1 35.3 %copy-start.1 = (bf16[64,2176]{1,0:T(8,128)(2,1)}, bf16[64,2176]{1,0:T(8,128)(2,1)S(1)}, u32[]{:S(2)}) copy-start(bf16[64,2176]{1,0:T(8,128)(2,1)S(1)} %pad_maximum_fusion.refs_0_) | copy-start | bytes 835588
  4.1 15.6 %collective-permute-start = (bf16[64,2176]{1,0:T(8,128)(2,1)S(1)}, bf16[64,2176]{1,0:T(8,128)(2,1)S(1)}, u32[]{:S(2)}, u32[]{:S(2)}) collective-permute-start(bf16[64,2176]{1,0:T(8,128)(2,1)S(1)} %pad_maximum_fusion.refs_0_), channel_id=1, source_target_pairs={{0,8},{4,12},{8,0},{12,4},{16,24},{20,28},{24,16},{28,20},{1,9},{5... | collective-permute-start | bytes 835592 | tf_op jit(solution)/shard_map/ppermute | solution.py:274
  7.2 15.0 %collective-permute-start.1 = (bf16[64,2176]{1,0:T(8,128)(2,1)S(1)}, bf16[64,2176]{1,0:T(8,128)(2,1)S(1)}, u32[]{:S(2)}, u32[]{:S(2)}) collective-permute-start(bf16[64,2176]{1,0:T(8,128)(2,1)S(1)} %pad_maximum_fusion.refs_0_), channel_id=1, source_target_pairs={{0,16},{4,20},{8,24},{12,28},{16,0},{20,4},{24,8},{28,12},{1,17},{... | collective-permute-start | bytes 835592 | tf_op jit(solution)/shard_map/ppermute | solution.py:274
  9.8 12.4 %collective-permute-start.2 = (bf16[64,2176]{1,0:T(8,128)(2,1)S(1)}, bf16[64,2176]{1,0:T(8,128)(2,1)S(1)}, u32[]{:S(2)}, u32[]{:S(2)}) collective-permute-start(bf16[64,2176]{1,0:T(8,128)(2,1)S(1)} %pad_maximum_fusion.refs_0_), channel_id=1, source_target_pairs={{0,4},{4,0},{8,12},{12,8},{16,20},{20,16},{24,28},{28,24},{1,5},{5... | collective-permute-start | bytes 835592 | tf_op jit(solution)/shard_map/ppermute | solution.py:274
  19.7 19.7 %copy-start.5 = (bf16[64,2176]{1,0:T(8,128)(2,1)}, bf16[64,2176]{1,0:T(8,128)(2,1)S(1)}, u32[]{:S(2)}) copy-start(bf16[64,2176]{1,0:T(8,128)(2,1)S(1)} %collective-permute-done.refs_1_) | copy-start | bytes 835588
  22.3 17.2 %copy-start.6 = (bf16[64,2176]{1,0:T(8,128)(2,1)}, bf16[64,2176]{1,0:T(8,128)(2,1)S(1)}, u32[]{:S(2)}) copy-start(bf16[64,2176]{1,0:T(8,128)(2,1)S(1)} %collective-permute-done.1.refs_2_) | copy-start | bytes 835588
  22.3 26.3 %copy-start.22 = (bf16[64,2176]{1,0:T(8,128)(2,1)}, bf16[64,2176]{1,0:T(8,128)(2,1)S(1)}, u32[]{:S(2)}) copy-start(bf16[64,2176]{1,0:T(8,128)(2,1)S(1)} %collective-permute-done.2.refs_4_) | copy-start | bytes 835588
  22.3 15.5 %collective-permute-start.3 = (bf16[64,2176]{1,0:T(8,128)(2,1)S(1)}, bf16[64,2176]{1,0:T(8,128)(2,1)S(1)}, u32[]{:S(2)}, u32[]{:S(2)}) collective-permute-start(bf16[64,2176]{1,0:T(8,128)(2,1)S(1)} %collective-permute-done.1.refs_2_), channel_id=1, source_target_pairs={{0,8},{4,12},{8,0},{12,4},{16,24},{20,28},{24,16},{28,20},{1,9},{5... | collective-permute-start | bytes 835592 | tf_op jit(solution)/shard_map/ppermute | solution.py:274
  22.8 15.0 %collective-permute-start.5 = (bf16[64,2176]{1,0:T(8,128)(2,1)S(1)}, bf16[64,2176]{1,0:T(8,128)(2,1)S(1)}, u32[]{:S(2)}, u32[]{:S(2)}) collective-permute-start(bf16[64,2176]{1,0:T(8,128)(2,1)S(1)} %collective-permute-done.refs_1_), channel_id=1, source_target_pairs={{0,4},{4,0},{8,12},{12,8},{16,20},{20,16},{24,28},{28,24},{1,5},{5... | collective-permute-start | bytes 835592 | tf_op jit(solution)/shard_map/ppermute | solution.py:274
  24.3 13.6 %collective-permute-start.6 = (bf16[64,2176]{1,0:T(8,128)(2,1)S(1)}, bf16[64,2176]{1,0:T(8,128)(2,1)S(1)}, u32[]{:S(2)}, u32[]{:S(2)}) collective-permute-start(bf16[64,2176]{1,0:T(8,128)(2,1)S(1)} %collective-permute-done.1.refs_2_), channel_id=1, source_target_pairs={{0,4},{4,0},{8,12},{12,8},{16,20},{20,16},{24,28},{28,24},{1,5},{5... | collective-permute-start | bytes 835592 | tf_op jit(solution)/shard_map/ppermute | solution.py:274
  24.8 13.0 %collective-permute-start.4 = (bf16[64,2048]{1,0:T(8,128)(2,1)}, bf16[64,2048]{1,0:T(8,128)(2,1)S(1)}, u32[]{:S(2)}, u32[]{:S(2)}) collective-permute-start(bf16[64,2048]{1,0:T(8,128)(2,1)} %refs_0_.1), channel_id=1, source_target_pairs={{0,16},{4,20},{8,24},{12,28},{16,0},{20,4},{24,8},{28,12},{1,17},{... | collective-permute-start | bytes 786440 | tf_op jit(solution)/shard_map/ppermute | solution.py:274
  37.8 23.6 %copy-start.9 = (bf16[64,2048]{1,0:T(8,128)(2,1)}, bf16[64,2048]{1,0:T(8,128)(2,1)S(1)}, u32[]{:S(2)}) copy-start(bf16[64,2048]{1,0:T(8,128)(2,1)S(1)} %collective-permute-done.4.refs_2_) | copy-start | bytes 786436
  37.8 10.7 %copy-start.23 = (bf16[64,2176]{1,0:T(8,128)(2,1)}, bf16[64,2176]{1,0:T(8,128)(2,1)S(1)}, u32[]{:S(2)}) copy-start(bf16[64,2176]{1,0:T(8,128)(2,1)S(1)} %collective-permute-done.5.refs_5_) | copy-start | bytes 835588
  37.8 10.7 %copy-start.24 = (bf16[64,2176]{1,0:T(8,128)(2,1)}, bf16[64,2176]{1,0:T(8,128)(2,1)S(1)}, u32[]{:S(2)}) copy-start(bf16[64,2176]{1,0:T(8,128)(2,1)S(1)} %collective-permute-done.6.refs_6_) | copy-start | bytes 835588
  37.8 8.6 %collective-permute-start.7 = (bf16[64,2176]{1,0:T(8,128)(2,1)S(1)}, bf16[64,2176]{1,0:T(8,128)(2,1)S(1)}, u32[]{:S(2)}, u32[]{:S(2)}) collective-permute-start(bf16[64,2176]{1,0:T(8,128)(2,1)S(1)} %collective-permute-done.3.refs_3_), channel_id=1, source_target_pairs={{0,4},{4,0},{8,12},{12,8},{16,20},{20,16},{24,28},{28,24},{1,5},{5... | collective-permute-start | bytes 835592 | tf_op jit(solution)/shard_map/ppermute | solution.py:274
  41.3 22.2 %collective-permute-start.12 = (bf16[256,1024]{1,0:T(8,128)(2,1)}, bf16[256,1024]{1,0:T(8,128)(2,1)S(1)}, u32[]{:S(2)}, u32[]{:S(2)}) collective-permute-start(bf16[256,1024]{1,0:T(8,128)(2,1)} %cut_x.1), channel_id=1, source_target_pairs={{0,2},{1,3},{2,0},{3,1},{4,6},{5,7},{6,4},{7,5},{8,10},{9,11},{10,... | collective-permute-start | bytes 1572872 | tf_op jit(solution)/shard_map/ppermute | solution.py:270
  42.9 18.5 %collective-permute-start.8 = (bf16[64,2048]{1,0:T(8,128)(2,1)S(1)}, bf16[64,2048]{1,0:T(8,128)(2,1)S(1)}, u32[]{:S(2)}, u32[]{:S(2)}) collective-permute-start(bf16[64,2048]{1,0:T(8,128)(2,1)S(1)} %copy-done.8), channel_id=1, source_target_pairs={{0,8},{4,12},{8,0},{12,4},{16,24},{20,28},{24,16},{28,20},{1,9},{5... | collective-permute-start | bytes 786440 | tf_op jit(solution)/shard_map/ppermute | solution.py:274
  42.9 20.6 %collective-permute-start.10 = (bf16[64,2048]{1,0:T(8,128)(2,1)S(1)}, bf16[64,2048]{1,0:T(8,128)(2,1)S(1)}, u32[]{:S(2)}, u32[]{:S(2)}) collective-permute-start(bf16[64,2048]{1,0:T(8,128)(2,1)S(1)} %copy-done.8), channel_id=1, source_target_pairs={{0,4},{4,0},{8,12},{12,8},{16,20},{20,16},{24,28},{28,24},{1,5},{5... | collective-permute-start | bytes 786440 | tf_op jit(solution)/shard_map/ppermute | solution.py:274
  43.6 19.9 %collective-permute-start.9 = (bf16[64,2048]{1,0:T(8,128)(2,1)S(1)}, bf16[64,2048]{1,0:T(8,128)(2,1)S(1)}, u32[]{:S(2)}, u32[]{:S(2)}) collective-permute-start(bf16[64,2048]{1,0:T(8,128)(2,1)S(1)} %collective-permute-done.4.refs_2_), channel_id=1, source_target_pairs={{0,8},{4,12},{8,0},{12,4},{16,24},{20,28},{24,16},{28,20},{1,9},{5... | collective-permute-start | bytes 786440 | tf_op jit(solution)/shard_map/ppermute | solution.py:274
  46.4 2.1 %copy-start.25 = (bf16[64,2176]{1,0:T(8,128)(2,1)}, bf16[64,2176]{1,0:T(8,128)(2,1)S(1)}, u32[]{:S(2)}) copy-start(bf16[64,2176]{1,0:T(8,128)(2,1)S(1)} %collective-permute-done.7.refs_7_) | copy-start | bytes 835588
  46.4 17.1 %collective-permute-start.11 = (bf16[64,2048]{1,0:T(8,128)(2,1)S(1)}, bf16[64,2048]{1,0:T(8,128)(2,1)S(1)}, u32[]{:S(2)}, u32[]{:S(2)}) collective-permute-start(bf16[64,2048]{1,0:T(8,128)(2,1)S(1)} %collective-permute-done.4.refs_2_), channel_id=1, source_target_pairs={{0,4},{4,0},{8,12},{12,8},{16,20},{20,16},{24,28},{28,24},{1,5},{5... | collective-permute-start | bytes 786440 | tf_op jit(solution)/shard_map/ppermute | solution.py:274
  61.4 4.2 %copy-start.10 = (bf16[64,2048]{1,0:T(8,128)(2,1)}, bf16[64,2048]{1,0:T(8,128)(2,1)S(1)}, u32[]{:S(2)}) copy-start(bf16[64,2048]{1,0:T(8,128)(2,1)S(1)} %collective-permute-done.8.refs_1_) | copy-start | bytes 786436
  61.5 13.8 %collective-permute-start.15 = (bf16[256,1024]{1,0:T(8,128)(2,1)}, bf16[256,1024]{1,0:T(8,128)(2,1)S(1)}, u32[]{:S(2)}, u32[]{:S(2)}) collective-permute-start(bf16[256,1024]{1,0:T(8,128)(2,1)} %get-tuple-element.132), channel_id=1, source_target_pairs={{0,2},{1,3},{2,0},{3,1},{4,6},{5,7},{6,4},{7,5},{8,10},{9,11},{10,... | collective-permute-start | bytes 1572872 | tf_op jit(solution)/shard_map/ppermute | solution.py:270
  63.5 2.2 %copy-start.11 = (bf16[64,2048]{1,0:T(8,128)(2,1)}, bf16[64,2048]{1,0:T(8,128)(2,1)S(1)}, u32[]{:S(2)}) copy-start(bf16[64,2048]{1,0:T(8,128)(2,1)S(1)} %collective-permute-done.9.refs_3_) | copy-start | bytes 786436
  63.5 16.5 %copy-start.26 = (bf16[64,2048]{1,0:T(8,128)(2,1)}, bf16[64,2048]{1,0:T(8,128)(2,1)S(1)}, u32[]{:S(2)}) copy-start(bf16[64,2048]{1,0:T(8,128)(2,1)S(1)} %collective-permute-done.10.refs_4_) | copy-start | bytes 786436
  63.5 16.5 %copy-start.27 = (bf16[64,2048]{1,0:T(8,128)(2,1)}, bf16[64,2048]{1,0:T(8,128)(2,1)S(1)}, u32[]{:S(2)}) copy-start(bf16[64,2048]{1,0:T(8,128)(2,1)S(1)} %collective-permute-done.11.refs_6_) | copy-start | bytes 786436
  63.5 2.1 %copy-start.15 = (bf16[256,1024]{1,0:T(8,128)(2,1)}, bf16[256,1024]{1,0:T(8,128)(2,1)S(1)}, u32[]{:S(2)}) copy-start(bf16[256,1024]{1,0:T(8,128)(2,1)S(1)} %collective-permute-done.12.refs_1_) | copy-start | bytes 1572868
  63.6 11.6 %collective-permute-start.13 = (bf16[64,2048]{1,0:T(8,128)(2,1)S(1)}, bf16[64,2048]{1,0:T(8,128)(2,1)S(1)}, u32[]{:S(2)}, u32[]{:S(2)}) collective-permute-start(bf16[64,2048]{1,0:T(8,128)(2,1)S(1)} %collective-permute-done.8.refs_1_), channel_id=1, source_target_pairs={{0,4},{4,0},{8,12},{12,8},{16,20},{20,16},{24,28},{28,24},{1,5},{5... | collective-permute-start | bytes 786440 | tf_op jit(solution)/shard_map/ppermute | solution.py:274
  64.3 10.9 %collective-permute-start.14 = (bf16[64,2048]{1,0:T(8,128)(2,1)S(1)}, bf16[64,2048]{1,0:T(8,128)(2,1)S(1)}, u32[]{:S(2)}, u32[]{:S(2)}) collective-permute-start(bf16[64,2048]{1,0:T(8,128)(2,1)S(1)} %collective-permute-done.9.refs_3_), channel_id=1, source_target_pairs={{0,4},{4,0},{8,12},{12,8},{16,20},{20,16},{24,28},{28,24},{1,5},{5... | collective-permute-start | bytes 786440 | tf_op jit(solution)/shard_map/ppermute | solution.py:274
  65.7 11.0 %copy-start = (bf16[4,160,512]{2,1,0:T(8,128)(2,1)S(1)}, bf16[4,160,512]{2,1,0:T(8,128)(2,1)}, u32[]{:S(2)}) copy-start(bf16[4,160,512]{2,1,0:T(8,128)(2,1)} %get-tuple-element.123.act_ref.refs_6_) | copy-start | bytes 1966084
  75.2 4.8 %copy-start.28 = (bf16[64,2048]{1,0:T(8,128)(2,1)}, bf16[64,2048]{1,0:T(8,128)(2,1)S(1)}, u32[]{:S(2)}) copy-start(bf16[64,2048]{1,0:T(8,128)(2,1)S(1)} %collective-permute-done.13.refs_5_) | copy-start | bytes 786436
  75.2 4.8 %copy-start.16 = (bf16[256,1024]{1,0:T(8,128)(2,1)}, bf16[256,1024]{1,0:T(8,128)(2,1)S(1)}, u32[]{:S(2)}) copy-start(bf16[256,1024]{1,0:T(8,128)(2,1)S(1)} %collective-permute-done.15.refs_2_) | copy-start | bytes 1572868
  76.0 15.4 %collective-permute-start.16 = (bf16[64,2048]{1,0:T(8,128)(2,1)}, bf16[64,2048]{1,0:T(8,128)(2,1)S(1)}, u32[]{:S(2)}, u32[]{:S(2)}) collective-permute-start(bf16[64,2048]{1,0:T(8,128)(2,1)} %get-tuple-element.134), channel_id=1, source_target_pairs={{0,4},{4,0},{8,12},{12,8},{16,20},{20,16},{24,28},{28,24},{1,5},{5... | collective-permute-start | bytes 786440 | tf_op jit(solution)/shard_map/ppermute | solution.py:274
  76.6 17.7 %collective-permute-start.18 = (bf16[4,160,512]{2,1,0:T(8,128)(2,1)S(1)}, bf16[4,160,512]{2,1,0:T(8,128)(2,1)S(1)}, u32[]{:S(2)}, u32[]{:S(2)}) collective-permute-start(bf16[4,160,512]{2,1,0:T(8,128)(2,1)S(1)} %copy-done), channel_id=1, source_target_pairs={{0,2},{1,3},{2,0},{3,1},{4,6},{5,7},{6,4},{7,5},{8,10},{9,11},{10,... | collective-permute-start | bytes 1966088 | tf_op jit(solution)/shard_map/ppermute | solution.py:270
  76.7 14.8 %collective-permute-start.17 = (bf16[64,2048]{1,0:T(8,128)(2,1)}, bf16[64,2048]{1,0:T(8,128)(2,1)S(1)}, u32[]{:S(2)}, u32[]{:S(2)}) collective-permute-start(bf16[64,2048]{1,0:T(8,128)(2,1)} %get-tuple-element.135), channel_id=1, source_target_pairs={{0,4},{4,0},{8,12},{12,8},{16,20},{20,16},{24,28},{28,24},{1,5},{5... | collective-permute-start | bytes 786440 | tf_op jit(solution)/shard_map/ppermute | solution.py:274
  78.0 29.4 %collective-permute-start.21 = (bf16[256,1024]{1,0:T(8,128)(2,1)}, bf16[256,1024]{1,0:T(8,128)(2,1)}, u32[]{:S(2)}, u32[]{:S(2)}) collective-permute-start(bf16[256,1024]{1,0:T(8,128)(2,1)} %get-tuple-element.158), channel_id=1, source_target_pairs={{0,2},{1,3},{2,0},{3,1},{4,6},{5,7},{6,4},{7,5},{8,10},{9,11},{10,... | collective-permute-start | bytes 1572872 | tf_op jit(solution)/shard_map/ppermute | solution.py:270
  80.0 11.4 %copy-start.12 = (bf16[256,2048]{1,0:T(8,128)(2,1)S(1)}, bf16[256,2048]{1,0:T(8,128)(2,1)}, u32[]{:S(2)}) copy-start(bf16[256,2048]{1,0:T(8,128)(2,1)} %get-tuple-element.133) | copy-start | bytes 3145732
  91.5 5.0 %copy-start.31 = (bf16[64,2048]{1,0:T(8,128)(2,1)}, bf16[64,2048]{1,0:T(8,128)(2,1)S(1)}, u32[]{:S(2)}) copy-start(bf16[64,2048]{1,0:T(8,128)(2,1)S(1)} %collective-permute-done.17) | copy-start | bytes 786436
  94.3 13.1 %copy-start.14 = (bf16[4,160,512]{2,1,0:T(8,128)(2,1)}, bf16[4,160,512]{2,1,0:T(8,128)(2,1)S(1)}, u32[]{:S(2)}) copy-start(bf16[4,160,512]{2,1,0:T(8,128)(2,1)S(1)} %collective-permute-done.18.refs_7_) | copy-start | bytes 1966084
  94.3 13.2 %collective-permute-start.20 = (bf16[128,2048]{1,0:T(8,128)(2,1)}, bf16[128,2048]{1,0:T(8,128)(2,1)S(1)}, u32[]{:S(2)}, u32[]{:S(2)}) collective-permute-start(bf16[128,2048]{1,0:T(8,128)(2,1)} %get-tuple-element.157), channel_id=1, source_target_pairs={{0,4},{4,0},{8,12},{12,8},{16,20},{20,16},{24,28},{28,24},{1,5},{5... | collective-permute-start | bytes 1572872 | tf_op jit(solution)/shard_map/ppermute | solution.py:274
  95.7 11.8 %collective-permute-start.19 = (bf16[64,2048]{1,0:T(8,128)(2,1)S(1)}, bf16[64,2048]{1,0:T(8,128)(2,1)}, u32[]{:S(2)}, u32[]{:S(2)}) collective-permute-start(bf16[64,2048]{1,0:T(8,128)(2,1)S(1)} %add_convert_fusion.6), channel_id=1, source_target_pairs={{0,8},{4,12},{8,0},{12,4},{16,24},{20,28},{24,16},{28,20},{1,9},{5... | collective-permute-start | bytes 786440 | tf_op jit(solution)/shard_map/ppermute | solution.py:274
  96.4 19.7 %collective-permute-start.23 = (bf16[256,1024]{1,0:T(8,128)(2,1)}, bf16[256,1024]{1,0:T(8,128)(2,1)S(1)}, u32[]{:S(2)}, u32[]{:S(2)}) collective-permute-start(bf16[256,1024]{1,0:T(8,128)(2,1)} %get-tuple-element.163), channel_id=1, source_target_pairs={{0,2},{1,3},{2,0},{3,1},{4,6},{5,7},{6,4},{7,5},{8,10},{9,11},{10,... | collective-permute-start | bytes 1572872 | tf_op jit(solution)/shard_map/ppermute | solution.py:270
  107.4 12.1 %copy-start.32 = (bf16[64,2048]{1,0:T(8,128)(2,1)S(1)}, bf16[64,2048]{1,0:T(8,128)(2,1)}, u32[]{:S(2)}) copy-start(bf16[64,2048]{1,0:T(8,128)(2,1)} %copy-done.31) | copy-start | bytes 786436
  107.5 13.8 %copy-start.2 = (bf16[4,160,384]{2,1,0:T(8,128)(2,1)S(1)}, bf16[4,160,384]{2,1,0:T(8,128)(2,1)}, u32[]{:S(2)}) copy-start(bf16[4,160,384]{2,1,0:T(8,128)(2,1)} %get-tuple-element.181.d_gate_ref) | copy-start | bytes 1474564
  107.5 26.7 %copy-start.18 = (bf16[128,2048]{1,0:T(8,128)(2,1)}, bf16[128,2048]{1,0:T(8,128)(2,1)S(1)}, u32[]{:S(2)}) copy-start(bf16[128,2048]{1,0:T(8,128)(2,1)S(1)} %collective-permute-done.20) | copy-start | bytes 1572868
  107.5 6.8 %collective-permute-start.22 = (bf16[64,2176]{1,0:T(8,128)(2,1)}, bf16[64,2176]{1,0:T(8,128)(2,1)S(1)}, u32[]{:S(2)}, u32[]{:S(2)}) collective-permute-start(bf16[64,2176]{1,0:T(8,128)(2,1)} %get-tuple-element.160), channel_id=1, source_target_pairs={{0,4},{4,0},{8,12},{12,8},{16,20},{20,16},{24,28},{28,24},{1,5},{5... | collective-permute-start | bytes 835592 | tf_op jit(solution)/shard_map/ppermute | solution.py:274
  108.9 25.3 %collective-permute-start.24 = (bf16[64,2176]{1,0:T(8,128)(2,1)}, bf16[64,2176]{1,0:T(8,128)(2,1)S(1)}, u32[]{:S(2)}, u32[]{:S(2)}) collective-permute-start(bf16[64,2176]{1,0:T(8,128)(2,1)} %get-tuple-element.161), channel_id=1, source_target_pairs={{0,4},{4,0},{8,12},{12,8},{16,20},{20,16},{24,28},{28,24},{1,5},{5... | collective-permute-start | bytes 835592 | tf_op jit(solution)/shard_map/ppermute | solution.py:274
  116.1 8.3 %copy-start.17 = (bf16[256,1024]{1,0:T(8,128)(2,1)}, bf16[256,1024]{1,0:T(8,128)(2,1)S(1)}, u32[]{:S(2)}) copy-start(bf16[256,1024]{1,0:T(8,128)(2,1)S(1)} %collective-permute-done.23.refs_5_) | copy-start | bytes 1572868
  116.1 18.3 %collective-permute-start.25 = (bf16[64,2176]{1,0:T(8,128)(2,1)}, bf16[64,2176]{1,0:T(8,128)(2,1)}, u32[]{:S(2)}, u32[]{:S(2)}) collective-permute-start(bf16[64,2176]{1,0:T(8,128)(2,1)} %add_convert_fusion.4), channel_id=1, source_target_pairs={{0,8},{4,12},{8,0},{12,4},{16,24},{20,28},{24,16},{28,20},{1,9},{5... | collective-permute-start | bytes 835592 | tf_op jit(solution)/shard_map/ppermute | solution.py:274
  121.3 15.8 %collective-permute-start.26 = (bf16[64,2048]{1,0:T(8,128)(2,1)}, bf16[64,2048]{1,0:T(8,128)(2,1)}, u32[]{:S(2)}, u32[]{:S(2)}) collective-permute-start(bf16[64,2048]{1,0:T(8,128)(2,1)} %add_convert_fusion.5), channel_id=1, source_target_pairs={{0,16},{4,20},{8,24},{12,28},{16,0},{20,4},{24,8},{28,12},{1,17},{... | collective-permute-start | bytes 786440 | tf_op jit(solution)/shard_map/ppermute | solution.py:274
  121.3 21.4 %collective-permute-start.29 = (bf16[4,160,384]{2,1,0:T(8,128)(2,1)S(1)}, bf16[4,160,384]{2,1,0:T(8,128)(2,1)}, u32[]{:S(2)}, u32[]{:S(2)}) collective-permute-start(bf16[4,160,384]{2,1,0:T(8,128)(2,1)S(1)} %copy-done.2), channel_id=1, source_target_pairs={{0,2},{1,3},{2,0},{3,1},{4,6},{5,7},{6,4},{7,5},{8,10},{9,11},{10,... | collective-permute-start | bytes 1474568 | tf_op jit(solution)/shard_map/ppermute | solution.py:270
  124.2 14.3 %collective-permute-start.27 = (bf16[128,2176]{1,0:T(8,128)(2,1)}, bf16[128,2176]{1,0:T(8,128)(2,1)}, u32[]{:S(2)}, u32[]{:S(2)}) collective-permute-start(bf16[128,2176]{1,0:T(8,128)(2,1)} %get-tuple-element.182), channel_id=1, source_target_pairs={{0,4},{4,0},{8,12},{12,8},{16,20},{20,16},{24,28},{28,24},{1,5},{5... | collective-permute-start | bytes 1671176 | tf_op jit(solution)/shard_map/ppermute | solution.py:274
  124.4 9.8 %copy-start.3 = (bf16[4,160,384]{2,1,0:T(8,128)(2,1)S(1)}, bf16[4,160,384]{2,1,0:T(8,128)(2,1)}, u32[]{:S(2)}) copy-start(bf16[4,160,384]{2,1,0:T(8,128)(2,1)} %get-tuple-element.184.d_up_ref) | copy-start | bytes 1474564
  134.2 8.9 %collective-permute-start.30 = (bf16[4,160,384]{2,1,0:T(8,128)(2,1)S(1)}, bf16[4,160,384]{2,1,0:T(8,128)(2,1)S(1)}, u32[]{:S(2)}, u32[]{:S(2)}) collective-permute-start(bf16[4,160,384]{2,1,0:T(8,128)(2,1)S(1)} %copy-done.3), channel_id=1, source_target_pairs={{0,2},{1,3},{2,0},{3,1},{4,6},{5,7},{6,4},{7,5},{8,10},{9,11},{10,... | collective-permute-start | bytes 1474568 | tf_op jit(solution)/shard_map/ppermute | solution.py:270
  135.5 5.1 %copy-start.13 = (bf16[64,2048]{1,0:T(8,128)(2,1)S(1)}, bf16[64,2048]{1,0:T(8,128)(2,1)}, u32[]{:S(2)}) copy-start(bf16[64,2048]{1,0:T(8,128)(2,1)} %get-tuple-element.219) | copy-start | bytes 786436
  135.5 5.1 %copy-start.19 = (bf16[128,2048]{1,0:T(8,128)(2,1)S(1)}, bf16[128,2048]{1,0:T(8,128)(2,1)}, u32[]{:S(2)}) copy-start(bf16[128,2048]{1,0:T(8,128)(2,1)} %copy-done.18) | copy-start | bytes 1572868
  137.1 8.9 %collective-permute-start.28 = (bf16[64,2176]{1,0:T(8,128)(2,1)S(1)}, bf16[64,2176]{1,0:T(8,128)(2,1)S(1)}, u32[]{:S(2)}, u32[]{:S(2)}) collective-permute-start(bf16[64,2176]{1,0:T(8,128)(2,1)S(1)} %add_convert_fusion.3), channel_id=1, source_target_pairs={{0,16},{4,20},{8,24},{12,28},{16,0},{20,4},{24,8},{28,12},{1,17},{... | collective-permute-start | bytes 835592 | tf_op jit(solution)/shard_map/ppermute | solution.py:274
  140.4 13.5 %collective-permute-start.31 = (bf16[64,2176]{1,0:T(8,128)(2,1)}, bf16[64,2176]{1,0:T(8,128)(2,1)}, u32[]{:S(2)}, u32[]{:S(2)}) collective-permute-start(bf16[64,2176]{1,0:T(8,128)(2,1)} %slice.130), channel_id=1, source_target_pairs={{0,8},{4,12},{8,0},{12,4},{16,24},{20,28},{24,16},{28,20},{1,9},{5... | collective-permute-start | bytes 835592 | tf_op jit(solution)/shard_map/ppermute | solution.py:274
  140.8 13.1 %collective-permute-start.32 = (bf16[64,2048]{1,0:T(8,128)(2,1)S(1)}, bf16[64,2048]{1,0:T(8,128)(2,1)S(1)}, u32[]{:S(2)}, u32[]{:S(2)}) collective-permute-start(bf16[64,2048]{1,0:T(8,128)(2,1)S(1)} %slice.132), channel_id=1, source_target_pairs={{0,8},{4,12},{8,0},{12,4},{16,24},{20,28},{24,16},{28,20},{1,9},{5... | collective-permute-start | bytes 786440 | tf_op jit(solution)/shard_map/ppermute | solution.py:274
  146.1 7.8 %copy-start.21 = (bf16[64,2176]{1,0:T(8,128)(2,1)}, bf16[64,2176]{1,0:T(8,128)(2,1)S(1)}, u32[]{:S(2)}) copy-start(bf16[64,2176]{1,0:T(8,128)(2,1)S(1)} %collective-permute-done.28) | copy-start | bytes 835588
  154.6 8.3 %collective-permute-start.33 = (bf16[4,512,768]{2,1,0:T(8,128)(2,1)}, bf16[4,512,768]{2,1,0:T(8,128)(2,1)}, u32[]{:S(2)}, u32[]{:S(2)}) collective-permute-start(bf16[4,512,768]{2,1,0:T(8,128)(2,1)} %get-tuple-element.196), channel_id=1, source_target_pairs={{0,1},{1,0},{2,3},{3,2},{4,5},{5,4},{6,7},{7,6},{8,9},{9,8},{10,11... | collective-permute-start | bytes 9437192 | tf_op jit(solution)/shard_map/ppermute | solution.py:270
  154.6 13.6 %collective-permute-start.34 = (bf16[4,512,384]{2,1,0:T(8,128)(2,1)}, bf16[4,512,384]{2,1,0:T(8,128)(2,1)S(1)}, u32[]{:S(2)}, u32[]{:S(2)}) collective-permute-start(bf16[4,512,384]{2,1,0:T(8,128)(2,1)} %get-tuple-element.197), channel_id=1, source_target_pairs={{0,1},{1,0},{2,3},{3,2},{4,5},{5,4},{6,7},{7,6},{8,9},{9,8},{10,11... | collective-permute-start | bytes 4718600 | tf_op jit(solution)/shard_map/ppermute | solution.py:270
  162.8 5.4 %copy-start.4 = (bf16[4,512,384]{2,1,0:T(8,128)(2,1)S(1)}, bf16[4,512,384]{2,1,0:T(8,128)(2,1)}, u32[]{:S(2)}) copy-start(bf16[4,512,384]{2,1,0:T(8,128)(2,1)} %get-tuple-element.200) | copy-start | bytes 4718596
  (4 other events, 3.8 us)

commit v6 on v4

--- a/solution.py
+++ b/solution.py
@@ -466,8 +466,8 @@
         cost_estimate=cost(6, 12),
         name="hidden_grads",
     )(far_word, *[c_line[k] for k in line_blocks], *[c_pair[k] for k in line_blocks], pick, combine, w_down, pre, info)
-    mixed_sides, mixed_got, mixed_out, d_gate, d_up, tail, c_give, act_far = fence(
-        pair_sums(mixed_keep, mixed_got[0], sides).astype(BF16), mixed_got, mixed_out, d_gate, d_up, tail, c_give, act_far)
+    mixed_sides, mixed_got, mixed_out, d_gate, d_up, tail, c_give = fence(
+        pair_sums(mixed_keep, mixed_got[0], sides).astype(BF16), mixed_got, mixed_out, d_gate, d_up, tail, c_give)
 
     mixed_sides = send(mixed_sides, 2)
     mixed_got.append(send(mixed_out[2], 1))
@@ -485,8 +485,8 @@
         cost_estimate=cost(6, 16),
         name="input_grads",
     )(d_gate, d_up, combine, tail, w_gate, w_up)
-    input_keep, input_out, mixed_sides, mixed_got, c_far, d_gate = fence(
-        input_keep, input_out, mixed_sides, mixed_got, c_far, d_gate)
+    input_keep, input_out, mixed_sides, mixed_got, c_far, act_far, d_gate = fence(
+        input_keep, input_out, mixed_sides, mixed_got, c_far, act_far, d_gate)
 
     input_got = [send(part, 1) for part in input_out[:2]]
     mixed_landed = fold_upper(back_rows(pair_sums(mixed_keep, mixed_got[1], folds), mixed_sides))

time: 168 us -> 166 us (0.988)
  waiting for transfers between devices: 36 us -> 33.1 us
    ppermute x9, waiting for transfers between devices: 7.89 us -> 5.01 us  [swap(): return lax.ppermute(value, 'dp', [(i, i ^ bit) for i in range(count)])]
    unnamed x56 -> x54, local copies, waits for them, and re-layouts: 3.99 us -> 2.36 us
  transfers between devices with their start and end apart: 35 -> 35, of which waited for: 9 -> 7; matrix products, arithmetic and copies ran while one was open for 10% -> 11% of each run, Pallas kernels for 38% -> 39%
where the time goes in v6:
time: 166 us; the launch traced here: 165 us
  Pallas kernels  64.2 us (39%)
  starting transfers between devices  42.2 us (25%)
  waiting for transfers between devices  33.1 us (20%)
  other arithmetic  18.5 us (11%)
  local copies, waits for them, and re-layouts  5.79 us (3%)
    ppermute x26, starting transfers between devices, exchange(): return lax.ppermute(value, 'expert', [(i, i ^ bit) for i in range(count)])  33.8 us
    ppermute x26, waiting for transfers between devices, exchange(): return lax.ppermute(value, 'expert', [(i, i ^ bit) for i in range(count)])  28.1 us
    pallas_call x1, Pallas kernels, shards(): pl.pallas_call(functools.partial(hidden_kernel, cfg), grid=(local,), in_s...  12.9 us
    pallas_call x1, Pallas kernels, shards(): pl.pallas_call(functools.partial(grad_kernel, cfg), grid=(local,), in_spe...  11.4 us
    pallas_call x1, Pallas kernels, shards(): pl.pallas_call(functools.partial(input_kernel, (plan, local, cap, cap_pad...  11 us
    pallas_call x1, Pallas kernels, shards(): pl.pallas_call(functools.partial(down_kernel, cap), grid=(local,), in_spe...  9.81 us
    pallas_call x1, Pallas kernels, shards(): pl.pallas_call(functools.partial(mixed_kernel, (plan, levels, local, cap,...  9.53 us
    ppermute x9, starting transfers between devices, swap(): return lax.ppermute(value, 'dp', [(i, i ^ bit) for i in range(count)])  8.36 us
  transfers between devices with their start and end apart: 35, of which 7 were waited for; matrix products, arithmetic and copies ran while one was open for 11% of the time, Pallas kernels for 39%

profile of v6, /device:TPU:0, one launch (start us, length us, event | category | flops | bytes accessed | tf_op | source)
XLA Modules:
  0.0 164.8 jit_solution(4329817760474870801)
XLA Ops:
  0.6 0.8 copy.16
  1.5 0.7 reduce_sum.18
  2.2 0.7 convert_element_type.113
  2.9 0.1 copy.18
  3.1 1.0 pad_maximum_fusion.refs_0_
  4.1 3.1 %collective-permute-start = (bf16[64,2176]{1,0:T(8,128)(2,1)S(1)}, bf16[64,2176]{1,0:T(8,128)(2,1)S(1)}, u32[]{:S(2)}, u32[]{:S(2)}) collective-permute-start(bf16[64,2176]{1,0:T(8,128)(2,1)S(1)} %pad_maximum_fusion.refs_0_), channel_id=1, source_target_pairs={{0,8},{4,12},{8,0},{12,4},{16,24},{20,28},{24,16},{28,20},{1,9},{5... | collective-permute-start | bytes 835592 | tf_op jit(solution)/shard_map/ppermute | solution.py:274
  7.2 2.6 %collective-permute-start.1 = (bf16[64,2176]{1,0:T(8,128)(2,1)S(1)}, bf16[64,2176]{1,0:T(8,128)(2,1)S(1)}, u32[]{:S(2)}, u32[]{:S(2)}) collective-permute-start(bf16[64,2176]{1,0:T(8,128)(2,1)S(1)} %pad_maximum_fusion.refs_0_), channel_id=1, source_target_pairs={{0,16},{4,20},{8,24},{12,28},{16,0},{20,4},{24,8},{28,12},{1,17},{... | collective-permute-start | bytes 835592 | tf_op jit(solution)/shard_map/ppermute | solution.py:274
  9.8 1.5 collective-permute-start.2
  11.3 8.4 %collective-permute-done.refs_1_ = bf16[64,2176]{1,0:T(8,128)(2,1)S(1)} collective-permute-done((bf16[64,2176]{1,0:T(8,128)(2,1)S(1)}, bf16[64,2176]{1,0:T(8,128)(2,1)S(1)}, u32[]{:S(2)}, u32[]{:S(2)}) %collective-permute-start) | collective-permute-done | bytes 278560 | tf_op jit(solution)/shard_map/ppermute | solution.py:274
  19.7 2.5 %collective-permute-done.1.refs_2_ = bf16[64,2176]{1,0:T(8,128)(2,1)S(1)} collective-permute-done((bf16[64,2176]{1,0:T(8,128)(2,1)S(1)}, bf16[64,2176]{1,0:T(8,128)(2,1)S(1)}, u32[]{:S(2)}, u32[]{:S(2)}) %collective-permute-start.1) | collective-permute-done | bytes 278560 | tf_op jit(solution)/shard_map/ppermute | solution.py:274
  22.3 0.5 collective-permute-start.3
  22.8 1.5 collective-permute-start.5
  24.3 0.5 collective-permute-start.6
  24.8 2.7 %collective-permute-start.4 = (bf16[64,2048]{1,0:T(8,128)(2,1)}, bf16[64,2048]{1,0:T(8,128)(2,1)S(1)}, u32[]{:S(2)}, u32[]{:S(2)}) collective-permute-start(bf16[64,2048]{1,0:T(8,128)(2,1)} %refs_0_.1), channel_id=1, source_target_pairs={{0,16},{4,20},{8,24},{12,28},{16,0},{20,4},{24,8},{28,12},{1,17},{... | collective-permute-start | bytes 786440 | tf_op jit(solution)/shard_map/ppermute | solution.py:274
  27.5 10.3 %collective-permute-done.4.refs_2_ = bf16[64,2048]{1,0:T(8,128)(2,1)S(1)} collective-permute-done((bf16[64,2048]{1,0:T(8,128)(2,1)}, bf16[64,2048]{1,0:T(8,128)(2,1)S(1)}, u32[]{:S(2)}, u32[]{:S(2)}) %collective-permute-start.4) | collective-permute-done | bytes 262176 | tf_op jit(solution)/shard_map/ppermute | solution.py:274
  37.8 1.6 collective-permute-start.7
  39.4 1.9 %cut_x.1 = bf16[256,1024]{1,0:T(8,128)(2,1)} custom-call(s32[1]{0:T(128)} %bitcast.1.far_ref.word_ref, bf16[64,2176]{1,0:T(8,128)(2,1)} %copy-done.1, bf16[64,2176]{1,0:T(8,128)(2,1)} %copy-done.6, bf16[64,2176]{1,0:T(8,128)(2,1)} %copy-done.7, bf16[64,2176]{1,0:T(8,128)(2,1)} %copy-done.8), custom_call_target="tpu_custom_call" | custom-call | bytes 2000 | tf_op jit(solution)/shard_map/cut_x/pallas_call | solution.py:350
  41.3 1.6 collective-permute-start.12
  42.9 0.6 collective-permute-start.10
  43.6 2.0 %collective-permute-start.9 = (bf16[64,2048]{1,0:T(8,128)(2,1)S(1)}, bf16[64,2048]{1,0:T(8,128)(2,1)S(1)}, u32[]{:S(2)}, u32[]{:S(2)}) collective-permute-start(bf16[64,2048]{1,0:T(8,128)(2,1)S(1)} %collective-permute-done.4.refs_2_), channel_id=1, source_target_pairs={{0,8},{4,12},{8,0},{12,4},{16,24},{20,28},{24,16},{28,20},{1,9},{5... | collective-permute-start | bytes 786440 | tf_op jit(solution)/shard_map/ppermute | solution.py:274
  45.6 0.9 collective-permute-done.7.refs_7_
  46.4 2.1 %collective-permute-start.11 = (bf16[64,2048]{1,0:T(8,128)(2,1)S(1)}, bf16[64,2048]{1,0:T(8,128)(2,1)S(1)}, u32[]{:S(2)}, u32[]{:S(2)}) collective-permute-start(bf16[64,2048]{1,0:T(8,128)(2,1)S(1)} %collective-permute-done.4.refs_2_), channel_id=1, source_target_pairs={{0,4},{4,0},{8,12},{12,8},{16,20},{20,16},{24,28},{28,24},{1,5},{5... | collective-permute-start | bytes 786440 | tf_op jit(solution)/shard_map/ppermute | solution.py:274
  48.6 12.9 %hidden.1 = (f32[4,160,768]{2,1,0:T(8,128)}, bf16[4,160,512]{2,1,0:T(8,128)(2,1)}, f32[4,160,128]{2,1,0:T(8,128)}, bf16[640,512]{1,0:T(8,128)(2,1)}, bf16[512,10...) custom-call(s32[1]{0:T(128)} %bitcast.first_ref, s32[1]{0:T(128)} %bitcast.1.far_ref.word_ref, ...), custom_call_target="tpu_custom_call" | custom-call | flops 6000000 | bytes 20000 | tf_op jit(solution)/shard_map/hidden/pallas_call | solution.py:389
  61.5 2.0 %collective-permute-start.15 = (bf16[256,1024]{1,0:T(8,128)(2,1)}, bf16[256,1024]{1,0:T(8,128)(2,1)S(1)}, u32[]{:S(2)}, u32[]{:S(2)}) collective-permute-start(bf16[256,1024]{1,0:T(8,128)(2,1)} %get-tuple-element.131), channel_id=1, source_target_pairs={{0,2},{1,3},{2,0},{3,1},{4,6},{5,7},{6,4},{7,5},{8,10},{9,11},{10,... | collective-permute-start | bytes 1572872 | tf_op jit(solution)/shard_map/ppermute | solution.py:270
  63.6 0.7 collective-permute-start.13
  64.3 1.4 collective-permute-start.14
  65.7 9.5 %mixed.1 = (bf16[256,2048]{1,0:T(8,128)(2,1)}, bf16[64,2048]{1,0:T(8,128)(2,1)}, bf16[64,2048]{1,0:T(8,128)(2,1)}, bf16[128,2048]{1,0:T(8,128)(2,1)}, bf16[256,1024]{1,0:T(8,128)(2,1)}) custom-call(s32[1]{0:T(128)} %bitcast.1.far_ref.word_ref, bf16[4,160,512]{2,1,0:T(8,128)(2,1)} %get-tuple-element.122.act_ref.refs_6_, ...), custom_call_target="tpu_custom_call" | custom-call | flops 6000000 | bytes 10000 | tf_op jit(solution)/shard_map/mixed/pallas_call | solution.py:414
  75.3 0.7 collective-permute-start.16
  76.1 1.4 collective-permute-start.17
  77.5 2.0 %collective-permute-start.20 = (bf16[256,1024]{1,0:T(8,128)(2,1)}, bf16[256,1024]{1,0:T(8,128)(2,1)}, u32[]{:S(2)}, u32[]{:S(2)}) collective-permute-start(bf16[256,1024]{1,0:T(8,128)(2,1)} %get-tuple-element.157), channel_id=1, source_target_pairs={{0,2},{1,3},{2,0},{3,1},{4,6},{5,7},{6,4},{7,5},{8,10},{9,11},{10,... | collective-permute-start | bytes 1572872 | tf_op jit(solution)/shard_map/ppermute | solution.py:270
  79.5 11.4 %hidden_grads.1 = (bf16[4,160,384]{2,1,0:T(8,128)(2,1)}, bf16[4,160,384]{2,1,0:T(8,128)(2,1)}, bf16[512,128]{1,0:T(8,128)(2,1)}, bf16[512,1024]{1,0:T(8,128)(2,1)}, bf16[256,1024]{1,0:T(8,128)(2,1)}) custom-call(s32[1]{0:T(128)} %bitcast.1.far_ref.word_ref, bf16[64,2048]{1,0:T(8,128)(2,1)} %refs_0_.1, bf16[64,2048]{1,0:T(8,128)(2,1)} %copy-done.11, ...), custom_call_target="tpu_custom_call" | custom-call | flops 6000000 | bytes 12000 | tf_op jit(solution)/shard_map/hidden_grads/pallas_call | solution.py:451
  90.8 0.8 add_convert_fusion.6
  91.6 0.6 collective-permute-start.19
  92.3 0.7 fusion.11
  93.1 11.0 %input_grads.1 = (bf16[256,2176]{1,0:T(8,128)(2,1)}, bf16[64,2176]{1,0:T(8,128)(2,1)}, bf16[64,2176]{1,0:T(8,128)(2,1)}, bf16[128,2176]{1,0:T(8,128)(2,1)}) custom-call(bf16[4,160,384]{2,1,0:T(8,128)(2,1)} %get-tuple-element.182.d_gate_ref, bf16[4,160,384]{2,1,0:T(8,128)(2,1)} %get-tuple-element.183.d_up_ref, ...), custom_call_target="tpu_custom_call" | custom-call | flops 6000000 | bytes 16000 | tf_op jit(solution)/shard_map/input_grads/pallas_call | solution.py:476
  104.1 1.4 collective-permute-start.22
  105.5 0.7 collective-permute-start.24
  106.2 1.8 %add_convert_fusion.5 = bf16[64,2048]{1,0:T(8,128)(2,1)} fusion(bf16[64,2048]{1,0:T(8,128)(2,1)} %collective-permute-done.18, bf16[64,2048]{1,0:T(8,128)(2,1)S(1)} %collective-permute-done.17, bf16[256,2048]{1,0:T(8,128)(2,1)S(1)} %copy-done.13), kind=kLoop, calls=%fused_computation.14 | loop fusion | flops 786432 | bytes 1048576 | tf_op jit(solution)/shard_map/convert_element_type | solution.py:439
  108.0 2.6 %collective-permute-start.26 = (bf16[64,2048]{1,0:T(8,128)(2,1)}, bf16[64,2048]{1,0:T(8,128)(2,1)}, u32[]{:S(2)}, u32[]{:S(2)}) collective-permute-start(bf16[64,2048]{1,0:T(8,128)(2,1)} %add_convert_fusion.5), channel_id=1, source_target_pairs={{0,16},{4,20},{8,24},{12,28},{16,0},{20,4},{24,8},{28,12},{1,17},{... | collective-permute-start | bytes 786440 | tf_op jit(solution)/shard_map/ppermute | solution.py:274
  110.6 1.1 fusion.10
  111.7 2.1 %collective-permute-start.30 = (bf16[4,160,384]{2,1,0:T(8,128)(2,1)S(1)}, bf16[4,160,384]{2,1,0:T(8,128)(2,1)}, u32[]{:S(2)}, u32[]{:S(2)}) collective-permute-start(bf16[4,160,384]{2,1,0:T(8,128)(2,1)S(1)} %copy-done.2), channel_id=1, source_target_pairs={{0,2},{1,3},{2,0},{3,1},{4,6},{5,7},{6,4},{7,5},{8,10},{9,11},{10,... | collective-permute-start | bytes 1474568 | tf_op jit(solution)/shard_map/ppermute | solution.py:270
  113.8 0.8 add_convert_fusion.4
  114.6 1.2 convert_add_fusion.1
  115.8 0.7 slice.132
  116.5 2.0 %collective-permute-start.27 = (bf16[64,2048]{1,0:T(8,128)(2,1)}, bf16[64,2048]{1,0:T(8,128)(2,1)}, u32[]{:S(2)}, u32[]{:S(2)}) collective-permute-start(bf16[64,2048]{1,0:T(8,128)(2,1)} %slice.132), channel_id=1, source_target_pairs={{0,8},{4,12},{8,0},{12,4},{16,24},{20,28},{24,16},{28,20},{1,9},{5... | collective-permute-start | bytes 786440 | tf_op jit(solution)/shard_map/ppermute | solution.py:274
  118.5 9.8 %down_grads.1 = (bf16[4,320,1024]{2,1,0:T(8,128)(2,1)}, bf16[4,512,384]{2,1,0:T(8,128)(2,1)}, bf16[4,512,384]{2,1,0:T(8,128)(2,1)}) custom-call(s32[1]{0:T(128)} %bitcast.2.near_ref, bf16[640,512]{1,0:T(8,128)(2,1)} %get-tuple-element.140.refs_8_.pick_ref, bf16[512,1024]{1,0:T(8,128)(2,1)} %get-tuple-element.169.refs_0_, bf16[256,1024]{1,0:T(8,128)(2,1)} %copy-done.15, ...), custom_call_target="tpu_custom_call" | custom-call | flops 6000000 | bytes 12000 | tf_op jit(solution)/shard_map/down_grads/pallas_call | solution.py:502
  128.3 1.7 %collective-permute-start.28 = (bf16[128,2176]{1,0:T(8,128)(2,1)}, bf16[128,2176]{1,0:T(8,128)(2,1)S(1)}, u32[]{:S(2)}, u32[]{:S(2)}) collective-permute-start(bf16[128,2176]{1,0:T(8,128)(2,1)} %get-tuple-element.180), channel_id=1, source_target_pairs={{0,4},{4,0},{8,12},{12,8},{16,20},{20,16},{24,28},{28,24},{1,5},{5... | collective-permute-start | bytes 1671176 | tf_op jit(solution)/shard_map/ppermute | solution.py:274
  130.1 1.2 add_convert_fusion.3
  131.3 1.8 %collective-permute-start.29 = (bf16[64,2176]{1,0:T(8,128)(2,1)S(1)}, bf16[64,2176]{1,0:T(8,128)(2,1)}, u32[]{:S(2)}, u32[]{:S(2)}) collective-permute-start(bf16[64,2176]{1,0:T(8,128)(2,1)S(1)} %add_convert_fusion.3), channel_id=1, source_target_pairs={{0,16},{4,20},{8,24},{12,28},{16,0},{20,4},{24,8},{28,12},{1,17},{... | collective-permute-start | bytes 835592 | tf_op jit(solution)/shard_map/ppermute | solution.py:274
  133.1 5.1 %collective-permute-done.28 = bf16[128,2176]{1,0:T(8,128)(2,1)S(1)} collective-permute-done((bf16[128,2176]{1,0:T(8,128)(2,1)}, bf16[128,2176]{1,0:T(8,128)(2,1)S(1)}, u32[]{:S(2)}, u32[]{:S(2)}) %collective-permute-start.28) | collective-permute-done | bytes 557088 | tf_op jit(solution)/shard_map/ppermute | solution.py:274
  138.2 0.1 convert_add_fusion
  138.4 1.8 %fusion.1 = bf16[64,2048]{1,0:T(8,128)(2,1)} fusion(f32[128,2048]{1,0:T(8,128)S(1)} %convert_add_fusion.1, bf16[64,2048]{1,0:T(8,128)(2,1)} %collective-permute-done.27, bf16[64,2048]{1,0:T(8,128)(2,1)} %collective-permute-done.26), kind=kLoop, calls=%fused_computation.13 | loop fusion | flops 655360 | bytes 1310720 | tf_op jit(solution)/shard_map/convert_element_type | solution.py:523
  140.2 0.8 copy-done.17
  141.0 0.8 collective-permute-done.29
  141.9 7.7 %gate_up_grads.1 = (bf16[4,512,768]{2,1,0:T(8,128)(2,1)}, bf16[4,512,768]{2,1,0:T(8,128)(2,1)}) custom-call(s32[1]{0:T(128)} %bitcast.2.near_ref, bf16[4,320,1024]{2,1,0:T(8,128)(2,1)} %get-tuple-element.186.rows_ref, bf16[4,160,384]{2,1,0:T(8,128)(2,1)} %get-tuple-element.182.d_gate_ref, bf16[4,160,384]{2,1,0:T(8,128)(2,1)} %collective-permute-done.30.gate_far_ref, ...), custom_call_target="tpu_custom_call" | custom-call | flops 3000000 | bytes 10000 | tf_op jit(solution)/shard_map/gate_up_grads/pallas_call | solution.py:527
  149.7 0.5 collective-permute-start.34
  150.1 1.1 convert_add_fusion.2
  151.2 0.7 slice.131
  151.9 0.2 multiply_reduce_fusion
  152.1 0.1 subtract_divide_fusion
  152.2 0.7 copy.20
  152.9 5.0 %collective-permute-done.33 = bf16[4,512,768]{2,1,0:T(8,128)(2,1)} collective-permute-done((bf16[4,512,768]{2,1,0:T(8,128)(2,1)}, bf16[4,512,768]{2,1,0:T(8,128)(2,1)}, u32[]{:S(2)}, u32[]{:S(2)}) %collective-permute-start.33) | collective-permute-done | bytes 3145760 | tf_op jit(solution)/shard_map/ppermute | solution.py:270
  157.9 5.4 %add_convert_fusion.1 = (bf16[4,512,384]{2,1,0:T(8,128)(2,1)}, bf16[4,512,384]{2,1,0:T(8,128)(2,1)}) fusion(bf16[4,512,768]{2,1,0:T(8,128)(2,1)} %collective-permute-done.33, bf16[4,512,768]{2,1,0:T(8,128)(2,1)} %get-tuple-element.193), kind=kLoop, calls=%fused_computation.1 | loop fusion | flops 6291456 | bytes 9437184 | tf_op jit(solution)/shard_map/convert_element_type | solution.py:541
  163.3 1.6 add_convert_fusion
  (90 shorter events, 0.7 us)
Async XLA Ops:
  0.6 42.3 %copy-start.9 = (bf16[64,2048]{1,0:T(8,128)(2,1)S(1)}, bf16[64,2048]{1,0:T(8,128)(2,1)}, u32[]{:S(2)}) copy-start(bf16[64,2048]{1,0:T(8,128)(2,1)} %refs_0_.1) | copy-start | bytes 786436
  4.1 35.3 %copy-start.1 = (bf16[64,2176]{1,0:T(8,128)(2,1)}, bf16[64,2176]{1,0:T(8,128)(2,1)S(1)}, u32[]{:S(2)}) copy-start(bf16[64,2176]{1,0:T(8,128)(2,1)S(1)} %pad_maximum_fusion.refs_0_) | copy-start | bytes 835588
  4.1 15.6 %collective-permute-start = (bf16[64,2176]{1,0:T(8,128)(2,1)S(1)}, bf16[64,2176]{1,0:T(8,128)(2,1)S(1)}, u32[]{:S(2)}, u32[]{:S(2)}) collective-permute-start(bf16[64,2176]{1,0:T(8,128)(2,1)S(1)} %pad_maximum_fusion.refs_0_), channel_id=1, source_target_pairs={{0,8},{4,12},{8,0},{12,4},{16,24},{20,28},{24,16},{28,20},{1,9},{5... | collective-permute-start | bytes 835592 | tf_op jit(solution)/shard_map/ppermute | solution.py:274
  7.2 15.0 %collective-permute-start.1 = (bf16[64,2176]{1,0:T(8,128)(2,1)S(1)}, bf16[64,2176]{1,0:T(8,128)(2,1)S(1)}, u32[]{:S(2)}, u32[]{:S(2)}) collective-permute-start(bf16[64,2176]{1,0:T(8,128)(2,1)S(1)} %pad_maximum_fusion.refs_0_), channel_id=1, source_target_pairs={{0,16},{4,20},{8,24},{12,28},{16,0},{20,4},{24,8},{28,12},{1,17},{... | collective-permute-start | bytes 835592 | tf_op jit(solution)/shard_map/ppermute | solution.py:274
  9.8 12.4 %collective-permute-start.2 = (bf16[64,2176]{1,0:T(8,128)(2,1)S(1)}, bf16[64,2176]{1,0:T(8,128)(2,1)S(1)}, u32[]{:S(2)}, u32[]{:S(2)}) collective-permute-start(bf16[64,2176]{1,0:T(8,128)(2,1)S(1)} %pad_maximum_fusion.refs_0_), channel_id=1, source_target_pairs={{0,4},{4,0},{8,12},{12,8},{16,20},{20,16},{24,28},{28,24},{1,5},{5... | collective-permute-start | bytes 835592 | tf_op jit(solution)/shard_map/ppermute | solution.py:274
  19.7 19.7 %copy-start.6 = (bf16[64,2176]{1,0:T(8,128)(2,1)}, bf16[64,2176]{1,0:T(8,128)(2,1)S(1)}, u32[]{:S(2)}) copy-start(bf16[64,2176]{1,0:T(8,128)(2,1)S(1)} %collective-permute-done.refs_1_) | copy-start | bytes 835588
  22.3 17.2 %copy-start.7 = (bf16[64,2176]{1,0:T(8,128)(2,1)}, bf16[64,2176]{1,0:T(8,128)(2,1)S(1)}, u32[]{:S(2)}) copy-start(bf16[64,2176]{1,0:T(8,128)(2,1)S(1)} %collective-permute-done.1.refs_2_) | copy-start | bytes 835588
  22.3 26.3 %copy-start.18 = (bf16[64,2176]{1,0:T(8,128)(2,1)}, bf16[64,2176]{1,0:T(8,128)(2,1)S(1)}, u32[]{:S(2)}) copy-start(bf16[64,2176]{1,0:T(8,128)(2,1)S(1)} %collective-permute-done.2.refs_4_) | copy-start | bytes 835588
  22.3 15.5 %collective-permute-start.3 = (bf16[64,2176]{1,0:T(8,128)(2,1)S(1)}, bf16[64,2176]{1,0:T(8,128)(2,1)S(1)}, u32[]{:S(2)}, u32[]{:S(2)}) collective-permute-start(bf16[64,2176]{1,0:T(8,128)(2,1)S(1)} %collective-permute-done.1.refs_2_), channel_id=1, source_target_pairs={{0,8},{4,12},{8,0},{12,4},{16,24},{20,28},{24,16},{28,20},{1,9},{5... | collective-permute-start | bytes 835592 | tf_op jit(solution)/shard_map/ppermute | solution.py:274
  22.8 15.0 %collective-permute-start.5 = (bf16[64,2176]{1,0:T(8,128)(2,1)S(1)}, bf16[64,2176]{1,0:T(8,128)(2,1)S(1)}, u32[]{:S(2)}, u32[]{:S(2)}) collective-permute-start(bf16[64,2176]{1,0:T(8,128)(2,1)S(1)} %collective-permute-done.refs_1_), channel_id=1, source_target_pairs={{0,4},{4,0},{8,12},{12,8},{16,20},{20,16},{24,28},{28,24},{1,5},{5... | collective-permute-start | bytes 835592 | tf_op jit(solution)/shard_map/ppermute | solution.py:274
  24.3 13.6 %collective-permute-start.6 = (bf16[64,2176]{1,0:T(8,128)(2,1)S(1)}, bf16[64,2176]{1,0:T(8,128)(2,1)S(1)}, u32[]{:S(2)}, u32[]{:S(2)}) collective-permute-start(bf16[64,2176]{1,0:T(8,128)(2,1)S(1)} %collective-permute-done.1.refs_2_), channel_id=1, source_target_pairs={{0,4},{4,0},{8,12},{12,8},{16,20},{20,16},{24,28},{28,24},{1,5},{5... | collective-permute-start | bytes 835592 | tf_op jit(solution)/shard_map/ppermute | solution.py:274
  24.8 13.0 %collective-permute-start.4 = (bf16[64,2048]{1,0:T(8,128)(2,1)}, bf16[64,2048]{1,0:T(8,128)(2,1)S(1)}, u32[]{:S(2)}, u32[]{:S(2)}) collective-permute-start(bf16[64,2048]{1,0:T(8,128)(2,1)} %refs_0_.1), channel_id=1, source_target_pairs={{0,16},{4,20},{8,24},{12,28},{16,0},{20,4},{24,8},{28,12},{1,17},{... | collective-permute-start | bytes 786440 | tf_op jit(solution)/shard_map/ppermute | solution.py:274
  37.8 23.7 %copy-start.10 = (bf16[64,2048]{1,0:T(8,128)(2,1)}, bf16[64,2048]{1,0:T(8,128)(2,1)S(1)}, u32[]{:S(2)}) copy-start(bf16[64,2048]{1,0:T(8,128)(2,1)S(1)} %collective-permute-done.4.refs_2_) | copy-start | bytes 786436
  37.8 1.6 copy-start.8
  37.8 10.7 %copy-start.19 = (bf16[64,2176]{1,0:T(8,128)(2,1)}, bf16[64,2176]{1,0:T(8,128)(2,1)S(1)}, u32[]{:S(2)}) copy-start(bf16[64,2176]{1,0:T(8,128)(2,1)S(1)} %collective-permute-done.5.refs_5_) | copy-start | bytes 835588
  37.8 10.7 %copy-start.20 = (bf16[64,2176]{1,0:T(8,128)(2,1)}, bf16[64,2176]{1,0:T(8,128)(2,1)S(1)}, u32[]{:S(2)}) copy-start(bf16[64,2176]{1,0:T(8,128)(2,1)S(1)} %collective-permute-done.6.refs_6_) | copy-start | bytes 835588
  37.8 8.6 %collective-permute-start.7 = (bf16[64,2176]{1,0:T(8,128)(2,1)S(1)}, bf16[64,2176]{1,0:T(8,128)(2,1)S(1)}, u32[]{:S(2)}, u32[]{:S(2)}) collective-permute-start(bf16[64,2176]{1,0:T(8,128)(2,1)S(1)} %collective-permute-done.3.refs_3_), channel_id=1, source_target_pairs={{0,4},{4,0},{8,12},{12,8},{16,20},{20,16},{24,28},{28,24},{1,5},{5... | collective-permute-start | bytes 835592 | tf_op jit(solution)/shard_map/ppermute | solution.py:274
  41.3 22.2 %collective-permute-start.12 = (bf16[256,1024]{1,0:T(8,128)(2,1)}, bf16[256,1024]{1,0:T(8,128)(2,1)S(1)}, u32[]{:S(2)}, u32[]{:S(2)}) collective-permute-start(bf16[256,1024]{1,0:T(8,128)(2,1)} %cut_x.1), channel_id=1, source_target_pairs={{0,2},{1,3},{2,0},{3,1},{4,6},{5,7},{6,4},{7,5},{8,10},{9,11},{10,... | collective-permute-start | bytes 1572872 | tf_op jit(solution)/shard_map/ppermute | solution.py:270
  42.9 18.5 %collective-permute-start.8 = (bf16[64,2048]{1,0:T(8,128)(2,1)S(1)}, bf16[64,2048]{1,0:T(8,128)(2,1)S(1)}, u32[]{:S(2)}, u32[]{:S(2)}) collective-permute-start(bf16[64,2048]{1,0:T(8,128)(2,1)S(1)} %copy-done.9), channel_id=1, source_target_pairs={{0,8},{4,12},{8,0},{12,4},{16,24},{20,28},{24,16},{28,20},{1,9},{5... | collective-permute-start | bytes 786440 | tf_op jit(solution)/shard_map/ppermute | solution.py:274
  42.9 20.6 %collective-permute-start.10 = (bf16[64,2048]{1,0:T(8,128)(2,1)S(1)}, bf16[64,2048]{1,0:T(8,128)(2,1)S(1)}, u32[]{:S(2)}, u32[]{:S(2)}) collective-permute-start(bf16[64,2048]{1,0:T(8,128)(2,1)S(1)} %copy-done.9), channel_id=1, source_target_pairs={{0,4},{4,0},{8,12},{12,8},{16,20},{20,16},{24,28},{28,24},{1,5},{5... | collective-permute-start | bytes 786440 | tf_op jit(solution)/shard_map/ppermute | solution.py:274
  43.6 20.0 %collective-permute-start.9 = (bf16[64,2048]{1,0:T(8,128)(2,1)S(1)}, bf16[64,2048]{1,0:T(8,128)(2,1)S(1)}, u32[]{:S(2)}, u32[]{:S(2)}) collective-permute-start(bf16[64,2048]{1,0:T(8,128)(2,1)S(1)} %collective-permute-done.4.refs_2_), channel_id=1, source_target_pairs={{0,8},{4,12},{8,0},{12,4},{16,24},{20,28},{24,16},{28,20},{1,9},{5... | collective-permute-start | bytes 786440 | tf_op jit(solution)/shard_map/ppermute | solution.py:274
  46.4 2.1 %copy-start.21 = (bf16[64,2176]{1,0:T(8,128)(2,1)}, bf16[64,2176]{1,0:T(8,128)(2,1)S(1)}, u32[]{:S(2)}) copy-start(bf16[64,2176]{1,0:T(8,128)(2,1)S(1)} %collective-permute-done.7.refs_7_) | copy-start | bytes 835588
  46.4 17.1 %collective-permute-start.11 = (bf16[64,2048]{1,0:T(8,128)(2,1)S(1)}, bf16[64,2048]{1,0:T(8,128)(2,1)S(1)}, u32[]{:S(2)}, u32[]{:S(2)}) collective-permute-start(bf16[64,2048]{1,0:T(8,128)(2,1)S(1)} %collective-permute-done.4.refs_2_), channel_id=1, source_target_pairs={{0,4},{4,0},{8,12},{12,8},{16,20},{20,16},{24,28},{28,24},{1,5},{5... | collective-permute-start | bytes 786440 | tf_op jit(solution)/shard_map/ppermute | solution.py:274
  61.5 4.2 %copy-start.11 = (bf16[64,2048]{1,0:T(8,128)(2,1)}, bf16[64,2048]{1,0:T(8,128)(2,1)S(1)}, u32[]{:S(2)}) copy-start(bf16[64,2048]{1,0:T(8,128)(2,1)S(1)} %collective-permute-done.8.refs_1_) | copy-start | bytes 786436
  61.5 13.8 %collective-permute-start.15 = (bf16[256,1024]{1,0:T(8,128)(2,1)}, bf16[256,1024]{1,0:T(8,128)(2,1)S(1)}, u32[]{:S(2)}, u32[]{:S(2)}) collective-permute-start(bf16[256,1024]{1,0:T(8,128)(2,1)} %get-tuple-element.131), channel_id=1, source_target_pairs={{0,2},{1,3},{2,0},{3,1},{4,6},{5,7},{6,4},{7,5},{8,10},{9,11},{10,... | collective-permute-start | bytes 1572872 | tf_op jit(solution)/shard_map/ppermute | solution.py:270
  63.5 2.2 %copy-start.12 = (bf16[64,2048]{1,0:T(8,128)(2,1)}, bf16[64,2048]{1,0:T(8,128)(2,1)S(1)}, u32[]{:S(2)}) copy-start(bf16[64,2048]{1,0:T(8,128)(2,1)S(1)} %collective-permute-done.9.refs_3_) | copy-start | bytes 786436
  63.5 11.7 %copy-start.22 = (bf16[64,2048]{1,0:T(8,128)(2,1)}, bf16[64,2048]{1,0:T(8,128)(2,1)S(1)}, u32[]{:S(2)}) copy-start(bf16[64,2048]{1,0:T(8,128)(2,1)S(1)} %collective-permute-done.10.refs_4_) | copy-start | bytes 786436
  63.6 2.1 %copy-start.23 = (bf16[64,2048]{1,0:T(8,128)(2,1)}, bf16[64,2048]{1,0:T(8,128)(2,1)S(1)}, u32[]{:S(2)}) copy-start(bf16[64,2048]{1,0:T(8,128)(2,1)S(1)} %collective-permute-done.11.refs_6_) | copy-start | bytes 786436
  63.6 11.7 %copy-start.15 = (bf16[256,1024]{1,0:T(8,128)(2,1)}, bf16[256,1024]{1,0:T(8,128)(2,1)S(1)}, u32[]{:S(2)}) copy-start(bf16[256,1024]{1,0:T(8,128)(2,1)S(1)} %collective-permute-done.12.refs_1_) | copy-start | bytes 1572868
  63.6 11.7 %collective-permute-start.13 = (bf16[64,2048]{1,0:T(8,128)(2,1)S(1)}, bf16[64,2048]{1,0:T(8,128)(2,1)S(1)}, u32[]{:S(2)}, u32[]{:S(2)}) collective-permute-start(bf16[64,2048]{1,0:T(8,128)(2,1)S(1)} %collective-permute-done.8.refs_1_), channel_id=1, source_target_pairs={{0,4},{4,0},{8,12},{12,8},{16,20},{20,16},{24,28},{28,24},{1,5},{5... | collective-permute-start | bytes 786440 | tf_op jit(solution)/shard_map/ppermute | solution.py:274
  64.3 11.0 %collective-permute-start.14 = (bf16[64,2048]{1,0:T(8,128)(2,1)S(1)}, bf16[64,2048]{1,0:T(8,128)(2,1)S(1)}, u32[]{:S(2)}, u32[]{:S(2)}) collective-permute-start(bf16[64,2048]{1,0:T(8,128)(2,1)S(1)} %collective-permute-done.9.refs_3_), channel_id=1, source_target_pairs={{0,4},{4,0},{8,12},{12,8},{16,20},{20,16},{24,28},{28,24},{1,5},{5... | collective-permute-start | bytes 786440 | tf_op jit(solution)/shard_map/ppermute | solution.py:274
  65.7 10.3 %copy-start = (bf16[4,160,512]{2,1,0:T(8,128)(2,1)S(1)}, bf16[4,160,512]{2,1,0:T(8,128)(2,1)}, u32[]{:S(2)}) copy-start(bf16[4,160,512]{2,1,0:T(8,128)(2,1)} %get-tuple-element.122.act_ref.refs_6_) | copy-start | bytes 1966084
  75.3 4.2 %copy-start.24 = (bf16[64,2048]{1,0:T(8,128)(2,1)}, bf16[64,2048]{1,0:T(8,128)(2,1)S(1)}, u32[]{:S(2)}) copy-start(bf16[64,2048]{1,0:T(8,128)(2,1)S(1)} %collective-permute-done.13.refs_5_) | copy-start | bytes 786436
  75.3 4.2 %copy-start.25 = (bf16[64,2048]{1,0:T(8,128)(2,1)}, bf16[64,2048]{1,0:T(8,128)(2,1)S(1)}, u32[]{:S(2)}) copy-start(bf16[64,2048]{1,0:T(8,128)(2,1)S(1)} %collective-permute-done.14.refs_7_) | copy-start | bytes 786436
  75.3 15.5 %copy-start.16 = (bf16[256,1024]{1,0:T(8,128)(2,1)}, bf16[256,1024]{1,0:T(8,128)(2,1)S(1)}, u32[]{:S(2)}) copy-start(bf16[256,1024]{1,0:T(8,128)(2,1)S(1)} %collective-permute-done.15.refs_2_) | copy-start | bytes 1572868
  75.3 15.5 %collective-permute-start.16 = (bf16[64,2048]{1,0:T(8,128)(2,1)}, bf16[64,2048]{1,0:T(8,128)(2,1)S(1)}, u32[]{:S(2)}, u32[]{:S(2)}) collective-permute-start(bf16[64,2048]{1,0:T(8,128)(2,1)} %get-tuple-element.133), channel_id=1, source_target_pairs={{0,4},{4,0},{8,12},{12,8},{16,20},{20,16},{24,28},{28,24},{1,5},{5... | collective-permute-start | bytes 786440 | tf_op jit(solution)/shard_map/ppermute | solution.py:274
  76.1 28.0 %collective-permute-start.21 = (bf16[4,160,512]{2,1,0:T(8,128)(2,1)S(1)}, bf16[4,160,512]{2,1,0:T(8,128)(2,1)}, u32[]{:S(2)}, u32[]{:S(2)}) collective-permute-start(bf16[4,160,512]{2,1,0:T(8,128)(2,1)S(1)} %copy-done), channel_id=1, source_target_pairs={{0,2},{1,3},{2,0},{3,1},{4,6},{5,7},{6,4},{7,5},{8,10},{9,11},{10,... | collective-permute-start | bytes 1966088 | tf_op jit(solution)/shard_map/ppermute | solution.py:270
  76.1 15.5 %collective-permute-start.17 = (bf16[64,2048]{1,0:T(8,128)(2,1)}, bf16[64,2048]{1,0:T(8,128)(2,1)S(1)}, u32[]{:S(2)}, u32[]{:S(2)}) collective-permute-start(bf16[64,2048]{1,0:T(8,128)(2,1)} %get-tuple-element.134), channel_id=1, source_target_pairs={{0,4},{4,0},{8,12},{12,8},{16,20},{20,16},{24,28},{28,24},{1,5},{5... | collective-permute-start | bytes 786440 | tf_op jit(solution)/shard_map/ppermute | solution.py:274
  77.5 26.6 %collective-permute-start.20 = (bf16[256,1024]{1,0:T(8,128)(2,1)}, bf16[256,1024]{1,0:T(8,128)(2,1)}, u32[]{:S(2)}, u32[]{:S(2)}) collective-permute-start(bf16[256,1024]{1,0:T(8,128)(2,1)} %get-tuple-element.157), channel_id=1, source_target_pairs={{0,2},{1,3},{2,0},{3,1},{4,6},{5,7},{6,4},{7,5},{8,10},{9,11},{10,... | collective-permute-start | bytes 1572872 | tf_op jit(solution)/shard_map/ppermute | solution.py:270
  79.5 11.4 %copy-start.13 = (bf16[256,2048]{1,0:T(8,128)(2,1)S(1)}, bf16[256,2048]{1,0:T(8,128)(2,1)}, u32[]{:S(2)}) copy-start(bf16[256,2048]{1,0:T(8,128)(2,1)} %get-tuple-element.132) | copy-start | bytes 3145732
  91.6 12.5 %collective-permute-start.19 = (bf16[128,2048]{1,0:T(8,128)(2,1)}, bf16[128,2048]{1,0:T(8,128)(2,1)}, u32[]{:S(2)}, u32[]{:S(2)}) collective-permute-start(bf16[128,2048]{1,0:T(8,128)(2,1)} %get-tuple-element.156), channel_id=1, source_target_pairs={{0,4},{4,0},{8,12},{12,8},{16,20},{20,16},{24,28},{28,24},{1,5},{5... | collective-permute-start | bytes 1572872 | tf_op jit(solution)/shard_map/ppermute | solution.py:274
  92.3 11.8 %collective-permute-start.18 = (bf16[64,2048]{1,0:T(8,128)(2,1)}, bf16[64,2048]{1,0:T(8,128)(2,1)}, u32[]{:S(2)}, u32[]{:S(2)}) collective-permute-start(bf16[64,2048]{1,0:T(8,128)(2,1)} %add_convert_fusion.6), channel_id=1, source_target_pairs={{0,8},{4,12},{8,0},{12,4},{16,24},{20,28},{24,16},{28,20},{1,9},{5... | collective-permute-start | bytes 786440 | tf_op jit(solution)/shard_map/ppermute | solution.py:274
  93.0 21.5 %collective-permute-start.23 = (bf16[256,1024]{1,0:T(8,128)(2,1)}, bf16[256,1024]{1,0:T(8,128)(2,1)}, u32[]{:S(2)}, u32[]{:S(2)}) collective-permute-start(bf16[256,1024]{1,0:T(8,128)(2,1)} %get-tuple-element.162), channel_id=1, source_target_pairs={{0,2},{1,3},{2,0},{3,1},{4,6},{5,7},{6,4},{7,5},{8,10},{9,11},{10,... | collective-permute-start | bytes 1572872 | tf_op jit(solution)/shard_map/ppermute | solution.py:270
  104.1 7.6 %copy-start.2 = (bf16[4,160,384]{2,1,0:T(8,128)(2,1)S(1)}, bf16[4,160,384]{2,1,0:T(8,128)(2,1)}, u32[]{:S(2)}) copy-start(bf16[4,160,384]{2,1,0:T(8,128)(2,1)} %get-tuple-element.182.d_gate_ref) | copy-start | bytes 1474564
  104.1 9.7 %copy-start.5 = (bf16[256,2176]{1,0:T(8,128)(2,1)S(1)}, bf16[256,2176]{1,0:T(8,128)(2,1)}, u32[]{:S(2)}) copy-start(bf16[256,2176]{1,0:T(8,128)(2,1)} %get-tuple-element.158) | copy-start | bytes 3342340
  104.1 10.5 %copy-start.14 = (bf16[64,2048]{1,0:T(8,128)(2,1)S(1)}, bf16[64,2048]{1,0:T(8,128)(2,1)}, u32[]{:S(2)}) copy-start(bf16[64,2048]{1,0:T(8,128)(2,1)} %get-tuple-element.217) | copy-start | bytes 786436
  104.1 9.6 %collective-permute-start.22 = (bf16[64,2176]{1,0:T(8,128)(2,1)}, bf16[64,2176]{1,0:T(8,128)(2,1)S(1)}, u32[]{:S(2)}, u32[]{:S(2)}) collective-permute-start(bf16[64,2176]{1,0:T(8,128)(2,1)} %get-tuple-element.159), channel_id=1, source_target_pairs={{0,4},{4,0},{8,12},{12,8},{16,20},{20,16},{24,28},{28,24},{1,5},{5... | collective-permute-start | bytes 835592 | tf_op jit(solution)/shard_map/ppermute | solution.py:274
  105.5 22.8 %collective-permute-start.24 = (bf16[64,2176]{1,0:T(8,128)(2,1)}, bf16[64,2176]{1,0:T(8,128)(2,1)}, u32[]{:S(2)}, u32[]{:S(2)}) collective-permute-start(bf16[64,2176]{1,0:T(8,128)(2,1)} %get-tuple-element.160), channel_id=1, source_target_pairs={{0,4},{4,0},{8,12},{12,8},{16,20},{20,16},{24,28},{28,24},{1,5},{5... | collective-permute-start | bytes 835592 | tf_op jit(solution)/shard_map/ppermute | solution.py:274
  108.0 23.3 %collective-permute-start.26 = (bf16[64,2048]{1,0:T(8,128)(2,1)}, bf16[64,2048]{1,0:T(8,128)(2,1)}, u32[]{:S(2)}, u32[]{:S(2)}) collective-permute-start(bf16[64,2048]{1,0:T(8,128)(2,1)} %add_convert_fusion.5), channel_id=1, source_target_pairs={{0,16},{4,20},{8,24},{12,28},{16,0},{20,4},{24,8},{28,12},{1,17},{... | collective-permute-start | bytes 786440 | tf_op jit(solution)/shard_map/ppermute | solution.py:274
  111.7 28.5 %collective-permute-start.30 = (bf16[4,160,384]{2,1,0:T(8,128)(2,1)S(1)}, bf16[4,160,384]{2,1,0:T(8,128)(2,1)}, u32[]{:S(2)}, u32[]{:S(2)}) collective-permute-start(bf16[4,160,384]{2,1,0:T(8,128)(2,1)S(1)} %copy-done.2), channel_id=1, source_target_pairs={{0,2},{1,3},{2,0},{3,1},{4,6},{5,7},{6,4},{7,5},{8,10},{9,11},{10,... | collective-permute-start | bytes 1474568 | tf_op jit(solution)/shard_map/ppermute | solution.py:270
  114.5 15.5 %collective-permute-start.25 = (bf16[64,2176]{1,0:T(8,128)(2,1)}, bf16[64,2176]{1,0:T(8,128)(2,1)}, u32[]{:S(2)}, u32[]{:S(2)}) collective-permute-start(bf16[64,2176]{1,0:T(8,128)(2,1)} %add_convert_fusion.4), channel_id=1, source_target_pairs={{0,8},{4,12},{8,0},{12,4},{16,24},{20,28},{24,16},{28,20},{1,9},{5... | collective-permute-start | bytes 835592 | tf_op jit(solution)/shard_map/ppermute | solution.py:274
  116.5 21.9 %collective-permute-start.27 = (bf16[64,2048]{1,0:T(8,128)(2,1)}, bf16[64,2048]{1,0:T(8,128)(2,1)}, u32[]{:S(2)}, u32[]{:S(2)}) collective-permute-start(bf16[64,2048]{1,0:T(8,128)(2,1)} %slice.132), channel_id=1, source_target_pairs={{0,8},{4,12},{8,0},{12,4},{16,24},{20,28},{24,16},{28,20},{1,9},{5... | collective-permute-start | bytes 786440 | tf_op jit(solution)/shard_map/ppermute | solution.py:274
  118.5 11.5 %copy-start.3 = (bf16[4,160,384]{2,1,0:T(8,128)(2,1)S(1)}, bf16[4,160,384]{2,1,0:T(8,128)(2,1)}, u32[]{:S(2)}) copy-start(bf16[4,160,384]{2,1,0:T(8,128)(2,1)} %get-tuple-element.183.d_up_ref) | copy-start | bytes 1474564
  128.3 9.8 %collective-permute-start.28 = (bf16[128,2176]{1,0:T(8,128)(2,1)}, bf16[128,2176]{1,0:T(8,128)(2,1)S(1)}, u32[]{:S(2)}, u32[]{:S(2)}) collective-permute-start(bf16[128,2176]{1,0:T(8,128)(2,1)} %get-tuple-element.180), channel_id=1, source_target_pairs={{0,4},{4,0},{8,12},{12,8},{16,20},{20,16},{24,28},{28,24},{1,5},{5... | collective-permute-start | bytes 1671176 | tf_op jit(solution)/shard_map/ppermute | solution.py:274
  130.1 10.2 %collective-permute-start.31 = (bf16[4,160,384]{2,1,0:T(8,128)(2,1)S(1)}, bf16[4,160,384]{2,1,0:T(8,128)(2,1)S(1)}, u32[]{:S(2)}, u32[]{:S(2)}) collective-permute-start(bf16[4,160,384]{2,1,0:T(8,128)(2,1)S(1)} %copy-done.3), channel_id=1, source_target_pairs={{0,2},{1,3},{2,0},{3,1},{4,6},{5,7},{6,4},{7,5},{8,10},{9,11},{10,... | collective-permute-start | bytes 1474568 | tf_op jit(solution)/shard_map/ppermute | solution.py:270
  131.3 10.6 %collective-permute-start.29 = (bf16[64,2176]{1,0:T(8,128)(2,1)S(1)}, bf16[64,2176]{1,0:T(8,128)(2,1)}, u32[]{:S(2)}, u32[]{:S(2)}) collective-permute-start(bf16[64,2176]{1,0:T(8,128)(2,1)S(1)} %add_convert_fusion.3), channel_id=1, source_target_pairs={{0,16},{4,20},{8,24},{12,28},{16,0},{20,4},{24,8},{28,12},{1,17},{... | collective-permute-start | bytes 835592 | tf_op jit(solution)/shard_map/ppermute | solution.py:274
  138.3 11.3 %collective-permute-start.32 = (bf16[64,2176]{1,0:T(8,128)(2,1)S(1)}, bf16[64,2176]{1,0:T(8,128)(2,1)S(1)}, u32[]{:S(2)}, u32[]{:S(2)}) collective-permute-start(bf16[64,2176]{1,0:T(8,128)(2,1)S(1)} %slice.130), channel_id=1, source_target_pairs={{0,8},{4,12},{8,0},{12,4},{16,24},{20,28},{24,16},{28,20},{1,9},{5... | collective-permute-start | bytes 835592 | tf_op jit(solution)/shard_map/ppermute | solution.py:274
  140.2 0.8 copy-start.17
  149.6 8.3 %collective-permute-start.33 = (bf16[4,512,768]{2,1,0:T(8,128)(2,1)}, bf16[4,512,768]{2,1,0:T(8,128)(2,1)}, u32[]{:S(2)}, u32[]{:S(2)}) collective-permute-start(bf16[4,512,768]{2,1,0:T(8,128)(2,1)} %get-tuple-element.194), channel_id=1, source_target_pairs={{0,1},{1,0},{2,3},{3,2},{4,5},{5,4},{6,7},{7,6},{8,9},{9,8},{10,11... | collective-permute-start | bytes 9437192 | tf_op jit(solution)/shard_map/ppermute | solution.py:270
  149.7 13.6 %collective-permute-start.34 = (bf16[4,512,384]{2,1,0:T(8,128)(2,1)}, bf16[4,512,384]{2,1,0:T(8,128)(2,1)S(1)}, u32[]{:S(2)}, u32[]{:S(2)}) collective-permute-start(bf16[4,512,384]{2,1,0:T(8,128)(2,1)} %get-tuple-element.195), channel_id=1, source_target_pairs={{0,1},{1,0},{2,3},{3,2},{4,5},{5,4},{6,7},{7,6},{8,9},{9,8},{10,11... | collective-permute-start | bytes 4718600 | tf_op jit(solution)/shard_map/ppermute | solution.py:270
  157.9 5.4 %copy-start.4 = (bf16[4,512,384]{2,1,0:T(8,128)(2,1)S(1)}, bf16[4,512,384]{2,1,0:T(8,128)(2,1)}, u32[]{:S(2)}) copy-start(bf16[4,512,384]{2,1,0:T(8,128)(2,1)} %get-tuple-element.198) | copy-start | bytes 4718596
